TPU v7x, 256 devices: a whole 4x4x8 slice. The times are simulated.
256 devices in a mesh: tm: 4 (over z_lo, core), space: 64 (over y, z_hi, x).
Axes of the slice: x: 4, y: 4, z: 8 (z_hi: 4, z_lo: 2; z = z_hi * 2 + z_lo), core: 2. Of those that a mesh axis runs over, the one named last changes fastest.
Arguments:
- starts: float32 [4, 2, 256, 128, 128], P('tm', None, 'space'), may hold values from 0 to 1
- feed_rate: float32 [256, 128, 128], P('space'), may hold values from 0.02 to 0.2
- kill_rate: float32 [256, 128, 128], P('space'), may hold values from 0.04 to 0.2
Outputs:
- slice_ends: float32 [4, 2, 256, 128, 128], P('tm', None, 'space')
All inputs are finite; a program needn't handle non-finite values.
Results may differ from a plain program's by a relative error of at most 0.00002.
Values sent between devices are 32-bit elements; how exact they have to be, the bound alone decides.
No kernel may reach another device: no remote copies, remote signals or barrier semaphores. Data moves between devices by JAX's collectives and lax.ppermute only.
A program may use at most 64 MiB of HBM per device.

v0:
```python
import jax
import jax.numpy as jnp
from jax import lax
from jax.experimental import pallas as pl
from jax.experimental.pallas import tpu as pltpu
from jax.sharding import PartitionSpec as P

SUBSTEPS = 4
SWEEPS = 4
FINE_RATES = (0.4, 0.2)
TIME_STEP = 0.25
COARSE_STEP = SUBSTEPS * TIME_STEP
VMEM = pl.BlockSpec(memory_space=pltpu.VMEM)
SMEM = pl.BlockSpec(memory_space=pltpu.SMEM)
AXES = ("tm", "space")


def triple(values, axis):
    pairs = values + pltpu.roll(values, 1, axis)
    return pairs + pltpu.roll(pairs, values.shape[axis] - 1, axis)


def around(values):
    lines = pltpu.roll(values, 1, 0) + pltpu.roll(values, values.shape[0] - 1, 0)
    rows = pltpu.roll(values, 1, 1) + pltpu.roll(values, values.shape[1] - 1, 1)
    return lines + rows


def rates_of(substrate, catalyst, feed, kill):
    encounter = substrate * catalyst * catalyst
    return feed * (1.0 - substrate) - encounter, encounter - (feed + kill) * catalyst


def fine_layer(below, centre, above, feed, kill):
    reactions = rates_of(centre[0], centre[1], feed, kill)
    fields = []
    for species, rate in enumerate(FINE_RATES):
        sums = (below[species] + above[species]) + 2.0 * centre[species]
        sums = triple(triple(sums, 0), 1)
        fields.append(
            (1.0 - 4.0 * rate) * centre[species]
            + (rate / 16.0) * sums
            + TIME_STEP * reactions[species]
        )
    return fields


def sweep_layer(species, below, centre, above, explicit):
    implicit = SUBSTEPS * FINE_RATES[species]
    scale = 1.0 / (1.0 + 6.0 * implicit)
    return scale * explicit + (implicit * scale) * ((below + above) + around(centre))


def explicit_layer(substrate, catalyst, feed, kill):
    first, second = rates_of(substrate, catalyst, feed, kill)
    return substrate + COARSE_STEP * first, catalyst + COARSE_STEP * second


def joined(low, own, high, depth):
    def read(species, layer):
        part = (low, own, high)[layer // depth]
        return part[species, layer % depth]

    return read


def fine_levels(read, coefficient, levels, out, depth):
    count = 3 * depth - 2
    first = levels[0]
    for layer in range(count):
        fields = [[read(species, layer + shift) for species in (0, 1)] for shift in (0, 1, 2)]
        new = fine_layer(*fields, coefficient(0, layer + 1), coefficient(1, layer + 1))
        first[0, layer] = new[0]
        first[1, layer] = new[1]
    source = first
    for substep in range(1, SUBSTEPS):
        count -= 2
        target = out if substep == SUBSTEPS - 1 else levels[substep % 2]
        for layer in range(count):
            place = layer + substep + 1
            fields = [[source[species, layer + shift] for species in (0, 1)] for shift in (0, 1, 2)]
            new = fine_layer(*fields, coefficient(0, place), coefficient(1, place))
            target[0, layer] = new[0]
            target[1, layer] = new[1]
        source = target


def coarse_levels(read, levels, finish, depth):
    count = 3 * depth - 2
    for layer in range(count):
        for species in (0, 1):
            centre = read(species, layer + 1)
            levels[0][species, layer] = sweep_layer(
                species, read(species, layer), centre, read(species, layer + 2), centre
            )
    for sweep in range(1, SWEEPS):
        count -= 2
        source, target = levels[(sweep - 1) % 2], levels[sweep % 2]
        for layer in range(count):
            new = [
                sweep_layer(
                    species,
                    source[species, layer],
                    source[species, layer + 1],
                    source[species, layer + 2],
                    read(species, layer + sweep + 1),
                )
                for species in (0, 1)
            ]
            if sweep == SWEEPS - 1:
                finish(layer, new)
            else:
                target[0, layer] = new[0]
                target[1, layer] = new[1]


def fine_kernel(flag, low, own, high, low_c, feed, kill, high_c, state, explicit, level_a, level_b):
    depth = own.shape[1]

    @pl.when(flag[0] == 1)
    def _():
        def coefficient(which, layer):
            if layer < depth:
                return low_c[2 + which, layer]
            if layer >= 2 * depth:
                return high_c[2 + which, layer - 2 * depth]
            return (feed, kill)[which][layer - depth]

        fine_levels(joined(low, own, high, depth), coefficient, (level_a, level_b), state, depth)
        for layer in range(depth):
            new = explicit_layer(state[0, layer], state[1, layer], feed[layer], kill[layer])
            explicit[0, layer] = new[0]
            explicit[1, layer] = new[1]


def correction_kernel(flag, low, own, feed, kill, high, correction, level_a, level_b, wide):
    depth = own.shape[1]

    @pl.when(flag[0] == 1)
    def _():
        def coefficient(which, layer):
            if layer < depth:
                return low[2 + which, layer]
            if layer >= 2 * depth:
                return high[2 + which, layer - 2 * depth]
            return (feed, kill)[which][layer - depth]

        read = joined(low, own, high, depth)
        fine_levels(read, coefficient, (level_a, level_b), correction, depth)
        for layer in range(3 * depth):
            new = explicit_layer(
                read(0, layer), read(1, layer), coefficient(0, layer), coefficient(1, layer)
            )
            wide[0, layer] = new[0]
            wide[1, layer] = new[1]

        def finish(layer, new):
            for species in (0, 1):
                correction[species, layer] = correction[species, layer] - new[species]

        coarse_levels(lambda species, layer: wide[species, layer], (level_a, level_b), finish, depth)


def coarse_kernel(flag, low, own, high, correction, feed, kill, state, explicit, level_a, level_b):
    depth = own.shape[1]

    @pl.when(flag[0] == 1)
    def _():
        def finish(layer, new):
            first = new[0] + correction[0, layer]
            second = new[1] + correction[1, layer]
            state[0, layer] = first
            state[1, layer] = second
            explicit[0, layer], explicit[1, layer] = explicit_layer(
                first, second, feed[layer], kill[layer]
            )

        coarse_levels(joined(low, own, high, depth), (level_a, level_b), finish, depth)


def run(body, flag, operands, outputs, wide=False):
    shape = operands[1].shape
    depth, plane = shape[1], shape[2:]
    slab = jax.ShapeDtypeStruct((2, depth, *plane), jnp.float32)
    scratch = [
        pltpu.VMEM((2, 3 * depth - 2, *plane), jnp.float32),
        pltpu.VMEM((2, 3 * depth - 4, *plane), jnp.float32),
    ]
    if wide:
        scratch.append(pltpu.VMEM((2, 3 * depth, *plane), jnp.float32))
    return pl.pallas_call(
        body,
        out_shape=[slab] * outputs,
        in_specs=[SMEM] + [VMEM] * len(operands),
        out_specs=[VMEM] * outputs,
        scratch_shapes=scratch,
        compiler_params=pltpu.CompilerParams(vmem_limit_bytes=24 * 2**20),
        cost_estimate=pl.CostEstimate(flops=10**7, bytes_accessed=2**21, transcendentals=0),
    )(flag.astype(jnp.int32).reshape(1), *operands)


def shards(starts, feed, kill):
    own = starts[0]
    slabs = lax.axis_size("space")
    slices = lax.axis_size("tm")
    position = lax.axis_index("tm")

    def moved(array, routes, shift=0):
        pairs = []
        for source, target in routes:
            for slab in range(slabs):
                pairs.append((source * slabs + slab, target * slabs + (slab + shift) % slabs))
        return lax.ppermute(array, AXES, pairs)

    def spread(array, source, target):
        low = moved(array, [(source, target)], 1)
        high = moved(array, [(source, target)], -1)
        return low, moved(array, [(source, target)]), high

    everyone = [(index, index) for index in range(slices)]
    crossed = moved(own, [(0, 3)])
    package = jnp.concatenate([own, feed[None], kill[None]])
    low = moved(package, everyone, 1)
    high = moved(package, everyone, -1)
    first = spread(crossed, 3, 2)
    state, explicit = run(
        fine_kernel, position == 2, (*first, low, feed, kill, high), 2
    )
    second = spread(explicit, 2, 3)
    (correction,) = run(
        correction_kernel, position >= 1, (low, own, feed, kill, high), 1, wide=True
    )
    lent = moved(correction, [(1, 3)])
    state_b, explicit = run(
        coarse_kernel, position == 3, (*second, lent, feed, kill), 2
    )
    third = spread(explicit, 3, 2)
    back = moved(jnp.where(position == 2, state, state_b), [(2, 0), (3, 1)])
    state_c, explicit = run(
        coarse_kernel, position == 2, (*third, correction, feed, kill), 2
    )
    fourth = spread(explicit, 2, 3)
    state_d, _ = run(
        coarse_kernel, position == 3, (*fourth, correction, feed, kill), 2
    )
    result = jnp.where(position < 2, back, jnp.where(position == 2, state_c, state_d))
    return result[None]


def solution(mesh):
    placed = (P("tm", None, "space", None, None), P("space", None, None), P("space", None, None))
    return jax.shard_map(
        shards,
        mesh=mesh,
        in_specs=placed,
        out_specs=P("tm", None, "space", None, None),
        check_vma=False,
    )
```

profile of v0, /device:TPU:0, one launch (start us, length us, event | category | flops | bytes accessed | tf_op | source)
XLA Modules:
  0.0 135.4 jit_solution(11581485987631852197)
XLA Ops:
  0.0 0.0 copy-start.2
  0.0 0.0 copy-start
  0.0 0.0 copy-start.1
  0.0 2.4 %pad_maximum_fusion = f32[4,4,128,128]{3,2,1,0:T(8,128)} fusion(f32[1,4,128,128]{3,2,1,0:T(8,128)} %bitcast.8, f32[1,4,128,128]{3,2,1,0:T(8,128)} %bitcast.9, f32[2,4,128,128]{3,2,1,0:T(8,128)} %bitcast.10), kind=kLoop, calls=%fused_computation | loop fusion | flops 524288 | bytes 2097152 | tf_op jit(solution)/shard_map/concatenate | solution.py:222
  2.4 0.0 collective-permute-start.4
  2.4 9.2 %collective-permute-start.5 = (f32[4,4,128,128]{3,2,1,0:T(8,128)}, f32[4,4,128,128]{3,2,1,0:T(8,128)S(1)}, u32[]{:S(2)}, u32[]{:S(2)}) collective-permute-start(f32[4,4,128,128]{3,2,1,0:T(8,128)} %pad_maximum_fusion), channel_id=1, source_target_pairs={{0,63},{1,0},{2,1},{3,2},{4,3},{5,4},{6,5},{7,6},{8,7},{9,8},{10,9... | collective-permute-start | bytes 3145736 | tf_op jit(solution)/shard_map/ppermute | solution.py:213
  11.6 0.0 copy-done.2
  11.6 2.9 %collective-permute-start = (f32[2,4,128,128]{3,2,1,0:T(8,128)S(1)}, f32[2,4,128,128]{3,2,1,0:T(8,128)}, u32[]{:S(2)}, u32[]{:S(2)}) collective-permute-start(f32[2,4,128,128]{3,2,1,0:T(8,128)S(1)} %bitcast.11), channel_id=1, source_target_pairs={{0,192},{1,193},{2,194},{3,195},{4,196},{5,197},{6,198},{7,199},{8... | collective-permute-start | bytes 1572872 | tf_op jit(solution)/shard_map/ppermute | solution.py:213
  14.5 5.9 %collective-permute-done = f32[2,4,128,128]{3,2,1,0:T(8,128)} collective-permute-done((f32[2,4,128,128]{3,2,1,0:T(8,128)S(1)}, f32[2,4,128,128]{3,2,1,0:T(8,128)}, u32[]{:S(2)}, u32[]{:S(2)}) %collective-permute-start) | collective-permute-done | bytes 524320 | tf_op jit(solution)/shard_map/ppermute | solution.py:213
  20.4 0.7 collective-permute-start.1
  21.1 1.5 %collective-permute-start.2 = (f32[2,4,128,128]{3,2,1,0:T(8,128)}, f32[2,4,128,128]{3,2,1,0:T(8,128)}, u32[]{:S(2)}, u32[]{:S(2)}) collective-permute-start(f32[2,4,128,128]{3,2,1,0:T(8,128)} %collective-permute-done), channel_id=1, source_target_pairs={{192,128},{193,129},{194,130},{195,131},{196,132},{197,133},{198,1... | collective-permute-start | bytes 1572872 | tf_op jit(solution)/shard_map/ppermute | solution.py:213
  22.5 1.5 %collective-permute-start.3 = (f32[2,4,128,128]{3,2,1,0:T(8,128)}, f32[2,4,128,128]{3,2,1,0:T(8,128)}, u32[]{:S(2)}, u32[]{:S(2)}) collective-permute-start(f32[2,4,128,128]{3,2,1,0:T(8,128)} %collective-permute-done), channel_id=1, source_target_pairs={{192,191},{193,128},{194,129},{195,130},{196,131},{197,132},{198,1... | collective-permute-start | bytes 1572872 | tf_op jit(solution)/shard_map/ppermute | solution.py:213
  24.0 20.0 %collective-permute-done.4.low_c.low = f32[4,4,128,128]{3,2,1,0:T(8,128)S(1)} collective-permute-done((f32[4,4,128,128]{3,2,1,0:T(8,128)}, f32[4,4,128,128]{3,2,1,0:T(8,128)S(1)}, u32[]{:S(2)}, u32[]{:S(2)}) %collective-permute-start.4) | collective-permute-done | bytes 1048608 | tf_op jit(solution)/shard_map/ppermute | solution.py:213
  44.0 18.4 %collective-permute-done.5.high_c.high = f32[4,4,128,128]{3,2,1,0:T(8,128)S(1)} collective-permute-done((f32[4,4,128,128]{3,2,1,0:T(8,128)}, f32[4,4,128,128]{3,2,1,0:T(8,128)S(1)}, u32[]{:S(2)}, u32[]{:S(2)}) %collective-permute-start.5) | collective-permute-done | bytes 1048608 | tf_op jit(solution)/shard_map/ppermute | solution.py:213
  62.5 0.0 collective-permute-done.1.low
  62.5 0.0 collective-permute-done.2.own
  62.5 0.0 collective-permute-done.3.high
  62.5 0.0 copy-done
  62.5 0.0 copy-done.1
  62.5 0.0 copy-start.3
  62.5 2.1 %shard_map.37 = (f32[2,4,128,128]{3,2,1,0:T(8,128)S(1)}, f32[2,4,128,128]{3,2,1,0:T(8,128)}) custom-call(s32[1]{0:T(128)} %bitcast.flag, f32[2,4,128,128]{3,2,1,0:T(8,128)S(1)} %collective-permute-done.1.low, f32[2,4,128,128]{3,2,1,0:T(8,128)} %collective-permute-done.2.own, f32[2,4,128,128]{3,2,1,0:T(8,128)} %collective-permute-done.3.high, ...), custom_call_target="tpu_custom_call" | custom-call | flops 10000000 | bytes 2097152 | tf_op jit(solution)/shard_map/pallas_call | solution.py:191
  64.6 0.0 copy-start.4
  64.6 1.5 %collective-permute-start.6 = (f32[2,4,128,128]{3,2,1,0:T(8,128)}, f32[2,4,128,128]{3,2,1,0:T(8,128)}, u32[]{:S(2)}, u32[]{:S(2)}) collective-permute-start(f32[2,4,128,128]{3,2,1,0:T(8,128)} %get-tuple-element.13), channel_id=1, source_target_pairs={{128,193},{129,194},{130,195},{131,196},{132,197},{133,198},{134,1... | collective-permute-start | bytes 1572872 | tf_op jit(solution)/shard_map/ppermute | solution.py:213
  66.0 1.5 %collective-permute-start.7 = (f32[2,4,128,128]{3,2,1,0:T(8,128)}, f32[2,4,128,128]{3,2,1,0:T(8,128)}, u32[]{:S(2)}, u32[]{:S(2)}) collective-permute-start(f32[2,4,128,128]{3,2,1,0:T(8,128)} %get-tuple-element.13), channel_id=1, source_target_pairs={{128,192},{129,193},{130,194},{131,195},{132,196},{133,197},{134,1... | collective-permute-start | bytes 1572872 | tf_op jit(solution)/shard_map/ppermute | solution.py:213
  67.5 1.5 %collective-permute-start.8 = (f32[2,4,128,128]{3,2,1,0:T(8,128)}, f32[2,4,128,128]{3,2,1,0:T(8,128)}, u32[]{:S(2)}, u32[]{:S(2)}) collective-permute-start(f32[2,4,128,128]{3,2,1,0:T(8,128)} %get-tuple-element.13), channel_id=1, source_target_pairs={{128,255},{129,192},{130,193},{131,194},{132,195},{133,196},{134,1... | collective-permute-start | bytes 1572872 | tf_op jit(solution)/shard_map/ppermute | solution.py:213
  69.0 0.0 copy-done.3
  69.0 0.0 copy-done.4
  69.0 0.7 collective-permute-start.9
  69.7 0.0 collective-permute-done.6.low
  69.7 0.0 collective-permute-done.7.own
  69.7 0.0 collective-permute-done.8.high
  69.7 0.0 collective-permute-done.9.correction
  69.7 1.4 %shard_map.39 = (f32[2,4,128,128]{3,2,1,0:T(8,128)S(1)}, f32[2,4,128,128]{3,2,1,0:T(8,128)S(1)}) custom-call(s32[1]{0:T(128)} %bitcast.4.flag, f32[2,4,128,128]{3,2,1,0:T(8,128)} %collective-permute-done.6.low, f32[2,4,128,128]{3,2,1,0:T(8,128)} %collective-permute-done.7.own, f32[2,4,128,128]{3,2,1,0:T(8,128)} %collective-permute-done.8.high, ...), custom_call_target="tpu_custom_call" | custom-call | flops 10000000 | bytes 2097152 | tf_op jit(solution)/shard_map/pallas_call | solution.py:191
  71.1 0.0 copy-start.5
  71.1 0.8 collective-permute-start.11
  71.9 0.7 collective-permute-start.12
  72.6 0.7 collective-permute-start.13
  73.3 0.0 collective-permute-done.11.low
  73.3 0.0 collective-permute-done.12.own
  73.3 0.0 collective-permute-done.13.high
  73.3 0.8 shard_map.40
  74.2 0.7 collective-permute-start.14
  74.8 0.7 collective-permute-start.15
  75.5 0.7 collective-permute-start.16
  76.3 0.0 copy-done.5
  76.3 0.9 broadcast_select_fusion
  77.1 1.3 collective-permute-start.10
  78.4 0.0 collective-permute-done.14.low
  78.4 0.0 collective-permute-done.15.own
  78.4 0.0 collective-permute-done.16.high
  78.4 0.8 shard_map.41
  79.3 54.2 %collective-permute-done.10 = f32[2,4,128,128]{3,2,1,0:T(8,128)} collective-permute-done((f32[2,4,128,128]{3,2,1,0:T(8,128)}, f32[2,4,128,128]{3,2,1,0:T(8,128)}, u32[]{:S(2)}, u32[]{:S(2)}) %collective-permute-start.10) | collective-permute-done | bytes 524320 | tf_op jit(solution)/shard_map/ppermute | solution.py:213
  133.5 1.9 %select_bitcast_fusion = f32[1,2,4,128,128]{4,3,2,1,0:T(8,128)} fusion(f32[2,4,128,128]{3,2,1,0:T(8,128)} %collective-permute-done.10, f32[2,4,128,128]{3,2,1,0:T(8,128)S(1)} %get-tuple-element.16, f32[2,4,128,128]{3,2,1,0:T(8,128)S(1)} %get-tuple-element.18, pred[]{:T(512)S(6)} %eq.4, pred[]{:T(512)S(6)} %lt.3), kind=kLoop, calls=%fused_computation.1 | loop fusion | flops 262144 | bytes 2097154 | tf_op jit(solution)/shard_map/broadcast_in_dim | solution.py:247
  (1 shorter events, 0.0 us)
Async XLA Ops:
  0.0 11.6 %copy-start.2 = (f32[1,2,4,128,128]{4,3,2,1,0:T(8,128)S(1)}, f32[1,2,4,128,128]{4,3,2,1,0:T(8,128)}, u32[]{:S(2)}) copy-start(f32[1,2,4,128,128]{4,3,2,1,0:T(8,128)} %param.3) | copy-start | bytes 1572868
  0.0 62.5 %copy-start = (f32[4,128,128]{2,1,0:T(8,128)S(1)}, f32[4,128,128]{2,1,0:T(8,128)}, u32[]{:S(2)}) copy-start(f32[4,128,128]{2,1,0:T(8,128)} %kill.9) | copy-start | bytes 786436
  0.0 62.5 %copy-start.1 = (f32[4,128,128]{2,1,0:T(8,128)S(1)}, f32[4,128,128]{2,1,0:T(8,128)}, u32[]{:S(2)}) copy-start(f32[4,128,128]{2,1,0:T(8,128)} %feed.9) | copy-start | bytes 786436
  2.4 41.6 %collective-permute-start.4 = (f32[4,4,128,128]{3,2,1,0:T(8,128)}, f32[4,4,128,128]{3,2,1,0:T(8,128)S(1)}, u32[]{:S(2)}, u32[]{:S(2)}) collective-permute-start(f32[4,4,128,128]{3,2,1,0:T(8,128)} %pad_maximum_fusion), channel_id=1, source_target_pairs={{0,1},{1,2},{2,3},{3,4},{4,5},{5,6},{6,7},{7,8},{8,9},{9,10},{10,1... | collective-permute-start | bytes 3145736 | tf_op jit(solution)/shard_map/ppermute | solution.py:213
  2.4 60.1 %collective-permute-start.5 = (f32[4,4,128,128]{3,2,1,0:T(8,128)}, f32[4,4,128,128]{3,2,1,0:T(8,128)S(1)}, u32[]{:S(2)}, u32[]{:S(2)}) collective-permute-start(f32[4,4,128,128]{3,2,1,0:T(8,128)} %pad_maximum_fusion), channel_id=1, source_target_pairs={{0,63},{1,0},{2,1},{3,2},{4,3},{5,4},{6,5},{7,6},{8,7},{9,8},{10,9... | collective-permute-start | bytes 3145736 | tf_op jit(solution)/shard_map/ppermute | solution.py:213
  11.6 8.8 %collective-permute-start = (f32[2,4,128,128]{3,2,1,0:T(8,128)S(1)}, f32[2,4,128,128]{3,2,1,0:T(8,128)}, u32[]{:S(2)}, u32[]{:S(2)}) collective-permute-start(f32[2,4,128,128]{3,2,1,0:T(8,128)S(1)} %bitcast.11), channel_id=1, source_target_pairs={{0,192},{1,193},{2,194},{3,195},{4,196},{5,197},{6,198},{7,199},{8... | collective-permute-start | bytes 1572872 | tf_op jit(solution)/shard_map/ppermute | solution.py:213
  20.4 42.1 %collective-permute-start.1 = (f32[2,4,128,128]{3,2,1,0:T(8,128)}, f32[2,4,128,128]{3,2,1,0:T(8,128)S(1)}, u32[]{:S(2)}, u32[]{:S(2)}) collective-permute-start(f32[2,4,128,128]{3,2,1,0:T(8,128)} %collective-permute-done), channel_id=1, source_target_pairs={{192,129},{193,130},{194,131},{195,132},{196,133},{197,134},{198,1... | collective-permute-start | bytes 1572872 | tf_op jit(solution)/shard_map/ppermute | solution.py:213
  21.1 41.4 %collective-permute-start.2 = (f32[2,4,128,128]{3,2,1,0:T(8,128)}, f32[2,4,128,128]{3,2,1,0:T(8,128)}, u32[]{:S(2)}, u32[]{:S(2)}) collective-permute-start(f32[2,4,128,128]{3,2,1,0:T(8,128)} %collective-permute-done), channel_id=1, source_target_pairs={{192,128},{193,129},{194,130},{195,131},{196,132},{197,133},{198,1... | collective-permute-start | bytes 1572872 | tf_op jit(solution)/shard_map/ppermute | solution.py:213
  22.5 39.9 %collective-permute-start.3 = (f32[2,4,128,128]{3,2,1,0:T(8,128)}, f32[2,4,128,128]{3,2,1,0:T(8,128)}, u32[]{:S(2)}, u32[]{:S(2)}) collective-permute-start(f32[2,4,128,128]{3,2,1,0:T(8,128)} %collective-permute-done), channel_id=1, source_target_pairs={{192,191},{193,128},{194,129},{195,130},{196,131},{197,132},{198,1... | collective-permute-start | bytes 1572872 | tf_op jit(solution)/shard_map/ppermute | solution.py:213
  62.5 6.5 %copy-start.3 = (f32[1,2,4,128,128]{4,3,2,1,0:T(8,128)S(1)}, f32[1,2,4,128,128]{4,3,2,1,0:T(8,128)}, u32[]{:S(2)}) copy-start(f32[1,2,4,128,128]{4,3,2,1,0:T(8,128)} %param.3) | copy-start | bytes 1572868
  64.6 4.4 %copy-start.4 = (f32[2,4,128,128]{3,2,1,0:T(8,128)}, f32[2,4,128,128]{3,2,1,0:T(8,128)S(1)}, u32[]{:S(2)}) copy-start(f32[2,4,128,128]{3,2,1,0:T(8,128)S(1)} %get-tuple-element.12) | copy-start | bytes 1572868
  64.6 5.1 %collective-permute-start.6 = (f32[2,4,128,128]{3,2,1,0:T(8,128)}, f32[2,4,128,128]{3,2,1,0:T(8,128)}, u32[]{:S(2)}, u32[]{:S(2)}) collective-permute-start(f32[2,4,128,128]{3,2,1,0:T(8,128)} %get-tuple-element.13), channel_id=1, source_target_pairs={{128,193},{129,194},{130,195},{131,196},{132,197},{133,198},{134,1... | collective-permute-start | bytes 1572872 | tf_op jit(solution)/shard_map/ppermute | solution.py:213
  66.0 3.6 %collective-permute-start.7 = (f32[2,4,128,128]{3,2,1,0:T(8,128)}, f32[2,4,128,128]{3,2,1,0:T(8,128)}, u32[]{:S(2)}, u32[]{:S(2)}) collective-permute-start(f32[2,4,128,128]{3,2,1,0:T(8,128)} %get-tuple-element.13), channel_id=1, source_target_pairs={{128,192},{129,193},{130,194},{131,195},{132,196},{133,197},{134,1... | collective-permute-start | bytes 1572872 | tf_op jit(solution)/shard_map/ppermute | solution.py:213
  67.5 2.2 %collective-permute-start.8 = (f32[2,4,128,128]{3,2,1,0:T(8,128)}, f32[2,4,128,128]{3,2,1,0:T(8,128)}, u32[]{:S(2)}, u32[]{:S(2)}) collective-permute-start(f32[2,4,128,128]{3,2,1,0:T(8,128)} %get-tuple-element.13), channel_id=1, source_target_pairs={{128,255},{129,192},{130,193},{131,194},{132,195},{133,196},{134,1... | collective-permute-start | bytes 1572872 | tf_op jit(solution)/shard_map/ppermute | solution.py:213
  69.0 0.7 collective-permute-start.9
  71.1 5.2 %copy-start.5 = (f32[2,4,128,128]{3,2,1,0:T(8,128)S(1)}, f32[2,4,128,128]{3,2,1,0:T(8,128)}, u32[]{:S(2)}) copy-start(f32[2,4,128,128]{3,2,1,0:T(8,128)} %copy-done.4) | copy-start | bytes 1572868
  71.1 2.2 %collective-permute-start.11 = (f32[2,4,128,128]{3,2,1,0:T(8,128)S(1)}, f32[2,4,128,128]{3,2,1,0:T(8,128)S(1)}, u32[]{:S(2)}, u32[]{:S(2)}) collective-permute-start(f32[2,4,128,128]{3,2,1,0:T(8,128)S(1)} %get-tuple-element.15), channel_id=1, source_target_pairs={{192,129},{193,130},{194,131},{195,132},{196,133},{197,134},{198,1... | collective-permute-start | bytes 1572872 | tf_op jit(solution)/shard_map/ppermute | solution.py:213
  71.9 1.4 %collective-permute-start.12 = (f32[2,4,128,128]{3,2,1,0:T(8,128)S(1)}, f32[2,4,128,128]{3,2,1,0:T(8,128)S(1)}, u32[]{:S(2)}, u32[]{:S(2)}) collective-permute-start(f32[2,4,128,128]{3,2,1,0:T(8,128)S(1)} %get-tuple-element.15), channel_id=1, source_target_pairs={{192,128},{193,129},{194,130},{195,131},{196,132},{197,133},{198,1... | collective-permute-start | bytes 1572872 | tf_op jit(solution)/shard_map/ppermute | solution.py:213
  72.6 0.7 collective-permute-start.13
  74.2 4.3 %collective-permute-start.14 = (f32[2,4,128,128]{3,2,1,0:T(8,128)}, f32[2,4,128,128]{3,2,1,0:T(8,128)S(1)}, u32[]{:S(2)}, u32[]{:S(2)}) collective-permute-start(f32[2,4,128,128]{3,2,1,0:T(8,128)} %get-tuple-element.17), channel_id=1, source_target_pairs={{128,193},{129,194},{130,195},{131,196},{132,197},{133,198},{134,1... | collective-permute-start | bytes 1572872 | tf_op jit(solution)/shard_map/ppermute | solution.py:213
  74.8 3.6 %collective-permute-start.15 = (f32[2,4,128,128]{3,2,1,0:T(8,128)}, f32[2,4,128,128]{3,2,1,0:T(8,128)S(1)}, u32[]{:S(2)}, u32[]{:S(2)}) collective-permute-start(f32[2,4,128,128]{3,2,1,0:T(8,128)} %get-tuple-element.17), channel_id=1, source_target_pairs={{128,192},{129,193},{130,194},{131,195},{132,196},{133,197},{134,1... | collective-permute-start | bytes 1572872 | tf_op jit(solution)/shard_map/ppermute | solution.py:213
  75.5 2.9 %collective-permute-start.16 = (f32[2,4,128,128]{3,2,1,0:T(8,128)}, f32[2,4,128,128]{3,2,1,0:T(8,128)S(1)}, u32[]{:S(2)}, u32[]{:S(2)}) collective-permute-start(f32[2,4,128,128]{3,2,1,0:T(8,128)} %get-tuple-element.17), channel_id=1, source_target_pairs={{128,255},{129,192},{130,193},{131,194},{132,195},{133,196},{134,1... | collective-permute-start | bytes 1572872 | tf_op jit(solution)/shard_map/ppermute | solution.py:213
  77.1 56.3 %collective-permute-start.10 = (f32[2,4,128,128]{3,2,1,0:T(8,128)}, f32[2,4,128,128]{3,2,1,0:T(8,128)}, u32[]{:S(2)}, u32[]{:S(2)}) collective-permute-start(f32[2,4,128,128]{3,2,1,0:T(8,128)} %broadcast_select_fusion), channel_id=1, source_target_pairs={{128,0},{129,1},{130,2},{131,3},{132,4},{133,5},{134,6},{135,7},{1... | collective-permute-start | bytes 1572872 | tf_op jit(solution)/shard_map/ppermute | solution.py:213
where the time goes:
time: 136 us; the launch traced here: 135 us
  waiting for transfers between devices  98.6 us (72%)
  starting transfers between devices  26.3 us (19%)
  other arithmetic  5.17 us (4%)
  Pallas kernels  5.05 us (4%)
    ppermute x17, waiting for transfers between devices, moved(): return lax.ppermute(array, AXES, pairs)  98.6 us
    ppermute x17, starting transfers between devices, moved(): return lax.ppermute(array, AXES, pairs)  26.3 us
    pallas_call x5, Pallas kernels, run(): pl.pallas_call(body, out_shape=[slab] * outputs, in_specs=[SMEM] + [VMEM]...  5.05 us
  transfers between devices with their start and end apart: 17, of which 4 were waited for; matrix products, arithmetic and copies ran while one was open for 1% of the time, Pallas kernels for 1%

commit v1 on v0

--- a/solution.py
+++ b/solution.py
@@ -12,6 +12,7 @@
 COARSE_STEP = SUBSTEPS * TIME_STEP
 VMEM = pl.BlockSpec(memory_space=pltpu.VMEM)
 SMEM = pl.BlockSpec(memory_space=pltpu.SMEM)
+ANY = pl.BlockSpec(memory_space=pl.ANY)
 AXES = ("tm", "space")
 
 
@@ -114,37 +115,38 @@
                 target[1, layer] = new[1]
 
 
-def fine_kernel(flag, low, own, high, low_c, feed, kill, high_c, state, explicit, level_a, level_b):
+def coefficients_of(low, feed, kill, high, depth):
+    def coefficient(which, layer):
+        if layer < depth:
+            return low[which, layer]
+        if layer >= 2 * depth:
+            return high[which, layer - 2 * depth]
+        return (feed, kill)[which][layer - depth]
+
+    return coefficient
+
+
+def fine_kernel(worker, position, low, own, high, low_c, feed, kill, high_c, state, explicit, *levels):
     depth = own.shape[1]
 
-    @pl.when(flag[0] == 1)
-    def _():
-        def coefficient(which, layer):
-            if layer < depth:
-                return low_c[2 + which, layer]
-            if layer >= 2 * depth:
-                return high_c[2 + which, layer - 2 * depth]
-            return (feed, kill)[which][layer - depth]
-
-        fine_levels(joined(low, own, high, depth), coefficient, (level_a, level_b), state, depth)
+    @pl.when((position[0] == worker[0]) | (position[0] == worker[-1]))
+    def _():
+        coefficient = coefficients_of(low_c, feed, kill, high_c, depth)
+        fine_levels(joined(low, own, high, depth), coefficient, levels, state, depth)
         for layer in range(depth):
             new = explicit_layer(state[0, layer], state[1, layer], feed[layer], kill[layer])
             explicit[0, layer] = new[0]
             explicit[1, layer] = new[1]
 
 
-def correction_kernel(flag, low, own, feed, kill, high, correction, level_a, level_b, wide):
+def correction_kernel(
+    worker, position, low, own, high, low_c, feed, kill, high_c, correction, level_a, level_b, wide
+):
     depth = own.shape[1]
 
-    @pl.when(flag[0] == 1)
-    def _():
-        def coefficient(which, layer):
-            if layer < depth:
-                return low[2 + which, layer]
-            if layer >= 2 * depth:
-                return high[2 + which, layer - 2 * depth]
-            return (feed, kill)[which][layer - depth]
-
+    @pl.when((position[0] == worker[0]) | (position[0] == worker[-1]))
+    def _():
+        coefficient = coefficients_of(low_c, feed, kill, high_c, depth)
         read = joined(low, own, high, depth)
         fine_levels(read, coefficient, (level_a, level_b), correction, depth)
         for layer in range(3 * depth):
@@ -161,10 +163,10 @@
         coarse_levels(lambda species, layer: wide[species, layer], (level_a, level_b), finish, depth)
 
 
-def coarse_kernel(flag, low, own, high, correction, feed, kill, state, explicit, level_a, level_b):
+def coarse_kernel(worker, position, low, own, high, correction, feed, kill, state, explicit, *levels):
     depth = own.shape[1]
 
-    @pl.when(flag[0] == 1)
+    @pl.when((position[0] == worker[0]) | (position[0] == worker[-1]))
     def _():
         def finish(layer, new):
             first = new[0] + correction[0, layer]
@@ -175,35 +177,79 @@
                 first, second, feed[layer], kill[layer]
             )
 
-        coarse_levels(joined(low, own, high, depth), (level_a, level_b), finish, depth)
-
-
-def run(body, flag, operands, outputs, wide=False):
-    shape = operands[1].shape
-    depth, plane = shape[1], shape[2:]
-    slab = jax.ShapeDtypeStruct((2, depth, *plane), jnp.float32)
-    scratch = [
-        pltpu.VMEM((2, 3 * depth - 2, *plane), jnp.float32),
-        pltpu.VMEM((2, 3 * depth - 4, *plane), jnp.float32),
-    ]
-    if wide:
-        scratch.append(pltpu.VMEM((2, 3 * depth, *plane), jnp.float32))
+        coarse_levels(joined(low, own, high, depth), levels, finish, depth)
+
+
+def last_kernel(worker, position, low, own, high, correction, third, back, state, *levels):
+    depth = own.shape[1]
+
+    @pl.when(position[0] < worker[0] - 1)
+    def _():
+        state[...] = back[...]
+
+    @pl.when(position[0] == worker[0] - 1)
+    def _():
+        state[...] = third[...]
+
+    @pl.when((position[0] == worker[0]) | (position[0] == worker[-1]))
+    def _():
+        def finish(layer, new):
+            for species in (0, 1):
+                state[species, layer] = new[species] + correction[species, layer]
+
+        coarse_levels(joined(low, own, high, depth), levels, finish, depth)
+
+
+def stack_kernel(position, feed, kill, both):
+    both[0] = feed[...]
+    both[1] = kill[...]
+
+
+def run(body, position, operands, outputs, scratch=2, pinned=True, worker=None, tokens=()):
+    depth, plane = operands[0].shape[-3], operands[0].shape[-2:]
+    shape = (2, depth, *plane)
+    if pinned:
+        out_shape = [pltpu.VMEM(shape, jnp.float32)] * outputs
+    else:
+        out_shape = [jax.ShapeDtypeStruct(shape, jnp.float32)] * outputs
+    layers = (3 * depth - 2, 3 * depth - 4, 3 * depth)[:scratch]
+    operands = [pltpu.with_memory_space_constraint(array, pltpu.VMEM) for array in operands]
+
+    count = 1 + len(operands)
+
+    def kernel(*refs):
+        refs = refs[:count] + refs[count + len(tokens) :]
+        body(*(() if worker is None else (worker,)), *refs)
+
     return pl.pallas_call(
-        body,
-        out_shape=[slab] * outputs,
-        in_specs=[SMEM] + [VMEM] * len(operands),
+        kernel,
+        out_shape=out_shape,
+        in_specs=[SMEM] + [VMEM] * len(operands) + [ANY] * len(tokens),
         out_specs=[VMEM] * outputs,
-        scratch_shapes=scratch,
-        compiler_params=pltpu.CompilerParams(vmem_limit_bytes=24 * 2**20),
-        cost_estimate=pl.CostEstimate(flops=10**7, bytes_accessed=2**21, transcendentals=0),
-    )(flag.astype(jnp.int32).reshape(1), *operands)
+        scratch_shapes=[pltpu.VMEM((2, count, *plane), jnp.float32) for count in layers],
+        compiler_params=pltpu.CompilerParams(vmem_limit_bytes=12 * 2**20),
+        cost_estimate=pl.CostEstimate(flops=10**10, bytes_accessed=2**21, transcendentals=0),
+    )(position, *operands, *tokens)
+
+
+def copy_kernel(array, token, copied):
+    copied[...] = array[...]
+
+
+def after(array, token):
+    return pl.pallas_call(
+        copy_kernel,
+        out_shape=pltpu.VMEM(array.shape, array.dtype),
+        in_specs=[VMEM, ANY],
+        out_specs=VMEM,
+        compiler_params=pltpu.CompilerParams(vmem_limit_bytes=4 * 2**20),
+    )(array, token)
 
 
 def shards(starts, feed, kill):
     own = starts[0]
     slabs = lax.axis_size("space")
-    slices = lax.axis_size("tm")
-    position = lax.axis_index("tm")
+    position = lax.axis_index("tm").astype(jnp.int32).reshape(1)
 
     def moved(array, routes, shift=0):
         pairs = []
@@ -212,38 +258,76 @@
                 pairs.append((source * slabs + slab, target * slabs + (slab + shift) % slabs))
         return lax.ppermute(array, AXES, pairs)
 
+    def sides(array, routes):
+        return moved(array, routes, 1), moved(array, routes, -1)
+
     def spread(array, source, target):
-        low = moved(array, [(source, target)], 1)
-        high = moved(array, [(source, target)], -1)
+        low, high = sides(array, [(source, target)])
         return low, moved(array, [(source, target)]), high
 
-    everyone = [(index, index) for index in range(slices)]
     crossed = moved(own, [(0, 3)])
-    package = jnp.concatenate([own, feed[None], kill[None]])
-    low = moved(package, everyone, 1)
-    high = moved(package, everyone, -1)
+    lent = moved(own, [(1, 0)])
+    (both,) = run(stack_kernel, position, (feed, kill), 1, 0)
+    low_c, high_c = sides(both, [(2, 2)])
     first = spread(crossed, 3, 2)
-    state, explicit = run(
-        fine_kernel, position == 2, (*first, low, feed, kill, high), 2
+    lent = moved(after(lent, crossed), [(0, 3)])
+    low_d = moved(after(low_c, first[1]), [(2, 3)])
+    high_d = moved(after(high_c, first[1]), [(2, 3)])
+    low_1, high_1 = sides(lent, [(3, 3)])
+    ends, explicit = run(
+        fine_kernel,
+        position,
+        (*first, low_c, feed, kill, high_c),
+        2,
+        worker=(2,),
+        tokens=(low_d, high_d, lent),
     )
     second = spread(explicit, 2, 3)
     (correction,) = run(
-        correction_kernel, position >= 1, (low, own, feed, kill, high), 1, wide=True
-    )
-    lent = moved(correction, [(1, 3)])
-    state_b, explicit = run(
-        coarse_kernel, position == 3, (*second, lent, feed, kill), 2
+        correction_kernel,
+        position,
+        (low_1, lent, high_1, low_d, feed, kill, high_d),
+        1,
+        3,
+        worker=(3,),
+    )
+    own_2 = after(own, second[1])
+    low_2, high_2 = sides(own_2, [(2, 2)])
+    ends_b, explicit = run(
+        coarse_kernel,
+        position,
+        (*second, correction, feed, kill),
+        2,
+        worker=(3,),
+        tokens=(own_2,),
     )
     third = spread(explicit, 3, 2)
-    back = moved(jnp.where(position == 2, state, state_b), [(2, 0), (3, 1)])
-    state_c, explicit = run(
-        coarse_kernel, position == 2, (*third, correction, feed, kill), 2
+    back = moved(jnp.where(position[0] == 2, ends, ends_b), [(2, 0), (3, 1)])
+    own_3 = after(own, third[1])
+    low_3, high_3 = sides(own_3, [(3, 3)])
+    (correction,) = run(
+        correction_kernel,
+        position,
+        (low_2, own_2, high_2, low_c, feed, kill, high_c),
+        1,
+        3,
+        worker=(2,),
+    )
+    ends_c, explicit = run(
+        coarse_kernel, position, (*third, correction, feed, kill), 2, worker=(2,)
     )
     fourth = spread(explicit, 2, 3)
-    state_d, _ = run(
-        coarse_kernel, position == 3, (*fourth, correction, feed, kill), 2
-    )
-    result = jnp.where(position < 2, back, jnp.where(position == 2, state_c, state_d))
+    (correction,) = run(
+        correction_kernel,
+        position,
+        (low_3, own_3, high_3, low_d, feed, kill, high_d),
+        1,
+        3,
+        worker=(3,),
+    )
+    (result,) = run(
+        last_kernel, position, (*fourth, correction, ends_c, back), 1, pinned=False, worker=(3,)
+    )
     return result[None]
 
 

time: 136 us -> 116 us (0.85)
  the two profiles are of different devices: /device:TPU:0 before, /device:TPU:111 now
where the time goes in v1:
time: 116 us
  waiting for transfers between devices  46 us (40%)
  starting transfers between devices  42.8 us (37%)
  Pallas kernels  22.6 us (19%)
  local copies, waits for them, and re-layouts  2.74 us (2%)
    ppermute x26, waiting for transfers between devices, moved(): return lax.ppermute(array, AXES, pairs)  46 us
    ppermute x26, starting transfers between devices, moved(): return lax.ppermute(array, AXES, pairs)  42.8 us
    pallas_call x8, Pallas kernels, run(): pl.pallas_call(kernel, out_shape=out_shape, in_specs=[SMEM] + [VMEM] * le...  22.4 us
    unnamed x22, local copies, waits for them, and re-layouts  2.74 us
  transfers between devices with their start and end apart: 26, of which 6 were waited for; matrix products, arithmetic and copies ran while one was open for 1% of the time, Pallas kernels for 14%

profile of v1, /device:TPU:111, one launch (start us, length us, event | category | flops | bytes accessed | tf_op | source)
XLA Modules:
  0.0 115.7 jit_solution(14911930703337664149)
XLA Ops:
  0.0 1.3 %collective-permute-start = (f32[2,4,128,128]{3,2,1,0:T(8,128)}, f32[2,4,128,128]{3,2,1,0:T(8,128)S(1)}, u32[]{:S(2)}, u32[]{:S(2)}) collective-permute-start(f32[2,4,128,128]{3,2,1,0:T(8,128)} %bitcast.3), channel_id=1, source_target_pairs={{0,192},{1,193},{2,194},{3,195},{4,196},{5,197},{6,198},{7,199},{8... | collective-permute-start | bytes 1572872 | tf_op jit(solution)/shard_map/ppermute | solution.py:259
  1.3 0.7 collective-permute-start.8
  2.0 0.0 copy-start.6
  2.0 0.9 copy-done.6
  3.0 0.9 copy-done.8
  3.9 0.7 collective-permute-start.4
  4.6 11.7 %collective-permute-done.token = f32[2,4,128,128]{3,2,1,0:T(8,128)S(1)} collective-permute-done((f32[2,4,128,128]{3,2,1,0:T(8,128)}, f32[2,4,128,128]{3,2,1,0:T(8,128)S(1)}, u32[]{:S(2)}, u32[]{:S(2)}) %collective-permute-start) | collective-permute-done | bytes 524320 | tf_op jit(solution)/shard_map/ppermute | solution.py:259
  16.3 1.3 %collective-permute-start.2 = (f32[2,4,128,128]{3,2,1,0:T(8,128)S(1)}, f32[2,4,128,128]{3,2,1,0:T(8,128)S(1)}, u32[]{:S(2)}, u32[]{:S(2)}) collective-permute-start(f32[2,4,128,128]{3,2,1,0:T(8,128)S(1)} %collective-permute-done.token), channel_id=1, source_target_pairs={{192,128},{193,129},{194,130},{195,131},{196,132},{197,133},{198,1... | collective-permute-start | bytes 1572872 | tf_op jit(solution)/shard_map/ppermute | solution.py:259
  17.6 0.7 collective-permute-start.5
  18.3 0.0 collective-permute-done.8.array
  18.4 1.3 %collective-permute-start.9 = (f32[2,4,128,128]{3,2,1,0:T(8,128)S(1)}, f32[2,4,128,128]{3,2,1,0:T(8,128)S(1)}, u32[]{:S(2)}, u32[]{:S(2)}) collective-permute-start(f32[2,4,128,128]{3,2,1,0:T(8,128)S(1)} %shard_map.40), channel_id=1, source_target_pairs={{0,192},{1,193},{2,194},{3,195},{4,196},{5,197},{6,198},{7,199},{8... | collective-permute-start | bytes 1572872 | tf_op jit(solution)/shard_map/ppermute | solution.py:259
  19.7 1.5 %collective-permute-start.1 = (f32[2,4,128,128]{3,2,1,0:T(8,128)S(1)}, f32[2,4,128,128]{3,2,1,0:T(8,128)S(1)}, u32[]{:S(2)}, u32[]{:S(2)}) collective-permute-start(f32[2,4,128,128]{3,2,1,0:T(8,128)S(1)} %collective-permute-done.token), channel_id=1, source_target_pairs={{192,129},{193,130},{194,131},{195,132},{196,133},{197,134},{198,1... | collective-permute-start | bytes 1572872 | tf_op jit(solution)/shard_map/ppermute | solution.py:259
  21.2 0.0 collective-permute-done.4.array.refs_4_
  21.2 1.3 %collective-permute-start.3 = (f32[2,4,128,128]{3,2,1,0:T(8,128)S(1)}, f32[2,4,128,128]{3,2,1,0:T(8,128)S(1)}, u32[]{:S(2)}, u32[]{:S(2)}) collective-permute-start(f32[2,4,128,128]{3,2,1,0:T(8,128)S(1)} %collective-permute-done.token), channel_id=1, source_target_pairs={{192,191},{193,128},{194,129},{195,130},{196,131},{197,132},{198,1... | collective-permute-start | bytes 1572872 | tf_op jit(solution)/shard_map/ppermute | solution.py:259
  22.5 0.0 collective-permute-done.2.token.refs_2_
  22.6 0.0 copy-start.7
  22.6 0.0 copy-start.9
  22.6 1.4 %collective-permute-start.6 = (f32[2,4,128,128]{3,2,1,0:T(8,128)S(1)}, f32[2,4,128,128]{3,2,1,0:T(8,128)S(1)}, u32[]{:S(2)}, u32[]{:S(2)}) collective-permute-start(f32[2,4,128,128]{3,2,1,0:T(8,128)S(1)} %shard_map.38), channel_id=1, source_target_pairs={{128,192},{129,193},{130,194},{131,195},{132,196},{133,197},{134,1... | collective-permute-start | bytes 1572872 | tf_op jit(solution)/shard_map/ppermute | solution.py:259
  24.1 0.0 collective-permute-done.5.array.refs_7_
  24.1 1.3 %collective-permute-start.7 = (f32[2,4,128,128]{3,2,1,0:T(8,128)S(1)}, f32[2,4,128,128]{3,2,1,0:T(8,128)S(1)}, u32[]{:S(2)}, u32[]{:S(2)}) collective-permute-start(f32[2,4,128,128]{3,2,1,0:T(8,128)S(1)} %shard_map.39), channel_id=1, source_target_pairs={{128,192},{129,193},{130,194},{131,195},{132,196},{133,197},{134,1... | collective-permute-start | bytes 1572872 | tf_op jit(solution)/shard_map/ppermute | solution.py:259
  25.4 11.4 %collective-permute-done.9.refs_10_.refs_2_ = f32[2,4,128,128]{3,2,1,0:T(8,128)S(1)} collective-permute-done((f32[2,4,128,128]{3,2,1,0:T(8,128)S(1)}, f32[2,4,128,128]{3,2,1,0:T(8,128)S(1)}, u32[]{:S(2)}, u32[]{:S(2)}) %collective-permute-start.9) | collective-permute-done | bytes 524320 | tf_op jit(solution)/shard_map/ppermute | solution.py:259
  36.8 1.9 %collective-permute-start.13 = (f32[2,4,128,128]{3,2,1,0:T(8,128)S(1)}, f32[2,4,128,128]{3,2,1,0:T(8,128)S(1)}, u32[]{:S(2)}, u32[]{:S(2)}) collective-permute-start(f32[2,4,128,128]{3,2,1,0:T(8,128)S(1)} %collective-permute-done.9.refs_10_.refs_2_), channel_id=1, source_target_pairs={{192,193},{193,194},{194,195},{195,196},{196,197},{197,198},{198,1... | collective-permute-start | bytes 1572872 | tf_op jit(solution)/shard_map/ppermute | solution.py:259
  38.7 0.0 collective-permute-done.1.refs_1_
  38.7 3.4 %collective-permute-start.14 = (f32[2,4,128,128]{3,2,1,0:T(8,128)S(1)}, f32[2,4,128,128]{3,2,1,0:T(8,128)S(1)}, u32[]{:S(2)}, u32[]{:S(2)}) collective-permute-start(f32[2,4,128,128]{3,2,1,0:T(8,128)S(1)} %collective-permute-done.9.refs_10_.refs_2_), channel_id=1, source_target_pairs={{192,255},{193,192},{194,193},{195,194},{196,195},{197,196},{198,1... | collective-permute-start | bytes 1572872 | tf_op jit(solution)/shard_map/ppermute | solution.py:259
  42.1 0.0 collective-permute-done.3.refs_3_
  42.1 0.0 collective-permute-done.6.refs_8_.refs_4_
  42.1 0.0 collective-permute-done.7.refs_9_.refs_7_
  42.2 0.0 copy-start
  42.2 1.4 %collective-permute-start.11 = (f32[2,4,128,128]{3,2,1,0:T(8,128)S(1)}, f32[2,4,128,128]{3,2,1,0:T(8,128)S(1)}, u32[]{:S(2)}, u32[]{:S(2)}) collective-permute-start(f32[2,4,128,128]{3,2,1,0:T(8,128)S(1)} %get-tuple-element.11), channel_id=1, source_target_pairs={{128,192},{129,193},{130,194},{131,195},{132,196},{133,197},{134,1... | collective-permute-start | bytes 1572872 | tf_op jit(solution)/shard_map/ppermute | solution.py:259
  43.6 1.3 %collective-permute-start.10 = (f32[2,4,128,128]{3,2,1,0:T(8,128)S(1)}, f32[2,4,128,128]{3,2,1,0:T(8,128)S(1)}, u32[]{:S(2)}, u32[]{:S(2)}) collective-permute-start(f32[2,4,128,128]{3,2,1,0:T(8,128)S(1)} %get-tuple-element.11), channel_id=1, source_target_pairs={{128,193},{129,194},{130,195},{131,196},{132,197},{133,198},{134,1... | collective-permute-start | bytes 1572872 | tf_op jit(solution)/shard_map/ppermute | solution.py:259
  44.9 1.3 %collective-permute-start.12 = (f32[2,4,128,128]{3,2,1,0:T(8,128)S(1)}, f32[2,4,128,128]{3,2,1,0:T(8,128)S(1)}, u32[]{:S(2)}, u32[]{:S(2)}) collective-permute-start(f32[2,4,128,128]{3,2,1,0:T(8,128)S(1)} %get-tuple-element.11), channel_id=1, source_target_pairs={{128,255},{129,192},{130,193},{131,194},{132,195},{133,196},{134,1... | collective-permute-start | bytes 1572872 | tf_op jit(solution)/shard_map/ppermute | solution.py:259
  46.2 0.5 collective-permute-done.13.refs_1_
  46.7 6.2 %collective-permute-done.14.refs_3_ = f32[2,4,128,128]{3,2,1,0:T(8,128)S(1)} collective-permute-done((f32[2,4,128,128]{3,2,1,0:T(8,128)S(1)}, f32[2,4,128,128]{3,2,1,0:T(8,128)S(1)}, u32[]{:S(2)}, u32[]{:S(2)}) %collective-permute-start.14) | collective-permute-done | bytes 524320 | tf_op jit(solution)/shard_map/ppermute | solution.py:259
  52.9 7.2 %shard_map.42.refs_4_ = f32[2,4,128,128]{3,2,1,0:T(8,128)S(1)} custom-call(s32[1]{0:T(128)} %bitcast.refs_0_, f32[2,4,128,128]{3,2,1,0:T(8,128)S(1)} %collective-permute-done.13.refs_1_, f32[2,4,128,128]{3,2,1,0:T(8,128)S(1)} %collective-permute-done.9.refs_10_.refs_2_, f32[2,4,128,128]{3,2,1,0:T(8,128)S(1)} %collective-permute-done.14.refs_3_, ...), custom_call_target="tpu_custom_call" | custom-call | flops 10000000000 | bytes 2097152 | tf_op jit(solution)/shard_map/pallas_call | solution.py:224
  60.1 0.0 collective-permute-done.11.token.refs_2_
  60.2 0.0 collective-permute-done.10.refs_1_
  60.2 0.0 collective-permute-done.12.refs_3_
  60.2 3.5 %shard_map.44 = (f32[2,4,128,128]{3,2,1,0:T(8,128)S(1)}, f32[2,4,128,128]{3,2,1,0:T(8,128)}) custom-call(s32[1]{0:T(128)} %bitcast.refs_0_, f32[2,4,128,128]{3,2,1,0:T(8,128)S(1)} %collective-permute-done.10.refs_1_, f32[2,4,128,128]{3,2,1,0:T(8,128)S(1)} %collective-permute-done.11.token.refs_2_, f32[2,4,128,128]{3,2,1,0:T(8,128)S(1)} %collective-permute-done.12.refs_3_, ...), custom_call_target="tpu_custom_call" | custom-call | flops 10000000000 | bytes 2097152 | tf_op jit(solution)/shard_map/pallas_call | solution.py:224
  63.7 0.8 copy-done.1
  64.5 1.3 %collective-permute-start.16 = (f32[2,4,128,128]{3,2,1,0:T(8,128)}, f32[2,4,128,128]{3,2,1,0:T(8,128)S(1)}, u32[]{:S(2)}, u32[]{:S(2)}) collective-permute-start(f32[2,4,128,128]{3,2,1,0:T(8,128)} %get-tuple-element.12), channel_id=1, source_target_pairs={{192,128},{193,129},{194,130},{195,131},{196,132},{197,133},{198,1... | collective-permute-start | bytes 1572872 | tf_op jit(solution)/shard_map/ppermute | solution.py:259
  65.8 1.5 %collective-permute-start.18 = (f32[2,4,128,128]{3,2,1,0:T(8,128)S(1)}, f32[2,4,128,128]{3,2,1,0:T(8,128)}, u32[]{:S(2)}, u32[]{:S(2)}) collective-permute-start(f32[2,4,128,128]{3,2,1,0:T(8,128)S(1)} %shard_map.43.refs_7_.refs_2_), channel_id=1, source_target_pairs={{128,129},{129,130},{130,131},{131,132},{132,133},{133,134},{134,1... | collective-permute-start | bytes 1572872 | tf_op jit(solution)/shard_map/ppermute | solution.py:259
  67.3 1.5 %collective-permute-start.19 = (f32[2,4,128,128]{3,2,1,0:T(8,128)S(1)}, f32[2,4,128,128]{3,2,1,0:T(8,128)}, u32[]{:S(2)}, u32[]{:S(2)}) collective-permute-start(f32[2,4,128,128]{3,2,1,0:T(8,128)S(1)} %shard_map.43.refs_7_.refs_2_), channel_id=1, source_target_pairs={{128,191},{129,128},{130,129},{131,130},{132,131},{133,132},{134,1... | collective-permute-start | bytes 1572872 | tf_op jit(solution)/shard_map/ppermute | solution.py:259
  68.7 5.7 %collective-permute-start.15 = (f32[2,4,128,128]{3,2,1,0:T(8,128)}, f32[2,4,128,128]{3,2,1,0:T(8,128)S(1)}, u32[]{:S(2)}, u32[]{:S(2)}) collective-permute-start(f32[2,4,128,128]{3,2,1,0:T(8,128)} %get-tuple-element.12), channel_id=1, source_target_pairs={{192,129},{193,130},{194,131},{195,132},{196,133},{197,134},{198,1... | collective-permute-start | bytes 1572872 | tf_op jit(solution)/shard_map/ppermute | solution.py:259
  74.4 1.3 %collective-permute-start.17 = (f32[2,4,128,128]{3,2,1,0:T(8,128)}, f32[2,4,128,128]{3,2,1,0:T(8,128)S(1)}, u32[]{:S(2)}, u32[]{:S(2)}) collective-permute-start(f32[2,4,128,128]{3,2,1,0:T(8,128)} %get-tuple-element.12), channel_id=1, source_target_pairs={{192,191},{193,128},{194,129},{195,130},{196,131},{197,132},{198,1... | collective-permute-start | bytes 1572872 | tf_op jit(solution)/shard_map/ppermute | solution.py:259
  75.7 1.1 broadcast_select_fusion
  76.9 0.0 copy-start.10
  76.9 0.0 collective-permute-done.16.refs_2_.token
  76.9 1.5 %collective-permute-start.25 = (f32[2,4,128,128]{3,2,1,0:T(8,128)S(1)}, f32[2,4,128,128]{3,2,1,0:T(8,128)S(1)}, u32[]{:S(2)}, u32[]{:S(2)}) collective-permute-start(f32[2,4,128,128]{3,2,1,0:T(8,128)S(1)} %broadcast_select_fusion), channel_id=1, source_target_pairs={{128,0},{129,1},{130,2},{131,3},{132,4},{133,5},{134,6},{135,7},{1... | collective-permute-start | bytes 1572872 | tf_op jit(solution)/shard_map/ppermute | solution.py:259
  78.4 0.0 collective-permute-done.18.refs_1_
  78.4 1.9 %collective-permute-start.23 = (f32[2,4,128,128]{3,2,1,0:T(8,128)S(1)}, f32[2,4,128,128]{3,2,1,0:T(8,128)S(1)}, u32[]{:S(2)}, u32[]{:S(2)}) collective-permute-start(f32[2,4,128,128]{3,2,1,0:T(8,128)S(1)} %shard_map.47.refs_2_), channel_id=1, source_target_pairs={{192,193},{193,194},{194,195},{195,196},{196,197},{197,198},{198,1... | collective-permute-start | bytes 1572872 | tf_op jit(solution)/shard_map/ppermute | solution.py:259
  80.3 0.0 collective-permute-done.19.refs_3_
  80.3 3.4 %collective-permute-start.24 = (f32[2,4,128,128]{3,2,1,0:T(8,128)S(1)}, f32[2,4,128,128]{3,2,1,0:T(8,128)S(1)}, u32[]{:S(2)}, u32[]{:S(2)}) collective-permute-start(f32[2,4,128,128]{3,2,1,0:T(8,128)S(1)} %shard_map.47.refs_2_), channel_id=1, source_target_pairs={{192,255},{193,192},{194,193},{195,194},{196,195},{197,196},{198,1... | collective-permute-start | bytes 1572872 | tf_op jit(solution)/shard_map/ppermute | solution.py:259
  83.7 1.2 %shard_map.45.refs_4_ = f32[2,4,128,128]{3,2,1,0:T(8,128)S(1)} custom-call(s32[1]{0:T(128)} %bitcast.refs_0_, f32[2,4,128,128]{3,2,1,0:T(8,128)} %collective-permute-done.18.refs_1_, f32[2,4,128,128]{3,2,1,0:T(8,128)S(1)} %shard_map.43.refs_7_.refs_2_, f32[2,4,128,128]{3,2,1,0:T(8,128)} %collective-permute-done.19.refs_3_, ...), custom_call_target="tpu_custom_call" | custom-call | flops 10000000000 | bytes 2097152 | tf_op jit(solution)/shard_map/pallas_call | solution.py:224
  84.9 0.0 collective-permute-done.15.refs_1_
  84.9 0.0 collective-permute-done.17.refs_3_
  85.0 1.4 %collective-permute-start.20 = (f32[2,4,128,128]{3,2,1,0:T(8,128)S(1)}, f32[2,4,128,128]{3,2,1,0:T(8,128)S(1)}, u32[]{:S(2)}, u32[]{:S(2)}) collective-permute-start(f32[2,4,128,128]{3,2,1,0:T(8,128)S(1)} %get-tuple-element.13), channel_id=1, source_target_pairs={{128,193},{129,194},{130,195},{131,196},{132,197},{133,198},{134,1... | collective-permute-start | bytes 1572872 | tf_op jit(solution)/shard_map/ppermute | solution.py:259
  86.4 1.3 %collective-permute-start.21 = (f32[2,4,128,128]{3,2,1,0:T(8,128)S(1)}, f32[2,4,128,128]{3,2,1,0:T(8,128)S(1)}, u32[]{:S(2)}, u32[]{:S(2)}) collective-permute-start(f32[2,4,128,128]{3,2,1,0:T(8,128)S(1)} %get-tuple-element.13), channel_id=1, source_target_pairs={{128,192},{129,193},{130,194},{131,195},{132,196},{133,197},{134,1... | collective-permute-start | bytes 1572872 | tf_op jit(solution)/shard_map/ppermute | solution.py:259
  87.7 0.8 collective-permute-done.23.refs_1_
  88.5 1.3 %collective-permute-start.22 = (f32[2,4,128,128]{3,2,1,0:T(8,128)S(1)}, f32[2,4,128,128]{3,2,1,0:T(8,128)S(1)}, u32[]{:S(2)}, u32[]{:S(2)}) collective-permute-start(f32[2,4,128,128]{3,2,1,0:T(8,128)S(1)} %get-tuple-element.13), channel_id=1, source_target_pairs={{128,255},{129,192},{130,193},{131,194},{132,195},{133,196},{134,1... | collective-permute-start | bytes 1572872 | tf_op jit(solution)/shard_map/ppermute | solution.py:259
  89.7 15.4 %collective-permute-done.24.refs_3_ = f32[2,4,128,128]{3,2,1,0:T(8,128)S(1)} collective-permute-done((f32[2,4,128,128]{3,2,1,0:T(8,128)S(1)}, f32[2,4,128,128]{3,2,1,0:T(8,128)S(1)}, u32[]{:S(2)}, u32[]{:S(2)}) %collective-permute-start.24) | collective-permute-done | bytes 524320 | tf_op jit(solution)/shard_map/ppermute | solution.py:259
  105.2 7.2 %shard_map.48.refs_4_ = f32[2,4,128,128]{3,2,1,0:T(8,128)S(1)} custom-call(s32[1]{0:T(128)} %bitcast.refs_0_, f32[2,4,128,128]{3,2,1,0:T(8,128)S(1)} %collective-permute-done.23.refs_1_, f32[2,4,128,128]{3,2,1,0:T(8,128)S(1)} %shard_map.47.refs_2_, f32[2,4,128,128]{3,2,1,0:T(8,128)S(1)} %collective-permute-done.24.refs_3_, f32[2,4,128,128]{3,2,1,0:T(8,128)S(1)} %copy-done.3, ...), custom_call_target="tpu_custom_call" | custom-call | flops 10000000000 | bytes 2097152 | tf_op jit(solution)/shard_map/pallas_call | solution.py:224
  112.4 0.0 collective-permute-done.20.refs_1_
  112.4 0.0 collective-permute-done.21.refs_2_
  112.4 3.3 %shard_map.49 = f32[2,4,128,128]{3,2,1,0:T(8,128)} custom-call(s32[1]{0:T(128)} %bitcast.refs_0_, f32[2,4,128,128]{3,2,1,0:T(8,128)S(1)} %collective-permute-done.20.refs_1_, f32[2,4,128,128]{3,2,1,0:T(8,128)S(1)} %collective-permute-done.21.refs_2_, f32[2,4,128,128]{3,2,1,0:T(8,128)S(1)} %collective-permute-done.22.refs_3_, ...), custom_call_target="tpu_custom_call" | custom-call | flops 10000000000 | bytes 2097152 | tf_op jit(solution)/shard_map/pallas_call | solution.py:224
  (24 shorter events, 0.3 us)
Async XLA Ops:
  0.0 16.3 %collective-permute-start = (f32[2,4,128,128]{3,2,1,0:T(8,128)}, f32[2,4,128,128]{3,2,1,0:T(8,128)S(1)}, u32[]{:S(2)}, u32[]{:S(2)}) collective-permute-start(f32[2,4,128,128]{3,2,1,0:T(8,128)} %bitcast.3), channel_id=1, source_target_pairs={{0,192},{1,193},{2,194},{3,195},{4,196},{5,197},{6,198},{7,199},{8... | collective-permute-start | bytes 1572872 | tf_op jit(solution)/shard_map/ppermute | solution.py:259
  1.3 17.1 %collective-permute-start.8 = (f32[2,4,128,128]{3,2,1,0:T(8,128)}, f32[2,4,128,128]{3,2,1,0:T(8,128)S(1)}, u32[]{:S(2)}, u32[]{:S(2)}) collective-permute-start(f32[2,4,128,128]{3,2,1,0:T(8,128)} %bitcast.4), channel_id=1, source_target_pairs={{64,0},{65,1},{66,2},{67,3},{68,4},{69,5},{70,6},{71,7},{72,8},{73... | collective-permute-start | bytes 1572872 | tf_op jit(solution)/shard_map/ppermute | solution.py:259
  2.0 1.0 copy-start.6
  2.9 0.9 copy-start.8
  3.9 17.3 %collective-permute-start.4 = (f32[2,4,128,128]{3,2,1,0:T(8,128)S(1)}, f32[2,4,128,128]{3,2,1,0:T(8,128)S(1)}, u32[]{:S(2)}, u32[]{:S(2)}) collective-permute-start(f32[2,4,128,128]{3,2,1,0:T(8,128)S(1)} %shard_map.37), channel_id=1, source_target_pairs={{128,129},{129,130},{130,131},{131,132},{132,133},{133,134},{134,1... | collective-permute-start | bytes 1572872 | tf_op jit(solution)/shard_map/ppermute | solution.py:259
  16.3 6.2 %collective-permute-start.2 = (f32[2,4,128,128]{3,2,1,0:T(8,128)S(1)}, f32[2,4,128,128]{3,2,1,0:T(8,128)S(1)}, u32[]{:S(2)}, u32[]{:S(2)}) collective-permute-start(f32[2,4,128,128]{3,2,1,0:T(8,128)S(1)} %collective-permute-done.token), channel_id=1, source_target_pairs={{192,128},{193,129},{194,130},{195,131},{196,132},{197,133},{198,1... | collective-permute-start | bytes 1572872 | tf_op jit(solution)/shard_map/ppermute | solution.py:259
  17.6 6.4 %collective-permute-start.5 = (f32[2,4,128,128]{3,2,1,0:T(8,128)S(1)}, f32[2,4,128,128]{3,2,1,0:T(8,128)S(1)}, u32[]{:S(2)}, u32[]{:S(2)}) collective-permute-start(f32[2,4,128,128]{3,2,1,0:T(8,128)S(1)} %shard_map.37), channel_id=1, source_target_pairs={{128,191},{129,128},{130,129},{131,130},{132,131},{133,132},{134,1... | collective-permute-start | bytes 1572872 | tf_op jit(solution)/shard_map/ppermute | solution.py:259
  18.4 18.4 %collective-permute-start.9 = (f32[2,4,128,128]{3,2,1,0:T(8,128)S(1)}, f32[2,4,128,128]{3,2,1,0:T(8,128)S(1)}, u32[]{:S(2)}, u32[]{:S(2)}) collective-permute-start(f32[2,4,128,128]{3,2,1,0:T(8,128)S(1)} %shard_map.40), channel_id=1, source_target_pairs={{0,192},{1,193},{2,194},{3,195},{4,196},{5,197},{6,198},{7,199},{8... | collective-permute-start | bytes 1572872 | tf_op jit(solution)/shard_map/ppermute | solution.py:259
  19.7 19.0 %collective-permute-start.1 = (f32[2,4,128,128]{3,2,1,0:T(8,128)S(1)}, f32[2,4,128,128]{3,2,1,0:T(8,128)S(1)}, u32[]{:S(2)}, u32[]{:S(2)}) collective-permute-start(f32[2,4,128,128]{3,2,1,0:T(8,128)S(1)} %collective-permute-done.token), channel_id=1, source_target_pairs={{192,129},{193,130},{194,131},{195,132},{196,133},{197,134},{198,1... | collective-permute-start | bytes 1572872 | tf_op jit(solution)/shard_map/ppermute | solution.py:259
  21.2 20.9 %collective-permute-start.3 = (f32[2,4,128,128]{3,2,1,0:T(8,128)S(1)}, f32[2,4,128,128]{3,2,1,0:T(8,128)S(1)}, u32[]{:S(2)}, u32[]{:S(2)}) collective-permute-start(f32[2,4,128,128]{3,2,1,0:T(8,128)S(1)} %collective-permute-done.token), channel_id=1, source_target_pairs={{192,191},{193,128},{194,129},{195,130},{196,131},{197,132},{198,1... | collective-permute-start | bytes 1572872 | tf_op jit(solution)/shard_map/ppermute | solution.py:259
  22.6 19.5 %copy-start.7 = (f32[4,128,128]{2,1,0:T(8,128)S(1)}, f32[4,128,128]{2,1,0:T(8,128)}, u32[]{:S(2)}) copy-start(f32[4,128,128]{2,1,0:T(8,128)} %refs_5_.11) | copy-start | bytes 786436
  22.6 19.5 %copy-start.9 = (f32[4,128,128]{2,1,0:T(8,128)S(1)}, f32[4,128,128]{2,1,0:T(8,128)}, u32[]{:S(2)}) copy-start(f32[4,128,128]{2,1,0:T(8,128)} %refs_6_.11) | copy-start | bytes 786436
  22.6 19.5 %collective-permute-start.6 = (f32[2,4,128,128]{3,2,1,0:T(8,128)S(1)}, f32[2,4,128,128]{3,2,1,0:T(8,128)S(1)}, u32[]{:S(2)}, u32[]{:S(2)}) collective-permute-start(f32[2,4,128,128]{3,2,1,0:T(8,128)S(1)} %shard_map.38), channel_id=1, source_target_pairs={{128,192},{129,193},{130,194},{131,195},{132,196},{133,197},{134,1... | collective-permute-start | bytes 1572872 | tf_op jit(solution)/shard_map/ppermute | solution.py:259
  24.1 18.0 %collective-permute-start.7 = (f32[2,4,128,128]{3,2,1,0:T(8,128)S(1)}, f32[2,4,128,128]{3,2,1,0:T(8,128)S(1)}, u32[]{:S(2)}, u32[]{:S(2)}) collective-permute-start(f32[2,4,128,128]{3,2,1,0:T(8,128)S(1)} %shard_map.39), channel_id=1, source_target_pairs={{128,192},{129,193},{130,194},{131,195},{132,196},{133,197},{134,1... | collective-permute-start | bytes 1572872 | tf_op jit(solution)/shard_map/ppermute | solution.py:259
  36.8 9.9 %collective-permute-start.13 = (f32[2,4,128,128]{3,2,1,0:T(8,128)S(1)}, f32[2,4,128,128]{3,2,1,0:T(8,128)S(1)}, u32[]{:S(2)}, u32[]{:S(2)}) collective-permute-start(f32[2,4,128,128]{3,2,1,0:T(8,128)S(1)} %collective-permute-done.9.refs_10_.refs_2_), channel_id=1, source_target_pairs={{192,193},{193,194},{194,195},{195,196},{196,197},{197,198},{198,1... | collective-permute-start | bytes 1572872 | tf_op jit(solution)/shard_map/ppermute | solution.py:259
  38.7 14.1 %collective-permute-start.14 = (f32[2,4,128,128]{3,2,1,0:T(8,128)S(1)}, f32[2,4,128,128]{3,2,1,0:T(8,128)S(1)}, u32[]{:S(2)}, u32[]{:S(2)}) collective-permute-start(f32[2,4,128,128]{3,2,1,0:T(8,128)S(1)} %collective-permute-done.9.refs_10_.refs_2_), channel_id=1, source_target_pairs={{192,255},{193,192},{194,193},{195,194},{196,195},{197,196},{198,1... | collective-permute-start | bytes 1572872 | tf_op jit(solution)/shard_map/ppermute | solution.py:259
  42.1 10.8 %copy-start.2 = (f32[2,4,128,128]{3,2,1,0:T(8,128)}, f32[2,4,128,128]{3,2,1,0:T(8,128)S(1)}, u32[]{:S(2)}) copy-start(f32[2,4,128,128]{3,2,1,0:T(8,128)S(1)} %collective-permute-done.6.refs_8_.refs_4_) | copy-start | bytes 1572868
  42.2 10.7 %copy-start.4 = (f32[2,4,128,128]{3,2,1,0:T(8,128)}, f32[2,4,128,128]{3,2,1,0:T(8,128)S(1)}, u32[]{:S(2)}) copy-start(f32[2,4,128,128]{3,2,1,0:T(8,128)S(1)} %collective-permute-done.7.refs_9_.refs_7_) | copy-start | bytes 1572868
  42.2 17.9 %copy-start = (f32[1,2,4,128,128]{4,3,2,1,0:T(8,128)S(1)}, f32[1,2,4,128,128]{4,3,2,1,0:T(8,128)}, u32[]{:S(2)}) copy-start(f32[1,2,4,128,128]{4,3,2,1,0:T(8,128)} %param.3) | copy-start | bytes 1572868
  42.2 17.9 %collective-permute-start.11 = (f32[2,4,128,128]{3,2,1,0:T(8,128)S(1)}, f32[2,4,128,128]{3,2,1,0:T(8,128)S(1)}, u32[]{:S(2)}, u32[]{:S(2)}) collective-permute-start(f32[2,4,128,128]{3,2,1,0:T(8,128)S(1)} %get-tuple-element.11), channel_id=1, source_target_pairs={{128,192},{129,193},{130,194},{131,195},{132,196},{133,197},{134,1... | collective-permute-start | bytes 1572872 | tf_op jit(solution)/shard_map/ppermute | solution.py:259
  43.6 16.5 %collective-permute-start.10 = (f32[2,4,128,128]{3,2,1,0:T(8,128)S(1)}, f32[2,4,128,128]{3,2,1,0:T(8,128)S(1)}, u32[]{:S(2)}, u32[]{:S(2)}) collective-permute-start(f32[2,4,128,128]{3,2,1,0:T(8,128)S(1)} %get-tuple-element.11), channel_id=1, source_target_pairs={{128,193},{129,194},{130,195},{131,196},{132,197},{133,198},{134,1... | collective-permute-start | bytes 1572872 | tf_op jit(solution)/shard_map/ppermute | solution.py:259
  44.9 15.2 %collective-permute-start.12 = (f32[2,4,128,128]{3,2,1,0:T(8,128)S(1)}, f32[2,4,128,128]{3,2,1,0:T(8,128)S(1)}, u32[]{:S(2)}, u32[]{:S(2)}) collective-permute-start(f32[2,4,128,128]{3,2,1,0:T(8,128)S(1)} %get-tuple-element.11), channel_id=1, source_target_pairs={{128,255},{129,192},{130,193},{131,194},{132,195},{133,196},{134,1... | collective-permute-start | bytes 1572872 | tf_op jit(solution)/shard_map/ppermute | solution.py:259
  63.7 0.8 copy-start.1
  64.5 12.4 %collective-permute-start.16 = (f32[2,4,128,128]{3,2,1,0:T(8,128)}, f32[2,4,128,128]{3,2,1,0:T(8,128)S(1)}, u32[]{:S(2)}, u32[]{:S(2)}) collective-permute-start(f32[2,4,128,128]{3,2,1,0:T(8,128)} %get-tuple-element.12), channel_id=1, source_target_pairs={{192,128},{193,129},{194,130},{195,131},{196,132},{197,133},{198,1... | collective-permute-start | bytes 1572872 | tf_op jit(solution)/shard_map/ppermute | solution.py:259
  65.8 12.6 %collective-permute-start.18 = (f32[2,4,128,128]{3,2,1,0:T(8,128)S(1)}, f32[2,4,128,128]{3,2,1,0:T(8,128)}, u32[]{:S(2)}, u32[]{:S(2)}) collective-permute-start(f32[2,4,128,128]{3,2,1,0:T(8,128)S(1)} %shard_map.43.refs_7_.refs_2_), channel_id=1, source_target_pairs={{128,129},{129,130},{130,131},{131,132},{132,133},{133,134},{134,1... | collective-permute-start | bytes 1572872 | tf_op jit(solution)/shard_map/ppermute | solution.py:259
  67.3 13.1 %collective-permute-start.19 = (f32[2,4,128,128]{3,2,1,0:T(8,128)S(1)}, f32[2,4,128,128]{3,2,1,0:T(8,128)}, u32[]{:S(2)}, u32[]{:S(2)}) collective-permute-start(f32[2,4,128,128]{3,2,1,0:T(8,128)S(1)} %shard_map.43.refs_7_.refs_2_), channel_id=1, source_target_pairs={{128,191},{129,128},{130,129},{131,130},{132,131},{133,132},{134,1... | collective-permute-start | bytes 1572872 | tf_op jit(solution)/shard_map/ppermute | solution.py:259
  68.7 16.2 %collective-permute-start.15 = (f32[2,4,128,128]{3,2,1,0:T(8,128)}, f32[2,4,128,128]{3,2,1,0:T(8,128)S(1)}, u32[]{:S(2)}, u32[]{:S(2)}) collective-permute-start(f32[2,4,128,128]{3,2,1,0:T(8,128)} %get-tuple-element.12), channel_id=1, source_target_pairs={{192,129},{193,130},{194,131},{195,132},{196,133},{197,134},{198,1... | collective-permute-start | bytes 1572872 | tf_op jit(solution)/shard_map/ppermute | solution.py:259
  74.4 10.5 %collective-permute-start.17 = (f32[2,4,128,128]{3,2,1,0:T(8,128)}, f32[2,4,128,128]{3,2,1,0:T(8,128)S(1)}, u32[]{:S(2)}, u32[]{:S(2)}) collective-permute-start(f32[2,4,128,128]{3,2,1,0:T(8,128)} %get-tuple-element.12), channel_id=1, source_target_pairs={{192,191},{193,128},{194,129},{195,130},{196,131},{197,132},{198,1... | collective-permute-start | bytes 1572872 | tf_op jit(solution)/shard_map/ppermute | solution.py:259
  76.9 6.9 %copy-start.10 = (f32[4,128,128]{2,1,0:T(8,128)S(1)}, f32[4,128,128]{2,1,0:T(8,128)}, u32[]{:S(2)}) copy-start(f32[4,128,128]{2,1,0:T(8,128)} %refs_6_.11) | copy-start | bytes 786436
  76.9 35.5 %collective-permute-start.25 = (f32[2,4,128,128]{3,2,1,0:T(8,128)S(1)}, f32[2,4,128,128]{3,2,1,0:T(8,128)S(1)}, u32[]{:S(2)}, u32[]{:S(2)}) collective-permute-start(f32[2,4,128,128]{3,2,1,0:T(8,128)S(1)} %broadcast_select_fusion), channel_id=1, source_target_pairs={{128,0},{129,1},{130,2},{131,3},{132,4},{133,5},{134,6},{135,7},{1... | collective-permute-start | bytes 1572872 | tf_op jit(solution)/shard_map/ppermute | solution.py:259
  78.4 10.1 %collective-permute-start.23 = (f32[2,4,128,128]{3,2,1,0:T(8,128)S(1)}, f32[2,4,128,128]{3,2,1,0:T(8,128)S(1)}, u32[]{:S(2)}, u32[]{:S(2)}) collective-permute-start(f32[2,4,128,128]{3,2,1,0:T(8,128)S(1)} %shard_map.47.refs_2_), channel_id=1, source_target_pairs={{192,193},{193,194},{194,195},{195,196},{196,197},{197,198},{198,1... | collective-permute-start | bytes 1572872 | tf_op jit(solution)/shard_map/ppermute | solution.py:259
  80.3 24.8 %collective-permute-start.24 = (f32[2,4,128,128]{3,2,1,0:T(8,128)S(1)}, f32[2,4,128,128]{3,2,1,0:T(8,128)S(1)}, u32[]{:S(2)}, u32[]{:S(2)}) collective-permute-start(f32[2,4,128,128]{3,2,1,0:T(8,128)S(1)} %shard_map.47.refs_2_), channel_id=1, source_target_pairs={{192,255},{193,192},{194,193},{195,194},{196,195},{197,196},{198,1... | collective-permute-start | bytes 1572872 | tf_op jit(solution)/shard_map/ppermute | solution.py:259
  84.9 20.3 %copy-start.3 = (f32[2,4,128,128]{3,2,1,0:T(8,128)S(1)}, f32[2,4,128,128]{3,2,1,0:T(8,128)}, u32[]{:S(2)}) copy-start(f32[2,4,128,128]{3,2,1,0:T(8,128)} %copy-done.2) | copy-start | bytes 1572868
  84.9 20.3 %copy-start.5 = (f32[2,4,128,128]{3,2,1,0:T(8,128)S(1)}, f32[2,4,128,128]{3,2,1,0:T(8,128)}, u32[]{:S(2)}) copy-start(f32[2,4,128,128]{3,2,1,0:T(8,128)} %copy-done.4) | copy-start | bytes 1572868
  85.0 27.5 %collective-permute-start.20 = (f32[2,4,128,128]{3,2,1,0:T(8,128)S(1)}, f32[2,4,128,128]{3,2,1,0:T(8,128)S(1)}, u32[]{:S(2)}, u32[]{:S(2)}) collective-permute-start(f32[2,4,128,128]{3,2,1,0:T(8,128)S(1)} %get-tuple-element.13), channel_id=1, source_target_pairs={{128,193},{129,194},{130,195},{131,196},{132,197},{133,198},{134,1... | collective-permute-start | bytes 1572872 | tf_op jit(solution)/shard_map/ppermute | solution.py:259
  86.4 26.0 %collective-permute-start.21 = (f32[2,4,128,128]{3,2,1,0:T(8,128)S(1)}, f32[2,4,128,128]{3,2,1,0:T(8,128)S(1)}, u32[]{:S(2)}, u32[]{:S(2)}) collective-permute-start(f32[2,4,128,128]{3,2,1,0:T(8,128)S(1)} %get-tuple-element.13), channel_id=1, source_target_pairs={{128,192},{129,193},{130,194},{131,195},{132,196},{133,197},{134,1... | collective-permute-start | bytes 1572872 | tf_op jit(solution)/shard_map/ppermute | solution.py:259
  88.5 24.0 %collective-permute-start.22 = (f32[2,4,128,128]{3,2,1,0:T(8,128)S(1)}, f32[2,4,128,128]{3,2,1,0:T(8,128)S(1)}, u32[]{:S(2)}, u32[]{:S(2)}) collective-permute-start(f32[2,4,128,128]{3,2,1,0:T(8,128)S(1)} %get-tuple-element.13), channel_id=1, source_target_pairs={{128,255},{129,192},{130,193},{131,194},{132,195},{133,196},{134,1... | collective-permute-start | bytes 1572872 | tf_op jit(solution)/shard_map/ppermute | solution.py:259

commit v2 on v1

--- a/solution.py
+++ b/solution.py
@@ -126,10 +126,10 @@
     return coefficient
 
 
-def fine_kernel(worker, position, low, own, high, low_c, feed, kill, high_c, state, explicit, *levels):
+def fine_kernel(worker, position, low, own, high, low_c, feed, kill, high_c, explicit, state, *levels):
     depth = own.shape[1]
 
-    @pl.when((position[0] == worker[0]) | (position[0] == worker[-1]))
+    @pl.when((position[0] >= worker[0]) & (position[0] <= worker[-1]))
     def _():
         coefficient = coefficients_of(low_c, feed, kill, high_c, depth)
         fine_levels(joined(low, own, high, depth), coefficient, levels, state, depth)
@@ -144,7 +144,7 @@
 ):
     depth = own.shape[1]
 
-    @pl.when((position[0] == worker[0]) | (position[0] == worker[-1]))
+    @pl.when((position[0] >= worker[0]) & (position[0] <= worker[-1]))
     def _():
         coefficient = coefficients_of(low_c, feed, kill, high_c, depth)
         read = joined(low, own, high, depth)
@@ -163,10 +163,10 @@
         coarse_levels(lambda species, layer: wide[species, layer], (level_a, level_b), finish, depth)
 
 
-def coarse_kernel(worker, position, low, own, high, correction, feed, kill, state, explicit, *levels):
+def coarse_kernel(worker, position, low, own, high, correction, feed, kill, explicit, state, *levels):
     depth = own.shape[1]
 
-    @pl.when((position[0] == worker[0]) | (position[0] == worker[-1]))
+    @pl.when((position[0] >= worker[0]) & (position[0] <= worker[-1]))
     def _():
         def finish(layer, new):
             first = new[0] + correction[0, layer]
@@ -180,18 +180,14 @@
         coarse_levels(joined(low, own, high, depth), levels, finish, depth)
 
 
-def last_kernel(worker, position, low, own, high, correction, third, back, state, *levels):
+def last_kernel(worker, position, low, own, high, correction, third, state, *levels):
     depth = own.shape[1]
 
-    @pl.when(position[0] < worker[0] - 1)
-    def _():
-        state[...] = back[...]
-
-    @pl.when(position[0] == worker[0] - 1)
+    @pl.when(position[0] != worker[0])
     def _():
         state[...] = third[...]
 
-    @pl.when((position[0] == worker[0]) | (position[0] == worker[-1]))
+    @pl.when(position[0] == worker[0])
     def _():
         def finish(layer, new):
             for species in (0, 1):
@@ -200,9 +196,33 @@
         coarse_levels(joined(low, own, high, depth), levels, finish, depth)
 
 
+def result_kernel(position, first, second, received, result):
+    @pl.when(position[0] == 0)
+    def _():
+        result[...] = first[...]
+
+    @pl.when(position[0] == 1)
+    def _():
+        result[...] = second[...]
+
+    @pl.when(position[0] > 1)
+    def _():
+        result[...] = received[...]
+
+
 def stack_kernel(position, feed, kill, both):
     both[0] = feed[...]
     both[1] = kill[...]
+
+
+def pick_kernel(flag, array, other, picked):
+    @pl.when(flag[0] != 0)
+    def _():
+        picked[...] = array[...]
+
+    @pl.when(flag[0] == 0)
+    def _():
+        picked[...] = other[...]
 
 
 def run(body, position, operands, outputs, scratch=2, pinned=True, worker=None, tokens=()):
@@ -228,105 +248,105 @@
         out_specs=[VMEM] * outputs,
         scratch_shapes=[pltpu.VMEM((2, count, *plane), jnp.float32) for count in layers],
         compiler_params=pltpu.CompilerParams(vmem_limit_bytes=12 * 2**20),
-        cost_estimate=pl.CostEstimate(flops=10**10, bytes_accessed=2**21, transcendentals=0),
+        cost_estimate=pl.CostEstimate(
+            flops=10**10 if scratch else 10**5, bytes_accessed=2**20, transcendentals=0
+        ),
     )(position, *operands, *tokens)
 
 
-def copy_kernel(array, token, copied):
-    copied[...] = array[...]
-
-
-def after(array, token):
-    return pl.pallas_call(
-        copy_kernel,
-        out_shape=pltpu.VMEM(array.shape, array.dtype),
-        in_specs=[VMEM, ANY],
-        out_specs=VMEM,
-        compiler_params=pltpu.CompilerParams(vmem_limit_bytes=4 * 2**20),
-    )(array, token)
+def pick(flag, array, other, tokens=()):
+    flag = flag.astype(jnp.int32).reshape(1)
+    return run(pick_kernel, flag, (array, other), 1, 0, tokens=tokens)[0]
 
 
 def shards(starts, feed, kill):
     own = starts[0]
     slabs = lax.axis_size("space")
-    position = lax.axis_index("tm").astype(jnp.int32).reshape(1)
-
-    def moved(array, routes, shift=0):
+    ring = 4
+    index = lax.axis_index("tm")
+    position = index.astype(jnp.int32).reshape(1)
+    place = lax.axis_index("space") % ring
+
+    def moved(array, target_of):
         pairs = []
-        for source, target in routes:
+        for source in range(4):
             for slab in range(slabs):
-                pairs.append((source * slabs + slab, target * slabs + (slab + shift) % slabs))
+                target = target_of(source, slab)
+                if target is not None:
+                    pairs.append((source * slabs + slab, target[0] * slabs + target[1] % slabs))
         return lax.ppermute(array, AXES, pairs)
 
-    def sides(array, routes):
-        return moved(array, routes, 1), moved(array, routes, -1)
+    def beside(slab, step):
+        return slab // ring * ring + (slab + step) % ring
+
+    def onward(step):
+        return lambda source, slab: (source, slab + step if source < 2 else beside(slab, step))
+
+    def halves(source, slab):
+        return onward(1 if source % 2 == 0 else -1)(source, slab)
+
+    def far_half(source, slab):
+        if source == 2 and slab % ring == 0:
+            return source, slab + ring
+        if source == 3 and slab % ring == ring - 1:
+            return source, slab - ring
+        return None
+
+    def far(source, slab):
+        if source >= 2 and slab % ring == 0:
+            return source, slab + ring
+        if source >= 2 and slab % ring == ring - 1:
+            return source, slab - ring
+        return None
+
+    def route(source, target, shift=0):
+        return lambda origin, slab: (target, slab + shift) if origin == source else None
 
     def spread(array, source, target):
-        low, high = sides(array, [(source, target)])
-        return low, moved(array, [(source, target)]), high
-
-    crossed = moved(own, [(0, 3)])
-    lent = moved(own, [(1, 0)])
+        low = moved(array, route(source, target, 1))
+        high = moved(array, route(source, target, -1))
+        return low, moved(array, route(source, target)), high
+
     (both,) = run(stack_kernel, position, (feed, kill), 1, 0)
-    low_c, high_c = sides(both, [(2, 2)])
-    first = spread(crossed, 3, 2)
-    lent = moved(after(lent, crossed), [(0, 3)])
-    low_d = moved(after(low_c, first[1]), [(2, 3)])
-    high_d = moved(after(high_c, first[1]), [(2, 3)])
-    low_1, high_1 = sides(lent, [(3, 3)])
-    ends, explicit = run(
-        fine_kernel,
-        position,
-        (*first, low_c, feed, kill, high_c),
-        2,
-        worker=(2,),
-        tokens=(low_d, high_d, lent),
-    )
-    second = spread(explicit, 2, 3)
+    half = moved(both, halves)
+    low = moved(own, onward(1))
+    high = moved(own, onward(-1))
+    half_far = moved(half, far_half)
+    lowest = (index >= 2) & (place == 0)
+    highest = (index >= 2) & (place == ring - 1)
+    half = pick((lowest & (index == 2)) | (highest & (index == 3)), half_far, half)
+    other = moved(half, lambda source, slab: (source ^ 1, slab))
+    explicit, first_end = run(
+        fine_kernel, position, (low, own, high, half, feed, kill, other), 2, worker=(0,)
+    )
+    second = spread(explicit, 0, 1)
+    sides_far = moved(pick(place == 0, low, high), far)
+    low = pick(lowest, sides_far, low)
+    high = pick(highest, sides_far, high)
+    even = index % 2 == 0
+    low_c = pick(even, half, other)
+    high_c = pick(even, other, half)
     (correction,) = run(
         correction_kernel,
         position,
-        (low_1, lent, high_1, low_d, feed, kill, high_d),
+        (low, own, high, low_c, feed, kill, high_c),
         1,
         3,
-        worker=(3,),
-    )
-    own_2 = after(own, second[1])
-    low_2, high_2 = sides(own_2, [(2, 2)])
-    ends_b, explicit = run(
-        coarse_kernel,
-        position,
-        (*second, correction, feed, kill),
-        2,
-        worker=(3,),
-        tokens=(own_2,),
-    )
-    third = spread(explicit, 3, 2)
-    back = moved(jnp.where(position[0] == 2, ends, ends_b), [(2, 0), (3, 1)])
-    own_3 = after(own, third[1])
-    low_3, high_3 = sides(own_3, [(3, 3)])
-    (correction,) = run(
-        correction_kernel,
-        position,
-        (low_2, own_2, high_2, low_c, feed, kill, high_c),
-        1,
-        3,
-        worker=(2,),
-    )
-    ends_c, explicit = run(
-        coarse_kernel, position, (*third, correction, feed, kill), 2, worker=(2,)
-    )
-    fourth = spread(explicit, 2, 3)
-    (correction,) = run(
-        correction_kernel,
-        position,
-        (low_3, own_3, high_3, low_d, feed, kill, high_d),
-        1,
-        3,
-        worker=(3,),
-    )
+        worker=(1, 3),
+    )
+    crossed = moved(correction, lambda source, slab: (source - 2, slab) if source >= 2 else None)
+    explicit, second_end = run(
+        coarse_kernel, position, (*second, correction, feed, kill), 2, worker=(1,)
+    )
+    third = spread(explicit, 1, 0)
+    explicit, third_end = run(
+        coarse_kernel, position, (*third, crossed, feed, kill), 2, worker=(0,)
+    )
+    fourth = spread(explicit, 0, 1)
+    (last_end,) = run(last_kernel, position, (*fourth, crossed, third_end), 1, worker=(1,))
+    received = moved(last_end, lambda source, slab: (source + 2, slab) if source < 2 else None)
     (result,) = run(
-        last_kernel, position, (*fourth, correction, ends_c, back), 1, pinned=False, worker=(3,)
+        result_kernel, position, (first_end, second_end, received), 1, 0, pinned=False
     )
     return result[None]
 

time: 116 us -> 104 us (0.90)
  the two profiles are of different devices: /device:TPU:111 before, /device:TPU:1 now
where the time goes in v2:
time: 104 us
  waiting for transfers between devices  56.7 us (55%)
  starting transfers between devices  30.7 us (30%)
  Pallas kernels  14.5 us (14%)
  local copies, waits for them, and re-layouts  1.92 us (2%)
    ppermute x17, waiting for transfers between devices, moved(): return lax.ppermute(array, AXES, pairs)  56.7 us
    ppermute x17, starting transfers between devices, moved(): return lax.ppermute(array, AXES, pairs)  30.7 us
    pallas_call x13, Pallas kernels, run(): pl.pallas_call(kernel, out_shape=out_shape, in_specs=[SMEM] + [VMEM] * le...  14.5 us
  transfers between devices with their start and end apart: 17, of which 10 were waited for; matrix products, arithmetic and copies ran while one was open for 0% of the time, Pallas kernels for 11%

profile of v2, /device:TPU:1, one launch (start us, length us, event | category | flops | bytes accessed | tf_op | source)
XLA Modules:
  0.0 104.0 jit_solution(14621610776844952675)
XLA Ops:
  0.0 0.0 copy-start
  0.0 0.9 copy-done
  1.0 0.0 copy-start.2
  1.0 0.9 copy-done.2
  1.9 0.0 copy-start.4
  1.9 11.6 %collective-permute-start.2 = (f32[2,4,128,128]{3,2,1,0:T(8,128)S(1)}, f32[2,4,128,128]{3,2,1,0:T(8,128)S(1)}, u32[]{:S(2)}, u32[]{:S(2)}) collective-permute-start(f32[2,4,128,128]{3,2,1,0:T(8,128)S(1)} %shard_map.37), channel_id=1, source_target_pairs={{0,1},{1,2},{2,3},{3,4},{4,5},{5,6},{6,7},{7,8},{8,9},{9,10},{10,1... | collective-permute-start | bytes 1572872 | tf_op jit(solution)/shard_map/ppermute | solution.py:277
  13.5 0.0 copy-done.4
  13.5 0.9 collective-permute-start.1
  14.4 0.5 collective-permute-start
  15.0 8.1 %collective-permute-done.2.refs_2_ = f32[2,4,128,128]{3,2,1,0:T(8,128)S(1)} collective-permute-done((f32[2,4,128,128]{3,2,1,0:T(8,128)S(1)}, f32[2,4,128,128]{3,2,1,0:T(8,128)S(1)}, u32[]{:S(2)}, u32[]{:S(2)}) %collective-permute-start.2) | collective-permute-done | bytes 524320 | tf_op jit(solution)/shard_map/ppermute | solution.py:277
  23.1 0.7 collective-permute-start.3
  23.9 7.0 %collective-permute-done.1.refs_3_.refs_2_ = f32[2,4,128,128]{3,2,1,0:T(8,128)S(1)} collective-permute-done((f32[2,4,128,128]{3,2,1,0:T(8,128)S(1)}, f32[2,4,128,128]{3,2,1,0:T(8,128)S(1)}, u32[]{:S(2)}, u32[]{:S(2)}) %collective-permute-start.1) | collective-permute-done | bytes 524320 | tf_op jit(solution)/shard_map/ppermute | solution.py:277
  30.9 2.4 %collective-permute-done.refs_1_.refs_2_ = f32[2,4,128,128]{3,2,1,0:T(8,128)S(1)} collective-permute-done((f32[2,4,128,128]{3,2,1,0:T(8,128)S(1)}, f32[2,4,128,128]{3,2,1,0:T(8,128)S(1)}, u32[]{:S(2)}, u32[]{:S(2)}) %collective-permute-start) | collective-permute-done | bytes 524320 | tf_op jit(solution)/shard_map/ppermute | solution.py:277
  33.2 0.8 shard_map.40
  34.1 0.7 collective-permute-start.8
  34.8 0.0 collective-permute-done.3.refs_1_
  34.8 2.0 %collective-permute-start.4 = (f32[2,4,128,128]{3,2,1,0:T(8,128)S(1)}, f32[2,4,128,128]{3,2,1,0:T(8,128)S(1)}, u32[]{:S(2)}, u32[]{:S(2)}) collective-permute-start(f32[2,4,128,128]{3,2,1,0:T(8,128)S(1)} %shard_map.38.refs_4_.refs_1_.refs_2_), channel_id=1, source_target_pairs={{0,64},{1,65},{2,66},{3,67},{4,68},{5,69},{6,70},{7,71},{8,72},{9,... | collective-permute-start | bytes 1572872 | tf_op jit(solution)/shard_map/ppermute | solution.py:277
  36.8 0.0 collective-permute-done.8.refs_1_
  36.8 0.0 copy-start.1
  36.8 0.0 copy-start.3
  36.9 0.0 copy-start.5
  36.9 1.4 %collective-permute-done.4.refs_7_.refs_2_.refs_1_ = f32[2,4,128,128]{3,2,1,0:T(8,128)S(1)} collective-permute-done((f32[2,4,128,128]{3,2,1,0:T(8,128)S(1)}, f32[2,4,128,128]{3,2,1,0:T(8,128)S(1)}, u32[]{:S(2)}, u32[]{:S(2)}) %collective-permute-start.4) | collective-permute-done | bytes 524320 | tf_op jit(solution)/shard_map/ppermute | solution.py:277
  38.3 0.0 copy-done.1
  38.3 0.0 copy-done.3
  38.3 0.0 copy-done.5
  38.3 1.3 %collective-permute-start.7 = (f32[2,4,128,128]{3,2,1,0:T(8,128)S(1)}, f32[2,4,128,128]{3,2,1,0:T(8,128)S(1)}, u32[]{:S(2)}, u32[]{:S(2)}) collective-permute-start(f32[2,4,128,128]{3,2,1,0:T(8,128)S(1)} %get-tuple-element.12), channel_id=1, source_target_pairs={{0,127},{1,64},{2,65},{3,66},{4,67},{5,68},{6,69},{7,70},{8,71},{9... | collective-permute-start | bytes 1572872 | tf_op jit(solution)/shard_map/ppermute | solution.py:277
  39.6 1.3 %collective-permute-start.6 = (f32[2,4,128,128]{3,2,1,0:T(8,128)S(1)}, f32[2,4,128,128]{3,2,1,0:T(8,128)S(1)}, u32[]{:S(2)}, u32[]{:S(2)}) collective-permute-start(f32[2,4,128,128]{3,2,1,0:T(8,128)S(1)} %get-tuple-element.12), channel_id=1, source_target_pairs={{0,64},{1,65},{2,66},{3,67},{4,68},{5,69},{6,70},{7,71},{8,72},{9,... | collective-permute-start | bytes 1572872 | tf_op jit(solution)/shard_map/ppermute | solution.py:277
  40.9 1.3 %collective-permute-start.5 = (f32[2,4,128,128]{3,2,1,0:T(8,128)S(1)}, f32[2,4,128,128]{3,2,1,0:T(8,128)S(1)}, u32[]{:S(2)}, u32[]{:S(2)}) collective-permute-start(f32[2,4,128,128]{3,2,1,0:T(8,128)S(1)} %get-tuple-element.12), channel_id=1, source_target_pairs={{0,65},{1,66},{2,67},{3,68},{4,69},{5,70},{6,71},{7,72},{8,73},{9,... | collective-permute-start | bytes 1572872 | tf_op jit(solution)/shard_map/ppermute | solution.py:277
  42.3 7.5 %shard_map.45.refs_4_ = f32[2,4,128,128]{3,2,1,0:T(8,128)S(1)} custom-call(s32[1]{0:T(128)} %bitcast.refs_0_, f32[2,4,128,128]{3,2,1,0:T(8,128)S(1)} %shard_map.41.refs_1_, f32[2,4,128,128]{3,2,1,0:T(8,128)S(1)} %bitcast.11, f32[2,4,128,128]{3,2,1,0:T(8,128)S(1)} %shard_map.42.refs_3_, f32[2,4,128,128]{3,2,1,0:T(8,128)S(1)} %shard_map.43.refs_4_, ...), custom_call_target="tpu_custom_call" | custom-call | flops 10000000000 | bytes 1048576 | tf_op jit(solution)/shard_map/pallas_call | solution.py:244
  49.8 1.3 %collective-permute-start.12 = (f32[2,4,128,128]{3,2,1,0:T(8,128)S(1)}, f32[2,4,128,128]{3,2,1,0:T(8,128)S(1)}, u32[]{:S(2)}, u32[]{:S(2)}) collective-permute-start(f32[2,4,128,128]{3,2,1,0:T(8,128)S(1)} %shard_map.45.refs_4_), channel_id=1, source_target_pairs={{128,0},{129,1},{130,2},{131,3},{132,4},{133,5},{134,6},{135,7},{1... | collective-permute-start | bytes 1572872 | tf_op jit(solution)/shard_map/ppermute | solution.py:277
  51.1 0.0 collective-permute-done.7.refs_3_
  51.1 0.0 collective-permute-done.6.refs_2_
  51.1 7.3 %collective-permute-done.5.refs_1_ = f32[2,4,128,128]{3,2,1,0:T(8,128)S(1)} collective-permute-done((f32[2,4,128,128]{3,2,1,0:T(8,128)S(1)}, f32[2,4,128,128]{3,2,1,0:T(8,128)S(1)}, u32[]{:S(2)}, u32[]{:S(2)}) %collective-permute-start.5) | collective-permute-done | bytes 524320 | tf_op jit(solution)/shard_map/ppermute | solution.py:277
  58.4 2.5 %shard_map.46 = (f32[2,4,128,128]{3,2,1,0:T(8,128)S(1)}, f32[2,4,128,128]{3,2,1,0:T(8,128)S(1)}) custom-call(s32[1]{0:T(128)} %bitcast.refs_0_, f32[2,4,128,128]{3,2,1,0:T(8,128)S(1)} %collective-permute-done.5.refs_1_, f32[2,4,128,128]{3,2,1,0:T(8,128)S(1)} %collective-permute-done.6.refs_2_, f32[2,4,128,128]{3,2,1,0:T(8,128)S(1)} %collective-permute-done.7.refs_3_, ...), custom_call_target="tpu_custom_call" | custom-call | flops 10000000000 | bytes 1048576 | tf_op jit(solution)/shard_map/pallas_call | solution.py:244
  60.9 1.3 %collective-permute-start.11 = (f32[2,4,128,128]{3,2,1,0:T(8,128)S(1)}, f32[2,4,128,128]{3,2,1,0:T(8,128)S(1)}, u32[]{:S(2)}, u32[]{:S(2)}) collective-permute-start(f32[2,4,128,128]{3,2,1,0:T(8,128)S(1)} %get-tuple-element.14), channel_id=1, source_target_pairs={{64,63},{65,0},{66,1},{67,2},{68,3},{69,4},{70,5},{71,6},{72,7},{7... | collective-permute-start | bytes 1572872 | tf_op jit(solution)/shard_map/ppermute | solution.py:277
  62.3 1.3 %collective-permute-start.10 = (f32[2,4,128,128]{3,2,1,0:T(8,128)S(1)}, f32[2,4,128,128]{3,2,1,0:T(8,128)S(1)}, u32[]{:S(2)}, u32[]{:S(2)}) collective-permute-start(f32[2,4,128,128]{3,2,1,0:T(8,128)S(1)} %get-tuple-element.14), channel_id=1, source_target_pairs={{64,0},{65,1},{66,2},{67,3},{68,4},{69,5},{70,6},{71,7},{72,8},{73... | collective-permute-start | bytes 1572872 | tf_op jit(solution)/shard_map/ppermute | solution.py:277
  63.6 1.3 %collective-permute-start.9 = (f32[2,4,128,128]{3,2,1,0:T(8,128)S(1)}, f32[2,4,128,128]{3,2,1,0:T(8,128)S(1)}, u32[]{:S(2)}, u32[]{:S(2)}) collective-permute-start(f32[2,4,128,128]{3,2,1,0:T(8,128)S(1)} %get-tuple-element.14), channel_id=1, source_target_pairs={{64,1},{65,2},{66,3},{67,4},{68,5},{69,6},{70,7},{71,8},{72,9},{73... | collective-permute-start | bytes 1572872 | tf_op jit(solution)/shard_map/ppermute | solution.py:277
  64.9 4.8 %collective-permute-done.12.refs_4_ = f32[2,4,128,128]{3,2,1,0:T(8,128)S(1)} collective-permute-done((f32[2,4,128,128]{3,2,1,0:T(8,128)S(1)}, f32[2,4,128,128]{3,2,1,0:T(8,128)S(1)}, u32[]{:S(2)}, u32[]{:S(2)}) %collective-permute-start.12) | collective-permute-done | bytes 524320 | tf_op jit(solution)/shard_map/ppermute | solution.py:277
  69.7 0.0 collective-permute-done.11.refs_3_
  69.7 0.0 collective-permute-done.10.refs_2_
  69.7 1.3 %collective-permute-done.9.refs_1_ = f32[2,4,128,128]{3,2,1,0:T(8,128)S(1)} collective-permute-done((f32[2,4,128,128]{3,2,1,0:T(8,128)S(1)}, f32[2,4,128,128]{3,2,1,0:T(8,128)S(1)}, u32[]{:S(2)}, u32[]{:S(2)}) %collective-permute-start.9) | collective-permute-done | bytes 524320 | tf_op jit(solution)/shard_map/ppermute | solution.py:277
  71.0 1.3 %collective-permute-start.15 = (f32[2,4,128,128]{3,2,1,0:T(8,128)S(1)}, f32[2,4,128,128]{3,2,1,0:T(8,128)S(1)}, u32[]{:S(2)}, u32[]{:S(2)}) collective-permute-start(f32[2,4,128,128]{3,2,1,0:T(8,128)S(1)} %get-tuple-element.15), channel_id=1, source_target_pairs={{0,127},{1,64},{2,65},{3,66},{4,67},{5,68},{6,69},{7,70},{8,71},{9... | collective-permute-start | bytes 1572872 | tf_op jit(solution)/shard_map/ppermute | solution.py:277
  72.3 1.3 %collective-permute-start.14 = (f32[2,4,128,128]{3,2,1,0:T(8,128)S(1)}, f32[2,4,128,128]{3,2,1,0:T(8,128)S(1)}, u32[]{:S(2)}, u32[]{:S(2)}) collective-permute-start(f32[2,4,128,128]{3,2,1,0:T(8,128)S(1)} %get-tuple-element.15), channel_id=1, source_target_pairs={{0,64},{1,65},{2,66},{3,67},{4,68},{5,69},{6,70},{7,71},{8,72},{9,... | collective-permute-start | bytes 1572872 | tf_op jit(solution)/shard_map/ppermute | solution.py:277
  73.6 1.3 %collective-permute-start.13 = (f32[2,4,128,128]{3,2,1,0:T(8,128)S(1)}, f32[2,4,128,128]{3,2,1,0:T(8,128)S(1)}, u32[]{:S(2)}, u32[]{:S(2)}) collective-permute-start(f32[2,4,128,128]{3,2,1,0:T(8,128)S(1)} %get-tuple-element.15), channel_id=1, source_target_pairs={{0,65},{1,66},{2,67},{3,68},{4,69},{5,70},{6,71},{7,72},{8,73},{9,... | collective-permute-start | bytes 1572872 | tf_op jit(solution)/shard_map/ppermute | solution.py:277
  74.9 9.4 %collective-permute-done.15.refs_3_ = f32[2,4,128,128]{3,2,1,0:T(8,128)S(1)} collective-permute-done((f32[2,4,128,128]{3,2,1,0:T(8,128)S(1)}, f32[2,4,128,128]{3,2,1,0:T(8,128)S(1)}, u32[]{:S(2)}, u32[]{:S(2)}) %collective-permute-start.15) | collective-permute-done | bytes 524320 | tf_op jit(solution)/shard_map/ppermute | solution.py:277
  84.3 0.0 collective-permute-done.14.refs_2_
  84.3 8.9 %collective-permute-done.13.refs_1_ = f32[2,4,128,128]{3,2,1,0:T(8,128)S(1)} collective-permute-done((f32[2,4,128,128]{3,2,1,0:T(8,128)S(1)}, f32[2,4,128,128]{3,2,1,0:T(8,128)S(1)}, u32[]{:S(2)}, u32[]{:S(2)}) %collective-permute-start.13) | collective-permute-done | bytes 524320 | tf_op jit(solution)/shard_map/ppermute | solution.py:277
  93.2 2.6 %shard_map.48 = f32[2,4,128,128]{3,2,1,0:T(8,128)S(1)} custom-call(s32[1]{0:T(128)} %bitcast.refs_0_, f32[2,4,128,128]{3,2,1,0:T(8,128)S(1)} %collective-permute-done.13.refs_1_, f32[2,4,128,128]{3,2,1,0:T(8,128)S(1)} %collective-permute-done.14.refs_2_, f32[2,4,128,128]{3,2,1,0:T(8,128)S(1)} %collective-permute-done.15.refs_3_, ...), custom_call_target="tpu_custom_call" | custom-call | flops 10000000000 | bytes 1048576 | tf_op jit(solution)/shard_map/pallas_call | solution.py:244
  95.8 1.3 %collective-permute-start.16 = (f32[2,4,128,128]{3,2,1,0:T(8,128)S(1)}, f32[2,4,128,128]{3,2,1,0:T(8,128)S(1)}, u32[]{:S(2)}, u32[]{:S(2)}) collective-permute-start(f32[2,4,128,128]{3,2,1,0:T(8,128)S(1)} %shard_map.48), channel_id=1, source_target_pairs={{0,128},{1,129},{2,130},{3,131},{4,132},{5,133},{6,134},{7,135},{8... | collective-permute-start | bytes 1572872 | tf_op jit(solution)/shard_map/ppermute | solution.py:277
  97.1 6.1 %collective-permute-done.16.refs_3_ = f32[2,4,128,128]{3,2,1,0:T(8,128)S(1)} collective-permute-done((f32[2,4,128,128]{3,2,1,0:T(8,128)S(1)}, f32[2,4,128,128]{3,2,1,0:T(8,128)S(1)}, u32[]{:S(2)}, u32[]{:S(2)}) %collective-permute-start.16) | collective-permute-done | bytes 524320 | tf_op jit(solution)/shard_map/ppermute | solution.py:277
  103.2 0.8 shard_map.49
  (8 shorter events, 0.3 us)
Async XLA Ops:
  0.0 0.9 copy-start
  1.0 0.9 copy-start.2
  1.9 11.6 %copy-start.4 = (f32[1,2,4,128,128]{4,3,2,1,0:T(8,128)S(1)}, f32[1,2,4,128,128]{4,3,2,1,0:T(8,128)}, u32[]{:S(2)}) copy-start(f32[1,2,4,128,128]{4,3,2,1,0:T(8,128)} %param.3) | copy-start | bytes 1572868
  1.9 21.2 %collective-permute-start.2 = (f32[2,4,128,128]{3,2,1,0:T(8,128)S(1)}, f32[2,4,128,128]{3,2,1,0:T(8,128)S(1)}, u32[]{:S(2)}, u32[]{:S(2)}) collective-permute-start(f32[2,4,128,128]{3,2,1,0:T(8,128)S(1)} %shard_map.37), channel_id=1, source_target_pairs={{0,1},{1,2},{2,3},{3,4},{4,5},{5,6},{6,7},{7,8},{8,9},{9,10},{10,1... | collective-permute-start | bytes 1572872 | tf_op jit(solution)/shard_map/ppermute | solution.py:277
  13.5 17.4 %collective-permute-start.1 = (f32[2,4,128,128]{3,2,1,0:T(8,128)S(1)}, f32[2,4,128,128]{3,2,1,0:T(8,128)S(1)}, u32[]{:S(2)}, u32[]{:S(2)}) collective-permute-start(f32[2,4,128,128]{3,2,1,0:T(8,128)S(1)} %bitcast.8), channel_id=1, source_target_pairs={{0,63},{1,0},{2,1},{3,2},{4,3},{5,4},{6,5},{7,6},{8,7},{9,8},{10,9... | collective-permute-start | bytes 1572872 | tf_op jit(solution)/shard_map/ppermute | solution.py:277
  14.4 18.8 %collective-permute-start = (f32[2,4,128,128]{3,2,1,0:T(8,128)S(1)}, f32[2,4,128,128]{3,2,1,0:T(8,128)S(1)}, u32[]{:S(2)}, u32[]{:S(2)}) collective-permute-start(f32[2,4,128,128]{3,2,1,0:T(8,128)S(1)} %bitcast.9), channel_id=1, source_target_pairs={{0,1},{1,2},{2,3},{3,4},{4,5},{5,6},{6,7},{7,8},{8,9},{9,10},{10,1... | collective-permute-start | bytes 1572872 | tf_op jit(solution)/shard_map/ppermute | solution.py:277
  23.1 11.6 %collective-permute-start.3 = (f32[2,4,128,128]{3,2,1,0:T(8,128)S(1)}, f32[2,4,128,128]{3,2,1,0:T(8,128)S(1)}, u32[]{:S(2)}, u32[]{:S(2)}) collective-permute-start(f32[2,4,128,128]{3,2,1,0:T(8,128)S(1)} %collective-permute-done.2.refs_2_), channel_id=1, source_target_pairs={{128,132},{132,136},{136,140},{140,144},{144,148},{148,152},{152,1... | collective-permute-start | bytes 1572872 | tf_op jit(solution)/shard_map/ppermute | solution.py:277
  34.1 2.7 %collective-permute-start.8 = (f32[2,4,128,128]{3,2,1,0:T(8,128)}, f32[2,4,128,128]{3,2,1,0:T(8,128)S(1)}, u32[]{:S(2)}, u32[]{:S(2)}) collective-permute-start(f32[2,4,128,128]{3,2,1,0:T(8,128)} %shard_map.40), channel_id=1, source_target_pairs={{128,132},{131,191},{132,136},{135,131},{136,140},{139,135},{140,1... | collective-permute-start | bytes 1572872 | tf_op jit(solution)/shard_map/ppermute | solution.py:277
  34.8 3.5 %collective-permute-start.4 = (f32[2,4,128,128]{3,2,1,0:T(8,128)S(1)}, f32[2,4,128,128]{3,2,1,0:T(8,128)S(1)}, u32[]{:S(2)}, u32[]{:S(2)}) collective-permute-start(f32[2,4,128,128]{3,2,1,0:T(8,128)S(1)} %shard_map.38.refs_4_.refs_1_.refs_2_), channel_id=1, source_target_pairs={{0,64},{1,65},{2,66},{3,67},{4,68},{5,69},{6,70},{7,71},{8,72},{9,... | collective-permute-start | bytes 1572872 | tf_op jit(solution)/shard_map/ppermute | solution.py:277
  36.8 1.5 %copy-start.1 = (f32[4,128,128]{2,1,0:T(8,128)S(1)}, f32[4,128,128]{2,1,0:T(8,128)}, u32[]{:S(2)}) copy-start(f32[4,128,128]{2,1,0:T(8,128)} %refs_5_.7) | copy-start | bytes 786436
  36.8 1.5 %copy-start.3 = (f32[4,128,128]{2,1,0:T(8,128)S(1)}, f32[4,128,128]{2,1,0:T(8,128)}, u32[]{:S(2)}) copy-start(f32[4,128,128]{2,1,0:T(8,128)} %refs_6_.7) | copy-start | bytes 786436
  36.9 1.5 %copy-start.5 = (f32[1,2,4,128,128]{4,3,2,1,0:T(8,128)S(1)}, f32[1,2,4,128,128]{4,3,2,1,0:T(8,128)}, u32[]{:S(2)}) copy-start(f32[1,2,4,128,128]{4,3,2,1,0:T(8,128)} %param.3) | copy-start | bytes 1572868
  38.3 12.8 %collective-permute-start.7 = (f32[2,4,128,128]{3,2,1,0:T(8,128)S(1)}, f32[2,4,128,128]{3,2,1,0:T(8,128)S(1)}, u32[]{:S(2)}, u32[]{:S(2)}) collective-permute-start(f32[2,4,128,128]{3,2,1,0:T(8,128)S(1)} %get-tuple-element.12), channel_id=1, source_target_pairs={{0,127},{1,64},{2,65},{3,66},{4,67},{5,68},{6,69},{7,70},{8,71},{9... | collective-permute-start | bytes 1572872 | tf_op jit(solution)/shard_map/ppermute | solution.py:277
  39.6 11.5 %collective-permute-start.6 = (f32[2,4,128,128]{3,2,1,0:T(8,128)S(1)}, f32[2,4,128,128]{3,2,1,0:T(8,128)S(1)}, u32[]{:S(2)}, u32[]{:S(2)}) collective-permute-start(f32[2,4,128,128]{3,2,1,0:T(8,128)S(1)} %get-tuple-element.12), channel_id=1, source_target_pairs={{0,64},{1,65},{2,66},{3,67},{4,68},{5,69},{6,70},{7,71},{8,72},{9,... | collective-permute-start | bytes 1572872 | tf_op jit(solution)/shard_map/ppermute | solution.py:277
  40.9 17.5 %collective-permute-start.5 = (f32[2,4,128,128]{3,2,1,0:T(8,128)S(1)}, f32[2,4,128,128]{3,2,1,0:T(8,128)S(1)}, u32[]{:S(2)}, u32[]{:S(2)}) collective-permute-start(f32[2,4,128,128]{3,2,1,0:T(8,128)S(1)} %get-tuple-element.12), channel_id=1, source_target_pairs={{0,65},{1,66},{2,67},{3,68},{4,69},{5,70},{6,71},{7,72},{8,73},{9,... | collective-permute-start | bytes 1572872 | tf_op jit(solution)/shard_map/ppermute | solution.py:277
  49.8 19.9 %collective-permute-start.12 = (f32[2,4,128,128]{3,2,1,0:T(8,128)S(1)}, f32[2,4,128,128]{3,2,1,0:T(8,128)S(1)}, u32[]{:S(2)}, u32[]{:S(2)}) collective-permute-start(f32[2,4,128,128]{3,2,1,0:T(8,128)S(1)} %shard_map.45.refs_4_), channel_id=1, source_target_pairs={{128,0},{129,1},{130,2},{131,3},{132,4},{133,5},{134,6},{135,7},{1... | collective-permute-start | bytes 1572872 | tf_op jit(solution)/shard_map/ppermute | solution.py:277
  60.9 8.7 %collective-permute-start.11 = (f32[2,4,128,128]{3,2,1,0:T(8,128)S(1)}, f32[2,4,128,128]{3,2,1,0:T(8,128)S(1)}, u32[]{:S(2)}, u32[]{:S(2)}) collective-permute-start(f32[2,4,128,128]{3,2,1,0:T(8,128)S(1)} %get-tuple-element.14), channel_id=1, source_target_pairs={{64,63},{65,0},{66,1},{67,2},{68,3},{69,4},{70,5},{71,6},{72,7},{7... | collective-permute-start | bytes 1572872 | tf_op jit(solution)/shard_map/ppermute | solution.py:277
  62.3 7.4 %collective-permute-start.10 = (f32[2,4,128,128]{3,2,1,0:T(8,128)S(1)}, f32[2,4,128,128]{3,2,1,0:T(8,128)S(1)}, u32[]{:S(2)}, u32[]{:S(2)}) collective-permute-start(f32[2,4,128,128]{3,2,1,0:T(8,128)S(1)} %get-tuple-element.14), channel_id=1, source_target_pairs={{64,0},{65,1},{66,2},{67,3},{68,4},{69,5},{70,6},{71,7},{72,8},{73... | collective-permute-start | bytes 1572872 | tf_op jit(solution)/shard_map/ppermute | solution.py:277
  63.6 7.4 %collective-permute-start.9 = (f32[2,4,128,128]{3,2,1,0:T(8,128)S(1)}, f32[2,4,128,128]{3,2,1,0:T(8,128)S(1)}, u32[]{:S(2)}, u32[]{:S(2)}) collective-permute-start(f32[2,4,128,128]{3,2,1,0:T(8,128)S(1)} %get-tuple-element.14), channel_id=1, source_target_pairs={{64,1},{65,2},{66,3},{67,4},{68,5},{69,6},{70,7},{71,8},{72,9},{73... | collective-permute-start | bytes 1572872 | tf_op jit(solution)/shard_map/ppermute | solution.py:277
  71.0 13.3 %collective-permute-start.15 = (f32[2,4,128,128]{3,2,1,0:T(8,128)S(1)}, f32[2,4,128,128]{3,2,1,0:T(8,128)S(1)}, u32[]{:S(2)}, u32[]{:S(2)}) collective-permute-start(f32[2,4,128,128]{3,2,1,0:T(8,128)S(1)} %get-tuple-element.15), channel_id=1, source_target_pairs={{0,127},{1,64},{2,65},{3,66},{4,67},{5,68},{6,69},{7,70},{8,71},{9... | collective-permute-start | bytes 1572872 | tf_op jit(solution)/shard_map/ppermute | solution.py:277
  72.3 12.0 %collective-permute-start.14 = (f32[2,4,128,128]{3,2,1,0:T(8,128)S(1)}, f32[2,4,128,128]{3,2,1,0:T(8,128)S(1)}, u32[]{:S(2)}, u32[]{:S(2)}) collective-permute-start(f32[2,4,128,128]{3,2,1,0:T(8,128)S(1)} %get-tuple-element.15), channel_id=1, source_target_pairs={{0,64},{1,65},{2,66},{3,67},{4,68},{5,69},{6,70},{7,71},{8,72},{9,... | collective-permute-start | bytes 1572872 | tf_op jit(solution)/shard_map/ppermute | solution.py:277
  73.6 19.6 %collective-permute-start.13 = (f32[2,4,128,128]{3,2,1,0:T(8,128)S(1)}, f32[2,4,128,128]{3,2,1,0:T(8,128)S(1)}, u32[]{:S(2)}, u32[]{:S(2)}) collective-permute-start(f32[2,4,128,128]{3,2,1,0:T(8,128)S(1)} %get-tuple-element.15), channel_id=1, source_target_pairs={{0,65},{1,66},{2,67},{3,68},{4,69},{5,70},{6,71},{7,72},{8,73},{9,... | collective-permute-start | bytes 1572872 | tf_op jit(solution)/shard_map/ppermute | solution.py:277
  95.8 7.4 %collective-permute-start.16 = (f32[2,4,128,128]{3,2,1,0:T(8,128)S(1)}, f32[2,4,128,128]{3,2,1,0:T(8,128)S(1)}, u32[]{:S(2)}, u32[]{:S(2)}) collective-permute-start(f32[2,4,128,128]{3,2,1,0:T(8,128)S(1)} %shard_map.48), channel_id=1, source_target_pairs={{0,128},{1,129},{2,130},{3,131},{4,132},{5,133},{6,134},{7,135},{8... | collective-permute-start | bytes 1572872 | tf_op jit(solution)/shard_map/ppermute | solution.py:277

commit v3 on v2

--- a/solution.py
+++ b/solution.py
@@ -14,6 +14,7 @@
 SMEM = pl.BlockSpec(memory_space=pltpu.SMEM)
 ANY = pl.BlockSpec(memory_space=pl.ANY)
 AXES = ("tm", "space")
+SETTLE = 3 * 10**10
 
 
 def triple(values, axis):
@@ -115,38 +116,27 @@
                 target[1, layer] = new[1]
 
 
-def coefficients_of(low, feed, kill, high, depth):
-    def coefficient(which, layer):
-        if layer < depth:
-            return low[which, layer]
-        if layer >= 2 * depth:
-            return high[which, layer - 2 * depth]
-        return (feed, kill)[which][layer - depth]
-
-    return coefficient
-
-
-def fine_kernel(worker, position, low, own, high, low_c, feed, kill, high_c, explicit, state, *levels):
+def fine_kernel(worker, position, low, own, high, low_c, own_c, high_c, explicit, state, *levels):
     depth = own.shape[1]
 
     @pl.when((position[0] >= worker[0]) & (position[0] <= worker[-1]))
     def _():
-        coefficient = coefficients_of(low_c, feed, kill, high_c, depth)
+        coefficient = joined(low_c, own_c, high_c, depth)
         fine_levels(joined(low, own, high, depth), coefficient, levels, state, depth)
         for layer in range(depth):
-            new = explicit_layer(state[0, layer], state[1, layer], feed[layer], kill[layer])
+            new = explicit_layer(state[0, layer], state[1, layer], own_c[0, layer], own_c[1, layer])
             explicit[0, layer] = new[0]
             explicit[1, layer] = new[1]
 
 
 def correction_kernel(
-    worker, position, low, own, high, low_c, feed, kill, high_c, correction, level_a, level_b, wide
+    worker, position, low, own, high, low_c, own_c, high_c, correction, level_a, level_b, wide
 ):
     depth = own.shape[1]
 
     @pl.when((position[0] >= worker[0]) & (position[0] <= worker[-1]))
     def _():
-        coefficient = coefficients_of(low_c, feed, kill, high_c, depth)
+        coefficient = joined(low_c, own_c, high_c, depth)
         read = joined(low, own, high, depth)
         fine_levels(read, coefficient, (level_a, level_b), correction, depth)
         for layer in range(3 * depth):
@@ -163,7 +153,7 @@
         coarse_levels(lambda species, layer: wide[species, layer], (level_a, level_b), finish, depth)
 
 
-def coarse_kernel(worker, position, low, own, high, correction, feed, kill, explicit, state, *levels):
+def coarse_kernel(worker, position, low, high, own, correction, own_c, explicit, state, *levels):
     depth = own.shape[1]
 
     @pl.when((position[0] >= worker[0]) & (position[0] <= worker[-1]))
@@ -174,29 +164,40 @@
             state[0, layer] = first
             state[1, layer] = second
             explicit[0, layer], explicit[1, layer] = explicit_layer(
-                first, second, feed[layer], kill[layer]
+                first, second, own_c[0, layer], own_c[1, layer]
             )
 
         coarse_levels(joined(low, own, high, depth), levels, finish, depth)
 
 
-def last_kernel(worker, position, low, own, high, correction, third, state, *levels):
+def last_kernel(chosen, position, low, high, own, correction, third, state, level_a, level_b):
     depth = own.shape[1]
 
-    @pl.when(position[0] != worker[0])
-    def _():
-        state[...] = third[...]
-
-    @pl.when(position[0] == worker[0])
-    def _():
-        def finish(layer, new):
-            for species in (0, 1):
-                state[species, layer] = new[species] + correction[species, layer]
-
-        coarse_levels(joined(low, own, high, depth), levels, finish, depth)
-
-
-def result_kernel(position, first, second, received, result):
+    @pl.when(position[0] != 1)
+    def _():
+        state[0] = third[chosen]
+
+    @pl.when(position[0] == 1)
+    def _():
+        read = joined(low, own, high, depth)
+        levels = (level_a, level_b)
+        count = 3 * depth - 2
+        for sweep in range(SWEEPS):
+            for layer in range(count):
+                if sweep == 0:
+                    parts = [read(chosen, layer + shift) for shift in (0, 1, 2)]
+                else:
+                    source = levels[(sweep - 1) % 2]
+                    parts = [source[chosen, layer + shift] for shift in (0, 1, 2)]
+                new = sweep_layer(chosen, *parts, read(chosen, layer + sweep + 1))
+                if sweep == SWEEPS - 1:
+                    state[0, layer] = new + correction[chosen, layer]
+                else:
+                    levels[sweep % 2][chosen, layer] = new
+            count -= 2
+
+
+def result_kernel(position, first, second, received_a, received_b, result):
     @pl.when(position[0] == 0)
     def _():
         result[...] = first[...]
@@ -207,12 +208,31 @@
 
     @pl.when(position[0] > 1)
     def _():
-        result[...] = received[...]
-
-
-def stack_kernel(position, feed, kill, both):
-    both[0] = feed[...]
-    both[1] = kill[...]
+        result[0] = received_a[0]
+        result[1] = received_b[0]
+
+
+def stack_kernel(feed, kill, both, arrived):
+    copies = [
+        pltpu.make_async_copy(source, both.at[which], arrived.at[which])
+        for which, source in enumerate((feed, kill))
+    ]
+    for copy in copies:
+        copy.start()
+    for copy in copies:
+        copy.wait()
+
+
+def stacked(feed, kill):
+    return pl.pallas_call(
+        stack_kernel,
+        out_shape=pltpu.VMEM((2, *feed.shape), feed.dtype),
+        in_specs=[ANY, ANY],
+        out_specs=VMEM,
+        scratch_shapes=[pltpu.SemaphoreType.DMA((2,))],
+        compiler_params=pltpu.CompilerParams(vmem_limit_bytes=4 * 2**20),
+        cost_estimate=pl.CostEstimate(flops=10**5, bytes_accessed=2**20, transcendentals=0),
+    )(feed, kill)
 
 
 def pick_kernel(flag, array, other, picked):
@@ -225,9 +245,9 @@
         picked[...] = other[...]
 
 
-def run(body, position, operands, outputs, scratch=2, pinned=True, worker=None, tokens=()):
+def run(body, position, operands, outputs, scratch=2, pinned=True, worker=None, tokens=(), species=2):
     depth, plane = operands[0].shape[-3], operands[0].shape[-2:]
-    shape = (2, depth, *plane)
+    shape = (species, depth, *plane)
     if pinned:
         out_shape = [pltpu.VMEM(shape, jnp.float32)] * outputs
     else:
@@ -254,6 +274,39 @@
     )(position, *operands, *tokens)
 
 
+def copy_kernel(array, token, copied):
+    copied[...] = array[...]
+
+
+def after(array, token):
+    return pl.pallas_call(
+        copy_kernel,
+        out_shape=pltpu.VMEM(array.shape, array.dtype),
+        in_specs=[VMEM, ANY],
+        out_specs=VMEM,
+        compiler_params=pltpu.CompilerParams(vmem_limit_bytes=4 * 2**20),
+        cost_estimate=pl.CostEstimate(flops=10**5, bytes_accessed=2**20, transcendentals=0),
+    )(pltpu.with_memory_space_constraint(array, pltpu.VMEM), token)
+
+
+def settle_kernel(low, high, low_out, high_out):
+    pass
+
+
+def settled(low, high):
+    return pl.pallas_call(
+        settle_kernel,
+        out_shape=[jax.ShapeDtypeStruct(low.shape, low.dtype)] * 2,
+        in_specs=[ANY, ANY],
+        out_specs=[ANY, ANY],
+        input_output_aliases={0: 0, 1: 1},
+        cost_estimate=pl.CostEstimate(flops=SETTLE, bytes_accessed=2**20, transcendentals=0),
+    )(
+        pltpu.with_memory_space_constraint(low, pltpu.VMEM),
+        pltpu.with_memory_space_constraint(high, pltpu.VMEM),
+    )
+
+
 def pick(flag, array, other, tokens=()):
     flag = flag.astype(jnp.int32).reshape(1)
     return run(pick_kernel, flag, (array, other), 1, 0, tokens=tokens)[0]
@@ -279,11 +332,12 @@
     def beside(slab, step):
         return slab // ring * ring + (slab + step) % ring
 
-    def onward(step):
-        return lambda source, slab: (source, slab + step if source < 2 else beside(slab, step))
-
     def halves(source, slab):
-        return onward(1 if source % 2 == 0 else -1)(source, slab)
+        step = 1 if source % 2 == 0 else -1
+        return source, slab + step if source < 2 else beside(slab, step)
+
+    def around_x(step):
+        return lambda source, slab: (source, beside(slab, step)) if source >= 2 else None
 
     def far_half(source, slab):
         if source == 2 and slab % ring == 0:
@@ -299,54 +353,72 @@
             return source, slab - ring
         return None
 
+    def swapped(source, slab):
+        return source ^ 1, slab
+
     def route(source, target, shift=0):
         return lambda origin, slab: (target, slab + shift) if origin == source else None
 
     def spread(array, source, target):
         low = moved(array, route(source, target, 1))
         high = moved(array, route(source, target, -1))
-        return low, moved(array, route(source, target)), high
-
-    (both,) = run(stack_kernel, position, (feed, kill), 1, 0)
+        return low, high, moved(array, route(source, target))
+
+    both = stacked(feed, kill)
     half = moved(both, halves)
-    low = moved(own, onward(1))
-    high = moved(own, onward(-1))
+    low_0 = moved(own, route(0, 0, 1))
+    high_0 = moved(own, route(0, 0, -1))
+    low_x = moved(own, around_x(1))
+    high_x = moved(own, around_x(-1))
+    other = moved(half, swapped)
     half_far = moved(half, far_half)
-    lowest = (index >= 2) & (place == 0)
-    highest = (index >= 2) & (place == ring - 1)
-    half = pick((lowest & (index == 2)) | (highest & (index == 3)), half_far, half)
-    other = moved(half, lambda source, slab: (source ^ 1, slab))
+    lowest, highest = place == 0, place == ring - 1
+    mended = pick((lowest & (index == 2)) | (highest & (index == 3)), half_far, half)
+    other_x = moved(mended, lambda source, slab: swapped(source, slab) if source >= 2 else None)
+    own_1 = after(own, half)
+    low_1 = moved(own_1, route(1, 1, 1))
+    high_1 = moved(own_1, route(1, 1, -1))
+    outer = pick(lowest, low_x, high_x)
+    outer_far = moved(outer, far)
+    low_0, high_0 = settled(low_0, high_0)
     explicit, first_end = run(
-        fine_kernel, position, (low, own, high, half, feed, kill, other), 2, worker=(0,)
+        fine_kernel,
+        position,
+        (low_0, own, high_0, half, both, other),
+        2,
+        worker=(0,),
+        tokens=(outer, own_1),
     )
     second = spread(explicit, 0, 1)
-    sides_far = moved(pick(place == 0, low, high), far)
-    low = pick(lowest, sides_far, low)
-    high = pick(highest, sides_far, high)
     even = index % 2 == 0
-    low_c = pick(even, half, other)
-    high_c = pick(even, other, half)
+    other = pick(index == 1, other, other_x)
+    low_c = pick(even, mended, other)
+    high_c = pick(even, other, mended)
+    low = pick(index == 1, low_1, pick(lowest, outer_far, low_x))
+    high = pick(index == 1, high_1, pick(highest, outer_far, high_x))
     (correction,) = run(
-        correction_kernel,
-        position,
-        (low, own, high, low_c, feed, kill, high_c),
-        1,
-        3,
-        worker=(1, 3),
-    )
-    crossed = moved(correction, lambda source, slab: (source - 2, slab) if source >= 2 else None)
+        correction_kernel, position, (low, own, high, low_c, both, high_c), 1, 3, worker=(1, 3)
+    )
+    crossed_2 = moved(correction, route(2, 0))
     explicit, second_end = run(
-        coarse_kernel, position, (*second, correction, feed, kill), 2, worker=(1,)
+        coarse_kernel, position, (*second, correction, both), 2, worker=(1,)
     )
     third = spread(explicit, 1, 0)
+    crossed_3 = moved(after(correction, third[0]), route(3, 1))
     explicit, third_end = run(
-        coarse_kernel, position, (*third, crossed, feed, kill), 2, worker=(0,)
+        coarse_kernel, position, (*third, crossed_2, both), 2, worker=(0,)
     )
     fourth = spread(explicit, 0, 1)
-    (last_end,) = run(last_kernel, position, (*fourth, crossed, third_end), 1, worker=(1,))
-    received = moved(last_end, lambda source, slab: (source + 2, slab) if source < 2 else None)
+    received = []
+    for chosen in (0, 1):
+        (last_end,) = run(
+            last_kernel, position, (*fourth, crossed_3, third_end), 1, worker=chosen, species=1
+        )
+        received.append(
+            moved(last_end, lambda source, slab: (source + 2, slab) if source < 2 else None)
+        )
     (result,) = run(
-        result_kernel, position, (first_end, second_end, received), 1, 0, pinned=False
+        result_kernel, position, (first_end, second_end, *received), 1, 0, pinned=False
     )
     return result[None]
 

time: 104 us -> 117 us (1.12)
  starting transfers between devices: 30.7 us -> 47.1 us
  waiting for transfers between devices: 56.7 us -> 46.2 us
  Pallas kernels: 14.5 us -> 21.1 us
    ppermute x17 -> x24, starting transfers between devices: 30.7 us -> 47.1 us  [moved(): return lax.ppermute(array, AXES, pairs)]
    ppermute x17 -> x24, waiting for transfers between devices: 56.7 us -> 46.2 us  [moved(): return lax.ppermute(array, AXES, pairs)]
    pallas_call x13 -> x16, Pallas kernels: 14.5 us -> 20.2 us  [run(): pl.pallas_call(kernel, out_shape=out_shape, in_specs=[SMEM] + [VMEM] * le...]
  transfers between devices with their start and end apart: 17 -> 24, of which waited for: 10 -> 8; matrix products, arithmetic and copies ran while one was open for 0% -> 0% of each run, Pallas kernels for 11% -> 14%
where the time goes in v3:
time: 117 us
  starting transfers between devices  47.1 us (40%)
  waiting for transfers between devices  46.2 us (39%)
  Pallas kernels  21.1 us (18%)
  local copies, waits for them, and re-layouts  1.92 us (2%)
    ppermute x24, starting transfers between devices, moved(): return lax.ppermute(array, AXES, pairs)  47.1 us
    ppermute x24, waiting for transfers between devices, moved(): return lax.ppermute(array, AXES, pairs)  46.2 us
    pallas_call x16, Pallas kernels, run(): pl.pallas_call(kernel, out_shape=out_shape, in_specs=[SMEM] + [VMEM] * le...  20.2 us
  transfers between devices with their start and end apart: 24, of which 8 were waited for; matrix products, arithmetic and copies ran while one was open for 0% of the time, Pallas kernels for 14%

profile of v3, /device:TPU:1, one launch (start us, length us, event | category | flops | bytes accessed | tf_op | source)
XLA Modules:
  0.0 116.7 jit_solution(10872519971096025763)
XLA Ops:
  0.0 0.9 copy-done.4
  1.0 0.9 copy-done.5
  1.9 0.1 shard_map.38.refs_5_
  2.0 0.0 copy-start.2
  2.0 11.6 %collective-permute-start.2 = (f32[2,4,128,128]{3,2,1,0:T(8,128)S(1)}, f32[2,4,128,128]{3,2,1,0:T(8,128)S(1)}, u32[]{:S(2)}, u32[]{:S(2)}) collective-permute-start(f32[2,4,128,128]{3,2,1,0:T(8,128)S(1)} %shard_map.38.refs_5_), channel_id=1, source_target_pairs={{0,1},{1,2},{2,3},{3,4},{4,5},{5,6},{6,7},{7,8},{8,9},{9,10},{10,1... | collective-permute-start | bytes 1572872 | tf_op jit(solution)/shard_map/ppermute | solution.py:330
  13.6 0.7 collective-permute-start.4
  14.2 0.7 collective-permute-start.5
  14.9 1.5 %collective-permute-start = (f32[2,4,128,128]{3,2,1,0:T(8,128)S(1)}, f32[2,4,128,128]{3,2,1,0:T(8,128)}, u32[]{:S(2)}, u32[]{:S(2)}) collective-permute-start(f32[2,4,128,128]{3,2,1,0:T(8,128)S(1)} %bitcast.10), channel_id=1, source_target_pairs={{0,1},{1,2},{2,3},{3,4},{4,5},{5,6},{6,7},{7,8},{8,9},{9,10},{10,1... | collective-permute-start | bytes 1572872 | tf_op jit(solution)/shard_map/ppermute | solution.py:330
  16.4 1.4 %collective-permute-start.1 = (f32[2,4,128,128]{3,2,1,0:T(8,128)S(1)}, f32[2,4,128,128]{3,2,1,0:T(8,128)}, u32[]{:S(2)}, u32[]{:S(2)}) collective-permute-start(f32[2,4,128,128]{3,2,1,0:T(8,128)S(1)} %bitcast.11), channel_id=1, source_target_pairs={{0,63},{1,0},{2,1},{3,2},{4,3},{5,4},{6,5},{7,6},{8,7},{9,8},{10,9... | collective-permute-start | bytes 1572872 | tf_op jit(solution)/shard_map/ppermute | solution.py:330
  17.9 1.8 %collective-permute-done.2.token.refs_4_.refs_2_ = f32[2,4,128,128]{3,2,1,0:T(8,128)S(1)} collective-permute-done((f32[2,4,128,128]{3,2,1,0:T(8,128)S(1)}, f32[2,4,128,128]{3,2,1,0:T(8,128)S(1)}, u32[]{:S(2)}, u32[]{:S(2)}) %collective-permute-start.2) | collective-permute-done | bytes 524320 | tf_op jit(solution)/shard_map/ppermute | solution.py:330
  19.7 0.8 shard_map.40.refs_8_
  20.5 1.9 %collective-permute-start.9 = (f32[2,4,128,128]{3,2,1,0:T(8,128)}, f32[2,4,128,128]{3,2,1,0:T(8,128)}, u32[]{:S(2)}, u32[]{:S(2)}) collective-permute-start(f32[2,4,128,128]{3,2,1,0:T(8,128)} %shard_map.40.refs_8_), channel_id=1, source_target_pairs={{64,65},{65,66},{66,67},{67,68},{68,69},{69,70},{70,71},{71,72},{7... | collective-permute-start | bytes 1572872 | tf_op jit(solution)/shard_map/ppermute | solution.py:330
  22.4 0.0 collective-permute-done.4.refs_1_.refs_2_
  22.4 10.1 %collective-permute-start.11 = (f32[2,4,128,128]{3,2,1,0:T(8,128)}, f32[2,4,128,128]{3,2,1,0:T(8,128)}, u32[]{:S(2)}, u32[]{:S(2)}) collective-permute-start(f32[2,4,128,128]{3,2,1,0:T(8,128)} %shard_map.40.refs_8_), channel_id=1, source_target_pairs={{64,127},{65,64},{66,65},{67,66},{68,67},{69,68},{70,69},{71,70},{... | collective-permute-start | bytes 1572872 | tf_op jit(solution)/shard_map/ppermute | solution.py:330
  32.6 0.0 collective-permute-done.5.refs_2_
  32.6 0.9 shard_map.39.refs_7_
  33.4 0.7 collective-permute-start.10
  34.1 0.0 collective-permute-done.low
  34.1 1.5 %collective-permute-start.12 = (f32[2,4,128,128]{3,2,1,0:T(8,128)S(1)}, f32[2,4,128,128]{3,2,1,0:T(8,128)}, u32[]{:S(2)}, u32[]{:S(2)}) collective-permute-start(f32[2,4,128,128]{3,2,1,0:T(8,128)S(1)} %collective-permute-done.2.token.refs_4_.refs_2_), channel_id=1, source_target_pairs={{128,132},{132,136},{136,140},{140,144},{144,148},{148,152},{152,1... | collective-permute-start | bytes 1572872 | tf_op jit(solution)/shard_map/ppermute | solution.py:330
  35.6 0.0 collective-permute-done.1.high
  35.6 0.0 collective-permute-start.3
  35.6 0.0 collective-permute-done.12.refs_1_
  35.6 0.0 copy-start.1
  35.6 0.0 copy-start.3
  35.7 1.2 shard_map.46.refs_1_.refs_2_
  36.8 0.7 collective-permute-start.13
  37.5 0.1 collective-permute-done.3.refs_6_.refs_1_
  37.7 1.4 %shard_map.41 = (f32[2,4,128,128]{3,2,1,0:T(8,128)S(1)}, f32[2,4,128,128]{3,2,1,0:T(8,128)S(1)}) custom-call(s32[1]{0:T(128)} %bitcast.refs_0_, f32[2,4,128,128]{3,2,1,0:T(8,128)} %get-tuple-element.13.refs_1_, f32[2,4,128,128]{3,2,1,0:T(8,128)S(1)} %bitcast.13, f32[2,4,128,128]{3,2,1,0:T(8,128)} %get-tuple-element.14.refs_3_, ...), custom_call_target="tpu_custom_call" | custom-call | flops 10000000000 | bytes 1048576 | tf_op jit(solution)/shard_map/pallas_call | solution.py:264
  39.0 1.3 %collective-permute-start.6 = (f32[2,4,128,128]{3,2,1,0:T(8,128)S(1)}, f32[2,4,128,128]{3,2,1,0:T(8,128)S(1)}, u32[]{:S(2)}, u32[]{:S(2)}) collective-permute-start(f32[2,4,128,128]{3,2,1,0:T(8,128)S(1)} %get-tuple-element.16), channel_id=1, source_target_pairs={{0,65},{1,66},{2,67},{3,68},{4,69},{5,70},{6,71},{7,72},{8,73},{9,... | collective-permute-start | bytes 1572872 | tf_op jit(solution)/shard_map/ppermute | solution.py:330
  40.3 0.0 collective-permute-done.10.refs_1_
  40.3 1.3 %collective-permute-start.7 = (f32[2,4,128,128]{3,2,1,0:T(8,128)S(1)}, f32[2,4,128,128]{3,2,1,0:T(8,128)S(1)}, u32[]{:S(2)}, u32[]{:S(2)}) collective-permute-start(f32[2,4,128,128]{3,2,1,0:T(8,128)S(1)} %get-tuple-element.16), channel_id=1, source_target_pairs={{0,127},{1,64},{2,65},{3,66},{4,67},{5,68},{6,69},{7,70},{8,71},{9... | collective-permute-start | bytes 1572872 | tf_op jit(solution)/shard_map/ppermute | solution.py:330
  41.7 0.0 collective-permute-done.9.refs_1_
  41.7 1.3 %collective-permute-start.8 = (f32[2,4,128,128]{3,2,1,0:T(8,128)S(1)}, f32[2,4,128,128]{3,2,1,0:T(8,128)S(1)}, u32[]{:S(2)}, u32[]{:S(2)}) collective-permute-start(f32[2,4,128,128]{3,2,1,0:T(8,128)S(1)} %get-tuple-element.16), channel_id=1, source_target_pairs={{0,64},{1,65},{2,66},{3,67},{4,68},{5,69},{6,70},{7,71},{8,72},{9,... | collective-permute-start | bytes 1572872 | tf_op jit(solution)/shard_map/ppermute | solution.py:330
  43.0 1.1 shard_map.43.refs_1_
  44.1 0.0 collective-permute-done.11.refs_1_
  44.1 1.1 shard_map.45.refs_3_
  45.2 0.0 collective-permute-done.13.refs_2_
  45.3 1.1 shard_map.47.refs_2_.refs_1_
  46.5 7.5 %shard_map.50.refs_4_.array = f32[2,4,128,128]{3,2,1,0:T(8,128)S(1)} custom-call(s32[1]{0:T(128)} %bitcast.refs_0_, f32[2,4,128,128]{3,2,1,0:T(8,128)S(1)} %shard_map.43.refs_1_, f32[2,4,128,128]{3,2,1,0:T(8,128)S(1)} %bitcast.14, f32[2,4,128,128]{3,2,1,0:T(8,128)S(1)} %shard_map.45.refs_3_, f32[2,4,128,128]{3,2,1,0:T(8,128)S(1)} %shard_map.48.refs_4_, ...), custom_call_target="tpu_custom_call" | custom-call | flops 10000000000 | bytes 1048576 | tf_op jit(solution)/shard_map/pallas_call | solution.py:264
  53.9 1.9 %collective-permute-done.6.refs_1_ = f32[2,4,128,128]{3,2,1,0:T(8,128)S(1)} collective-permute-done((f32[2,4,128,128]{3,2,1,0:T(8,128)S(1)}, f32[2,4,128,128]{3,2,1,0:T(8,128)S(1)}, u32[]{:S(2)}, u32[]{:S(2)}) %collective-permute-start.6) | collective-permute-done | bytes 524320 | tf_op jit(solution)/shard_map/ppermute | solution.py:330
  55.8 0.0 collective-permute-done.8.refs_3_
  55.8 2.7 %shard_map.51 = (f32[2,4,128,128]{3,2,1,0:T(8,128)S(1)}, f32[2,4,128,128]{3,2,1,0:T(8,128)S(1)}) custom-call(s32[1]{0:T(128)} %bitcast.refs_0_, f32[2,4,128,128]{3,2,1,0:T(8,128)S(1)} %collective-permute-done.6.refs_1_, f32[2,4,128,128]{3,2,1,0:T(8,128)S(1)} %collective-permute-done.7.refs_2_, f32[2,4,128,128]{3,2,1,0:T(8,128)S(1)} %collective-permute-done.8.refs_3_, ...), custom_call_target="tpu_custom_call" | custom-call | flops 10000000000 | bytes 1048576 | tf_op jit(solution)/shard_map/pallas_call | solution.py:264
  58.5 1.3 %collective-permute-start.14 = (f32[2,4,128,128]{3,2,1,0:T(8,128)S(1)}, f32[2,4,128,128]{3,2,1,0:T(8,128)S(1)}, u32[]{:S(2)}, u32[]{:S(2)}) collective-permute-start(f32[2,4,128,128]{3,2,1,0:T(8,128)S(1)} %get-tuple-element.18), channel_id=1, source_target_pairs={{64,1},{65,2},{66,3},{67,4},{68,5},{69,6},{70,7},{71,8},{72,9},{73... | collective-permute-start | bytes 1572872 | tf_op jit(solution)/shard_map/ppermute | solution.py:330
  59.8 1.3 %collective-permute-start.15 = (f32[2,4,128,128]{3,2,1,0:T(8,128)S(1)}, f32[2,4,128,128]{3,2,1,0:T(8,128)S(1)}, u32[]{:S(2)}, u32[]{:S(2)}) collective-permute-start(f32[2,4,128,128]{3,2,1,0:T(8,128)S(1)} %get-tuple-element.18), channel_id=1, source_target_pairs={{64,63},{65,0},{66,1},{67,2},{68,3},{69,4},{70,5},{71,6},{72,7},{7... | collective-permute-start | bytes 1572872 | tf_op jit(solution)/shard_map/ppermute | solution.py:330
  61.2 1.3 %collective-permute-start.16 = (f32[2,4,128,128]{3,2,1,0:T(8,128)S(1)}, f32[2,4,128,128]{3,2,1,0:T(8,128)S(1)}, u32[]{:S(2)}, u32[]{:S(2)}) collective-permute-start(f32[2,4,128,128]{3,2,1,0:T(8,128)S(1)} %get-tuple-element.18), channel_id=1, source_target_pairs={{64,0},{65,1},{66,2},{67,3},{68,4},{69,5},{70,6},{71,7},{72,8},{73... | collective-permute-start | bytes 1572872 | tf_op jit(solution)/shard_map/ppermute | solution.py:330
  62.5 0.7 collective-permute-start.17
  63.2 2.7 %collective-permute-done.14.refs_1_.token = f32[2,4,128,128]{3,2,1,0:T(8,128)S(1)} collective-permute-done((f32[2,4,128,128]{3,2,1,0:T(8,128)S(1)}, f32[2,4,128,128]{3,2,1,0:T(8,128)S(1)}, u32[]{:S(2)}, u32[]{:S(2)}) %collective-permute-start.14) | collective-permute-done | bytes 524320 | tf_op jit(solution)/shard_map/ppermute | solution.py:330
  66.0 1.3 %collective-permute-start.21 = (f32[2,4,128,128]{3,2,1,0:T(8,128)S(1)}, f32[2,4,128,128]{3,2,1,0:T(8,128)S(1)}, u32[]{:S(2)}, u32[]{:S(2)}) collective-permute-start(f32[2,4,128,128]{3,2,1,0:T(8,128)S(1)} %shard_map.53), channel_id=1, source_target_pairs={{192,64},{193,65},{194,66},{195,67},{196,68},{197,69},{198,70},{19... | collective-permute-start | bytes 1572872 | tf_op jit(solution)/shard_map/ppermute | solution.py:330
  67.3 0.0 collective-permute-done.15.refs_2_
  67.3 0.0 collective-permute-done.17.refs_4_
  67.3 1.3 %collective-permute-start.18 = (f32[2,4,128,128]{3,2,1,0:T(8,128)S(1)}, f32[2,4,128,128]{3,2,1,0:T(8,128)S(1)}, u32[]{:S(2)}, u32[]{:S(2)}) collective-permute-start(f32[2,4,128,128]{3,2,1,0:T(8,128)S(1)} %get-tuple-element.19), channel_id=1, source_target_pairs={{0,65},{1,66},{2,67},{3,68},{4,69},{5,70},{6,71},{7,72},{8,73},{9,... | collective-permute-start | bytes 1572872 | tf_op jit(solution)/shard_map/ppermute | solution.py:330
  68.6 1.3 %collective-permute-start.19 = (f32[2,4,128,128]{3,2,1,0:T(8,128)S(1)}, f32[2,4,128,128]{3,2,1,0:T(8,128)S(1)}, u32[]{:S(2)}, u32[]{:S(2)}) collective-permute-start(f32[2,4,128,128]{3,2,1,0:T(8,128)S(1)} %get-tuple-element.19), channel_id=1, source_target_pairs={{0,127},{1,64},{2,65},{3,66},{4,67},{5,68},{6,69},{7,70},{8,71},{9... | collective-permute-start | bytes 1572872 | tf_op jit(solution)/shard_map/ppermute | solution.py:330
  69.9 1.3 %collective-permute-start.20 = (f32[2,4,128,128]{3,2,1,0:T(8,128)S(1)}, f32[2,4,128,128]{3,2,1,0:T(8,128)S(1)}, u32[]{:S(2)}, u32[]{:S(2)}) collective-permute-start(f32[2,4,128,128]{3,2,1,0:T(8,128)S(1)} %get-tuple-element.19), channel_id=1, source_target_pairs={{0,64},{1,65},{2,66},{3,67},{4,68},{5,69},{6,70},{7,71},{8,72},{9,... | collective-permute-start | bytes 1572872 | tf_op jit(solution)/shard_map/ppermute | solution.py:330
  71.2 16.9 %collective-permute-done.21.refs_4_ = f32[2,4,128,128]{3,2,1,0:T(8,128)S(1)} collective-permute-done((f32[2,4,128,128]{3,2,1,0:T(8,128)S(1)}, f32[2,4,128,128]{3,2,1,0:T(8,128)S(1)}, u32[]{:S(2)}, u32[]{:S(2)}) %collective-permute-start.21) | collective-permute-done | bytes 524320 | tf_op jit(solution)/shard_map/ppermute | solution.py:330
  88.1 19.2 %collective-permute-done.18.refs_1_ = f32[2,4,128,128]{3,2,1,0:T(8,128)S(1)} collective-permute-done((f32[2,4,128,128]{3,2,1,0:T(8,128)S(1)}, f32[2,4,128,128]{3,2,1,0:T(8,128)S(1)}, u32[]{:S(2)}, u32[]{:S(2)}) %collective-permute-start.18) | collective-permute-done | bytes 524320 | tf_op jit(solution)/shard_map/ppermute | solution.py:330
  107.3 0.0 collective-permute-done.19.refs_2_
  107.3 0.0 collective-permute-done.20.refs_3_
  107.3 1.2 %shard_map.55 = f32[1,4,128,128]{3,2,1,0:T(8,128)S(1)} custom-call(s32[1]{0:T(128)} %bitcast.refs_0_, f32[2,4,128,128]{3,2,1,0:T(8,128)S(1)} %collective-permute-done.18.refs_1_, f32[2,4,128,128]{3,2,1,0:T(8,128)S(1)} %collective-permute-done.19.refs_2_, f32[2,4,128,128]{3,2,1,0:T(8,128)S(1)} %collective-permute-done.20.refs_3_, ...), custom_call_target="tpu_custom_call" | custom-call | flops 10000000000 | bytes 1048576 | tf_op jit(solution)/shard_map/pallas_call | solution.py:264
  108.5 1.3 %collective-permute-start.23 = (f32[1,4,128,128]{3,2,1,0:T(8,128)S(1)}, f32[1,4,128,128]{3,2,1,0:T(8,128)S(1)}, u32[]{:S(2)}, u32[]{:S(2)}) collective-permute-start(f32[1,4,128,128]{3,2,1,0:T(8,128)S(1)} %shard_map.55), channel_id=1, source_target_pairs={{0,128},{1,129},{2,130},{3,131},{4,132},{5,133},{6,134},{7,135},{8... | collective-permute-start | bytes 786440 | tf_op jit(solution)/shard_map/ppermute | solution.py:330
  109.8 1.2 %shard_map.54 = f32[1,4,128,128]{3,2,1,0:T(8,128)S(1)} custom-call(s32[1]{0:T(128)} %bitcast.refs_0_, f32[2,4,128,128]{3,2,1,0:T(8,128)S(1)} %collective-permute-done.18.refs_1_, f32[2,4,128,128]{3,2,1,0:T(8,128)S(1)} %collective-permute-done.19.refs_2_, f32[2,4,128,128]{3,2,1,0:T(8,128)S(1)} %collective-permute-done.20.refs_3_, ...), custom_call_target="tpu_custom_call" | custom-call | flops 10000000000 | bytes 1048576 | tf_op jit(solution)/shard_map/pallas_call | solution.py:264
  111.0 1.3 %collective-permute-start.22 = (f32[1,4,128,128]{3,2,1,0:T(8,128)S(1)}, f32[1,4,128,128]{3,2,1,0:T(8,128)S(1)}, u32[]{:S(2)}, u32[]{:S(2)}) collective-permute-start(f32[1,4,128,128]{3,2,1,0:T(8,128)S(1)} %shard_map.54), channel_id=1, source_target_pairs={{0,128},{1,129},{2,130},{3,131},{4,132},{5,133},{6,134},{7,135},{8... | collective-permute-start | bytes 786440 | tf_op jit(solution)/shard_map/ppermute | solution.py:330
  112.3 0.7 collective-permute-done.23.refs_4_
  113.1 2.8 %collective-permute-done.22.refs_3_ = f32[1,4,128,128]{3,2,1,0:T(8,128)S(1)} collective-permute-done((f32[1,4,128,128]{3,2,1,0:T(8,128)S(1)}, f32[1,4,128,128]{3,2,1,0:T(8,128)S(1)}, u32[]{:S(2)}, u32[]{:S(2)}) %collective-permute-start.22) | collective-permute-done | bytes 262176 | tf_op jit(solution)/shard_map/ppermute | solution.py:330
  115.9 0.8 shard_map.56
  (16 shorter events, 0.3 us)
Async XLA Ops:
  0.0 0.9 copy-start.4
  1.0 0.9 copy-start.5
  1.9 11.7 %copy-start = (f32[1,2,4,128,128]{4,3,2,1,0:T(8,128)S(1)}, f32[1,2,4,128,128]{4,3,2,1,0:T(8,128)}, u32[]{:S(2)}) copy-start(f32[1,2,4,128,128]{4,3,2,1,0:T(8,128)} %param.3) | copy-start | bytes 1572868
  2.0 18.5 %copy-start.2 = (f32[2,4,128,128]{3,2,1,0:T(8,128)}, f32[2,4,128,128]{3,2,1,0:T(8,128)S(1)}, u32[]{:S(2)}) copy-start(f32[2,4,128,128]{3,2,1,0:T(8,128)S(1)} %shard_map.38.refs_5_) | copy-start | bytes 1572868
  2.0 17.7 %collective-permute-start.2 = (f32[2,4,128,128]{3,2,1,0:T(8,128)S(1)}, f32[2,4,128,128]{3,2,1,0:T(8,128)S(1)}, u32[]{:S(2)}, u32[]{:S(2)}) collective-permute-start(f32[2,4,128,128]{3,2,1,0:T(8,128)S(1)} %shard_map.38.refs_5_), channel_id=1, source_target_pairs={{0,1},{1,2},{2,3},{3,4},{4,5},{5,6},{6,7},{7,8},{8,9},{9,10},{10,1... | collective-permute-start | bytes 1572872 | tf_op jit(solution)/shard_map/ppermute | solution.py:330
  13.6 8.9 %collective-permute-start.4 = (f32[2,4,128,128]{3,2,1,0:T(8,128)S(1)}, f32[2,4,128,128]{3,2,1,0:T(8,128)S(1)}, u32[]{:S(2)}, u32[]{:S(2)}) collective-permute-start(f32[2,4,128,128]{3,2,1,0:T(8,128)S(1)} %bitcast.8), channel_id=1, source_target_pairs={{128,129},{129,130},{130,131},{131,128},{132,133},{133,134},{134,1... | collective-permute-start | bytes 1572872 | tf_op jit(solution)/shard_map/ppermute | solution.py:330
  14.2 18.3 %collective-permute-start.5 = (f32[2,4,128,128]{3,2,1,0:T(8,128)S(1)}, f32[2,4,128,128]{3,2,1,0:T(8,128)S(1)}, u32[]{:S(2)}, u32[]{:S(2)}) collective-permute-start(f32[2,4,128,128]{3,2,1,0:T(8,128)S(1)} %bitcast.9), channel_id=1, source_target_pairs={{128,131},{129,128},{130,129},{131,130},{132,135},{133,132},{134,1... | collective-permute-start | bytes 1572872 | tf_op jit(solution)/shard_map/ppermute | solution.py:330
  14.9 19.2 %collective-permute-start = (f32[2,4,128,128]{3,2,1,0:T(8,128)S(1)}, f32[2,4,128,128]{3,2,1,0:T(8,128)}, u32[]{:S(2)}, u32[]{:S(2)}) collective-permute-start(f32[2,4,128,128]{3,2,1,0:T(8,128)S(1)} %bitcast.10), channel_id=1, source_target_pairs={{0,1},{1,2},{2,3},{3,4},{4,5},{5,6},{6,7},{7,8},{8,9},{9,10},{10,1... | collective-permute-start | bytes 1572872 | tf_op jit(solution)/shard_map/ppermute | solution.py:330
  16.4 19.2 %collective-permute-start.1 = (f32[2,4,128,128]{3,2,1,0:T(8,128)S(1)}, f32[2,4,128,128]{3,2,1,0:T(8,128)}, u32[]{:S(2)}, u32[]{:S(2)}) collective-permute-start(f32[2,4,128,128]{3,2,1,0:T(8,128)S(1)} %bitcast.11), channel_id=1, source_target_pairs={{0,63},{1,0},{2,1},{3,2},{4,3},{5,4},{6,5},{7,6},{8,7},{9,8},{10,9... | collective-permute-start | bytes 1572872 | tf_op jit(solution)/shard_map/ppermute | solution.py:330
  20.5 21.2 %collective-permute-start.9 = (f32[2,4,128,128]{3,2,1,0:T(8,128)}, f32[2,4,128,128]{3,2,1,0:T(8,128)}, u32[]{:S(2)}, u32[]{:S(2)}) collective-permute-start(f32[2,4,128,128]{3,2,1,0:T(8,128)} %shard_map.40.refs_8_), channel_id=1, source_target_pairs={{64,65},{65,66},{66,67},{67,68},{68,69},{69,70},{70,71},{71,72},{7... | collective-permute-start | bytes 1572872 | tf_op jit(solution)/shard_map/ppermute | solution.py:330
  22.4 21.7 %collective-permute-start.11 = (f32[2,4,128,128]{3,2,1,0:T(8,128)}, f32[2,4,128,128]{3,2,1,0:T(8,128)}, u32[]{:S(2)}, u32[]{:S(2)}) collective-permute-start(f32[2,4,128,128]{3,2,1,0:T(8,128)} %shard_map.40.refs_8_), channel_id=1, source_target_pairs={{64,127},{65,64},{66,65},{67,66},{68,67},{69,68},{70,69},{71,70},{... | collective-permute-start | bytes 1572872 | tf_op jit(solution)/shard_map/ppermute | solution.py:330
  33.4 6.9 %collective-permute-start.10 = (f32[2,4,128,128]{3,2,1,0:T(8,128)}, f32[2,4,128,128]{3,2,1,0:T(8,128)S(1)}, u32[]{:S(2)}, u32[]{:S(2)}) collective-permute-start(f32[2,4,128,128]{3,2,1,0:T(8,128)} %shard_map.39.refs_7_), channel_id=1, source_target_pairs={{128,132},{131,191},{132,136},{135,131},{136,140},{139,135},{140,1... | collective-permute-start | bytes 1572872 | tf_op jit(solution)/shard_map/ppermute | solution.py:330
  34.1 1.5 %collective-permute-start.12 = (f32[2,4,128,128]{3,2,1,0:T(8,128)S(1)}, f32[2,4,128,128]{3,2,1,0:T(8,128)}, u32[]{:S(2)}, u32[]{:S(2)}) collective-permute-start(f32[2,4,128,128]{3,2,1,0:T(8,128)S(1)} %collective-permute-done.2.token.refs_4_.refs_2_), channel_id=1, source_target_pairs={{128,132},{132,136},{136,140},{140,144},{144,148},{148,152},{152,1... | collective-permute-start | bytes 1572872 | tf_op jit(solution)/shard_map/ppermute | solution.py:330
  35.6 2.0 %collective-permute-start.3 = (f32[2,4,128,128]{3,2,1,0:T(8,128)S(1)}, f32[2,4,128,128]{3,2,1,0:T(8,128)}, u32[]{:S(2)}, u32[]{:S(2)}) collective-permute-start(f32[2,4,128,128]{3,2,1,0:T(8,128)S(1)} %collective-permute-done.2.token.refs_4_.refs_2_), channel_id=1, source_target_pairs={{0,64},{1,65},{2,66},{3,67},{4,68},{5,69},{6,70},{7,71},{8,72},{9,... | collective-permute-start | bytes 1572872 | tf_op jit(solution)/shard_map/ppermute | solution.py:330
  35.6 2.0 %copy-start.1 = (f32[1,2,4,128,128]{4,3,2,1,0:T(8,128)S(1)}, f32[1,2,4,128,128]{4,3,2,1,0:T(8,128)}, u32[]{:S(2)}) copy-start(f32[1,2,4,128,128]{4,3,2,1,0:T(8,128)} %param.3) | copy-start | bytes 1572868
  35.6 2.0 %copy-start.3 = (f32[2,4,128,128]{3,2,1,0:T(8,128)S(1)}, f32[2,4,128,128]{3,2,1,0:T(8,128)}, u32[]{:S(2)}) copy-start(f32[2,4,128,128]{3,2,1,0:T(8,128)} %copy-done.2) | copy-start | bytes 1572868
  36.8 8.4 %collective-permute-start.13 = (f32[2,4,128,128]{3,2,1,0:T(8,128)S(1)}, f32[2,4,128,128]{3,2,1,0:T(8,128)S(1)}, u32[]{:S(2)}, u32[]{:S(2)}) collective-permute-start(f32[2,4,128,128]{3,2,1,0:T(8,128)S(1)} %shard_map.46.refs_1_.refs_2_), channel_id=1, source_target_pairs={{128,192},{129,193},{130,194},{131,195},{132,196},{133,197},{134,1... | collective-permute-start | bytes 1572872 | tf_op jit(solution)/shard_map/ppermute | solution.py:330
  39.0 16.8 %collective-permute-start.6 = (f32[2,4,128,128]{3,2,1,0:T(8,128)S(1)}, f32[2,4,128,128]{3,2,1,0:T(8,128)S(1)}, u32[]{:S(2)}, u32[]{:S(2)}) collective-permute-start(f32[2,4,128,128]{3,2,1,0:T(8,128)S(1)} %get-tuple-element.16), channel_id=1, source_target_pairs={{0,65},{1,66},{2,67},{3,68},{4,69},{5,70},{6,71},{7,72},{8,73},{9,... | collective-permute-start | bytes 1572872 | tf_op jit(solution)/shard_map/ppermute | solution.py:330
  40.3 15.5 %collective-permute-start.7 = (f32[2,4,128,128]{3,2,1,0:T(8,128)S(1)}, f32[2,4,128,128]{3,2,1,0:T(8,128)S(1)}, u32[]{:S(2)}, u32[]{:S(2)}) collective-permute-start(f32[2,4,128,128]{3,2,1,0:T(8,128)S(1)} %get-tuple-element.16), channel_id=1, source_target_pairs={{0,127},{1,64},{2,65},{3,66},{4,67},{5,68},{6,69},{7,70},{8,71},{9... | collective-permute-start | bytes 1572872 | tf_op jit(solution)/shard_map/ppermute | solution.py:330
  41.7 14.1 %collective-permute-start.8 = (f32[2,4,128,128]{3,2,1,0:T(8,128)S(1)}, f32[2,4,128,128]{3,2,1,0:T(8,128)S(1)}, u32[]{:S(2)}, u32[]{:S(2)}) collective-permute-start(f32[2,4,128,128]{3,2,1,0:T(8,128)S(1)} %get-tuple-element.16), channel_id=1, source_target_pairs={{0,64},{1,65},{2,66},{3,67},{4,68},{5,69},{6,70},{7,71},{8,72},{9,... | collective-permute-start | bytes 1572872 | tf_op jit(solution)/shard_map/ppermute | solution.py:330
  58.5 7.4 %collective-permute-start.14 = (f32[2,4,128,128]{3,2,1,0:T(8,128)S(1)}, f32[2,4,128,128]{3,2,1,0:T(8,128)S(1)}, u32[]{:S(2)}, u32[]{:S(2)}) collective-permute-start(f32[2,4,128,128]{3,2,1,0:T(8,128)S(1)} %get-tuple-element.18), channel_id=1, source_target_pairs={{64,1},{65,2},{66,3},{67,4},{68,5},{69,6},{70,7},{71,8},{72,9},{73... | collective-permute-start | bytes 1572872 | tf_op jit(solution)/shard_map/ppermute | solution.py:330
  59.8 7.4 %collective-permute-start.15 = (f32[2,4,128,128]{3,2,1,0:T(8,128)S(1)}, f32[2,4,128,128]{3,2,1,0:T(8,128)S(1)}, u32[]{:S(2)}, u32[]{:S(2)}) collective-permute-start(f32[2,4,128,128]{3,2,1,0:T(8,128)S(1)} %get-tuple-element.18), channel_id=1, source_target_pairs={{64,63},{65,0},{66,1},{67,2},{68,3},{69,4},{70,5},{71,6},{72,7},{7... | collective-permute-start | bytes 1572872 | tf_op jit(solution)/shard_map/ppermute | solution.py:330
  61.2 6.1 %collective-permute-start.16 = (f32[2,4,128,128]{3,2,1,0:T(8,128)S(1)}, f32[2,4,128,128]{3,2,1,0:T(8,128)S(1)}, u32[]{:S(2)}, u32[]{:S(2)}) collective-permute-start(f32[2,4,128,128]{3,2,1,0:T(8,128)S(1)} %get-tuple-element.18), channel_id=1, source_target_pairs={{64,0},{65,1},{66,2},{67,3},{68,4},{69,5},{70,6},{71,7},{72,8},{73... | collective-permute-start | bytes 1572872 | tf_op jit(solution)/shard_map/ppermute | solution.py:330
  62.5 4.8 %collective-permute-start.17 = (f32[2,4,128,128]{3,2,1,0:T(8,128)S(1)}, f32[2,4,128,128]{3,2,1,0:T(8,128)S(1)}, u32[]{:S(2)}, u32[]{:S(2)}) collective-permute-start(f32[2,4,128,128]{3,2,1,0:T(8,128)S(1)} %shard_map.50.refs_4_.array), channel_id=1, source_target_pairs={{128,0},{129,1},{130,2},{131,3},{132,4},{133,5},{134,6},{135,7},{1... | collective-permute-start | bytes 1572872 | tf_op jit(solution)/shard_map/ppermute | solution.py:330
  66.0 22.1 %collective-permute-start.21 = (f32[2,4,128,128]{3,2,1,0:T(8,128)S(1)}, f32[2,4,128,128]{3,2,1,0:T(8,128)S(1)}, u32[]{:S(2)}, u32[]{:S(2)}) collective-permute-start(f32[2,4,128,128]{3,2,1,0:T(8,128)S(1)} %shard_map.53), channel_id=1, source_target_pairs={{192,64},{193,65},{194,66},{195,67},{196,68},{197,69},{198,70},{19... | collective-permute-start | bytes 1572872 | tf_op jit(solution)/shard_map/ppermute | solution.py:330
  67.3 40.0 %collective-permute-start.18 = (f32[2,4,128,128]{3,2,1,0:T(8,128)S(1)}, f32[2,4,128,128]{3,2,1,0:T(8,128)S(1)}, u32[]{:S(2)}, u32[]{:S(2)}) collective-permute-start(f32[2,4,128,128]{3,2,1,0:T(8,128)S(1)} %get-tuple-element.19), channel_id=1, source_target_pairs={{0,65},{1,66},{2,67},{3,68},{4,69},{5,70},{6,71},{7,72},{8,73},{9,... | collective-permute-start | bytes 1572872 | tf_op jit(solution)/shard_map/ppermute | solution.py:330
  68.6 38.7 %collective-permute-start.19 = (f32[2,4,128,128]{3,2,1,0:T(8,128)S(1)}, f32[2,4,128,128]{3,2,1,0:T(8,128)S(1)}, u32[]{:S(2)}, u32[]{:S(2)}) collective-permute-start(f32[2,4,128,128]{3,2,1,0:T(8,128)S(1)} %get-tuple-element.19), channel_id=1, source_target_pairs={{0,127},{1,64},{2,65},{3,66},{4,67},{5,68},{6,69},{7,70},{8,71},{9... | collective-permute-start | bytes 1572872 | tf_op jit(solution)/shard_map/ppermute | solution.py:330
  69.9 37.4 %collective-permute-start.20 = (f32[2,4,128,128]{3,2,1,0:T(8,128)S(1)}, f32[2,4,128,128]{3,2,1,0:T(8,128)S(1)}, u32[]{:S(2)}, u32[]{:S(2)}) collective-permute-start(f32[2,4,128,128]{3,2,1,0:T(8,128)S(1)} %get-tuple-element.19), channel_id=1, source_target_pairs={{0,64},{1,65},{2,66},{3,67},{4,68},{5,69},{6,70},{7,71},{8,72},{9,... | collective-permute-start | bytes 1572872 | tf_op jit(solution)/shard_map/ppermute | solution.py:330
  108.5 4.6 %collective-permute-start.23 = (f32[1,4,128,128]{3,2,1,0:T(8,128)S(1)}, f32[1,4,128,128]{3,2,1,0:T(8,128)S(1)}, u32[]{:S(2)}, u32[]{:S(2)}) collective-permute-start(f32[1,4,128,128]{3,2,1,0:T(8,128)S(1)} %shard_map.55), channel_id=1, source_target_pairs={{0,128},{1,129},{2,130},{3,131},{4,132},{5,133},{6,134},{7,135},{8... | collective-permute-start | bytes 786440 | tf_op jit(solution)/shard_map/ppermute | solution.py:330
  111.0 4.9 %collective-permute-start.22 = (f32[1,4,128,128]{3,2,1,0:T(8,128)S(1)}, f32[1,4,128,128]{3,2,1,0:T(8,128)S(1)}, u32[]{:S(2)}, u32[]{:S(2)}) collective-permute-start(f32[1,4,128,128]{3,2,1,0:T(8,128)S(1)} %shard_map.54), channel_id=1, source_target_pairs={{0,128},{1,129},{2,130},{3,131},{4,132},{5,133},{6,134},{7,135},{8... | collective-permute-start | bytes 786440 | tf_op jit(solution)/shard_map/ppermute | solution.py:330

commit v4 on v3

--- a/solution.py
+++ b/solution.py
@@ -14,7 +14,7 @@
 SMEM = pl.BlockSpec(memory_space=pltpu.SMEM)
 ANY = pl.BlockSpec(memory_space=pl.ANY)
 AXES = ("tm", "space")
-SETTLE = 3 * 10**10
+SETTLE = 10**9
 
 
 def triple(values, axis):
@@ -153,7 +153,7 @@
         coarse_levels(lambda species, layer: wide[species, layer], (level_a, level_b), finish, depth)
 
 
-def coarse_kernel(worker, position, low, high, own, correction, own_c, explicit, state, *levels):
+def coarse_kernel(worker, position, own, low, high, correction, own_c, explicit, state, *levels):
     depth = own.shape[1]
 
     @pl.when((position[0] >= worker[0]) & (position[0] <= worker[-1]))
@@ -170,7 +170,7 @@
         coarse_levels(joined(low, own, high, depth), levels, finish, depth)
 
 
-def last_kernel(chosen, position, low, high, own, correction, third, state, level_a, level_b):
+def last_kernel(chosen, position, own, low, high, correction, third, state, level_a, level_b):
     depth = own.shape[1]
 
     @pl.when(position[0] != 1)
@@ -232,7 +232,10 @@
         scratch_shapes=[pltpu.SemaphoreType.DMA((2,))],
         compiler_params=pltpu.CompilerParams(vmem_limit_bytes=4 * 2**20),
         cost_estimate=pl.CostEstimate(flops=10**5, bytes_accessed=2**20, transcendentals=0),
-    )(feed, kill)
+    )(
+        pltpu.with_memory_space_constraint(feed, pltpu.HBM),
+        pltpu.with_memory_space_constraint(kill, pltpu.HBM),
+    )
 
 
 def pick_kernel(flag, array, other, picked):
@@ -289,21 +292,22 @@
     )(pltpu.with_memory_space_constraint(array, pltpu.VMEM), token)
 
 
-def settle_kernel(low, high, low_out, high_out):
+def settle_kernel(*refs):
     pass
 
 
-def settled(low, high):
+def settled(low, high, tokens):
     return pl.pallas_call(
         settle_kernel,
         out_shape=[jax.ShapeDtypeStruct(low.shape, low.dtype)] * 2,
-        in_specs=[ANY, ANY],
+        in_specs=[ANY] * (2 + len(tokens)),
         out_specs=[ANY, ANY],
         input_output_aliases={0: 0, 1: 1},
         cost_estimate=pl.CostEstimate(flops=SETTLE, bytes_accessed=2**20, transcendentals=0),
     )(
         pltpu.with_memory_space_constraint(low, pltpu.VMEM),
         pltpu.with_memory_space_constraint(high, pltpu.VMEM),
+        *tokens,
     )
 
 
@@ -336,8 +340,11 @@
         step = 1 if source % 2 == 0 else -1
         return source, slab + step if source < 2 else beside(slab, step)
 
+    def onward(step):
+        return lambda source, slab: (source, slab + step) if source < 2 else (source ^ 1, slab)
+
     def around_x(step):
-        return lambda source, slab: (source, beside(slab, step)) if source >= 2 else None
+        return lambda source, slab: (source, beside(slab, step)) if source > 1 else (source ^ 1, slab)
 
     def far_half(source, slab):
         if source == 2 and slab % ring == 0:
@@ -362,40 +369,33 @@
     def spread(array, source, target):
         low = moved(array, route(source, target, 1))
         high = moved(array, route(source, target, -1))
-        return low, high, moved(array, route(source, target))
+        return moved(array, route(source, target)), low, high
 
     both = stacked(feed, kill)
     half = moved(both, halves)
-    low_0 = moved(own, route(0, 0, 1))
-    high_0 = moved(own, route(0, 0, -1))
     low_x = moved(own, around_x(1))
     high_x = moved(own, around_x(-1))
+    low = moved(own, onward(1))
+    high = moved(own, onward(-1))
     other = moved(half, swapped)
     half_far = moved(half, far_half)
     lowest, highest = place == 0, place == ring - 1
+    outer = pick(lowest, low_x, high_x)
+    outer_far = moved(outer, far)
     mended = pick((lowest & (index == 2)) | (highest & (index == 3)), half_far, half)
     other_x = moved(mended, lambda source, slab: swapped(source, slab) if source >= 2 else None)
-    own_1 = after(own, half)
-    low_1 = moved(own_1, route(1, 1, 1))
-    high_1 = moved(own_1, route(1, 1, -1))
-    outer = pick(lowest, low_x, high_x)
-    outer_far = moved(outer, far)
-    low_0, high_0 = settled(low_0, high_0)
+    low, high = settled(low, high, ())
+    low, high = settled(low, high, (outer, mended))
     explicit, first_end = run(
-        fine_kernel,
-        position,
-        (low_0, own, high_0, half, both, other),
-        2,
-        worker=(0,),
-        tokens=(outer, own_1),
+        fine_kernel, position, (low, own, high, half, both, other), 2, worker=(0,)
     )
     second = spread(explicit, 0, 1)
     even = index % 2 == 0
     other = pick(index == 1, other, other_x)
     low_c = pick(even, mended, other)
     high_c = pick(even, other, mended)
-    low = pick(index == 1, low_1, pick(lowest, outer_far, low_x))
-    high = pick(index == 1, high_1, pick(highest, outer_far, high_x))
+    low = pick(index == 1, low, pick(lowest, outer_far, low_x))
+    high = pick(index == 1, high, pick(highest, outer_far, high_x))
     (correction,) = run(
         correction_kernel, position, (low, own, high, low_c, both, high_c), 1, 3, worker=(1, 3)
     )
@@ -404,7 +404,7 @@
         coarse_kernel, position, (*second, correction, both), 2, worker=(1,)
     )
     third = spread(explicit, 1, 0)
-    crossed_3 = moved(after(correction, third[0]), route(3, 1))
+    crossed_3 = moved(after(correction, third[1]), route(3, 1))
     explicit, third_end = run(
         coarse_kernel, position, (*third, crossed_2, both), 2, worker=(0,)
     )

time: 117 us -> 110 us (0.940)
  starting transfers between devices: 47.1 us -> 39.7 us
  local copies, waits for them, and re-layouts: 1.92 us -> 6.27 us
  waiting for transfers between devices: 46.2 us -> 42.6 us
    ppermute x24 -> x22, starting transfers between devices: 47.1 us -> 39.7 us  [moved(): return lax.ppermute(array, AXES, pairs)]
    unnamed x12 -> x22, local copies, waits for them, and re-layouts: 1.92 us -> 6.27 us
    ppermute x24 -> x22, waiting for transfers between devices: 46.2 us -> 42.6 us  [moved(): return lax.ppermute(array, AXES, pairs)]
  transfers between devices with their start and end apart: 24 -> 22, of which waited for: 8 -> 8; matrix products, arithmetic and copies ran while one was open for 0% -> 0% of each run, Pallas kernels for 14% -> 13%
where the time goes in v4:
time: 110 us; the launch traced here: 109 us
  waiting for transfers between devices  42.6 us (39%)
  starting transfers between devices  39.7 us (36%)
  Pallas kernels  20.2 us (18%)
  local copies, waits for them, and re-layouts  6.27 us (6%)
    ppermute x22, waiting for transfers between devices, moved(): return lax.ppermute(array, AXES, pairs)  42.6 us
    ppermute x22, starting transfers between devices, moved(): return lax.ppermute(array, AXES, pairs)  39.7 us
    pallas_call x16, Pallas kernels, run(): pl.pallas_call(kernel, out_shape=out_shape, in_specs=[SMEM] + [VMEM] * le...  19.2 us
    unnamed x22, local copies, waits for them, and re-layouts  6.27 us
  transfers between devices with their start and end apart: 22, of which 8 were waited for; matrix products, arithmetic and copies ran while one was open for 0% of the time, Pallas kernels for 13%

profile of v4, /device:TPU:1, one launch (start us, length us, event | category | flops | bytes accessed | tf_op | source)
XLA Modules:
  0.0 109.0 jit_solution(16332011211539621568)
XLA Ops:
  0.0 1.0 shard_map.39.refs_5_
  1.1 11.6 %collective-permute-start.4 = (f32[2,4,128,128]{3,2,1,0:T(8,128)S(1)}, f32[2,4,128,128]{3,2,1,0:T(8,128)}, u32[]{:S(2)}, u32[]{:S(2)}) collective-permute-start(f32[2,4,128,128]{3,2,1,0:T(8,128)S(1)} %shard_map.39.refs_5_), channel_id=1, source_target_pairs={{0,1},{1,2},{2,3},{3,4},{4,5},{5,6},{6,7},{7,8},{8,9},{9,10},{10,1... | collective-permute-start | bytes 1572872 | tf_op jit(solution)/shard_map/ppermute | solution.py:334
  12.6 0.8 copy-done.2
  13.4 0.0 collective-permute-start.2
  13.4 0.5 collective-permute-start.3
  13.9 0.0 collective-permute-start
  13.9 7.8 %collective-permute-start.1 = (f32[2,4,128,128]{3,2,1,0:T(8,128)}, f32[2,4,128,128]{3,2,1,0:T(8,128)S(1)}, u32[]{:S(2)}, u32[]{:S(2)}) collective-permute-start(f32[2,4,128,128]{3,2,1,0:T(8,128)} %bitcast.1.refs_2_), channel_id=1, source_target_pairs={{0,63},{1,0},{2,1},{3,2},{4,3},{5,4},{6,5},{7,6},{8,7},{9,8},{10,9... | collective-permute-start | bytes 1572872 | tf_op jit(solution)/shard_map/ppermute | solution.py:334
  21.7 0.0 collective-permute-done.4.refs_2_.refs_4_
  21.7 0.7 collective-permute-start.5
  22.4 0.0 collective-permute-done.2.refs_1_.refs_2_
  22.4 0.6 collective-permute-start.6
  23.1 0.0 collective-permute-done.3.refs_2_
  23.1 0.8 shard_map.38.refs_2_
  23.9 0.7 collective-permute-start.10
  24.6 9.4 %collective-permute-done.refs_0_ = f32[2,4,128,128]{3,2,1,0:T(8,128)S(1)} collective-permute-done((f32[2,4,128,128]{3,2,1,0:T(8,128)}, f32[2,4,128,128]{3,2,1,0:T(8,128)S(1)}, u32[]{:S(2)}, u32[]{:S(2)}) %collective-permute-start) | collective-permute-done | bytes 524320 | tf_op jit(solution)/shard_map/ppermute | solution.py:334
  34.0 0.0 collective-permute-done.1.refs_1_
  34.0 0.8 copy-done.5
  34.8 0.8 copy-done.7
  35.6 0.0 collective-permute-done.5.refs_1_
  35.6 0.8 copy-done.9
  36.4 1.0 copy-done.10
  37.5 1.2 %shard_map.40.refs_3_.refs_1_.refs_2_ = f32[2,4,128,128]{3,2,1,0:T(8,128)S(1)} custom-call(s32[1]{0:T(128)} %bitcast.3.refs_0_, f32[2,4,128,128]{3,2,1,0:T(8,128)S(1)} %copy-done.10, f32[2,4,128,128]{3,2,1,0:T(8,128)} %collective-permute-done.4.refs_2_.refs_4_), custom_call_target="tpu_custom_call" | custom-call | flops 100000 | bytes 1048576 | tf_op jit(solution)/shard_map/pallas_call | solution.py:267
  38.6 0.0 copy-start
  38.6 1.5 %collective-permute-start.11 = (f32[2,4,128,128]{3,2,1,0:T(8,128)S(1)}, f32[2,4,128,128]{3,2,1,0:T(8,128)}, u32[]{:S(2)}, u32[]{:S(2)}) collective-permute-start(f32[2,4,128,128]{3,2,1,0:T(8,128)S(1)} %shard_map.40.refs_3_.refs_1_.refs_2_), channel_id=1, source_target_pairs={{128,192},{129,193},{130,194},{131,195},{132,196},{133,197},{134,1... | collective-permute-start | bytes 1572872 | tf_op jit(solution)/shard_map/ppermute | solution.py:334
  40.1 0.0 copy-done
  40.1 0.0 collective-permute-done.6.refs_6_.refs_1_
  40.1 1.0 copy-done.3
  41.2 1.4 %shard_map.42 = (f32[2,4,128,128]{3,2,1,0:T(8,128)S(1)}, f32[2,4,128,128]{3,2,1,0:T(8,128)S(1)}) custom-call(s32[1]{0:T(128)} %bitcast.refs_0_, f32[2,4,128,128]{3,2,1,0:T(8,128)S(1)} %get-tuple-element.17.refs_1_, f32[2,4,128,128]{3,2,1,0:T(8,128)} %bitcast.1.refs_2_, f32[2,4,128,128]{3,2,1,0:T(8,128)S(1)} %get-tuple-element.18.refs_3_.refs_1_, ...), custom_call_target="tpu_custom_call" | custom-call | flops 10000000000 | bytes 1048576 | tf_op jit(solution)/shard_map/pallas_call | solution.py:267
  42.5 1.3 %collective-permute-start.7 = (f32[2,4,128,128]{3,2,1,0:T(8,128)S(1)}, f32[2,4,128,128]{3,2,1,0:T(8,128)S(1)}, u32[]{:S(2)}, u32[]{:S(2)}) collective-permute-start(f32[2,4,128,128]{3,2,1,0:T(8,128)S(1)} %get-tuple-element.20), channel_id=1, source_target_pairs={{0,64},{1,65},{2,66},{3,67},{4,68},{5,69},{6,70},{7,71},{8,72},{9,... | collective-permute-start | bytes 1572872 | tf_op jit(solution)/shard_map/ppermute | solution.py:334
  43.8 1.3 %collective-permute-start.8 = (f32[2,4,128,128]{3,2,1,0:T(8,128)S(1)}, f32[2,4,128,128]{3,2,1,0:T(8,128)S(1)}, u32[]{:S(2)}, u32[]{:S(2)}) collective-permute-start(f32[2,4,128,128]{3,2,1,0:T(8,128)S(1)} %get-tuple-element.20), channel_id=1, source_target_pairs={{0,65},{1,66},{2,67},{3,68},{4,69},{5,70},{6,71},{7,72},{8,73},{9,... | collective-permute-start | bytes 1572872 | tf_op jit(solution)/shard_map/ppermute | solution.py:334
  45.1 1.3 %collective-permute-start.9 = (f32[2,4,128,128]{3,2,1,0:T(8,128)S(1)}, f32[2,4,128,128]{3,2,1,0:T(8,128)S(1)}, u32[]{:S(2)}, u32[]{:S(2)}) collective-permute-start(f32[2,4,128,128]{3,2,1,0:T(8,128)S(1)} %get-tuple-element.20), channel_id=1, source_target_pairs={{0,127},{1,64},{2,65},{3,66},{4,67},{5,68},{6,69},{7,70},{8,71},{9... | collective-permute-start | bytes 1572872 | tf_op jit(solution)/shard_map/ppermute | solution.py:334
  46.4 0.0 collective-permute-done.10.refs_1_
  46.7 0.0 collective-permute-done.11.refs_2_
  46.7 1.3 %shard_map.47.refs_2_.refs_1_ = f32[2,4,128,128]{3,2,1,0:T(8,128)S(1)} custom-call(s32[1]{0:T(128)} %bitcast.4.refs_0_, f32[2,4,128,128]{3,2,1,0:T(8,128)} %collective-permute-done.6.refs_6_.refs_1_, f32[2,4,128,128]{3,2,1,0:T(8,128)} %collective-permute-done.11.refs_2_), custom_call_target="tpu_custom_call" | custom-call | flops 100000 | bytes 1048576 | tf_op jit(solution)/shard_map/pallas_call | solution.py:267
  48.0 0.0 copy-done.1
  48.1 1.0 copy-done.4
  49.1 8.3 %shard_map.50.refs_4_.array = f32[2,4,128,128]{3,2,1,0:T(8,128)S(1)} custom-call(s32[1]{0:T(128)} %bitcast.refs_0_, f32[2,4,128,128]{3,2,1,0:T(8,128)S(1)} %shard_map.44.refs_1_, f32[2,4,128,128]{3,2,1,0:T(8,128)} %bitcast.1.refs_2_, f32[2,4,128,128]{3,2,1,0:T(8,128)S(1)} %shard_map.46.refs_3_, f32[2,4,128,128]{3,2,1,0:T(8,128)S(1)} %shard_map.48.refs_4_, ...), custom_call_target="tpu_custom_call" | custom-call | flops 10000000000 | bytes 1048576 | tf_op jit(solution)/shard_map/pallas_call | solution.py:267
  57.4 0.0 collective-permute-done.7.refs_1_
  57.4 7.9 %collective-permute-done.8.refs_2_ = f32[2,4,128,128]{3,2,1,0:T(8,128)S(1)} collective-permute-done((f32[2,4,128,128]{3,2,1,0:T(8,128)S(1)}, f32[2,4,128,128]{3,2,1,0:T(8,128)S(1)}, u32[]{:S(2)}, u32[]{:S(2)}) %collective-permute-start.8) | collective-permute-done | bytes 524320 | tf_op jit(solution)/shard_map/ppermute | solution.py:334
  65.3 0.0 collective-permute-done.9.refs_3_
  65.3 2.7 %shard_map.51 = (f32[2,4,128,128]{3,2,1,0:T(8,128)S(1)}, f32[2,4,128,128]{3,2,1,0:T(8,128)S(1)}) custom-call(s32[1]{0:T(128)} %bitcast.refs_0_, f32[2,4,128,128]{3,2,1,0:T(8,128)S(1)} %collective-permute-done.7.refs_1_, f32[2,4,128,128]{3,2,1,0:T(8,128)S(1)} %collective-permute-done.8.refs_2_, f32[2,4,128,128]{3,2,1,0:T(8,128)S(1)} %collective-permute-done.9.refs_3_, ...), custom_call_target="tpu_custom_call" | custom-call | flops 10000000000 | bytes 1048576 | tf_op jit(solution)/shard_map/pallas_call | solution.py:267
  68.0 1.3 %collective-permute-start.13 = (f32[2,4,128,128]{3,2,1,0:T(8,128)S(1)}, f32[2,4,128,128]{3,2,1,0:T(8,128)S(1)}, u32[]{:S(2)}, u32[]{:S(2)}) collective-permute-start(f32[2,4,128,128]{3,2,1,0:T(8,128)S(1)} %get-tuple-element.22), channel_id=1, source_target_pairs={{64,1},{65,2},{66,3},{67,4},{68,5},{69,6},{70,7},{71,8},{72,9},{73... | collective-permute-start | bytes 1572872 | tf_op jit(solution)/shard_map/ppermute | solution.py:334
  69.3 1.3 %collective-permute-start.12 = (f32[2,4,128,128]{3,2,1,0:T(8,128)S(1)}, f32[2,4,128,128]{3,2,1,0:T(8,128)S(1)}, u32[]{:S(2)}, u32[]{:S(2)}) collective-permute-start(f32[2,4,128,128]{3,2,1,0:T(8,128)S(1)} %get-tuple-element.22), channel_id=1, source_target_pairs={{64,0},{65,1},{66,2},{67,3},{68,4},{69,5},{70,6},{71,7},{72,8},{73... | collective-permute-start | bytes 1572872 | tf_op jit(solution)/shard_map/ppermute | solution.py:334
  70.6 1.3 %collective-permute-start.14 = (f32[2,4,128,128]{3,2,1,0:T(8,128)S(1)}, f32[2,4,128,128]{3,2,1,0:T(8,128)S(1)}, u32[]{:S(2)}, u32[]{:S(2)}) collective-permute-start(f32[2,4,128,128]{3,2,1,0:T(8,128)S(1)} %get-tuple-element.22), channel_id=1, source_target_pairs={{64,63},{65,0},{66,1},{67,2},{68,3},{69,4},{70,5},{71,6},{72,7},{7... | collective-permute-start | bytes 1572872 | tf_op jit(solution)/shard_map/ppermute | solution.py:334
  72.0 0.7 collective-permute-start.15
  72.7 2.7 %collective-permute-done.13.refs_2_.token = f32[2,4,128,128]{3,2,1,0:T(8,128)S(1)} collective-permute-done((f32[2,4,128,128]{3,2,1,0:T(8,128)S(1)}, f32[2,4,128,128]{3,2,1,0:T(8,128)S(1)}, u32[]{:S(2)}, u32[]{:S(2)}) %collective-permute-start.13) | collective-permute-done | bytes 524320 | tf_op jit(solution)/shard_map/ppermute | solution.py:334
  75.4 1.3 %collective-permute-start.19 = (f32[2,4,128,128]{3,2,1,0:T(8,128)S(1)}, f32[2,4,128,128]{3,2,1,0:T(8,128)S(1)}, u32[]{:S(2)}, u32[]{:S(2)}) collective-permute-start(f32[2,4,128,128]{3,2,1,0:T(8,128)S(1)} %shard_map.53), channel_id=1, source_target_pairs={{192,64},{193,65},{194,66},{195,67},{196,68},{197,69},{198,70},{19... | collective-permute-start | bytes 1572872 | tf_op jit(solution)/shard_map/ppermute | solution.py:334
  76.7 0.0 collective-permute-done.12.refs_1_
  76.7 1.4 %collective-permute-done.14.refs_3_ = f32[2,4,128,128]{3,2,1,0:T(8,128)S(1)} collective-permute-done((f32[2,4,128,128]{3,2,1,0:T(8,128)S(1)}, f32[2,4,128,128]{3,2,1,0:T(8,128)S(1)}, u32[]{:S(2)}, u32[]{:S(2)}) %collective-permute-start.14) | collective-permute-done | bytes 524320 | tf_op jit(solution)/shard_map/ppermute | solution.py:334
  78.1 0.0 collective-permute-done.15.refs_4_
  78.1 1.3 %collective-permute-start.16 = (f32[2,4,128,128]{3,2,1,0:T(8,128)S(1)}, f32[2,4,128,128]{3,2,1,0:T(8,128)S(1)}, u32[]{:S(2)}, u32[]{:S(2)}) collective-permute-start(f32[2,4,128,128]{3,2,1,0:T(8,128)S(1)} %get-tuple-element.23), channel_id=1, source_target_pairs={{0,64},{1,65},{2,66},{3,67},{4,68},{5,69},{6,70},{7,71},{8,72},{9,... | collective-permute-start | bytes 1572872 | tf_op jit(solution)/shard_map/ppermute | solution.py:334
  79.4 1.3 %collective-permute-start.17 = (f32[2,4,128,128]{3,2,1,0:T(8,128)S(1)}, f32[2,4,128,128]{3,2,1,0:T(8,128)S(1)}, u32[]{:S(2)}, u32[]{:S(2)}) collective-permute-start(f32[2,4,128,128]{3,2,1,0:T(8,128)S(1)} %get-tuple-element.23), channel_id=1, source_target_pairs={{0,65},{1,66},{2,67},{3,68},{4,69},{5,70},{6,71},{7,72},{8,73},{9,... | collective-permute-start | bytes 1572872 | tf_op jit(solution)/shard_map/ppermute | solution.py:334
  80.7 1.3 %collective-permute-start.18 = (f32[2,4,128,128]{3,2,1,0:T(8,128)S(1)}, f32[2,4,128,128]{3,2,1,0:T(8,128)S(1)}, u32[]{:S(2)}, u32[]{:S(2)}) collective-permute-start(f32[2,4,128,128]{3,2,1,0:T(8,128)S(1)} %get-tuple-element.23), channel_id=1, source_target_pairs={{0,127},{1,64},{2,65},{3,66},{4,67},{5,68},{6,69},{7,70},{8,71},{9... | collective-permute-start | bytes 1572872 | tf_op jit(solution)/shard_map/ppermute | solution.py:334
  82.0 9.0 %collective-permute-done.19.refs_4_ = f32[2,4,128,128]{3,2,1,0:T(8,128)S(1)} collective-permute-done((f32[2,4,128,128]{3,2,1,0:T(8,128)S(1)}, f32[2,4,128,128]{3,2,1,0:T(8,128)S(1)}, u32[]{:S(2)}, u32[]{:S(2)}) %collective-permute-start.19) | collective-permute-done | bytes 524320 | tf_op jit(solution)/shard_map/ppermute | solution.py:334
  91.0 0.0 collective-permute-done.16.refs_1_
  91.0 8.1 %collective-permute-done.17.refs_2_ = f32[2,4,128,128]{3,2,1,0:T(8,128)S(1)} collective-permute-done((f32[2,4,128,128]{3,2,1,0:T(8,128)S(1)}, f32[2,4,128,128]{3,2,1,0:T(8,128)S(1)}, u32[]{:S(2)}, u32[]{:S(2)}) %collective-permute-start.17) | collective-permute-done | bytes 524320 | tf_op jit(solution)/shard_map/ppermute | solution.py:334
  99.1 0.0 collective-permute-done.18.refs_3_
  99.1 1.2 %shard_map.55 = f32[1,4,128,128]{3,2,1,0:T(8,128)S(1)} custom-call(s32[1]{0:T(128)} %bitcast.refs_0_, f32[2,4,128,128]{3,2,1,0:T(8,128)S(1)} %collective-permute-done.16.refs_1_, f32[2,4,128,128]{3,2,1,0:T(8,128)S(1)} %collective-permute-done.17.refs_2_, f32[2,4,128,128]{3,2,1,0:T(8,128)S(1)} %collective-permute-done.18.refs_3_, ...), custom_call_target="tpu_custom_call" | custom-call | flops 10000000000 | bytes 1048576 | tf_op jit(solution)/shard_map/pallas_call | solution.py:267
  100.3 1.3 %collective-permute-start.21 = (f32[1,4,128,128]{3,2,1,0:T(8,128)S(1)}, f32[1,4,128,128]{3,2,1,0:T(8,128)S(1)}, u32[]{:S(2)}, u32[]{:S(2)}) collective-permute-start(f32[1,4,128,128]{3,2,1,0:T(8,128)S(1)} %shard_map.55), channel_id=1, source_target_pairs={{0,128},{1,129},{2,130},{3,131},{4,132},{5,133},{6,134},{7,135},{8... | collective-permute-start | bytes 786440 | tf_op jit(solution)/shard_map/ppermute | solution.py:334
  101.6 1.2 %shard_map.54 = f32[1,4,128,128]{3,2,1,0:T(8,128)S(1)} custom-call(s32[1]{0:T(128)} %bitcast.refs_0_, f32[2,4,128,128]{3,2,1,0:T(8,128)S(1)} %collective-permute-done.16.refs_1_, f32[2,4,128,128]{3,2,1,0:T(8,128)S(1)} %collective-permute-done.17.refs_2_, f32[2,4,128,128]{3,2,1,0:T(8,128)S(1)} %collective-permute-done.18.refs_3_, ...), custom_call_target="tpu_custom_call" | custom-call | flops 10000000000 | bytes 1048576 | tf_op jit(solution)/shard_map/pallas_call | solution.py:267
  102.8 1.3 %collective-permute-start.20 = (f32[1,4,128,128]{3,2,1,0:T(8,128)S(1)}, f32[1,4,128,128]{3,2,1,0:T(8,128)S(1)}, u32[]{:S(2)}, u32[]{:S(2)}) collective-permute-start(f32[1,4,128,128]{3,2,1,0:T(8,128)S(1)} %shard_map.54), channel_id=1, source_target_pairs={{0,128},{1,129},{2,130},{3,131},{4,132},{5,133},{6,134},{7,135},{8... | collective-permute-start | bytes 786440 | tf_op jit(solution)/shard_map/ppermute | solution.py:334
  104.2 1.2 %collective-permute-done.21.refs_4_ = f32[1,4,128,128]{3,2,1,0:T(8,128)S(1)} collective-permute-done((f32[1,4,128,128]{3,2,1,0:T(8,128)S(1)}, f32[1,4,128,128]{3,2,1,0:T(8,128)S(1)}, u32[]{:S(2)}, u32[]{:S(2)}) %collective-permute-start.21) | collective-permute-done | bytes 262176 | tf_op jit(solution)/shard_map/ppermute | solution.py:334
  105.4 2.8 %collective-permute-done.20.refs_3_ = f32[1,4,128,128]{3,2,1,0:T(8,128)S(1)} collective-permute-done((f32[1,4,128,128]{3,2,1,0:T(8,128)S(1)}, f32[1,4,128,128]{3,2,1,0:T(8,128)S(1)}, u32[]{:S(2)}, u32[]{:S(2)}) %collective-permute-start.20) | collective-permute-done | bytes 262176 | tf_op jit(solution)/shard_map/ppermute | solution.py:334
  108.2 0.8 shard_map.56
  (22 shorter events, 0.3 us)
Async XLA Ops:
  1.1 20.7 %collective-permute-start.4 = (f32[2,4,128,128]{3,2,1,0:T(8,128)S(1)}, f32[2,4,128,128]{3,2,1,0:T(8,128)}, u32[]{:S(2)}, u32[]{:S(2)}) collective-permute-start(f32[2,4,128,128]{3,2,1,0:T(8,128)S(1)} %shard_map.39.refs_5_), channel_id=1, source_target_pairs={{0,1},{1,2},{2,3},{3,4},{4,5},{5,6},{6,7},{7,8},{8,9},{9,10},{10,1... | collective-permute-start | bytes 1572872 | tf_op jit(solution)/shard_map/ppermute | solution.py:334
  12.6 0.8 copy-start.2
  13.4 9.0 %collective-permute-start.2 = (f32[2,4,128,128]{3,2,1,0:T(8,128)}, f32[2,4,128,128]{3,2,1,0:T(8,128)S(1)}, u32[]{:S(2)}, u32[]{:S(2)}) collective-permute-start(f32[2,4,128,128]{3,2,1,0:T(8,128)} %bitcast.1.refs_2_), channel_id=1, source_target_pairs={{0,64},{1,65},{2,66},{3,67},{4,68},{5,69},{6,70},{7,71},{8,72},{9,... | collective-permute-start | bytes 1572872 | tf_op jit(solution)/shard_map/ppermute | solution.py:334
  13.4 9.7 %collective-permute-start.3 = (f32[2,4,128,128]{3,2,1,0:T(8,128)}, f32[2,4,128,128]{3,2,1,0:T(8,128)S(1)}, u32[]{:S(2)}, u32[]{:S(2)}) collective-permute-start(f32[2,4,128,128]{3,2,1,0:T(8,128)} %bitcast.1.refs_2_), channel_id=1, source_target_pairs={{0,64},{1,65},{2,66},{3,67},{4,68},{5,69},{6,70},{7,71},{8,72},{9,... | collective-permute-start | bytes 1572872 | tf_op jit(solution)/shard_map/ppermute | solution.py:334
  13.9 20.1 %collective-permute-start = (f32[2,4,128,128]{3,2,1,0:T(8,128)}, f32[2,4,128,128]{3,2,1,0:T(8,128)S(1)}, u32[]{:S(2)}, u32[]{:S(2)}) collective-permute-start(f32[2,4,128,128]{3,2,1,0:T(8,128)} %bitcast.1.refs_2_), channel_id=1, source_target_pairs={{0,1},{1,2},{2,3},{3,4},{4,5},{5,6},{6,7},{7,8},{8,9},{9,10},{10,1... | collective-permute-start | bytes 1572872 | tf_op jit(solution)/shard_map/ppermute | solution.py:334
  13.9 20.1 %collective-permute-start.1 = (f32[2,4,128,128]{3,2,1,0:T(8,128)}, f32[2,4,128,128]{3,2,1,0:T(8,128)S(1)}, u32[]{:S(2)}, u32[]{:S(2)}) collective-permute-start(f32[2,4,128,128]{3,2,1,0:T(8,128)} %bitcast.1.refs_2_), channel_id=1, source_target_pairs={{0,63},{1,0},{2,1},{3,2},{4,3},{5,4},{6,5},{7,6},{8,7},{9,8},{10,9... | collective-permute-start | bytes 1572872 | tf_op jit(solution)/shard_map/ppermute | solution.py:334
  21.7 13.9 %collective-permute-start.5 = (f32[2,4,128,128]{3,2,1,0:T(8,128)}, f32[2,4,128,128]{3,2,1,0:T(8,128)S(1)}, u32[]{:S(2)}, u32[]{:S(2)}) collective-permute-start(f32[2,4,128,128]{3,2,1,0:T(8,128)} %collective-permute-done.4.refs_2_.refs_4_), channel_id=1, source_target_pairs={{128,132},{132,136},{136,140},{140,144},{144,148},{148,152},{152,1... | collective-permute-start | bytes 1572872 | tf_op jit(solution)/shard_map/ppermute | solution.py:334
  22.4 17.7 %collective-permute-start.6 = (f32[2,4,128,128]{3,2,1,0:T(8,128)}, f32[2,4,128,128]{3,2,1,0:T(8,128)}, u32[]{:S(2)}, u32[]{:S(2)}) collective-permute-start(f32[2,4,128,128]{3,2,1,0:T(8,128)} %collective-permute-done.4.refs_2_.refs_4_), channel_id=1, source_target_pairs={{0,64},{1,65},{2,66},{3,67},{4,68},{5,69},{6,70},{7,71},{8,72},{9,... | collective-permute-start | bytes 1572872 | tf_op jit(solution)/shard_map/ppermute | solution.py:334
  23.9 22.5 %collective-permute-start.10 = (f32[2,4,128,128]{3,2,1,0:T(8,128)}, f32[2,4,128,128]{3,2,1,0:T(8,128)S(1)}, u32[]{:S(2)}, u32[]{:S(2)}) collective-permute-start(f32[2,4,128,128]{3,2,1,0:T(8,128)} %shard_map.38.refs_2_), channel_id=1, source_target_pairs={{128,132},{131,191},{132,136},{135,131},{136,140},{139,135},{140,1... | collective-permute-start | bytes 1572872 | tf_op jit(solution)/shard_map/ppermute | solution.py:334
  34.0 0.8 copy-start.5
  34.8 0.8 copy-start.7
  35.6 0.8 copy-start.9
  36.4 1.0 copy-start.10
  37.5 2.7 %copy-start.6 = (f32[2,4,128,128]{3,2,1,0:T(8,128)S(1)}, f32[2,4,128,128]{3,2,1,0:T(8,128)}, u32[]{:S(2)}) copy-start(f32[2,4,128,128]{3,2,1,0:T(8,128)} %copy-done.5) | copy-start | bytes 1572868
  37.5 2.7 %copy-start.8 = (f32[2,4,128,128]{3,2,1,0:T(8,128)S(1)}, f32[2,4,128,128]{3,2,1,0:T(8,128)}, u32[]{:S(2)}) copy-start(f32[2,4,128,128]{3,2,1,0:T(8,128)} %copy-done.7) | copy-start | bytes 1572868
  38.6 1.5 %copy-start = (f32[2,4,128,128]{3,2,1,0:T(8,128)}, f32[2,4,128,128]{3,2,1,0:T(8,128)S(1)}, u32[]{:S(2)}) copy-start(f32[2,4,128,128]{3,2,1,0:T(8,128)S(1)} %shard_map.40.refs_3_.refs_1_.refs_2_) | copy-start | bytes 1572868
  38.6 8.0 %collective-permute-start.11 = (f32[2,4,128,128]{3,2,1,0:T(8,128)S(1)}, f32[2,4,128,128]{3,2,1,0:T(8,128)}, u32[]{:S(2)}, u32[]{:S(2)}) collective-permute-start(f32[2,4,128,128]{3,2,1,0:T(8,128)S(1)} %shard_map.40.refs_3_.refs_1_.refs_2_), channel_id=1, source_target_pairs={{128,192},{129,193},{130,194},{131,195},{132,196},{133,197},{134,1... | collective-permute-start | bytes 1572872 | tf_op jit(solution)/shard_map/ppermute | solution.py:334
  40.1 1.0 copy-start.3
  42.5 14.9 %collective-permute-start.7 = (f32[2,4,128,128]{3,2,1,0:T(8,128)S(1)}, f32[2,4,128,128]{3,2,1,0:T(8,128)S(1)}, u32[]{:S(2)}, u32[]{:S(2)}) collective-permute-start(f32[2,4,128,128]{3,2,1,0:T(8,128)S(1)} %get-tuple-element.20), channel_id=1, source_target_pairs={{0,64},{1,65},{2,66},{3,67},{4,68},{5,69},{6,70},{7,71},{8,72},{9,... | collective-permute-start | bytes 1572872 | tf_op jit(solution)/shard_map/ppermute | solution.py:334
  43.8 21.5 %collective-permute-start.8 = (f32[2,4,128,128]{3,2,1,0:T(8,128)S(1)}, f32[2,4,128,128]{3,2,1,0:T(8,128)S(1)}, u32[]{:S(2)}, u32[]{:S(2)}) collective-permute-start(f32[2,4,128,128]{3,2,1,0:T(8,128)S(1)} %get-tuple-element.20), channel_id=1, source_target_pairs={{0,65},{1,66},{2,67},{3,68},{4,69},{5,70},{6,71},{7,72},{8,73},{9,... | collective-permute-start | bytes 1572872 | tf_op jit(solution)/shard_map/ppermute | solution.py:334
  45.1 20.2 %collective-permute-start.9 = (f32[2,4,128,128]{3,2,1,0:T(8,128)S(1)}, f32[2,4,128,128]{3,2,1,0:T(8,128)S(1)}, u32[]{:S(2)}, u32[]{:S(2)}) collective-permute-start(f32[2,4,128,128]{3,2,1,0:T(8,128)S(1)} %get-tuple-element.20), channel_id=1, source_target_pairs={{0,127},{1,64},{2,65},{3,66},{4,67},{5,68},{6,69},{7,70},{8,71},{9... | collective-permute-start | bytes 1572872 | tf_op jit(solution)/shard_map/ppermute | solution.py:334
  46.6 1.4 %copy-start.1 = (f32[2,4,128,128]{3,2,1,0:T(8,128)S(1)}, f32[2,4,128,128]{3,2,1,0:T(8,128)}, u32[]{:S(2)}) copy-start(f32[2,4,128,128]{3,2,1,0:T(8,128)} %copy-done) | copy-start | bytes 1572868
  48.0 1.0 copy-start.4
  68.0 7.4 %collective-permute-start.13 = (f32[2,4,128,128]{3,2,1,0:T(8,128)S(1)}, f32[2,4,128,128]{3,2,1,0:T(8,128)S(1)}, u32[]{:S(2)}, u32[]{:S(2)}) collective-permute-start(f32[2,4,128,128]{3,2,1,0:T(8,128)S(1)} %get-tuple-element.22), channel_id=1, source_target_pairs={{64,1},{65,2},{66,3},{67,4},{68,5},{69,6},{70,7},{71,8},{72,9},{73... | collective-permute-start | bytes 1572872 | tf_op jit(solution)/shard_map/ppermute | solution.py:334
  69.3 7.4 %collective-permute-start.12 = (f32[2,4,128,128]{3,2,1,0:T(8,128)S(1)}, f32[2,4,128,128]{3,2,1,0:T(8,128)S(1)}, u32[]{:S(2)}, u32[]{:S(2)}) collective-permute-start(f32[2,4,128,128]{3,2,1,0:T(8,128)S(1)} %get-tuple-element.22), channel_id=1, source_target_pairs={{64,0},{65,1},{66,2},{67,3},{68,4},{69,5},{70,6},{71,7},{72,8},{73... | collective-permute-start | bytes 1572872 | tf_op jit(solution)/shard_map/ppermute | solution.py:334
  70.6 7.4 %collective-permute-start.14 = (f32[2,4,128,128]{3,2,1,0:T(8,128)S(1)}, f32[2,4,128,128]{3,2,1,0:T(8,128)S(1)}, u32[]{:S(2)}, u32[]{:S(2)}) collective-permute-start(f32[2,4,128,128]{3,2,1,0:T(8,128)S(1)} %get-tuple-element.22), channel_id=1, source_target_pairs={{64,63},{65,0},{66,1},{67,2},{68,3},{69,4},{70,5},{71,6},{72,7},{7... | collective-permute-start | bytes 1572872 | tf_op jit(solution)/shard_map/ppermute | solution.py:334
  72.0 6.1 %collective-permute-start.15 = (f32[2,4,128,128]{3,2,1,0:T(8,128)S(1)}, f32[2,4,128,128]{3,2,1,0:T(8,128)S(1)}, u32[]{:S(2)}, u32[]{:S(2)}) collective-permute-start(f32[2,4,128,128]{3,2,1,0:T(8,128)S(1)} %shard_map.50.refs_4_.array), channel_id=1, source_target_pairs={{128,0},{129,1},{130,2},{131,3},{132,4},{133,5},{134,6},{135,7},{1... | collective-permute-start | bytes 1572872 | tf_op jit(solution)/shard_map/ppermute | solution.py:334
  75.4 15.5 %collective-permute-start.19 = (f32[2,4,128,128]{3,2,1,0:T(8,128)S(1)}, f32[2,4,128,128]{3,2,1,0:T(8,128)S(1)}, u32[]{:S(2)}, u32[]{:S(2)}) collective-permute-start(f32[2,4,128,128]{3,2,1,0:T(8,128)S(1)} %shard_map.53), channel_id=1, source_target_pairs={{192,64},{193,65},{194,66},{195,67},{196,68},{197,69},{198,70},{19... | collective-permute-start | bytes 1572872 | tf_op jit(solution)/shard_map/ppermute | solution.py:334
  78.1 12.9 %collective-permute-start.16 = (f32[2,4,128,128]{3,2,1,0:T(8,128)S(1)}, f32[2,4,128,128]{3,2,1,0:T(8,128)S(1)}, u32[]{:S(2)}, u32[]{:S(2)}) collective-permute-start(f32[2,4,128,128]{3,2,1,0:T(8,128)S(1)} %get-tuple-element.23), channel_id=1, source_target_pairs={{0,64},{1,65},{2,66},{3,67},{4,68},{5,69},{6,70},{7,71},{8,72},{9,... | collective-permute-start | bytes 1572872 | tf_op jit(solution)/shard_map/ppermute | solution.py:334
  79.4 19.7 %collective-permute-start.17 = (f32[2,4,128,128]{3,2,1,0:T(8,128)S(1)}, f32[2,4,128,128]{3,2,1,0:T(8,128)S(1)}, u32[]{:S(2)}, u32[]{:S(2)}) collective-permute-start(f32[2,4,128,128]{3,2,1,0:T(8,128)S(1)} %get-tuple-element.23), channel_id=1, source_target_pairs={{0,65},{1,66},{2,67},{3,68},{4,69},{5,70},{6,71},{7,72},{8,73},{9,... | collective-permute-start | bytes 1572872 | tf_op jit(solution)/shard_map/ppermute | solution.py:334
  80.7 18.4 %collective-permute-start.18 = (f32[2,4,128,128]{3,2,1,0:T(8,128)S(1)}, f32[2,4,128,128]{3,2,1,0:T(8,128)S(1)}, u32[]{:S(2)}, u32[]{:S(2)}) collective-permute-start(f32[2,4,128,128]{3,2,1,0:T(8,128)S(1)} %get-tuple-element.23), channel_id=1, source_target_pairs={{0,127},{1,64},{2,65},{3,66},{4,67},{5,68},{6,69},{7,70},{8,71},{9... | collective-permute-start | bytes 1572872 | tf_op jit(solution)/shard_map/ppermute | solution.py:334
  100.3 5.1 %collective-permute-start.21 = (f32[1,4,128,128]{3,2,1,0:T(8,128)S(1)}, f32[1,4,128,128]{3,2,1,0:T(8,128)S(1)}, u32[]{:S(2)}, u32[]{:S(2)}) collective-permute-start(f32[1,4,128,128]{3,2,1,0:T(8,128)S(1)} %shard_map.55), channel_id=1, source_target_pairs={{0,128},{1,129},{2,130},{3,131},{4,132},{5,133},{6,134},{7,135},{8... | collective-permute-start | bytes 786440 | tf_op jit(solution)/shard_map/ppermute | solution.py:334
  102.8 5.4 %collective-permute-start.20 = (f32[1,4,128,128]{3,2,1,0:T(8,128)S(1)}, f32[1,4,128,128]{3,2,1,0:T(8,128)S(1)}, u32[]{:S(2)}, u32[]{:S(2)}) collective-permute-start(f32[1,4,128,128]{3,2,1,0:T(8,128)S(1)} %shard_map.54), channel_id=1, source_target_pairs={{0,128},{1,129},{2,130},{3,131},{4,132},{5,133},{6,134},{7,135},{8... | collective-permute-start | bytes 786440 | tf_op jit(solution)/shard_map/ppermute | solution.py:334

commit v5 on v4

--- a/solution.py
+++ b/solution.py
@@ -270,7 +270,7 @@
         in_specs=[SMEM] + [VMEM] * len(operands) + [ANY] * len(tokens),
         out_specs=[VMEM] * outputs,
         scratch_shapes=[pltpu.VMEM((2, count, *plane), jnp.float32) for count in layers],
-        compiler_params=pltpu.CompilerParams(vmem_limit_bytes=12 * 2**20),
+        compiler_params=pltpu.CompilerParams(vmem_limit_bytes=10 * 2**20),
         cost_estimate=pl.CostEstimate(
             flops=10**10 if scratch else 10**5, bytes_accessed=2**20, transcendentals=0
         ),
@@ -299,10 +299,11 @@
 def settled(low, high, tokens):
     return pl.pallas_call(
         settle_kernel,
-        out_shape=[jax.ShapeDtypeStruct(low.shape, low.dtype)] * 2,
+        out_shape=[pltpu.VMEM(low.shape, low.dtype)] * 2,
         in_specs=[ANY] * (2 + len(tokens)),
         out_specs=[ANY, ANY],
         input_output_aliases={0: 0, 1: 1},
+        compiler_params=pltpu.CompilerParams(vmem_limit_bytes=2**20),
         cost_estimate=pl.CostEstimate(flops=SETTLE, bytes_accessed=2**20, transcendentals=0),
     )(
         pltpu.with_memory_space_constraint(low, pltpu.VMEM),

time: 110 us -> 103 us (0.936)
  local copies, waits for them, and re-layouts: 6.27 us -> 0 us
  Pallas kernels: 20.2 us -> 18.8 us
  waiting for transfers between devices: 42.6 us -> 44 us
    unnamed x22 -> x0, local copies, waits for them, and re-layouts: 6.27 us -> none
    ppermute x22, waiting for transfers between devices: 42.6 us -> 44 us  [moved(): return lax.ppermute(array, AXES, pairs)]
    pallas_call x16, Pallas kernels: 19.2 us -> 17.7 us  [run(): pl.pallas_call(kernel, out_shape=out_shape, in_specs=[SMEM] + [VMEM] * le...]
  transfers between devices with their start and end apart: 22 -> 22, of which waited for: 8 -> 9; matrix products, arithmetic and copies ran while one was open for 0% -> 0% of each run, Pallas kernels for 13% -> 13%
where the time goes in v5:
time: 103 us
  waiting for transfers between devices  44 us (43%)
  starting transfers between devices  39.6 us (38%)
  Pallas kernels  18.8 us (18%)
    ppermute x22, waiting for transfers between devices, moved(): return lax.ppermute(array, AXES, pairs)  44 us
    ppermute x22, starting transfers between devices, moved(): return lax.ppermute(array, AXES, pairs)  39.6 us
    pallas_call x16, Pallas kernels, run(): pl.pallas_call(kernel, out_shape=out_shape, in_specs=[SMEM] + [VMEM] * le...  17.7 us
  transfers between devices with their start and end apart: 22, of which 9 were waited for; matrix products, arithmetic and copies ran while one was open for 0% of the time, Pallas kernels for 13%

profile of v5, /device:TPU:1, one launch (start us, length us, event | category | flops | bytes accessed | tf_op | source)
XLA Modules:
  0.0 102.7 jit_solution(9744080167624798093)
XLA Ops:
  0.0 1.0 %shard_map.39.refs_5_ = f32[2,4,128,128]{3,2,1,0:T(8,128)S(1)} custom-call(f32[4,128,128]{2,1,0:T(8,128)} %feed.1, f32[4,128,128]{2,1,0:T(8,128)} %kill.1), custom_call_target="tpu_custom_call" | custom-call | flops 100000 | bytes 1048576 | tf_op jit(solution)/shard_map/pallas_call | solution.py:227
  1.1 11.6 %collective-permute-start.4 = (f32[2,4,128,128]{3,2,1,0:T(8,128)S(1)}, f32[2,4,128,128]{3,2,1,0:T(8,128)S(1)}, u32[]{:S(2)}, u32[]{:S(2)}) collective-permute-start(f32[2,4,128,128]{3,2,1,0:T(8,128)S(1)} %shard_map.39.refs_5_), channel_id=1, source_target_pairs={{0,1},{1,2},{2,3},{3,4},{4,5},{5,6},{6,7},{7,8},{8,9},{9,10},{10,1... | collective-permute-start | bytes 1572872 | tf_op jit(solution)/shard_map/ppermute | solution.py:335
  12.6 0.0 collective-permute-start.2
  12.6 0.5 collective-permute-start.3
  13.1 0.0 collective-permute-start
  13.1 7.8 %collective-permute-start.1 = (f32[2,4,128,128]{3,2,1,0:T(8,128)}, f32[2,4,128,128]{3,2,1,0:T(8,128)}, u32[]{:S(2)}, u32[]{:S(2)}) collective-permute-start(f32[2,4,128,128]{3,2,1,0:T(8,128)} %bitcast.1.refs_2_), channel_id=1, source_target_pairs={{0,63},{1,0},{2,1},{3,2},{4,3},{5,4},{6,5},{7,6},{8,7},{9,8},{10,9... | collective-permute-start | bytes 1572872 | tf_op jit(solution)/shard_map/ppermute | solution.py:335
  20.9 0.0 collective-permute-done.4.refs_2_.refs_4_
  20.9 1.5 %collective-permute-start.5 = (f32[2,4,128,128]{3,2,1,0:T(8,128)S(1)}, f32[2,4,128,128]{3,2,1,0:T(8,128)}, u32[]{:S(2)}, u32[]{:S(2)}) collective-permute-start(f32[2,4,128,128]{3,2,1,0:T(8,128)S(1)} %collective-permute-done.4.refs_2_.refs_4_), channel_id=1, source_target_pairs={{128,132},{132,136},{136,140},{140,144},{144,148},{148,152},{152,1... | collective-permute-start | bytes 1572872 | tf_op jit(solution)/shard_map/ppermute | solution.py:335
  22.4 0.0 collective-permute-done.2.refs_1_.refs_2_
  22.4 0.6 collective-permute-start.6
  23.0 0.0 collective-permute-done.3.refs_2_
  23.0 0.7 collective-permute-start.10
  23.7 9.5 %collective-permute-done.refs_0_ = f32[2,4,128,128]{3,2,1,0:T(8,128)S(1)} collective-permute-done((f32[2,4,128,128]{3,2,1,0:T(8,128)}, f32[2,4,128,128]{3,2,1,0:T(8,128)S(1)}, u32[]{:S(2)}, u32[]{:S(2)}) %collective-permute-start) | collective-permute-done | bytes 524320 | tf_op jit(solution)/shard_map/ppermute | solution.py:335
  33.2 0.0 collective-permute-done.1.refs_1_
  33.2 0.0 collective-permute-done.5.refs_1_
  33.2 1.1 %shard_map.40.refs_3_.refs_1_.refs_2_ = f32[2,4,128,128]{3,2,1,0:T(8,128)S(1)} custom-call(s32[1]{0:T(128)} %bitcast.3.refs_0_, f32[2,4,128,128]{3,2,1,0:T(8,128)} %collective-permute-done.5.refs_1_, f32[2,4,128,128]{3,2,1,0:T(8,128)S(1)} %collective-permute-done.4.refs_2_.refs_4_), custom_call_target="tpu_custom_call" | custom-call | flops 100000 | bytes 1048576 | tf_op jit(solution)/shard_map/pallas_call | solution.py:267
  34.3 0.7 collective-permute-start.11
  35.0 0.0 collective-permute-done.6.refs_6_.refs_1_
  35.0 1.2 %shard_map.42 = (f32[2,4,128,128]{3,2,1,0:T(8,128)S(1)}, f32[2,4,128,128]{3,2,1,0:T(8,128)S(1)}) custom-call(s32[1]{0:T(128)} %bitcast.refs_0_, f32[2,4,128,128]{3,2,1,0:T(8,128)S(1)} %get-tuple-element.17.refs_1_, f32[2,4,128,128]{3,2,1,0:T(8,128)} %bitcast.1.refs_2_, f32[2,4,128,128]{3,2,1,0:T(8,128)} %get-tuple-element.18.refs_3_.refs_1_, ...), custom_call_target="tpu_custom_call" | custom-call | flops 10000000000 | bytes 1048576 | tf_op jit(solution)/shard_map/pallas_call | solution.py:267
  36.2 1.3 %collective-permute-start.7 = (f32[2,4,128,128]{3,2,1,0:T(8,128)S(1)}, f32[2,4,128,128]{3,2,1,0:T(8,128)S(1)}, u32[]{:S(2)}, u32[]{:S(2)}) collective-permute-start(f32[2,4,128,128]{3,2,1,0:T(8,128)S(1)} %get-tuple-element.20), channel_id=1, source_target_pairs={{0,64},{1,65},{2,66},{3,67},{4,68},{5,69},{6,70},{7,71},{8,72},{9,... | collective-permute-start | bytes 1572872 | tf_op jit(solution)/shard_map/ppermute | solution.py:335
  37.5 1.3 %collective-permute-start.8 = (f32[2,4,128,128]{3,2,1,0:T(8,128)S(1)}, f32[2,4,128,128]{3,2,1,0:T(8,128)S(1)}, u32[]{:S(2)}, u32[]{:S(2)}) collective-permute-start(f32[2,4,128,128]{3,2,1,0:T(8,128)S(1)} %get-tuple-element.20), channel_id=1, source_target_pairs={{0,65},{1,66},{2,67},{3,68},{4,69},{5,70},{6,71},{7,72},{8,73},{9,... | collective-permute-start | bytes 1572872 | tf_op jit(solution)/shard_map/ppermute | solution.py:335
  38.8 1.3 %collective-permute-start.9 = (f32[2,4,128,128]{3,2,1,0:T(8,128)S(1)}, f32[2,4,128,128]{3,2,1,0:T(8,128)S(1)}, u32[]{:S(2)}, u32[]{:S(2)}) collective-permute-start(f32[2,4,128,128]{3,2,1,0:T(8,128)S(1)} %get-tuple-element.20), channel_id=1, source_target_pairs={{0,127},{1,64},{2,65},{3,66},{4,67},{5,68},{6,69},{7,70},{8,71},{9... | collective-permute-start | bytes 1572872 | tf_op jit(solution)/shard_map/ppermute | solution.py:335
  40.1 0.0 collective-permute-done.10.refs_1_
  40.3 1.1 %shard_map.46.refs_3_ = f32[2,4,128,128]{3,2,1,0:T(8,128)S(1)} custom-call(s32[1]{0:T(128)} %bitcast.4.refs_0_, f32[2,4,128,128]{3,2,1,0:T(8,128)} %get-tuple-element.18.refs_3_.refs_1_, f32[2,4,128,128]{3,2,1,0:T(8,128)S(1)} %shard_map.45.refs_2_), custom_call_target="tpu_custom_call" | custom-call | flops 100000 | bytes 1048576 | tf_op jit(solution)/shard_map/pallas_call | solution.py:267
  41.4 0.0 collective-permute-done.11.refs_2_
  41.6 8.2 %shard_map.50.refs_4_.array = f32[2,4,128,128]{3,2,1,0:T(8,128)S(1)} custom-call(s32[1]{0:T(128)} %bitcast.refs_0_, f32[2,4,128,128]{3,2,1,0:T(8,128)S(1)} %shard_map.44.refs_1_, f32[2,4,128,128]{3,2,1,0:T(8,128)} %bitcast.1.refs_2_, f32[2,4,128,128]{3,2,1,0:T(8,128)S(1)} %shard_map.46.refs_3_, f32[2,4,128,128]{3,2,1,0:T(8,128)S(1)} %shard_map.48.refs_4_, ...), custom_call_target="tpu_custom_call" | custom-call | flops 10000000000 | bytes 1048576 | tf_op jit(solution)/shard_map/pallas_call | solution.py:267
  49.8 0.0 collective-permute-done.7.refs_1_
  49.9 9.3 %collective-permute-done.8.refs_2_ = f32[2,4,128,128]{3,2,1,0:T(8,128)S(1)} collective-permute-done((f32[2,4,128,128]{3,2,1,0:T(8,128)S(1)}, f32[2,4,128,128]{3,2,1,0:T(8,128)S(1)}, u32[]{:S(2)}, u32[]{:S(2)}) %collective-permute-start.8) | collective-permute-done | bytes 524320 | tf_op jit(solution)/shard_map/ppermute | solution.py:335
  59.1 0.0 collective-permute-done.9.refs_3_
  59.1 2.5 %shard_map.51 = (f32[2,4,128,128]{3,2,1,0:T(8,128)S(1)}, f32[2,4,128,128]{3,2,1,0:T(8,128)S(1)}) custom-call(s32[1]{0:T(128)} %bitcast.refs_0_, f32[2,4,128,128]{3,2,1,0:T(8,128)S(1)} %collective-permute-done.7.refs_1_, f32[2,4,128,128]{3,2,1,0:T(8,128)S(1)} %collective-permute-done.8.refs_2_, f32[2,4,128,128]{3,2,1,0:T(8,128)S(1)} %collective-permute-done.9.refs_3_, ...), custom_call_target="tpu_custom_call" | custom-call | flops 10000000000 | bytes 1048576 | tf_op jit(solution)/shard_map/pallas_call | solution.py:267
  61.7 1.3 %collective-permute-start.13 = (f32[2,4,128,128]{3,2,1,0:T(8,128)S(1)}, f32[2,4,128,128]{3,2,1,0:T(8,128)S(1)}, u32[]{:S(2)}, u32[]{:S(2)}) collective-permute-start(f32[2,4,128,128]{3,2,1,0:T(8,128)S(1)} %get-tuple-element.22), channel_id=1, source_target_pairs={{64,1},{65,2},{66,3},{67,4},{68,5},{69,6},{70,7},{71,8},{72,9},{73... | collective-permute-start | bytes 1572872 | tf_op jit(solution)/shard_map/ppermute | solution.py:335
  63.0 1.3 %collective-permute-start.12 = (f32[2,4,128,128]{3,2,1,0:T(8,128)S(1)}, f32[2,4,128,128]{3,2,1,0:T(8,128)S(1)}, u32[]{:S(2)}, u32[]{:S(2)}) collective-permute-start(f32[2,4,128,128]{3,2,1,0:T(8,128)S(1)} %get-tuple-element.22), channel_id=1, source_target_pairs={{64,0},{65,1},{66,2},{67,3},{68,4},{69,5},{70,6},{71,7},{72,8},{73... | collective-permute-start | bytes 1572872 | tf_op jit(solution)/shard_map/ppermute | solution.py:335
  64.3 1.3 %collective-permute-start.14 = (f32[2,4,128,128]{3,2,1,0:T(8,128)S(1)}, f32[2,4,128,128]{3,2,1,0:T(8,128)S(1)}, u32[]{:S(2)}, u32[]{:S(2)}) collective-permute-start(f32[2,4,128,128]{3,2,1,0:T(8,128)S(1)} %get-tuple-element.22), channel_id=1, source_target_pairs={{64,63},{65,0},{66,1},{67,2},{68,3},{69,4},{70,5},{71,6},{72,7},{7... | collective-permute-start | bytes 1572872 | tf_op jit(solution)/shard_map/ppermute | solution.py:335
  65.7 0.7 collective-permute-start.15
  66.4 2.7 %collective-permute-done.13.refs_2_.token = f32[2,4,128,128]{3,2,1,0:T(8,128)S(1)} collective-permute-done((f32[2,4,128,128]{3,2,1,0:T(8,128)S(1)}, f32[2,4,128,128]{3,2,1,0:T(8,128)S(1)}, u32[]{:S(2)}, u32[]{:S(2)}) %collective-permute-start.13) | collective-permute-done | bytes 524320 | tf_op jit(solution)/shard_map/ppermute | solution.py:335
  69.1 1.3 %collective-permute-start.19 = (f32[2,4,128,128]{3,2,1,0:T(8,128)S(1)}, f32[2,4,128,128]{3,2,1,0:T(8,128)S(1)}, u32[]{:S(2)}, u32[]{:S(2)}) collective-permute-start(f32[2,4,128,128]{3,2,1,0:T(8,128)S(1)} %shard_map.53), channel_id=1, source_target_pairs={{192,64},{193,65},{194,66},{195,67},{196,68},{197,69},{198,70},{19... | collective-permute-start | bytes 1572872 | tf_op jit(solution)/shard_map/ppermute | solution.py:335
  70.4 0.0 collective-permute-done.12.refs_1_
  70.4 1.4 %collective-permute-done.14.refs_3_ = f32[2,4,128,128]{3,2,1,0:T(8,128)S(1)} collective-permute-done((f32[2,4,128,128]{3,2,1,0:T(8,128)S(1)}, f32[2,4,128,128]{3,2,1,0:T(8,128)S(1)}, u32[]{:S(2)}, u32[]{:S(2)}) %collective-permute-start.14) | collective-permute-done | bytes 524320 | tf_op jit(solution)/shard_map/ppermute | solution.py:335
  71.8 0.0 collective-permute-done.15.refs_4_
  71.8 1.3 %collective-permute-start.16 = (f32[2,4,128,128]{3,2,1,0:T(8,128)S(1)}, f32[2,4,128,128]{3,2,1,0:T(8,128)S(1)}, u32[]{:S(2)}, u32[]{:S(2)}) collective-permute-start(f32[2,4,128,128]{3,2,1,0:T(8,128)S(1)} %get-tuple-element.23), channel_id=1, source_target_pairs={{0,64},{1,65},{2,66},{3,67},{4,68},{5,69},{6,70},{7,71},{8,72},{9,... | collective-permute-start | bytes 1572872 | tf_op jit(solution)/shard_map/ppermute | solution.py:335
  73.1 1.3 %collective-permute-start.17 = (f32[2,4,128,128]{3,2,1,0:T(8,128)S(1)}, f32[2,4,128,128]{3,2,1,0:T(8,128)S(1)}, u32[]{:S(2)}, u32[]{:S(2)}) collective-permute-start(f32[2,4,128,128]{3,2,1,0:T(8,128)S(1)} %get-tuple-element.23), channel_id=1, source_target_pairs={{0,65},{1,66},{2,67},{3,68},{4,69},{5,70},{6,71},{7,72},{8,73},{9,... | collective-permute-start | bytes 1572872 | tf_op jit(solution)/shard_map/ppermute | solution.py:335
  74.4 1.3 %collective-permute-start.18 = (f32[2,4,128,128]{3,2,1,0:T(8,128)S(1)}, f32[2,4,128,128]{3,2,1,0:T(8,128)S(1)}, u32[]{:S(2)}, u32[]{:S(2)}) collective-permute-start(f32[2,4,128,128]{3,2,1,0:T(8,128)S(1)} %get-tuple-element.23), channel_id=1, source_target_pairs={{0,127},{1,64},{2,65},{3,66},{4,67},{5,68},{6,69},{7,70},{8,71},{9... | collective-permute-start | bytes 1572872 | tf_op jit(solution)/shard_map/ppermute | solution.py:335
  75.7 3.4 %collective-permute-done.19.refs_4_ = f32[2,4,128,128]{3,2,1,0:T(8,128)S(1)} collective-permute-done((f32[2,4,128,128]{3,2,1,0:T(8,128)S(1)}, f32[2,4,128,128]{3,2,1,0:T(8,128)S(1)}, u32[]{:S(2)}, u32[]{:S(2)}) %collective-permute-start.19) | collective-permute-done | bytes 524320 | tf_op jit(solution)/shard_map/ppermute | solution.py:335
  79.0 1.4 %collective-permute-done.16.refs_1_ = f32[2,4,128,128]{3,2,1,0:T(8,128)S(1)} collective-permute-done((f32[2,4,128,128]{3,2,1,0:T(8,128)S(1)}, f32[2,4,128,128]{3,2,1,0:T(8,128)S(1)}, u32[]{:S(2)}, u32[]{:S(2)}) %collective-permute-start.16) | collective-permute-done | bytes 524320 | tf_op jit(solution)/shard_map/ppermute | solution.py:335
  80.4 12.4 %collective-permute-done.17.refs_2_ = f32[2,4,128,128]{3,2,1,0:T(8,128)S(1)} collective-permute-done((f32[2,4,128,128]{3,2,1,0:T(8,128)S(1)}, f32[2,4,128,128]{3,2,1,0:T(8,128)S(1)}, u32[]{:S(2)}, u32[]{:S(2)}) %collective-permute-start.17) | collective-permute-done | bytes 524320 | tf_op jit(solution)/shard_map/ppermute | solution.py:335
  92.8 0.0 collective-permute-done.18.refs_3_
  92.8 1.2 %shard_map.55 = f32[1,4,128,128]{3,2,1,0:T(8,128)S(1)} custom-call(s32[1]{0:T(128)} %bitcast.refs_0_, f32[2,4,128,128]{3,2,1,0:T(8,128)S(1)} %collective-permute-done.16.refs_1_, f32[2,4,128,128]{3,2,1,0:T(8,128)S(1)} %collective-permute-done.17.refs_2_, f32[2,4,128,128]{3,2,1,0:T(8,128)S(1)} %collective-permute-done.18.refs_3_, ...), custom_call_target="tpu_custom_call" | custom-call | flops 10000000000 | bytes 1048576 | tf_op jit(solution)/shard_map/pallas_call | solution.py:267
  94.0 1.3 %collective-permute-start.21 = (f32[1,4,128,128]{3,2,1,0:T(8,128)S(1)}, f32[1,4,128,128]{3,2,1,0:T(8,128)S(1)}, u32[]{:S(2)}, u32[]{:S(2)}) collective-permute-start(f32[1,4,128,128]{3,2,1,0:T(8,128)S(1)} %shard_map.55), channel_id=1, source_target_pairs={{0,128},{1,129},{2,130},{3,131},{4,132},{5,133},{6,134},{7,135},{8... | collective-permute-start | bytes 786440 | tf_op jit(solution)/shard_map/ppermute | solution.py:335
  95.3 1.2 %shard_map.54 = f32[1,4,128,128]{3,2,1,0:T(8,128)S(1)} custom-call(s32[1]{0:T(128)} %bitcast.refs_0_, f32[2,4,128,128]{3,2,1,0:T(8,128)S(1)} %collective-permute-done.16.refs_1_, f32[2,4,128,128]{3,2,1,0:T(8,128)S(1)} %collective-permute-done.17.refs_2_, f32[2,4,128,128]{3,2,1,0:T(8,128)S(1)} %collective-permute-done.18.refs_3_, ...), custom_call_target="tpu_custom_call" | custom-call | flops 10000000000 | bytes 1048576 | tf_op jit(solution)/shard_map/pallas_call | solution.py:267
  96.5 1.3 %collective-permute-start.20 = (f32[1,4,128,128]{3,2,1,0:T(8,128)S(1)}, f32[1,4,128,128]{3,2,1,0:T(8,128)S(1)}, u32[]{:S(2)}, u32[]{:S(2)}) collective-permute-start(f32[1,4,128,128]{3,2,1,0:T(8,128)S(1)} %shard_map.54), channel_id=1, source_target_pairs={{0,128},{1,129},{2,130},{3,131},{4,132},{5,133},{6,134},{7,135},{8... | collective-permute-start | bytes 786440 | tf_op jit(solution)/shard_map/ppermute | solution.py:335
  97.8 1.2 %collective-permute-done.21.refs_4_ = f32[1,4,128,128]{3,2,1,0:T(8,128)S(1)} collective-permute-done((f32[1,4,128,128]{3,2,1,0:T(8,128)S(1)}, f32[1,4,128,128]{3,2,1,0:T(8,128)S(1)}, u32[]{:S(2)}, u32[]{:S(2)}) %collective-permute-start.21) | collective-permute-done | bytes 262176 | tf_op jit(solution)/shard_map/ppermute | solution.py:335
  99.0 2.8 %collective-permute-done.20.refs_3_ = f32[1,4,128,128]{3,2,1,0:T(8,128)S(1)} collective-permute-done((f32[1,4,128,128]{3,2,1,0:T(8,128)S(1)}, f32[1,4,128,128]{3,2,1,0:T(8,128)S(1)}, u32[]{:S(2)}, u32[]{:S(2)}) %collective-permute-start.20) | collective-permute-done | bytes 262176 | tf_op jit(solution)/shard_map/ppermute | solution.py:335
  101.8 0.8 shard_map.56
  (11 shorter events, 0.4 us)
Async XLA Ops:
  1.1 19.9 %collective-permute-start.4 = (f32[2,4,128,128]{3,2,1,0:T(8,128)S(1)}, f32[2,4,128,128]{3,2,1,0:T(8,128)S(1)}, u32[]{:S(2)}, u32[]{:S(2)}) collective-permute-start(f32[2,4,128,128]{3,2,1,0:T(8,128)S(1)} %shard_map.39.refs_5_), channel_id=1, source_target_pairs={{0,1},{1,2},{2,3},{3,4},{4,5},{5,6},{6,7},{7,8},{8,9},{9,10},{10,1... | collective-permute-start | bytes 1572872 | tf_op jit(solution)/shard_map/ppermute | solution.py:335
  12.6 9.8 %collective-permute-start.2 = (f32[2,4,128,128]{3,2,1,0:T(8,128)}, f32[2,4,128,128]{3,2,1,0:T(8,128)S(1)}, u32[]{:S(2)}, u32[]{:S(2)}) collective-permute-start(f32[2,4,128,128]{3,2,1,0:T(8,128)} %bitcast.1.refs_2_), channel_id=1, source_target_pairs={{0,64},{1,65},{2,66},{3,67},{4,68},{5,69},{6,70},{7,71},{8,72},{9,... | collective-permute-start | bytes 1572872 | tf_op jit(solution)/shard_map/ppermute | solution.py:335
  12.6 10.3 %collective-permute-start.3 = (f32[2,4,128,128]{3,2,1,0:T(8,128)}, f32[2,4,128,128]{3,2,1,0:T(8,128)S(1)}, u32[]{:S(2)}, u32[]{:S(2)}) collective-permute-start(f32[2,4,128,128]{3,2,1,0:T(8,128)} %bitcast.1.refs_2_), channel_id=1, source_target_pairs={{0,64},{1,65},{2,66},{3,67},{4,68},{5,69},{6,70},{7,71},{8,72},{9,... | collective-permute-start | bytes 1572872 | tf_op jit(solution)/shard_map/ppermute | solution.py:335
  13.1 20.1 %collective-permute-start = (f32[2,4,128,128]{3,2,1,0:T(8,128)}, f32[2,4,128,128]{3,2,1,0:T(8,128)S(1)}, u32[]{:S(2)}, u32[]{:S(2)}) collective-permute-start(f32[2,4,128,128]{3,2,1,0:T(8,128)} %bitcast.1.refs_2_), channel_id=1, source_target_pairs={{0,1},{1,2},{2,3},{3,4},{4,5},{5,6},{6,7},{7,8},{8,9},{9,10},{10,1... | collective-permute-start | bytes 1572872 | tf_op jit(solution)/shard_map/ppermute | solution.py:335
  13.1 20.1 %collective-permute-start.1 = (f32[2,4,128,128]{3,2,1,0:T(8,128)}, f32[2,4,128,128]{3,2,1,0:T(8,128)}, u32[]{:S(2)}, u32[]{:S(2)}) collective-permute-start(f32[2,4,128,128]{3,2,1,0:T(8,128)} %bitcast.1.refs_2_), channel_id=1, source_target_pairs={{0,63},{1,0},{2,1},{3,2},{4,3},{5,4},{6,5},{7,6},{8,7},{9,8},{10,9... | collective-permute-start | bytes 1572872 | tf_op jit(solution)/shard_map/ppermute | solution.py:335
  20.9 12.3 %collective-permute-start.5 = (f32[2,4,128,128]{3,2,1,0:T(8,128)S(1)}, f32[2,4,128,128]{3,2,1,0:T(8,128)}, u32[]{:S(2)}, u32[]{:S(2)}) collective-permute-start(f32[2,4,128,128]{3,2,1,0:T(8,128)S(1)} %collective-permute-done.4.refs_2_.refs_4_), channel_id=1, source_target_pairs={{128,132},{132,136},{136,140},{140,144},{144,148},{148,152},{152,1... | collective-permute-start | bytes 1572872 | tf_op jit(solution)/shard_map/ppermute | solution.py:335
  22.4 12.6 %collective-permute-start.6 = (f32[2,4,128,128]{3,2,1,0:T(8,128)S(1)}, f32[2,4,128,128]{3,2,1,0:T(8,128)S(1)}, u32[]{:S(2)}, u32[]{:S(2)}) collective-permute-start(f32[2,4,128,128]{3,2,1,0:T(8,128)S(1)} %collective-permute-done.4.refs_2_.refs_4_), channel_id=1, source_target_pairs={{0,64},{1,65},{2,66},{3,67},{4,68},{5,69},{6,70},{7,71},{8,72},{9,... | collective-permute-start | bytes 1572872 | tf_op jit(solution)/shard_map/ppermute | solution.py:335
  23.0 17.1 %collective-permute-start.10 = (f32[2,4,128,128]{3,2,1,0:T(8,128)S(1)}, f32[2,4,128,128]{3,2,1,0:T(8,128)S(1)}, u32[]{:S(2)}, u32[]{:S(2)}) collective-permute-start(f32[2,4,128,128]{3,2,1,0:T(8,128)S(1)} %shard_map.38.refs_2_), channel_id=1, source_target_pairs={{128,132},{131,191},{132,136},{135,131},{136,140},{139,135},{140,1... | collective-permute-start | bytes 1572872 | tf_op jit(solution)/shard_map/ppermute | solution.py:335
  34.3 7.1 %collective-permute-start.11 = (f32[2,4,128,128]{3,2,1,0:T(8,128)S(1)}, f32[2,4,128,128]{3,2,1,0:T(8,128)S(1)}, u32[]{:S(2)}, u32[]{:S(2)}) collective-permute-start(f32[2,4,128,128]{3,2,1,0:T(8,128)S(1)} %shard_map.40.refs_3_.refs_1_.refs_2_), channel_id=1, source_target_pairs={{128,192},{129,193},{130,194},{131,195},{132,196},{133,197},{134,1... | collective-permute-start | bytes 1572872 | tf_op jit(solution)/shard_map/ppermute | solution.py:335
  36.2 13.6 %collective-permute-start.7 = (f32[2,4,128,128]{3,2,1,0:T(8,128)S(1)}, f32[2,4,128,128]{3,2,1,0:T(8,128)S(1)}, u32[]{:S(2)}, u32[]{:S(2)}) collective-permute-start(f32[2,4,128,128]{3,2,1,0:T(8,128)S(1)} %get-tuple-element.20), channel_id=1, source_target_pairs={{0,64},{1,65},{2,66},{3,67},{4,68},{5,69},{6,70},{7,71},{8,72},{9,... | collective-permute-start | bytes 1572872 | tf_op jit(solution)/shard_map/ppermute | solution.py:335
  37.5 21.6 %collective-permute-start.8 = (f32[2,4,128,128]{3,2,1,0:T(8,128)S(1)}, f32[2,4,128,128]{3,2,1,0:T(8,128)S(1)}, u32[]{:S(2)}, u32[]{:S(2)}) collective-permute-start(f32[2,4,128,128]{3,2,1,0:T(8,128)S(1)} %get-tuple-element.20), channel_id=1, source_target_pairs={{0,65},{1,66},{2,67},{3,68},{4,69},{5,70},{6,71},{7,72},{8,73},{9,... | collective-permute-start | bytes 1572872 | tf_op jit(solution)/shard_map/ppermute | solution.py:335
  38.8 20.3 %collective-permute-start.9 = (f32[2,4,128,128]{3,2,1,0:T(8,128)S(1)}, f32[2,4,128,128]{3,2,1,0:T(8,128)S(1)}, u32[]{:S(2)}, u32[]{:S(2)}) collective-permute-start(f32[2,4,128,128]{3,2,1,0:T(8,128)S(1)} %get-tuple-element.20), channel_id=1, source_target_pairs={{0,127},{1,64},{2,65},{3,66},{4,67},{5,68},{6,69},{7,70},{8,71},{9... | collective-permute-start | bytes 1572872 | tf_op jit(solution)/shard_map/ppermute | solution.py:335
  61.7 7.4 %collective-permute-start.13 = (f32[2,4,128,128]{3,2,1,0:T(8,128)S(1)}, f32[2,4,128,128]{3,2,1,0:T(8,128)S(1)}, u32[]{:S(2)}, u32[]{:S(2)}) collective-permute-start(f32[2,4,128,128]{3,2,1,0:T(8,128)S(1)} %get-tuple-element.22), channel_id=1, source_target_pairs={{64,1},{65,2},{66,3},{67,4},{68,5},{69,6},{70,7},{71,8},{72,9},{73... | collective-permute-start | bytes 1572872 | tf_op jit(solution)/shard_map/ppermute | solution.py:335
  63.0 7.4 %collective-permute-start.12 = (f32[2,4,128,128]{3,2,1,0:T(8,128)S(1)}, f32[2,4,128,128]{3,2,1,0:T(8,128)S(1)}, u32[]{:S(2)}, u32[]{:S(2)}) collective-permute-start(f32[2,4,128,128]{3,2,1,0:T(8,128)S(1)} %get-tuple-element.22), channel_id=1, source_target_pairs={{64,0},{65,1},{66,2},{67,3},{68,4},{69,5},{70,6},{71,7},{72,8},{73... | collective-permute-start | bytes 1572872 | tf_op jit(solution)/shard_map/ppermute | solution.py:335
  64.3 7.5 %collective-permute-start.14 = (f32[2,4,128,128]{3,2,1,0:T(8,128)S(1)}, f32[2,4,128,128]{3,2,1,0:T(8,128)S(1)}, u32[]{:S(2)}, u32[]{:S(2)}) collective-permute-start(f32[2,4,128,128]{3,2,1,0:T(8,128)S(1)} %get-tuple-element.22), channel_id=1, source_target_pairs={{64,63},{65,0},{66,1},{67,2},{68,3},{69,4},{70,5},{71,6},{72,7},{7... | collective-permute-start | bytes 1572872 | tf_op jit(solution)/shard_map/ppermute | solution.py:335
  65.7 6.1 %collective-permute-start.15 = (f32[2,4,128,128]{3,2,1,0:T(8,128)S(1)}, f32[2,4,128,128]{3,2,1,0:T(8,128)S(1)}, u32[]{:S(2)}, u32[]{:S(2)}) collective-permute-start(f32[2,4,128,128]{3,2,1,0:T(8,128)S(1)} %shard_map.50.refs_4_.array), channel_id=1, source_target_pairs={{128,0},{129,1},{130,2},{131,3},{132,4},{133,5},{134,6},{135,7},{1... | collective-permute-start | bytes 1572872 | tf_op jit(solution)/shard_map/ppermute | solution.py:335
  69.1 9.9 %collective-permute-start.19 = (f32[2,4,128,128]{3,2,1,0:T(8,128)S(1)}, f32[2,4,128,128]{3,2,1,0:T(8,128)S(1)}, u32[]{:S(2)}, u32[]{:S(2)}) collective-permute-start(f32[2,4,128,128]{3,2,1,0:T(8,128)S(1)} %shard_map.53), channel_id=1, source_target_pairs={{192,64},{193,65},{194,66},{195,67},{196,68},{197,69},{198,70},{19... | collective-permute-start | bytes 1572872 | tf_op jit(solution)/shard_map/ppermute | solution.py:335
  71.8 8.6 %collective-permute-start.16 = (f32[2,4,128,128]{3,2,1,0:T(8,128)S(1)}, f32[2,4,128,128]{3,2,1,0:T(8,128)S(1)}, u32[]{:S(2)}, u32[]{:S(2)}) collective-permute-start(f32[2,4,128,128]{3,2,1,0:T(8,128)S(1)} %get-tuple-element.23), channel_id=1, source_target_pairs={{0,64},{1,65},{2,66},{3,67},{4,68},{5,69},{6,70},{7,71},{8,72},{9,... | collective-permute-start | bytes 1572872 | tf_op jit(solution)/shard_map/ppermute | solution.py:335
  73.1 19.7 %collective-permute-start.17 = (f32[2,4,128,128]{3,2,1,0:T(8,128)S(1)}, f32[2,4,128,128]{3,2,1,0:T(8,128)S(1)}, u32[]{:S(2)}, u32[]{:S(2)}) collective-permute-start(f32[2,4,128,128]{3,2,1,0:T(8,128)S(1)} %get-tuple-element.23), channel_id=1, source_target_pairs={{0,65},{1,66},{2,67},{3,68},{4,69},{5,70},{6,71},{7,72},{8,73},{9,... | collective-permute-start | bytes 1572872 | tf_op jit(solution)/shard_map/ppermute | solution.py:335
  74.4 18.4 %collective-permute-start.18 = (f32[2,4,128,128]{3,2,1,0:T(8,128)S(1)}, f32[2,4,128,128]{3,2,1,0:T(8,128)S(1)}, u32[]{:S(2)}, u32[]{:S(2)}) collective-permute-start(f32[2,4,128,128]{3,2,1,0:T(8,128)S(1)} %get-tuple-element.23), channel_id=1, source_target_pairs={{0,127},{1,64},{2,65},{3,66},{4,67},{5,68},{6,69},{7,70},{8,71},{9... | collective-permute-start | bytes 1572872 | tf_op jit(solution)/shard_map/ppermute | solution.py:335
  94.0 5.0 %collective-permute-start.21 = (f32[1,4,128,128]{3,2,1,0:T(8,128)S(1)}, f32[1,4,128,128]{3,2,1,0:T(8,128)S(1)}, u32[]{:S(2)}, u32[]{:S(2)}) collective-permute-start(f32[1,4,128,128]{3,2,1,0:T(8,128)S(1)} %shard_map.55), channel_id=1, source_target_pairs={{0,128},{1,129},{2,130},{3,131},{4,132},{5,133},{6,134},{7,135},{8... | collective-permute-start | bytes 786440 | tf_op jit(solution)/shard_map/ppermute | solution.py:335
  96.5 5.3 %collective-permute-start.20 = (f32[1,4,128,128]{3,2,1,0:T(8,128)S(1)}, f32[1,4,128,128]{3,2,1,0:T(8,128)S(1)}, u32[]{:S(2)}, u32[]{:S(2)}) collective-permute-start(f32[1,4,128,128]{3,2,1,0:T(8,128)S(1)} %shard_map.54), channel_id=1, source_target_pairs={{0,128},{1,129},{2,130},{3,131},{4,132},{5,133},{6,134},{7,135},{8... | collective-permute-start | bytes 786440 | tf_op jit(solution)/shard_map/ppermute | solution.py:335

commit v6 on v5

--- a/solution.py
+++ b/solution.py
@@ -272,7 +272,9 @@
         scratch_shapes=[pltpu.VMEM((2, count, *plane), jnp.float32) for count in layers],
         compiler_params=pltpu.CompilerParams(vmem_limit_bytes=10 * 2**20),
         cost_estimate=pl.CostEstimate(
-            flops=10**10 if scratch else 10**5, bytes_accessed=2**20, transcendentals=0
+            flops=10**10 if scratch else SETTLE if outputs > 1 else 10**5,
+            bytes_accessed=2**20,
+            transcendentals=0,
         ),
     )(position, *operands, *tokens)
 
@@ -292,24 +294,14 @@
     )(pltpu.with_memory_space_constraint(array, pltpu.VMEM), token)
 
 
-def settle_kernel(*refs):
-    pass
-
-
-def settled(low, high, tokens):
-    return pl.pallas_call(
-        settle_kernel,
-        out_shape=[pltpu.VMEM(low.shape, low.dtype)] * 2,
-        in_specs=[ANY] * (2 + len(tokens)),
-        out_specs=[ANY, ANY],
-        input_output_aliases={0: 0, 1: 1},
-        compiler_params=pltpu.CompilerParams(vmem_limit_bytes=2**20),
-        cost_estimate=pl.CostEstimate(flops=SETTLE, bytes_accessed=2**20, transcendentals=0),
-    )(
-        pltpu.with_memory_space_constraint(low, pltpu.VMEM),
-        pltpu.with_memory_space_constraint(high, pltpu.VMEM),
-        *tokens,
-    )
+def settle_kernel(flag, low, high, low_out, high_out):
+    low_out[...] = low[...]
+    high_out[...] = high[...]
+
+
+def settled(low, high):
+    flag = jnp.zeros(1, jnp.int32)
+    return run(settle_kernel, flag, (low, high), 2, 0)
 
 
 def pick(flag, array, other, tokens=()):
@@ -341,11 +333,13 @@
         step = 1 if source % 2 == 0 else -1
         return source, slab + step if source < 2 else beside(slab, step)
 
-    def onward(step):
-        return lambda source, slab: (source, slab + step) if source < 2 else (source ^ 1, slab)
-
-    def around_x(step):
-        return lambda source, slab: (source, beside(slab, step)) if source > 1 else (source ^ 1, slab)
+    def onward(first, step):
+        def target_of(source, slab):
+            if source == first:
+                return source, slab + step
+            return (source, beside(slab, step)) if source == first + 2 else None
+
+        return target_of
 
     def far_half(source, slab):
         if source == 2 and slab % ring == 0:
@@ -354,12 +348,15 @@
             return source, slab - ring
         return None
 
-    def far(source, slab):
-        if source >= 2 and slab % ring == 0:
-            return source, slab + ring
-        if source >= 2 and slab % ring == ring - 1:
-            return source, slab - ring
-        return None
+    def far(position):
+        def target_of(source, slab):
+            if source == position and slab % ring == 0:
+                return source, slab + ring
+            if source == position and slab % ring == ring - 1:
+                return source, slab - ring
+            return None
+
+        return target_of
 
     def swapped(source, slab):
         return source ^ 1, slab
@@ -374,38 +371,43 @@
 
     both = stacked(feed, kill)
     half = moved(both, halves)
-    low_x = moved(own, around_x(1))
-    high_x = moved(own, around_x(-1))
-    low = moved(own, onward(1))
-    high = moved(own, onward(-1))
+    low = moved(own, onward(0, 1))
+    high = moved(own, onward(0, -1))
     other = moved(half, swapped)
     half_far = moved(half, far_half)
+    own_b = after(own, half)
+    low_b = moved(own_b, onward(1, 1))
+    high_b = moved(own_b, onward(1, -1))
     lowest, highest = place == 0, place == ring - 1
-    outer = pick(lowest, low_x, high_x)
-    outer_far = moved(outer, far)
+    low, high = settled(low, high)
+    outer_2 = moved(pick(lowest, low, high), far(2))
+    explicit, first_end = run(
+        fine_kernel, position, (low, own, high, half, both, other), 2, worker=(0,), tokens=(own_b,)
+    )
+    second = spread(explicit, 0, 1)
     mended = pick((lowest & (index == 2)) | (highest & (index == 3)), half_far, half)
     other_x = moved(mended, lambda source, slab: swapped(source, slab) if source >= 2 else None)
-    low, high = settled(low, high, ())
-    low, high = settled(low, high, (outer, mended))
-    explicit, first_end = run(
-        fine_kernel, position, (low, own, high, half, both, other), 2, worker=(0,)
-    )
-    second = spread(explicit, 0, 1)
+    outer_3 = moved(pick(lowest, low_b, high_b, (explicit,)), far(3))
     even = index % 2 == 0
     other = pick(index == 1, other, other_x)
     low_c = pick(even, mended, other)
     high_c = pick(even, other, mended)
-    low = pick(index == 1, low, pick(lowest, outer_far, low_x))
-    high = pick(index == 1, high, pick(highest, outer_far, high_x))
+    low_2 = pick(index == 1, low_b, pick(lowest, outer_2, low))
+    high_2 = pick(index == 1, high_b, pick(highest, outer_2, high))
     (correction,) = run(
-        correction_kernel, position, (low, own, high, low_c, both, high_c), 1, 3, worker=(1, 3)
+        correction_kernel, position, (low_2, own, high_2, low_c, both, high_c), 1, 3, worker=(1, 2)
     )
     crossed_2 = moved(correction, route(2, 0))
+    low_3 = pick(lowest, outer_3, low_b)
+    high_3 = pick(highest, outer_3, high_b)
+    (correction_3,) = run(
+        correction_kernel, position, (low_3, own, high_3, low_c, both, high_c), 1, 3, worker=(3, 3)
+    )
     explicit, second_end = run(
         coarse_kernel, position, (*second, correction, both), 2, worker=(1,)
     )
     third = spread(explicit, 1, 0)
-    crossed_3 = moved(after(correction, third[1]), route(3, 1))
+    crossed_3 = moved(after(correction_3, third[1]), route(3, 1))
     explicit, third_end = run(
         coarse_kernel, position, (*third, crossed_2, both), 2, worker=(0,)
     )

time: 103 us -> 102 us (level)
  starting transfers between devices: 39.6 us -> 45.2 us
  waiting for transfers between devices: 44 us -> 39.2 us
  Pallas kernels: 18.8 us -> 16.4 us
    ppermute x22 -> x23, starting transfers between devices: 39.6 us -> 45.2 us  [moved(): return lax.ppermute(array, AXES, pairs)]
    ppermute x22 -> x23, waiting for transfers between devices: 44 us -> 39.2 us  [moved(): return lax.ppermute(array, AXES, pairs)]
    pallas_call x16 -> x21, Pallas kernels: 17.7 us -> 15.3 us  [run(): pl.pallas_call(kernel, out_shape=out_shape, in_specs=[SMEM] + [VMEM] * le...]
  transfers between devices with their start and end apart: 22 -> 23, of which waited for: 9 -> 9; matrix products, arithmetic and copies ran while one was open for 0% -> 0% of each run, Pallas kernels for 13% -> 13%
where the time goes in v6:
time: 102 us; the launch traced here: 101 us
  starting transfers between devices  45.2 us (44%)
  waiting for transfers between devices  39.2 us (38%)
  Pallas kernels  16.4 us (16%)
    ppermute x23, starting transfers between devices, moved(): return lax.ppermute(array, AXES, pairs)  45.2 us
    ppermute x23, waiting for transfers between devices, moved(): return lax.ppermute(array, AXES, pairs)  39.2 us
    pallas_call x21, Pallas kernels, run(): pl.pallas_call(kernel, out_shape=out_shape, in_specs=[SMEM] + [VMEM] * le...  15.3 us
  transfers between devices with their start and end apart: 23, of which 9 were waited for; matrix products, arithmetic and copies ran while one was open for 0% of the time, Pallas kernels for 13%

profile of v6, /device:TPU:1, one launch (start us, length us, event | category | flops | bytes accessed | tf_op | source)
XLA Modules:
  0.0 101.3 jit_solution(12527539565396752069)
XLA Ops:
  0.0 0.0 copy-start
  0.0 1.1 %shard_map.38.refs_5_ = f32[2,4,128,128]{3,2,1,0:T(8,128)S(1)} custom-call(f32[4,128,128]{2,1,0:T(8,128)} %feed.1, f32[4,128,128]{2,1,0:T(8,128)} %kill.1), custom_call_target="tpu_custom_call" | custom-call | flops 100000 | bytes 1048576 | tf_op jit(solution)/shard_map/pallas_call | solution.py:227
  1.1 11.6 %collective-permute-start.2 = (f32[2,4,128,128]{3,2,1,0:T(8,128)S(1)}, f32[2,4,128,128]{3,2,1,0:T(8,128)S(1)}, u32[]{:S(2)}, u32[]{:S(2)}) collective-permute-start(f32[2,4,128,128]{3,2,1,0:T(8,128)S(1)} %shard_map.38.refs_5_), channel_id=1, source_target_pairs={{0,1},{1,2},{2,3},{3,4},{4,5},{5,6},{6,7},{7,8},{8,9},{9,10},{10,1... | collective-permute-start | bytes 1572872 | tf_op jit(solution)/shard_map/ppermute | solution.py:327
  12.7 0.0 copy-done
  12.7 0.7 collective-permute-start.1
  13.4 1.5 %collective-permute-start = (f32[2,4,128,128]{3,2,1,0:T(8,128)S(1)}, f32[2,4,128,128]{3,2,1,0:T(8,128)}, u32[]{:S(2)}, u32[]{:S(2)}) collective-permute-start(f32[2,4,128,128]{3,2,1,0:T(8,128)S(1)} %bitcast.9), channel_id=1, source_target_pairs={{0,1},{1,2},{2,3},{3,4},{4,5},{5,6},{6,7},{7,8},{8,9},{9,10},{10,1... | collective-permute-start | bytes 1572872 | tf_op jit(solution)/shard_map/ppermute | solution.py:327
  14.9 6.4 %collective-permute-done.2.token.refs_4_.refs_2_ = f32[2,4,128,128]{3,2,1,0:T(8,128)S(1)} collective-permute-done((f32[2,4,128,128]{3,2,1,0:T(8,128)S(1)}, f32[2,4,128,128]{3,2,1,0:T(8,128)S(1)}, u32[]{:S(2)}, u32[]{:S(2)}) %collective-permute-start.2) | collective-permute-done | bytes 524320 | tf_op jit(solution)/shard_map/ppermute | solution.py:327
  21.3 0.7 collective-permute-start.10
  22.0 0.1 collective-permute-start.3
  22.2 10.4 %collective-permute-start.9 = (f32[2,4,128,128]{3,2,1,0:T(8,128)S(1)}, f32[2,4,128,128]{3,2,1,0:T(8,128)S(1)}, u32[]{:S(2)}, u32[]{:S(2)}) collective-permute-start(f32[2,4,128,128]{3,2,1,0:T(8,128)S(1)} %shard_map.39.refs_7_), channel_id=1, source_target_pairs={{64,127},{65,64},{66,65},{67,66},{68,67},{69,68},{70,69},{71,70},{... | collective-permute-start | bytes 1572872 | tf_op jit(solution)/shard_map/ppermute | solution.py:327
  32.6 0.0 collective-permute-done.1.refs_2_
  32.6 1.9 %collective-permute-start.7 = (f32[2,4,128,128]{3,2,1,0:T(8,128)S(1)}, f32[2,4,128,128]{3,2,1,0:T(8,128)S(1)}, u32[]{:S(2)}, u32[]{:S(2)}) collective-permute-start(f32[2,4,128,128]{3,2,1,0:T(8,128)S(1)} %shard_map.39.refs_7_), channel_id=1, source_target_pairs={{64,65},{65,66},{66,67},{67,68},{68,69},{69,70},{70,71},{71,72},{7... | collective-permute-start | bytes 1572872 | tf_op jit(solution)/shard_map/ppermute | solution.py:327
  34.6 0.0 collective-permute-done.refs_1_
  34.6 1.1 %shard_map.37 = (f32[2,4,128,128]{3,2,1,0:T(8,128)S(1)}, f32[2,4,128,128]{3,2,1,0:T(8,128)S(1)}) custom-call(s32[1]{0:T(128)} %constant.30.clone.1.refs_0_, f32[2,4,128,128]{3,2,1,0:T(8,128)} %collective-permute-done.refs_1_, f32[2,4,128,128]{3,2,1,0:T(8,128)S(1)} %collective-permute-done.1.refs_2_), custom_call_target="tpu_custom_call" | custom-call | flops 1000000000 | bytes 1048576 | tf_op jit(solution)/shard_map/pallas_call | solution.py:267
  35.7 0.7 collective-permute-start.8
  36.5 0.0 collective-permute-done.10.refs_1_
  36.5 0.7 collective-permute-start.11
  37.2 0.0 collective-permute-done.3.refs_6_.refs_1_
  37.2 1.3 %collective-permute-start.6 = (f32[2,4,128,128]{3,2,1,0:T(8,128)S(1)}, f32[2,4,128,128]{3,2,1,0:T(8,128)S(1)}, u32[]{:S(2)}, u32[]{:S(2)}) collective-permute-start(f32[2,4,128,128]{3,2,1,0:T(8,128)S(1)} %get-tuple-element.16.refs_3_), channel_id=1, source_target_pairs={{0,127},{1,64},{2,65},{3,66},{4,67},{5,68},{6,69},{7,70},{8,71},{9... | collective-permute-start | bytes 1572872 | tf_op jit(solution)/shard_map/ppermute | solution.py:327
  38.5 0.2 collective-permute-done.9.refs_1_.refs_2_
  38.7 1.3 %collective-permute-start.5 = (f32[2,4,128,128]{3,2,1,0:T(8,128)S(1)}, f32[2,4,128,128]{3,2,1,0:T(8,128)S(1)}, u32[]{:S(2)}, u32[]{:S(2)}) collective-permute-start(f32[2,4,128,128]{3,2,1,0:T(8,128)S(1)} %get-tuple-element.16.refs_3_), channel_id=1, source_target_pairs={{0,65},{1,66},{2,67},{3,68},{4,69},{5,70},{6,71},{7,72},{8,73},{9,... | collective-permute-start | bytes 1572872 | tf_op jit(solution)/shard_map/ppermute | solution.py:327
  40.0 8.9 %collective-permute-done.7.refs_1_.refs_2_ = f32[2,4,128,128]{3,2,1,0:T(8,128)S(1)} collective-permute-done((f32[2,4,128,128]{3,2,1,0:T(8,128)S(1)}, f32[2,4,128,128]{3,2,1,0:T(8,128)S(1)}, u32[]{:S(2)}, u32[]{:S(2)}) %collective-permute-start.7) | collective-permute-done | bytes 524320 | tf_op jit(solution)/shard_map/ppermute | solution.py:327
  48.9 1.3 %collective-permute-start.4 = (f32[2,4,128,128]{3,2,1,0:T(8,128)S(1)}, f32[2,4,128,128]{3,2,1,0:T(8,128)S(1)}, u32[]{:S(2)}, u32[]{:S(2)}) collective-permute-start(f32[2,4,128,128]{3,2,1,0:T(8,128)S(1)} %get-tuple-element.16.refs_3_), channel_id=1, source_target_pairs={{0,64},{1,65},{2,66},{3,67},{4,68},{5,69},{6,70},{7,71},{8,72},{9,... | collective-permute-start | bytes 1572872 | tf_op jit(solution)/shard_map/ppermute | solution.py:327
  50.2 0.0 collective-permute-done.8.refs_1_
  50.2 0.7 collective-permute-start.19
  51.2 0.0 collective-permute-done.11.refs_2_
  51.4 7.4 %shard_map.50.refs_4_ = f32[2,4,128,128]{3,2,1,0:T(8,128)S(1)} custom-call(s32[1]{0:T(128)} %bitcast.refs_0_, f32[2,4,128,128]{3,2,1,0:T(8,128)S(1)} %shard_map.43.refs_1_, f32[2,4,128,128]{3,2,1,0:T(8,128)S(1)} %bitcast.12, f32[2,4,128,128]{3,2,1,0:T(8,128)S(1)} %shard_map.45.refs_3_, f32[2,4,128,128]{3,2,1,0:T(8,128)S(1)} %shard_map.48.refs_4_, ...), custom_call_target="tpu_custom_call" | custom-call | flops 10000000000 | bytes 1048576 | tf_op jit(solution)/shard_map/pallas_call | solution.py:267
  58.8 0.7 collective-permute-start.15
  59.5 0.0 collective-permute-done.6.refs_3_
  59.5 0.0 collective-permute-done.5.refs_2_
  59.5 0.0 collective-permute-done.4.refs_1_
  59.5 2.7 %shard_map.51 = (f32[2,4,128,128]{3,2,1,0:T(8,128)S(1)}, f32[2,4,128,128]{3,2,1,0:T(8,128)S(1)}) custom-call(s32[1]{0:T(128)} %bitcast.refs_0_, f32[2,4,128,128]{3,2,1,0:T(8,128)S(1)} %collective-permute-done.4.refs_1_, f32[2,4,128,128]{3,2,1,0:T(8,128)S(1)} %collective-permute-done.5.refs_2_, f32[2,4,128,128]{3,2,1,0:T(8,128)S(1)} %collective-permute-done.6.refs_3_, ...), custom_call_target="tpu_custom_call" | custom-call | flops 10000000000 | bytes 1048576 | tf_op jit(solution)/shard_map/pallas_call | solution.py:267
  62.2 1.3 %collective-permute-start.14 = (f32[2,4,128,128]{3,2,1,0:T(8,128)S(1)}, f32[2,4,128,128]{3,2,1,0:T(8,128)S(1)}, u32[]{:S(2)}, u32[]{:S(2)}) collective-permute-start(f32[2,4,128,128]{3,2,1,0:T(8,128)S(1)} %get-tuple-element.18), channel_id=1, source_target_pairs={{64,63},{65,0},{66,1},{67,2},{68,3},{69,4},{70,5},{71,6},{72,7},{7... | collective-permute-start | bytes 1572872 | tf_op jit(solution)/shard_map/ppermute | solution.py:327
  63.5 1.3 %collective-permute-start.13 = (f32[2,4,128,128]{3,2,1,0:T(8,128)S(1)}, f32[2,4,128,128]{3,2,1,0:T(8,128)S(1)}, u32[]{:S(2)}, u32[]{:S(2)}) collective-permute-start(f32[2,4,128,128]{3,2,1,0:T(8,128)S(1)} %get-tuple-element.18), channel_id=1, source_target_pairs={{64,1},{65,2},{66,3},{67,4},{68,5},{69,6},{70,7},{71,8},{72,9},{73... | collective-permute-start | bytes 1572872 | tf_op jit(solution)/shard_map/ppermute | solution.py:327
  64.8 1.3 %collective-permute-start.12 = (f32[2,4,128,128]{3,2,1,0:T(8,128)S(1)}, f32[2,4,128,128]{3,2,1,0:T(8,128)S(1)}, u32[]{:S(2)}, u32[]{:S(2)}) collective-permute-start(f32[2,4,128,128]{3,2,1,0:T(8,128)S(1)} %get-tuple-element.18), channel_id=1, source_target_pairs={{64,0},{65,1},{66,2},{67,3},{68,4},{69,5},{70,6},{71,7},{72,8},{73... | collective-permute-start | bytes 1572872 | tf_op jit(solution)/shard_map/ppermute | solution.py:327
  66.2 0.0 collective-permute-done.19.refs_1_
  66.3 0.2 shard_map.56.array
  66.5 4.4 %collective-permute-done.13.refs_2_.token = f32[2,4,128,128]{3,2,1,0:T(8,128)S(1)} collective-permute-done((f32[2,4,128,128]{3,2,1,0:T(8,128)S(1)}, f32[2,4,128,128]{3,2,1,0:T(8,128)S(1)}, u32[]{:S(2)}, u32[]{:S(2)}) %collective-permute-start.13) | collective-permute-done | bytes 524320 | tf_op jit(solution)/shard_map/ppermute | solution.py:327
  70.9 1.3 %collective-permute-start.20 = (f32[2,4,128,128]{3,2,1,0:T(8,128)S(1)}, f32[2,4,128,128]{3,2,1,0:T(8,128)S(1)}, u32[]{:S(2)}, u32[]{:S(2)}) collective-permute-start(f32[2,4,128,128]{3,2,1,0:T(8,128)S(1)} %shard_map.57), channel_id=1, source_target_pairs={{192,64},{193,65},{194,66},{195,67},{196,68},{197,69},{198,70},{19... | collective-permute-start | bytes 1572872 | tf_op jit(solution)/shard_map/ppermute | solution.py:327
  72.2 0.0 collective-permute-done.15.refs_4_
  72.2 0.0 collective-permute-done.14.refs_3_
  72.3 0.0 collective-permute-done.12.refs_1_
  72.3 1.3 %collective-permute-start.18 = (f32[2,4,128,128]{3,2,1,0:T(8,128)S(1)}, f32[2,4,128,128]{3,2,1,0:T(8,128)S(1)}, u32[]{:S(2)}, u32[]{:S(2)}) collective-permute-start(f32[2,4,128,128]{3,2,1,0:T(8,128)S(1)} %get-tuple-element.19), channel_id=1, source_target_pairs={{0,127},{1,64},{2,65},{3,66},{4,67},{5,68},{6,69},{7,70},{8,71},{9... | collective-permute-start | bytes 1572872 | tf_op jit(solution)/shard_map/ppermute | solution.py:327
  73.6 1.3 %collective-permute-start.17 = (f32[2,4,128,128]{3,2,1,0:T(8,128)S(1)}, f32[2,4,128,128]{3,2,1,0:T(8,128)S(1)}, u32[]{:S(2)}, u32[]{:S(2)}) collective-permute-start(f32[2,4,128,128]{3,2,1,0:T(8,128)S(1)} %get-tuple-element.19), channel_id=1, source_target_pairs={{0,65},{1,66},{2,67},{3,68},{4,69},{5,70},{6,71},{7,72},{8,73},{9,... | collective-permute-start | bytes 1572872 | tf_op jit(solution)/shard_map/ppermute | solution.py:327
  74.9 1.3 %collective-permute-start.16 = (f32[2,4,128,128]{3,2,1,0:T(8,128)S(1)}, f32[2,4,128,128]{3,2,1,0:T(8,128)S(1)}, u32[]{:S(2)}, u32[]{:S(2)}) collective-permute-start(f32[2,4,128,128]{3,2,1,0:T(8,128)S(1)} %get-tuple-element.19), channel_id=1, source_target_pairs={{0,64},{1,65},{2,66},{3,67},{4,68},{5,69},{6,70},{7,71},{8,72},{9,... | collective-permute-start | bytes 1572872 | tf_op jit(solution)/shard_map/ppermute | solution.py:327
  76.2 4.7 %collective-permute-done.20.refs_4_ = f32[2,4,128,128]{3,2,1,0:T(8,128)S(1)} collective-permute-done((f32[2,4,128,128]{3,2,1,0:T(8,128)S(1)}, f32[2,4,128,128]{3,2,1,0:T(8,128)S(1)}, u32[]{:S(2)}, u32[]{:S(2)}) %collective-permute-start.20) | collective-permute-done | bytes 524320 | tf_op jit(solution)/shard_map/ppermute | solution.py:327
  80.9 4.1 %collective-permute-done.18.refs_3_ = f32[2,4,128,128]{3,2,1,0:T(8,128)S(1)} collective-permute-done((f32[2,4,128,128]{3,2,1,0:T(8,128)S(1)}, f32[2,4,128,128]{3,2,1,0:T(8,128)S(1)}, u32[]{:S(2)}, u32[]{:S(2)}) %collective-permute-start.18) | collective-permute-done | bytes 524320 | tf_op jit(solution)/shard_map/ppermute | solution.py:327
  85.0 5.7 %collective-permute-done.17.refs_2_ = f32[2,4,128,128]{3,2,1,0:T(8,128)S(1)} collective-permute-done((f32[2,4,128,128]{3,2,1,0:T(8,128)S(1)}, f32[2,4,128,128]{3,2,1,0:T(8,128)S(1)}, u32[]{:S(2)}, u32[]{:S(2)}) %collective-permute-start.17) | collective-permute-done | bytes 524320 | tf_op jit(solution)/shard_map/ppermute | solution.py:327
  90.6 0.0 collective-permute-done.16.refs_1_
  90.6 1.2 %shard_map.58 = f32[1,4,128,128]{3,2,1,0:T(8,128)S(1)} custom-call(s32[1]{0:T(128)} %bitcast.refs_0_, f32[2,4,128,128]{3,2,1,0:T(8,128)S(1)} %collective-permute-done.16.refs_1_, f32[2,4,128,128]{3,2,1,0:T(8,128)S(1)} %collective-permute-done.17.refs_2_, f32[2,4,128,128]{3,2,1,0:T(8,128)S(1)} %collective-permute-done.18.refs_3_, ...), custom_call_target="tpu_custom_call" | custom-call | flops 10000000000 | bytes 1048576 | tf_op jit(solution)/shard_map/pallas_call | solution.py:267
  91.8 1.3 %collective-permute-start.21 = (f32[1,4,128,128]{3,2,1,0:T(8,128)S(1)}, f32[1,4,128,128]{3,2,1,0:T(8,128)S(1)}, u32[]{:S(2)}, u32[]{:S(2)}) collective-permute-start(f32[1,4,128,128]{3,2,1,0:T(8,128)S(1)} %shard_map.58), channel_id=1, source_target_pairs={{0,128},{1,129},{2,130},{3,131},{4,132},{5,133},{6,134},{7,135},{8... | collective-permute-start | bytes 786440 | tf_op jit(solution)/shard_map/ppermute | solution.py:327
  93.1 1.2 %shard_map.59 = f32[1,4,128,128]{3,2,1,0:T(8,128)S(1)} custom-call(s32[1]{0:T(128)} %bitcast.refs_0_, f32[2,4,128,128]{3,2,1,0:T(8,128)S(1)} %collective-permute-done.16.refs_1_, f32[2,4,128,128]{3,2,1,0:T(8,128)S(1)} %collective-permute-done.17.refs_2_, f32[2,4,128,128]{3,2,1,0:T(8,128)S(1)} %collective-permute-done.18.refs_3_, ...), custom_call_target="tpu_custom_call" | custom-call | flops 10000000000 | bytes 1048576 | tf_op jit(solution)/shard_map/pallas_call | solution.py:267
  94.4 1.3 %collective-permute-start.22 = (f32[1,4,128,128]{3,2,1,0:T(8,128)S(1)}, f32[1,4,128,128]{3,2,1,0:T(8,128)S(1)}, u32[]{:S(2)}, u32[]{:S(2)}) collective-permute-start(f32[1,4,128,128]{3,2,1,0:T(8,128)S(1)} %shard_map.59), channel_id=1, source_target_pairs={{0,128},{1,129},{2,130},{3,131},{4,132},{5,133},{6,134},{7,135},{8... | collective-permute-start | bytes 786440 | tf_op jit(solution)/shard_map/ppermute | solution.py:327
  95.7 2.0 %collective-permute-done.21.refs_3_ = f32[1,4,128,128]{3,2,1,0:T(8,128)S(1)} collective-permute-done((f32[1,4,128,128]{3,2,1,0:T(8,128)S(1)}, f32[1,4,128,128]{3,2,1,0:T(8,128)S(1)}, u32[]{:S(2)}, u32[]{:S(2)}) %collective-permute-start.21) | collective-permute-done | bytes 262176 | tf_op jit(solution)/shard_map/ppermute | solution.py:327
  97.7 2.8 %collective-permute-done.22.refs_4_ = f32[1,4,128,128]{3,2,1,0:T(8,128)S(1)} collective-permute-done((f32[1,4,128,128]{3,2,1,0:T(8,128)S(1)}, f32[1,4,128,128]{3,2,1,0:T(8,128)S(1)}, u32[]{:S(2)}, u32[]{:S(2)}) %collective-permute-start.22) | collective-permute-done | bytes 262176 | tf_op jit(solution)/shard_map/ppermute | solution.py:327
  100.5 0.8 shard_map.60
  (16 shorter events, 0.7 us)
Async XLA Ops:
  0.0 12.7 %copy-start = (f32[1,2,4,128,128]{4,3,2,1,0:T(8,128)S(1)}, f32[1,2,4,128,128]{4,3,2,1,0:T(8,128)}, u32[]{:S(2)}) copy-start(f32[1,2,4,128,128]{4,3,2,1,0:T(8,128)} %param.3) | copy-start | bytes 1572868
  1.1 20.2 %collective-permute-start.2 = (f32[2,4,128,128]{3,2,1,0:T(8,128)S(1)}, f32[2,4,128,128]{3,2,1,0:T(8,128)S(1)}, u32[]{:S(2)}, u32[]{:S(2)}) collective-permute-start(f32[2,4,128,128]{3,2,1,0:T(8,128)S(1)} %shard_map.38.refs_5_), channel_id=1, source_target_pairs={{0,1},{1,2},{2,3},{3,4},{4,5},{5,6},{6,7},{7,8},{8,9},{9,10},{10,1... | collective-permute-start | bytes 1572872 | tf_op jit(solution)/shard_map/ppermute | solution.py:327
  12.7 19.9 %collective-permute-start.1 = (f32[2,4,128,128]{3,2,1,0:T(8,128)S(1)}, f32[2,4,128,128]{3,2,1,0:T(8,128)S(1)}, u32[]{:S(2)}, u32[]{:S(2)}) collective-permute-start(f32[2,4,128,128]{3,2,1,0:T(8,128)S(1)} %bitcast.8), channel_id=1, source_target_pairs={{0,63},{1,0},{2,1},{3,2},{4,3},{5,4},{6,5},{7,6},{8,7},{9,8},{10,9... | collective-permute-start | bytes 1572872 | tf_op jit(solution)/shard_map/ppermute | solution.py:327
  13.4 21.2 %collective-permute-start = (f32[2,4,128,128]{3,2,1,0:T(8,128)S(1)}, f32[2,4,128,128]{3,2,1,0:T(8,128)}, u32[]{:S(2)}, u32[]{:S(2)}) collective-permute-start(f32[2,4,128,128]{3,2,1,0:T(8,128)S(1)} %bitcast.9), channel_id=1, source_target_pairs={{0,1},{1,2},{2,3},{3,4},{4,5},{5,6},{6,7},{7,8},{8,9},{9,10},{10,1... | collective-permute-start | bytes 1572872 | tf_op jit(solution)/shard_map/ppermute | solution.py:327
  21.3 15.1 %collective-permute-start.10 = (f32[2,4,128,128]{3,2,1,0:T(8,128)S(1)}, f32[2,4,128,128]{3,2,1,0:T(8,128)S(1)}, u32[]{:S(2)}, u32[]{:S(2)}) collective-permute-start(f32[2,4,128,128]{3,2,1,0:T(8,128)S(1)} %collective-permute-done.2.token.refs_4_.refs_2_), channel_id=1, source_target_pairs={{128,132},{132,136},{136,140},{140,144},{144,148},{148,152},{152,1... | collective-permute-start | bytes 1572872 | tf_op jit(solution)/shard_map/ppermute | solution.py:327
  22.0 15.2 %collective-permute-start.3 = (f32[2,4,128,128]{3,2,1,0:T(8,128)S(1)}, f32[2,4,128,128]{3,2,1,0:T(8,128)S(1)}, u32[]{:S(2)}, u32[]{:S(2)}) collective-permute-start(f32[2,4,128,128]{3,2,1,0:T(8,128)S(1)} %collective-permute-done.2.token.refs_4_.refs_2_), channel_id=1, source_target_pairs={{0,64},{1,65},{2,66},{3,67},{4,68},{5,69},{6,70},{7,71},{8,72},{9,... | collective-permute-start | bytes 1572872 | tf_op jit(solution)/shard_map/ppermute | solution.py:327
  22.2 16.5 %collective-permute-start.9 = (f32[2,4,128,128]{3,2,1,0:T(8,128)S(1)}, f32[2,4,128,128]{3,2,1,0:T(8,128)S(1)}, u32[]{:S(2)}, u32[]{:S(2)}) collective-permute-start(f32[2,4,128,128]{3,2,1,0:T(8,128)S(1)} %shard_map.39.refs_7_), channel_id=1, source_target_pairs={{64,127},{65,64},{66,65},{67,66},{68,67},{69,68},{70,69},{71,70},{... | collective-permute-start | bytes 1572872 | tf_op jit(solution)/shard_map/ppermute | solution.py:327
  32.6 16.3 %collective-permute-start.7 = (f32[2,4,128,128]{3,2,1,0:T(8,128)S(1)}, f32[2,4,128,128]{3,2,1,0:T(8,128)S(1)}, u32[]{:S(2)}, u32[]{:S(2)}) collective-permute-start(f32[2,4,128,128]{3,2,1,0:T(8,128)S(1)} %shard_map.39.refs_7_), channel_id=1, source_target_pairs={{64,65},{65,66},{66,67},{67,68},{68,69},{69,70},{70,71},{71,72},{7... | collective-permute-start | bytes 1572872 | tf_op jit(solution)/shard_map/ppermute | solution.py:327
  35.7 14.5 %collective-permute-start.8 = (f32[2,4,128,128]{3,2,1,0:T(8,128)S(1)}, f32[2,4,128,128]{3,2,1,0:T(8,128)S(1)}, u32[]{:S(2)}, u32[]{:S(2)}) collective-permute-start(f32[2,4,128,128]{3,2,1,0:T(8,128)S(1)} %shard_map.41), channel_id=1, source_target_pairs={{128,132},{131,191},{132,136},{135,131},{136,140},{139,135},{140,1... | collective-permute-start | bytes 1572872 | tf_op jit(solution)/shard_map/ppermute | solution.py:327
  36.5 14.7 %collective-permute-start.11 = (f32[2,4,128,128]{3,2,1,0:T(8,128)S(1)}, f32[2,4,128,128]{3,2,1,0:T(8,128)S(1)}, u32[]{:S(2)}, u32[]{:S(2)}) collective-permute-start(f32[2,4,128,128]{3,2,1,0:T(8,128)S(1)} %shard_map.46.refs_1_.refs_2_), channel_id=1, source_target_pairs={{128,192},{129,193},{130,194},{131,195},{132,196},{133,197},{134,1... | collective-permute-start | bytes 1572872 | tf_op jit(solution)/shard_map/ppermute | solution.py:327
  37.2 22.2 %collective-permute-start.6 = (f32[2,4,128,128]{3,2,1,0:T(8,128)S(1)}, f32[2,4,128,128]{3,2,1,0:T(8,128)S(1)}, u32[]{:S(2)}, u32[]{:S(2)}) collective-permute-start(f32[2,4,128,128]{3,2,1,0:T(8,128)S(1)} %get-tuple-element.16.refs_3_), channel_id=1, source_target_pairs={{0,127},{1,64},{2,65},{3,66},{4,67},{5,68},{6,69},{7,70},{8,71},{9... | collective-permute-start | bytes 1572872 | tf_op jit(solution)/shard_map/ppermute | solution.py:327
  38.7 20.7 %collective-permute-start.5 = (f32[2,4,128,128]{3,2,1,0:T(8,128)S(1)}, f32[2,4,128,128]{3,2,1,0:T(8,128)S(1)}, u32[]{:S(2)}, u32[]{:S(2)}) collective-permute-start(f32[2,4,128,128]{3,2,1,0:T(8,128)S(1)} %get-tuple-element.16.refs_3_), channel_id=1, source_target_pairs={{0,65},{1,66},{2,67},{3,68},{4,69},{5,70},{6,71},{7,72},{8,73},{9,... | collective-permute-start | bytes 1572872 | tf_op jit(solution)/shard_map/ppermute | solution.py:327
  48.9 10.6 %collective-permute-start.4 = (f32[2,4,128,128]{3,2,1,0:T(8,128)S(1)}, f32[2,4,128,128]{3,2,1,0:T(8,128)S(1)}, u32[]{:S(2)}, u32[]{:S(2)}) collective-permute-start(f32[2,4,128,128]{3,2,1,0:T(8,128)S(1)} %get-tuple-element.16.refs_3_), channel_id=1, source_target_pairs={{0,64},{1,65},{2,66},{3,67},{4,68},{5,69},{6,70},{7,71},{8,72},{9,... | collective-permute-start | bytes 1572872 | tf_op jit(solution)/shard_map/ppermute | solution.py:327
  50.2 15.9 %collective-permute-start.19 = (f32[2,4,128,128]{3,2,1,0:T(8,128)S(1)}, f32[2,4,128,128]{3,2,1,0:T(8,128)S(1)}, u32[]{:S(2)}, u32[]{:S(2)}) collective-permute-start(f32[2,4,128,128]{3,2,1,0:T(8,128)S(1)} %shard_map.53), channel_id=1, source_target_pairs={{192,196},{195,255},{196,200},{199,195},{200,204},{203,199},{204,2... | collective-permute-start | bytes 1572872 | tf_op jit(solution)/shard_map/ppermute | solution.py:327
  58.8 13.5 %collective-permute-start.15 = (f32[2,4,128,128]{3,2,1,0:T(8,128)S(1)}, f32[2,4,128,128]{3,2,1,0:T(8,128)S(1)}, u32[]{:S(2)}, u32[]{:S(2)}) collective-permute-start(f32[2,4,128,128]{3,2,1,0:T(8,128)S(1)} %shard_map.50.refs_4_), channel_id=1, source_target_pairs={{128,0},{129,1},{130,2},{131,3},{132,4},{133,5},{134,6},{135,7},{1... | collective-permute-start | bytes 1572872 | tf_op jit(solution)/shard_map/ppermute | solution.py:327
  62.2 10.1 %collective-permute-start.14 = (f32[2,4,128,128]{3,2,1,0:T(8,128)S(1)}, f32[2,4,128,128]{3,2,1,0:T(8,128)S(1)}, u32[]{:S(2)}, u32[]{:S(2)}) collective-permute-start(f32[2,4,128,128]{3,2,1,0:T(8,128)S(1)} %get-tuple-element.18), channel_id=1, source_target_pairs={{64,63},{65,0},{66,1},{67,2},{68,3},{69,4},{70,5},{71,6},{72,7},{7... | collective-permute-start | bytes 1572872 | tf_op jit(solution)/shard_map/ppermute | solution.py:327
  63.5 7.4 %collective-permute-start.13 = (f32[2,4,128,128]{3,2,1,0:T(8,128)S(1)}, f32[2,4,128,128]{3,2,1,0:T(8,128)S(1)}, u32[]{:S(2)}, u32[]{:S(2)}) collective-permute-start(f32[2,4,128,128]{3,2,1,0:T(8,128)S(1)} %get-tuple-element.18), channel_id=1, source_target_pairs={{64,1},{65,2},{66,3},{67,4},{68,5},{69,6},{70,7},{71,8},{72,9},{73... | collective-permute-start | bytes 1572872 | tf_op jit(solution)/shard_map/ppermute | solution.py:327
  64.8 7.4 %collective-permute-start.12 = (f32[2,4,128,128]{3,2,1,0:T(8,128)S(1)}, f32[2,4,128,128]{3,2,1,0:T(8,128)S(1)}, u32[]{:S(2)}, u32[]{:S(2)}) collective-permute-start(f32[2,4,128,128]{3,2,1,0:T(8,128)S(1)} %get-tuple-element.18), channel_id=1, source_target_pairs={{64,0},{65,1},{66,2},{67,3},{68,4},{69,5},{70,6},{71,7},{72,8},{73... | collective-permute-start | bytes 1572872 | tf_op jit(solution)/shard_map/ppermute | solution.py:327
  70.9 9.9 %collective-permute-start.20 = (f32[2,4,128,128]{3,2,1,0:T(8,128)S(1)}, f32[2,4,128,128]{3,2,1,0:T(8,128)S(1)}, u32[]{:S(2)}, u32[]{:S(2)}) collective-permute-start(f32[2,4,128,128]{3,2,1,0:T(8,128)S(1)} %shard_map.57), channel_id=1, source_target_pairs={{192,64},{193,65},{194,66},{195,67},{196,68},{197,69},{198,70},{19... | collective-permute-start | bytes 1572872 | tf_op jit(solution)/shard_map/ppermute | solution.py:327
  72.3 12.7 %collective-permute-start.18 = (f32[2,4,128,128]{3,2,1,0:T(8,128)S(1)}, f32[2,4,128,128]{3,2,1,0:T(8,128)S(1)}, u32[]{:S(2)}, u32[]{:S(2)}) collective-permute-start(f32[2,4,128,128]{3,2,1,0:T(8,128)S(1)} %get-tuple-element.19), channel_id=1, source_target_pairs={{0,127},{1,64},{2,65},{3,66},{4,67},{5,68},{6,69},{7,70},{8,71},{9... | collective-permute-start | bytes 1572872 | tf_op jit(solution)/shard_map/ppermute | solution.py:327
  73.6 17.0 %collective-permute-start.17 = (f32[2,4,128,128]{3,2,1,0:T(8,128)S(1)}, f32[2,4,128,128]{3,2,1,0:T(8,128)S(1)}, u32[]{:S(2)}, u32[]{:S(2)}) collective-permute-start(f32[2,4,128,128]{3,2,1,0:T(8,128)S(1)} %get-tuple-element.19), channel_id=1, source_target_pairs={{0,65},{1,66},{2,67},{3,68},{4,69},{5,70},{6,71},{7,72},{8,73},{9,... | collective-permute-start | bytes 1572872 | tf_op jit(solution)/shard_map/ppermute | solution.py:327
  74.9 15.7 %collective-permute-start.16 = (f32[2,4,128,128]{3,2,1,0:T(8,128)S(1)}, f32[2,4,128,128]{3,2,1,0:T(8,128)S(1)}, u32[]{:S(2)}, u32[]{:S(2)}) collective-permute-start(f32[2,4,128,128]{3,2,1,0:T(8,128)S(1)} %get-tuple-element.19), channel_id=1, source_target_pairs={{0,64},{1,65},{2,66},{3,67},{4,68},{5,69},{6,70},{7,71},{8,72},{9,... | collective-permute-start | bytes 1572872 | tf_op jit(solution)/shard_map/ppermute | solution.py:327
  91.8 5.8 %collective-permute-start.21 = (f32[1,4,128,128]{3,2,1,0:T(8,128)S(1)}, f32[1,4,128,128]{3,2,1,0:T(8,128)S(1)}, u32[]{:S(2)}, u32[]{:S(2)}) collective-permute-start(f32[1,4,128,128]{3,2,1,0:T(8,128)S(1)} %shard_map.58), channel_id=1, source_target_pairs={{0,128},{1,129},{2,130},{3,131},{4,132},{5,133},{6,134},{7,135},{8... | collective-permute-start | bytes 786440 | tf_op jit(solution)/shard_map/ppermute | solution.py:327
  94.4 6.1 %collective-permute-start.22 = (f32[1,4,128,128]{3,2,1,0:T(8,128)S(1)}, f32[1,4,128,128]{3,2,1,0:T(8,128)S(1)}, u32[]{:S(2)}, u32[]{:S(2)}) collective-permute-start(f32[1,4,128,128]{3,2,1,0:T(8,128)S(1)} %shard_map.59), channel_id=1, source_target_pairs={{0,128},{1,129},{2,130},{3,131},{4,132},{5,133},{6,134},{7,135},{8... | collective-permute-start | bytes 786440 | tf_op jit(solution)/shard_map/ppermute | solution.py:327

commit v7 on v6

v7 whole, which is shorter than its diff:
```python
from math import comb

import jax
import jax.numpy as jnp
from jax import lax
from jax.experimental import pallas as pl
from jax.experimental.pallas import tpu as pltpu
from jax.sharding import PartitionSpec as P

SUBSTEPS = 4
SWEEPS = 4
FINE_RATES = (0.4, 0.2)
TIME_STEP = 0.25
COARSE_STEP = SUBSTEPS * TIME_STEP
VMEM = pl.BlockSpec(memory_space=pltpu.VMEM)
SMEM = pl.BlockSpec(memory_space=pltpu.SMEM)
ANY = pl.BlockSpec(memory_space=pl.ANY)
AXES = ("tm", "space")
SETTLE = 10**9


ROWS = (16, 8)


def turned(row, shift):
    return pltpu.roll(row, shift % row.shape[1], 1)


class Rows:
    def __init__(self, make):
        self.make = make
        self.made = {}

    def __getitem__(self, row):
        if row not in self.made:
            if row == ROWS[0]:
                self.made[row] = pltpu.roll(self[0], ROWS[1] - 1, 0)
            elif row == -1:
                self.made[row] = pltpu.roll(self[ROWS[0] - 1], 1, 0)
            else:
                self.made[row] = self.make(row)
        return self.made[row]


def fine_layer(below, centre, above, constants, target):
    spread = []
    for species, rate in enumerate(FINE_RATES):

        def column(row, species=species):
            value = centre[species][row]
            return (below[species][row] + above[species][row]) + (value + value)

        columns = Rows(column)
        pairs = Rows(lambda row, columns=columns: columns[row] + columns[row + 1])
        spread.append((rate, pairs))
    for row in range(ROWS[0]):
        sums = []
        for rate, pairs in spread:
            value = pairs[row - 1] + pairs[row]
            value = value + turned(value, 1)
            sums.append((rate / 16.0) * (value + turned(value, -1)))
        substrate, catalyst = centre[0][row], centre[1][row]
        encounter = (substrate * catalyst) * (TIME_STEP * catalyst)
        keep_first, fed, keep_second = [part[row] for part in constants]
        target[0][row] = keep_first * substrate + (fed + sums[0]) - encounter
        target[1][row] = keep_second * catalyst + (sums[1] + encounter)


def explicit_rows(substrate, catalyst, feed, kill):
    encounter = substrate * catalyst * catalyst
    first = (1.0 - COARSE_STEP * feed) * substrate + (COARSE_STEP * feed - COARSE_STEP * encounter)
    second = (1.0 - COARSE_STEP * (feed + kill)) * catalyst + COARSE_STEP * encounter
    return first, second


def explicit_layer(state, coefficient, target):
    for row in range(ROWS[0]):
        target[0][row], target[1][row] = explicit_rows(
            state[0][row], state[1][row], coefficient[0][row], coefficient[1][row]
        )


def joined(low, own, high, depth):
    def layer_of(which, layer):
        part = (low, own, high)[layer // depth]
        return part.at[which, layer % depth]

    return layer_of


def fine_levels(layer_of, coefficient, levels, constants, out, depth, rolled):
    count = 3 * depth - 2
    for layer in range(count):
        for row in range(ROWS[0]):
            feed = TIME_STEP * coefficient(0, layer + 1)[row]
            both = feed + TIME_STEP * coefficient(1, layer + 1)[row]
            constants[0, layer, row] = (1.0 - 4.0 * FINE_RATES[0]) - feed
            constants[1, layer, row] = feed
            constants[2, layer, row] = (1.0 - 4.0 * FINE_RATES[1]) - both
    for substep in range(SUBSTEPS):
        target = out if substep == SUBSTEPS - 1 else levels[substep % 2]

        def step(layer, source, target=target, substep=substep):
            fine_layer(
                *[[source(species, layer + shift) for species in (0, 1)] for shift in (0, 1, 2)],
                [constants.at[which, layer + substep] for which in (0, 1, 2)],
                [target.at[species, layer] for species in (0, 1)],
            )

        if substep == 0:
            for layer in range(count):
                step(layer, layer_of)
            continue
        count -= 2
        held = levels[(substep - 1) % 2]
        source = lambda species, layer, held=held: held.at[species, layer]
        if rolled:

            @pl.loop(0, count, step=2)
            def _(layer, step=step, source=source):
                step(layer, source)
                step(layer + 1, source)

        else:
            for layer in range(count):
                step(layer, source)


def sweep_weights(species):
    implicit = SUBSTEPS * FINE_RATES[species]
    scale = 1.0 / (1.0 + 6.0 * implicit)
    factor = implicit * scale
    powers = [scale * factor**power for power in range(SWEEPS)] + [factor**SWEEPS]
    weights = []
    for plane in range(SWEEPS + 1):
        line = [0.0] * (SWEEPS + 1 - plane)
        for power in range(plane, SWEEPS + 1):
            along = power - plane
            for distance in range(along, -1, -2):
                ways = comb(power, plane) * comb(along, (along - distance) // 2)
                line[distance] += powers[power] * ways
        weights.append(line)
    return weights


def coarse_layer(species, layer_of, layer, put):
    weights = sweep_weights(species)
    centre = layer_of(species, layer)
    sides = [
        (layer_of(species, layer - distance), layer_of(species, layer + distance))
        for distance in range(1, SWEEPS + 1)
    ]
    terms = [[None] * ROWS[0] for _ in range(SWEEPS)]
    first = [None] * ROWS[0]
    for row in range(ROWS[0]):
        sums = [centre[row]] + [below[row] + above[row] for below, above in sides]
        first[row] = weights[SWEEPS][0] * sums[0]
        for plane in range(SWEEPS):
            line = weights[plane]
            total = line[0] * sums[0]
            for distance in range(1, len(line)):
                total = total + line[distance] * sums[distance]
            terms[plane][row] = total
    held = Rows(lambda row, made=first: made[row])
    for plane in range(SWEEPS - 1, -1, -1):
        made = []
        for row in range(ROWS[0]):
            value = held[row]
            around = (held[row - 1] + held[row + 1]) + (turned(value, 1) + turned(value, -1))
            made.append(around + terms[plane][row])
        held = Rows(lambda row, made=made: made[row])
    for row in range(ROWS[0]):
        put(row, held[row])


def fine_kernel(
    worker, position, low, own, high, low_c, own_c, high_c, explicit, state, level_a, level_b, constants
):
    depth = own.shape[1]

    @pl.when((position[0] >= worker[0]) & (position[0] <= worker[-1]))
    def _():
        coefficient = joined(low_c, own_c, high_c, depth)
        layer_of = joined(low, own, high, depth)
        fine_levels(layer_of, coefficient, (level_a, level_b), constants, state, depth, False)
        for layer in range(depth):
            explicit_layer(
                [state.at[species, layer] for species in (0, 1)],
                [own_c.at[which, layer] for which in (0, 1)],
                [explicit.at[species, layer] for species in (0, 1)],
            )


def correction_kernel(
    worker,
    position,
    low,
    own,
    high,
    low_c,
    own_c,
    high_c,
    correction,
    level_a,
    level_b,
    constants,
    wide,
):
    depth = own.shape[1]

    @pl.when((position[0] >= worker[0]) & (position[0] <= worker[-1]))
    def _():
        coefficient = joined(low_c, own_c, high_c, depth)
        layer_of = joined(low, own, high, depth)
        fine_levels(layer_of, coefficient, (level_a, level_b), constants, correction, depth, True)
        for layer in range(3 * depth):
            explicit_layer(
                [layer_of(species, layer) for species in (0, 1)],
                [coefficient(which, layer) for which in (0, 1)],
                [wide.at[species, layer] for species in (0, 1)],
            )

        @pl.loop(0, depth, step=2)
        def _(first):
            for layer in (first, first + 1):
                for species in (0, 1):
                    target = correction.at[species, layer]

                    def put(row, value, target=target):
                        target[row] = target[row] - value

                    coarse_layer(
                        species, lambda which, place: wide.at[which, place], layer + depth, put
                    )


def coarse_kernel(worker, position, low, high, own, correction, own_c, explicit, state):
    depth = own.shape[1]

    @pl.when((position[0] >= worker[0]) & (position[0] <= worker[-1]))
    def _():
        layer_of = joined(low, own, high, depth)
        for layer in range(depth):
            for species in (0, 1):
                target, added = state.at[species, layer], correction.at[species, layer]

                def put(row, value, target=target, added=added):
                    target[row] = value + added[row]

                coarse_layer(species, layer_of, layer + depth, put)
            explicit_layer(
                [state.at[species, layer] for species in (0, 1)],
                [own_c.at[which, layer] for which in (0, 1)],
                [explicit.at[species, layer] for species in (0, 1)],
            )


def last_kernel(chosen, position, low, high, own, correction, third, state):
    depth = own.shape[1]

    @pl.when(position[0] != 1)
    def _():
        state[0] = third[chosen]

    @pl.when(position[0] == 1)
    def _():
        layer_of = joined(low, own, high, depth)
        for layer in range(depth):

            def put(row, value, layer=layer):
                state[0, layer, row] = value + correction[chosen, layer, row]

            coarse_layer(chosen, layer_of, layer + depth, put)


def result_kernel(position, first, second, received_a, received_b, result):
    def put(parts):
        for species in (0, 1):
            array, place = parts[species]
            for layer in range(result.shape[1]):
                for row in range(ROWS[0]):
                    result[species, layer, pl.ds(row, ROWS[1], stride=ROWS[0]), :] = array[
                        place, layer, row
                    ]

    @pl.when(position[0] == 0)
    def _():
        put([(first, 0), (first, 1)])

    @pl.when(position[0] == 1)
    def _():
        put([(second, 0), (second, 1)])

    @pl.when(position[0] > 1)
    def _():
        put([(received_a, 0), (received_b, 0)])


def entry_kernel(state, feed, kill, both, own, held_c, held, arrived):
    parts = ((feed, held_c.at[0]), (kill, held_c.at[1]), (state, held))
    copies = [
        pltpu.make_async_copy(source, target, arrived.at[index])
        for index, (source, target) in enumerate(parts)
    ]
    for copy in copies:
        copy.start()

    def put(array, target):
        for species in (0, 1):
            for layer in range(state.shape[1]):
                for row in range(ROWS[0]):
                    rows = pl.ds(row, ROWS[1], stride=ROWS[0])
                    target[species, layer, row] = array[species, layer, rows, :]

    copies[0].wait()
    copies[1].wait()
    put(held_c, both)
    copies[2].wait()
    put(held, own)


def entered(state, feed, kill):
    depth, _, columns = feed.shape
    shape = pltpu.VMEM((2, depth, *ROWS, columns), feed.dtype)
    return pl.pallas_call(
        entry_kernel,
        out_shape=[shape, shape],
        in_specs=[ANY] * 3,
        out_specs=[VMEM] * 2,
        scratch_shapes=[
            pltpu.VMEM(state.shape, state.dtype),
            pltpu.VMEM(state.shape, state.dtype),
            pltpu.SemaphoreType.DMA((3,)),
        ],
        compiler_params=pltpu.CompilerParams(vmem_limit_bytes=4 * 2**20),
        cost_estimate=pl.CostEstimate(flops=10**5, bytes_accessed=2**20, transcendentals=0),
    )(*[pltpu.with_memory_space_constraint(array, pltpu.HBM) for array in (state, feed, kill)])


LEVELS = ("level_a", "level_b")


def pick_kernel(flag, array, other, picked):
    @pl.when(flag[0] != 0)
    def _():
        picked[...] = array[...]

    @pl.when(flag[0] == 0)
    def _():
        picked[...] = other[...]


def run(
    body, position, operands, outputs, scratch=(), worker=None, tokens=(), species=2, result=None, settling=False
):
    depth, plane = operands[0].shape[1], operands[0].shape[2:]
    if result is None:
        out_shape = [pltpu.VMEM((species, depth, *plane), jnp.float32)] * outputs
    else:
        out_shape = [result]
    wide = 3 * depth
    shapes = {"level_a": (2, wide - 2), "level_b": (2, wide - 4), "constants": (3, wide - 2)}
    shapes["wide"] = (2, wide)
    operands = [pltpu.with_memory_space_constraint(array, pltpu.VMEM) for array in operands]

    count = 1 + len(operands)

    def kernel(*refs):
        refs = refs[:count] + refs[count + len(tokens) :]
        body(*(() if worker is None else (worker,)), *refs)

    return pl.pallas_call(
        kernel,
        out_shape=out_shape,
        in_specs=[SMEM] + [VMEM] * len(operands) + [ANY] * len(tokens),
        out_specs=[VMEM] * outputs,
        scratch_shapes=[pltpu.VMEM((*shapes[name], *plane), jnp.float32) for name in scratch],
        compiler_params=pltpu.CompilerParams(vmem_limit_bytes=10 * 2**20),
        cost_estimate=pl.CostEstimate(
            flops=10**10 if worker is not None else SETTLE if settling else 10**5,
            bytes_accessed=2**20,
            transcendentals=0,
        ),
    )(position, *operands, *tokens)


def copy_kernel(array, token, copied):
    copied[...] = array[...]


def after(array, token):
    return pl.pallas_call(
        copy_kernel,
        out_shape=pltpu.VMEM(array.shape, array.dtype),
        in_specs=[VMEM, ANY],
        out_specs=VMEM,
        compiler_params=pltpu.CompilerParams(vmem_limit_bytes=4 * 2**20),
        cost_estimate=pl.CostEstimate(flops=10**5, bytes_accessed=2**20, transcendentals=0),
    )(pltpu.with_memory_space_constraint(array, pltpu.VMEM), token)


def settle_kernel(flag, *refs):
    for source, target in zip(refs[: len(refs) // 2], refs[len(refs) // 2 :]):
        target[...] = source[...]


def settled(*arrays):
    flag = jnp.zeros(1, jnp.int32)
    return run(settle_kernel, flag, arrays, len(arrays), settling=True)


def pick(flag, array, other, tokens=()):
    flag = flag.astype(jnp.int32).reshape(1)
    return run(pick_kernel, flag, (array, other), 1, tokens=tokens)[0]


def shards(starts, feed, kill):
    own = starts[0]
    slabs = lax.axis_size("space")
    ring = 4
    index = lax.axis_index("tm")
    position = index.astype(jnp.int32).reshape(1)
    place = lax.axis_index("space") % ring

    def moved(array, target_of):
        pairs = []
        for source in range(4):
            for slab in range(slabs):
                target = target_of(source, slab)
                if target is not None:
                    pairs.append((source * slabs + slab, target[0] * slabs + target[1] % slabs))
        return lax.ppermute(array, AXES, pairs)

    def beside(slab, step):
        return slab // ring * ring + (slab + step) % ring

    def halves(source, slab):
        step = 1 if source % 2 == 0 else -1
        return source, slab + step if source < 2 else beside(slab, step)

    def onward(first, step):
        def target_of(source, slab):
            if source == first:
                return source, slab + step
            return (source, beside(slab, step)) if source == first + 2 else None

        return target_of

    def far_half(source, slab):
        if source == 2 and slab % ring == 0:
            return source, slab + ring
        if source == 3 and slab % ring == ring - 1:
            return source, slab - ring
        return None

    def far(position):
        def target_of(source, slab):
            if source == position and slab % ring == 0:
                return source, slab + ring
            if source == position and slab % ring == ring - 1:
                return source, slab - ring
            return None

        return target_of

    def swapped(source, slab):
        return source ^ 1, slab

    def route(source, target, shift=0):
        return lambda origin, slab: (target, slab + shift) if origin == source else None

    def spread(array, source, target, filled=False):
        def upper(origin, slab):
            if origin == source:
                return target, slab - 1
            return (origin ^ 1, slab) if filled else None

        low = moved(array, route(source, target, 1))
        high = moved(array, upper)
        return low, high, moved(array, route(source, target))

    both, own = entered(own, feed, kill)
    half = moved(both, halves)
    low = moved(own, onward(0, 1))
    high = moved(own, onward(0, -1))
    other = moved(half, swapped)
    half_far = moved(half, far_half)
    own_b = after(own, half)
    low_b = moved(own_b, onward(1, 1))
    high_b = moved(own_b, onward(1, -1))
    lowest, highest = place == 0, place == ring - 1
    low, high = settled(low, high)
    outer_2 = moved(pick(lowest, low, high), far(2))
    explicit, first_end = run(
        fine_kernel,
        position,
        (low, own, high, half, both, other),
        2,
        (*LEVELS, "constants"),
        worker=(0,),
        tokens=(own_b,),
    )
    second = spread(explicit, 0, 1)
    mended = pick((lowest & (index == 2)) | (highest & (index == 3)), half_far, half)
    other_x = moved(mended, lambda source, slab: swapped(source, slab) if source >= 2 else None)
    outer_3 = moved(pick(lowest, low_b, high_b, (explicit,)), far(3))
    even = index % 2 == 0
    other = pick(index == 1, other, other_x)
    low_c = pick(even, mended, other)
    high_c = pick(even, other, mended)
    low_2 = pick(index == 1, low_b, pick(lowest, outer_2, low))
    high_2 = pick(index == 1, high_b, pick(highest, outer_2, high))
    (correction,) = run(
        correction_kernel,
        position,
        (low_2, own, high_2, low_c, both, high_c),
        1,
        (*LEVELS, "constants", "wide"),
        worker=(1, 2),
    )
    (crossed_2,) = settled(moved(correction, route(2, 0)))
    low_3 = pick(lowest, outer_3, low_b)
    high_3 = pick(highest, outer_3, high_b)
    (correction_3,) = run(
        correction_kernel,
        position,
        (low_3, own, high_3, low_c, both, high_c),
        1,
        (*LEVELS, "constants", "wide"),
        worker=(3, 3),
    )
    explicit, second_end = run(
        coarse_kernel, position, (*second, correction, both), 2, worker=(1,)
    )
    third = spread(explicit, 1, 0)
    crossed_3 = moved(after(correction_3, third[0]), route(3, 1))
    explicit, third_end = run(
        coarse_kernel, position, (*third, crossed_2, both), 2, worker=(0,)
    )
    fourth = spread(explicit, 0, 1, True)
    received = []
    for chosen in (0, 1):
        (last_end,) = run(
            last_kernel, position, (*fourth, crossed_3, third_end), 1, worker=chosen, species=1
        )
        received.append(
            moved(last_end, lambda source, slab: (source ^ 2, slab))
        )
    (result,) = run(
        result_kernel,
        position,
        (first_end, second_end, *received),
        1,
        result=jax.ShapeDtypeStruct(starts.shape[1:], starts.dtype),
    )
    return result[None]


def solution(mesh):
    placed = (P("tm", None, "space", None, None), P("space", None, None), P("space", None, None))
    return jax.shard_map(
        shards,
        mesh=mesh,
        in_specs=placed,
        out_specs=P("tm", None, "space", None, None),
        check_vma=False,
    )
```

time: 102 us -> 93.4 us (0.916)
  waiting for transfers between devices: 39.2 us -> 30.1 us
  starting transfers between devices: 45.2 us -> 48.4 us
  Pallas kernels: 16.4 us -> 14.1 us
    ppermute x23, waiting for transfers between devices: 39.2 us -> 30.1 us  [moved(): return lax.ppermute(array, AXES, pairs)]
    ppermute x23, starting transfers between devices: 45.2 us -> 48.4 us  [moved(): return lax.ppermute(array, AXES, pairs)]
    pallas_call x21 -> x22, Pallas kernels: 15.3 us -> 12.6 us  [run(): pl.pallas_call(kernel, out_shape=out_shape, in_specs=[SMEM] + [VMEM] * le...]
  transfers between devices with their start and end apart: 23 -> 23, of which waited for: 9 -> 9; matrix products, arithmetic and copies ran while one was open for 0% -> 0% of each run, Pallas kernels for 13% -> 12%
where the time goes in v7:
time: 93.4 us; the launch traced here: 92.9 us
  starting transfers between devices  48.4 us (52%)
  waiting for transfers between devices  30.1 us (32%)
  Pallas kernels  14.1 us (15%)
    ppermute x23, starting transfers between devices, moved(): return lax.ppermute(array, AXES, pairs)  48.4 us
    ppermute x23, waiting for transfers between devices, moved(): return lax.ppermute(array, AXES, pairs)  30.1 us
    pallas_call x22, Pallas kernels, run(): pl.pallas_call(kernel, out_shape=out_shape, in_specs=[SMEM] + [VMEM] * le...  12.6 us
  transfers between devices with their start and end apart: 23, of which 9 were waited for; matrix products, arithmetic and copies ran while one was open for 0% of the time, Pallas kernels for 12%

profile of v7, /device:TPU:1, one launch (start us, length us, event | category | flops | bytes accessed | tf_op | source)
XLA Modules:
  0.0 92.9 jit_solution(5514655404045543583)
XLA Ops:
  0.0 1.4 %shard_map.37 = (f32[2,4,16,8,128]{4,3,2,1,0:T(8,128)S(1)}, f32[2,4,16,8,128]{4,3,2,1,0:T(8,128)S(1)}) custom-call(f32[2,4,128,128]{3,2,1,0:T(8,128)} %bitcast.8, f32[4,128,128]{2,1,0:T(8,128)} %feed.1, f32[4,128,128]{2,1,0:T(8,128)} %kill.1), custom_call_target="tpu_custom_call" | custom-call | flops 100000 | bytes 1048576 | tf_op jit(solution)/shard_map/pallas_call | solution.py:325
  1.4 11.6 %collective-permute-start.2 = (f32[2,4,16,8,128]{4,3,2,1,0:T(8,128)S(1)}, f32[2,4,16,8,128]{4,3,2,1,0:T(8,128)S(1)}, u32[]{:S(2)}, u32[]{:S(2)}) collective-permute-start(f32[2,4,16,8,128]{4,3,2,1,0:T(8,128)S(1)} %get-tuple-element.18.refs_5_), channel_id=1, source_target_pairs={{0,1},{1,2},{2,3},{3,4},{4,5},{5,6},{6,7},{7,8},{8,9},{9,10},{10,1... | collective-permute-start | bytes 1572872 | tf_op jit(solution)/shard_map/ppermute | solution.py:432
  13.0 0.7 collective-permute-start
  13.7 1.5 %collective-permute-start.1 = (f32[2,4,16,8,128]{4,3,2,1,0:T(8,128)S(1)}, f32[2,4,16,8,128]{4,3,2,1,0:T(8,128)}, u32[]{:S(2)}, u32[]{:S(2)}) collective-permute-start(f32[2,4,16,8,128]{4,3,2,1,0:T(8,128)S(1)} %get-tuple-element.15.array.refs_2_), channel_id=1, source_target_pairs={{0,63},{1,0},{2,1},{3,2},{4,3},{5,4},{6,5},{7,6},{8,7},{9,8},{10,9... | collective-permute-start | bytes 1572872 | tf_op jit(solution)/shard_map/ppermute | solution.py:432
  15.1 4.5 %collective-permute-done.2.token.refs_4_.refs_2_ = f32[2,4,16,8,128]{4,3,2,1,0:T(8,128)S(1)} collective-permute-done((f32[2,4,16,8,128]{4,3,2,1,0:T(8,128)S(1)}, f32[2,4,16,8,128]{4,3,2,1,0:T(8,128)S(1)}, u32[]{:S(2)}, u32[]{:S(2)}) %collective-permute-start.2) | collective-permute-done | bytes 524320 | tf_op jit(solution)/shard_map/ppermute | solution.py:432
  19.7 0.7 collective-permute-start.10
  20.4 1.5 %collective-permute-start.3 = (f32[2,4,16,8,128]{4,3,2,1,0:T(8,128)S(1)}, f32[2,4,16,8,128]{4,3,2,1,0:T(8,128)S(1)}, u32[]{:S(2)}, u32[]{:S(2)}) collective-permute-start(f32[2,4,16,8,128]{4,3,2,1,0:T(8,128)S(1)} %collective-permute-done.2.token.refs_4_.refs_2_), channel_id=1, source_target_pairs={{0,64},{1,65},{2,66},{3,67},{4,68},{5,69},{6,70},{7,71},{8,72},{9,... | collective-permute-start | bytes 1572872 | tf_op jit(solution)/shard_map/ppermute | solution.py:432
  21.9 1.9 %collective-permute-start.7 = (f32[2,4,16,8,128]{4,3,2,1,0:T(8,128)S(1)}, f32[2,4,16,8,128]{4,3,2,1,0:T(8,128)S(1)}, u32[]{:S(2)}, u32[]{:S(2)}) collective-permute-start(f32[2,4,16,8,128]{4,3,2,1,0:T(8,128)S(1)} %shard_map.39.refs_7_), channel_id=1, source_target_pairs={{64,65},{65,66},{66,67},{67,68},{68,69},{69,70},{70,71},{71,72},{7... | collective-permute-start | bytes 1572872 | tf_op jit(solution)/shard_map/ppermute | solution.py:432
  23.8 0.0 collective-permute-done.refs_1_
  23.8 9.7 %collective-permute-start.9 = (f32[2,4,16,8,128]{4,3,2,1,0:T(8,128)S(1)}, f32[2,4,16,8,128]{4,3,2,1,0:T(8,128)S(1)}, u32[]{:S(2)}, u32[]{:S(2)}) collective-permute-start(f32[2,4,16,8,128]{4,3,2,1,0:T(8,128)S(1)} %shard_map.39.refs_7_), channel_id=1, source_target_pairs={{64,127},{65,64},{66,65},{67,66},{68,67},{69,68},{70,69},{71,70},{... | collective-permute-start | bytes 1572872 | tf_op jit(solution)/shard_map/ppermute | solution.py:432
  33.5 0.0 collective-permute-done.1.refs_2_
  33.6 1.1 %shard_map.38 = (f32[2,4,16,8,128]{4,3,2,1,0:T(8,128)S(1)}, f32[2,4,16,8,128]{4,3,2,1,0:T(8,128)S(1)}) custom-call(s32[1]{0:T(128)} %constant.30.clone.1.refs_0_, f32[2,4,16,8,128]{4,3,2,1,0:T(8,128)S(1)} %collective-permute-done.refs_1_, f32[2,4,16,8,128]{4,3,2,1,0:T(8,128)} %collective-permute-done.1.refs_2_), custom_call_target="tpu_custom_call" | custom-call | flops 1000000000 | bytes 1048576 | tf_op jit(solution)/shard_map/pallas_call | solution.py:372
  34.7 0.7 collective-permute-start.8
  35.4 0.0 collective-permute-done.10.refs_1_
  35.5 0.7 collective-permute-start.11
  36.2 0.0 collective-permute-done.3.refs_6_.refs_1_
  36.2 1.3 %collective-permute-start.4 = (f32[2,4,16,8,128]{4,3,2,1,0:T(8,128)S(1)}, f32[2,4,16,8,128]{4,3,2,1,0:T(8,128)S(1)}, u32[]{:S(2)}, u32[]{:S(2)}) collective-permute-start(f32[2,4,16,8,128]{4,3,2,1,0:T(8,128)S(1)} %get-tuple-element.20.refs_3_), channel_id=1, source_target_pairs={{0,65},{1,66},{2,67},{3,68},{4,69},{5,70},{6,71},{7,72},{8,73},{9,... | collective-permute-start | bytes 1572872 | tf_op jit(solution)/shard_map/ppermute | solution.py:432
  37.5 0.6 collective-permute-done.7.refs_1_.refs_2_
  38.2 1.3 %collective-permute-start.5 = (f32[2,4,16,8,128]{4,3,2,1,0:T(8,128)S(1)}, f32[2,4,16,8,128]{4,3,2,1,0:T(8,128)S(1)}, u32[]{:S(2)}, u32[]{:S(2)}) collective-permute-start(f32[2,4,16,8,128]{4,3,2,1,0:T(8,128)S(1)} %get-tuple-element.20.refs_3_), channel_id=1, source_target_pairs={{0,127},{1,64},{2,65},{3,66},{4,67},{5,68},{6,69},{7,70},{8,71},{9... | collective-permute-start | bytes 1572872 | tf_op jit(solution)/shard_map/ppermute | solution.py:432
  39.5 0.2 collective-permute-done.9.refs_1_.refs_2_
  39.7 1.3 %collective-permute-start.6 = (f32[2,4,16,8,128]{4,3,2,1,0:T(8,128)S(1)}, f32[2,4,16,8,128]{4,3,2,1,0:T(8,128)S(1)}, u32[]{:S(2)}, u32[]{:S(2)}) collective-permute-start(f32[2,4,16,8,128]{4,3,2,1,0:T(8,128)S(1)} %get-tuple-element.20.refs_3_), channel_id=1, source_target_pairs={{0,64},{1,65},{2,66},{3,67},{4,68},{5,69},{6,70},{7,71},{8,72},{9,... | collective-permute-start | bytes 1572872 | tf_op jit(solution)/shard_map/ppermute | solution.py:432
  41.0 0.0 collective-permute-done.8.refs_1_
  41.0 0.7 collective-permute-start.19
  41.9 0.0 collective-permute-done.11.refs_2_
  42.1 5.8 %shard_map.50.refs_4_ = f32[2,4,16,8,128]{4,3,2,1,0:T(8,128)S(1)} custom-call(s32[1]{0:T(128)} %bitcast.refs_0_, f32[2,4,16,8,128]{4,3,2,1,0:T(8,128)S(1)} %shard_map.43.refs_1_, f32[2,4,16,8,128]{4,3,2,1,0:T(8,128)S(1)} %get-tuple-element.15.array.refs_2_, f32[2,4,16,8,128]{4,3,2,1,0:T(8,128)S(1)} %shard_map.45.refs_3_, ...), custom_call_target="tpu_custom_call" | custom-call | flops 10000000000 | bytes 1048576 | tf_op jit(solution)/shard_map/pallas_call | solution.py:372
  47.9 5.2 %collective-permute-done.4.refs_1_ = f32[2,4,16,8,128]{4,3,2,1,0:T(8,128)S(1)} collective-permute-done((f32[2,4,16,8,128]{4,3,2,1,0:T(8,128)S(1)}, f32[2,4,16,8,128]{4,3,2,1,0:T(8,128)S(1)}, u32[]{:S(2)}, u32[]{:S(2)}) %collective-permute-start.4) | collective-permute-done | bytes 524320 | tf_op jit(solution)/shard_map/ppermute | solution.py:432
  53.1 0.0 collective-permute-done.5.refs_2_
  53.1 0.0 collective-permute-done.6.refs_3_
  53.1 2.0 %shard_map.51 = (f32[2,4,16,8,128]{4,3,2,1,0:T(8,128)S(1)}, f32[2,4,16,8,128]{4,3,2,1,0:T(8,128)S(1)}) custom-call(s32[1]{0:T(128)} %bitcast.refs_0_, f32[2,4,16,8,128]{4,3,2,1,0:T(8,128)S(1)} %collective-permute-done.4.refs_1_, f32[2,4,16,8,128]{4,3,2,1,0:T(8,128)S(1)} %collective-permute-done.5.refs_2_, ...), custom_call_target="tpu_custom_call" | custom-call | flops 10000000000 | bytes 1048576 | tf_op jit(solution)/shard_map/pallas_call | solution.py:372
  55.1 1.3 %collective-permute-start.12 = (f32[2,4,16,8,128]{4,3,2,1,0:T(8,128)S(1)}, f32[2,4,16,8,128]{4,3,2,1,0:T(8,128)S(1)}, u32[]{:S(2)}, u32[]{:S(2)}) collective-permute-start(f32[2,4,16,8,128]{4,3,2,1,0:T(8,128)S(1)} %get-tuple-element.22), channel_id=1, source_target_pairs={{64,1},{65,2},{66,3},{67,4},{68,5},{69,6},{70,7},{71,8},{72,9},{73... | collective-permute-start | bytes 1572872 | tf_op jit(solution)/shard_map/ppermute | solution.py:432
  56.4 1.3 %collective-permute-start.13 = (f32[2,4,16,8,128]{4,3,2,1,0:T(8,128)S(1)}, f32[2,4,16,8,128]{4,3,2,1,0:T(8,128)S(1)}, u32[]{:S(2)}, u32[]{:S(2)}) collective-permute-start(f32[2,4,16,8,128]{4,3,2,1,0:T(8,128)S(1)} %get-tuple-element.22), channel_id=1, source_target_pairs={{64,63},{65,0},{66,1},{67,2},{68,3},{69,4},{70,5},{71,6},{72,7},{7... | collective-permute-start | bytes 1572872 | tf_op jit(solution)/shard_map/ppermute | solution.py:432
  57.7 1.3 %collective-permute-start.14 = (f32[2,4,16,8,128]{4,3,2,1,0:T(8,128)S(1)}, f32[2,4,16,8,128]{4,3,2,1,0:T(8,128)S(1)}, u32[]{:S(2)}, u32[]{:S(2)}) collective-permute-start(f32[2,4,16,8,128]{4,3,2,1,0:T(8,128)S(1)} %get-tuple-element.22), channel_id=1, source_target_pairs={{64,0},{65,1},{66,2},{67,3},{68,4},{69,5},{70,6},{71,7},{72,8},{73... | collective-permute-start | bytes 1572872 | tf_op jit(solution)/shard_map/ppermute | solution.py:432
  59.1 0.7 collective-permute-start.15
  59.8 0.0 collective-permute-done.19.refs_1_
  59.9 0.2 shard_map.57.array
  60.1 2.4 %collective-permute-done.12.refs_1_.token = f32[2,4,16,8,128]{4,3,2,1,0:T(8,128)S(1)} collective-permute-done((f32[2,4,16,8,128]{4,3,2,1,0:T(8,128)S(1)}, f32[2,4,16,8,128]{4,3,2,1,0:T(8,128)S(1)}, u32[]{:S(2)}, u32[]{:S(2)}) %collective-permute-start.12) | collective-permute-done | bytes 524320 | tf_op jit(solution)/shard_map/ppermute | solution.py:432
  62.5 1.3 %collective-permute-start.20 = (f32[2,4,16,8,128]{4,3,2,1,0:T(8,128)S(1)}, f32[2,4,16,8,128]{4,3,2,1,0:T(8,128)S(1)}, u32[]{:S(2)}, u32[]{:S(2)}) collective-permute-start(f32[2,4,16,8,128]{4,3,2,1,0:T(8,128)S(1)} %shard_map.58), channel_id=1, source_target_pairs={{192,64},{193,65},{194,66},{195,67},{196,68},{197,69},{198,70},{19... | collective-permute-start | bytes 1572872 | tf_op jit(solution)/shard_map/ppermute | solution.py:432
  63.8 0.0 collective-permute-done.15.refs_1_
  63.9 0.0 collective-permute-done.13.refs_2_
  63.9 0.0 collective-permute-done.14.refs_3_
  63.9 1.3 %collective-permute-start.16 = (f32[2,4,16,8,128]{4,3,2,1,0:T(8,128)S(1)}, f32[2,4,16,8,128]{4,3,2,1,0:T(8,128)S(1)}, u32[]{:S(2)}, u32[]{:S(2)}) collective-permute-start(f32[2,4,16,8,128]{4,3,2,1,0:T(8,128)S(1)} %get-tuple-element.23), channel_id=1, source_target_pairs={{0,65},{1,66},{2,67},{3,68},{4,69},{5,70},{6,71},{7,72},{8,73},{9,... | collective-permute-start | bytes 1572872 | tf_op jit(solution)/shard_map/ppermute | solution.py:432
  65.2 5.7 %collective-permute-start.17 = (f32[2,4,16,8,128]{4,3,2,1,0:T(8,128)S(1)}, f32[2,4,16,8,128]{4,3,2,1,0:T(8,128)S(1)}, u32[]{:S(2)}, u32[]{:S(2)}) collective-permute-start(f32[2,4,16,8,128]{4,3,2,1,0:T(8,128)S(1)} %get-tuple-element.23), channel_id=1, source_target_pairs={{0,127},{1,64},{2,65},{3,66},{4,67},{5,68},{6,69},{7,70},{8,71},{9... | collective-permute-start | bytes 1572872 | tf_op jit(solution)/shard_map/ppermute | solution.py:432
  71.0 1.3 %collective-permute-start.18 = (f32[2,4,16,8,128]{4,3,2,1,0:T(8,128)S(1)}, f32[2,4,16,8,128]{4,3,2,1,0:T(8,128)S(1)}, u32[]{:S(2)}, u32[]{:S(2)}) collective-permute-start(f32[2,4,16,8,128]{4,3,2,1,0:T(8,128)S(1)} %get-tuple-element.23), channel_id=1, source_target_pairs={{0,64},{1,65},{2,66},{3,67},{4,68},{5,69},{6,70},{7,71},{8,72},{9,... | collective-permute-start | bytes 1572872 | tf_op jit(solution)/shard_map/ppermute | solution.py:432
  72.2 1.5 %collective-permute-done.20.refs_4_ = f32[2,4,16,8,128]{4,3,2,1,0:T(8,128)S(1)} collective-permute-done((f32[2,4,16,8,128]{4,3,2,1,0:T(8,128)S(1)}, f32[2,4,16,8,128]{4,3,2,1,0:T(8,128)S(1)}, u32[]{:S(2)}, u32[]{:S(2)}) %collective-permute-start.20) | collective-permute-done | bytes 524320 | tf_op jit(solution)/shard_map/ppermute | solution.py:432
  73.8 9.1 %collective-permute-done.16.refs_1_ = f32[2,4,16,8,128]{4,3,2,1,0:T(8,128)S(1)} collective-permute-done((f32[2,4,16,8,128]{4,3,2,1,0:T(8,128)S(1)}, f32[2,4,16,8,128]{4,3,2,1,0:T(8,128)S(1)}, u32[]{:S(2)}, u32[]{:S(2)}) %collective-permute-start.16) | collective-permute-done | bytes 524320 | tf_op jit(solution)/shard_map/ppermute | solution.py:432
  82.9 0.0 collective-permute-done.17.refs_2_
  82.9 0.0 collective-permute-done.18.refs_3_
  82.9 1.0 %shard_map.60 = f32[1,4,16,8,128]{4,3,2,1,0:T(8,128)S(1)} custom-call(s32[1]{0:T(128)} %bitcast.refs_0_, f32[2,4,16,8,128]{4,3,2,1,0:T(8,128)S(1)} %collective-permute-done.16.refs_1_, f32[2,4,16,8,128]{4,3,2,1,0:T(8,128)S(1)} %collective-permute-done.17.refs_2_, f32[2,4,16,8,128]{4,3,2,1,0:T(8,128)S(1)} %collective-permute-done.18.refs_3_, ...), custom_call_target="tpu_custom_call" | custom-call | flops 10000000000 | bytes 1048576 | tf_op jit(solution)/shard_map/pallas_call | solution.py:372
  83.9 0.1 collective-permute-start.22
  84.0 1.0 %shard_map.59 = f32[1,4,16,8,128]{4,3,2,1,0:T(8,128)S(1)} custom-call(s32[1]{0:T(128)} %bitcast.refs_0_, f32[2,4,16,8,128]{4,3,2,1,0:T(8,128)S(1)} %collective-permute-done.16.refs_1_, f32[2,4,16,8,128]{4,3,2,1,0:T(8,128)S(1)} %collective-permute-done.17.refs_2_, f32[2,4,16,8,128]{4,3,2,1,0:T(8,128)S(1)} %collective-permute-done.18.refs_3_, ...), custom_call_target="tpu_custom_call" | custom-call | flops 10000000000 | bytes 1048576 | tf_op jit(solution)/shard_map/pallas_call | solution.py:372
  85.0 0.6 collective-permute-start.21
  85.6 3.6 %collective-permute-done.22.refs_4_ = f32[1,4,16,8,128]{4,3,2,1,0:T(8,128)S(1)} collective-permute-done((f32[1,4,16,8,128]{4,3,2,1,0:T(8,128)S(1)}, f32[1,4,16,8,128]{4,3,2,1,0:T(8,128)S(1)}, u32[]{:S(2)}, u32[]{:S(2)}) %collective-permute-start.22) | collective-permute-done | bytes 262176 | tf_op jit(solution)/shard_map/ppermute | solution.py:432
  89.2 2.8 %collective-permute-done.21.refs_3_ = f32[1,4,16,8,128]{4,3,2,1,0:T(8,128)S(1)} collective-permute-done((f32[1,4,16,8,128]{4,3,2,1,0:T(8,128)S(1)}, f32[1,4,16,8,128]{4,3,2,1,0:T(8,128)S(1)}, u32[]{:S(2)}, u32[]{:S(2)}) %collective-permute-start.21) | collective-permute-done | bytes 262176 | tf_op jit(solution)/shard_map/ppermute | solution.py:432
  92.0 0.9 %shard_map.61 = f32[2,4,128,128]{3,2,1,0:T(8,128)} custom-call(s32[1]{0:T(128)} %bitcast.refs_0_, f32[2,4,16,8,128]{4,3,2,1,0:T(8,128)S(1)} %get-tuple-element.19.refs_1_, f32[2,4,16,8,128]{4,3,2,1,0:T(8,128)S(1)} %get-tuple-element.21.refs_2_, f32[1,4,16,8,128]{4,3,2,1,0:T(8,128)S(1)} %collective-permute-done.21.refs_3_, ...), custom_call_target="tpu_custom_call" | custom-call | flops 100000 | bytes 1048576 | tf_op jit(solution)/shard_map/pallas_call | solution.py:372
  (17 shorter events, 0.7 us)
Async XLA Ops:
  1.4 18.3 %collective-permute-start.2 = (f32[2,4,16,8,128]{4,3,2,1,0:T(8,128)S(1)}, f32[2,4,16,8,128]{4,3,2,1,0:T(8,128)S(1)}, u32[]{:S(2)}, u32[]{:S(2)}) collective-permute-start(f32[2,4,16,8,128]{4,3,2,1,0:T(8,128)S(1)} %get-tuple-element.18.refs_5_), channel_id=1, source_target_pairs={{0,1},{1,2},{2,3},{3,4},{4,5},{5,6},{6,7},{7,8},{8,9},{9,10},{10,1... | collective-permute-start | bytes 1572872 | tf_op jit(solution)/shard_map/ppermute | solution.py:432
  13.0 10.9 %collective-permute-start = (f32[2,4,16,8,128]{4,3,2,1,0:T(8,128)S(1)}, f32[2,4,16,8,128]{4,3,2,1,0:T(8,128)S(1)}, u32[]{:S(2)}, u32[]{:S(2)}) collective-permute-start(f32[2,4,16,8,128]{4,3,2,1,0:T(8,128)S(1)} %get-tuple-element.15.array.refs_2_), channel_id=1, source_target_pairs={{0,1},{1,2},{2,3},{3,4},{4,5},{5,6},{6,7},{7,8},{8,9},{9,10},{10,1... | collective-permute-start | bytes 1572872 | tf_op jit(solution)/shard_map/ppermute | solution.py:432
  13.7 19.9 %collective-permute-start.1 = (f32[2,4,16,8,128]{4,3,2,1,0:T(8,128)S(1)}, f32[2,4,16,8,128]{4,3,2,1,0:T(8,128)}, u32[]{:S(2)}, u32[]{:S(2)}) collective-permute-start(f32[2,4,16,8,128]{4,3,2,1,0:T(8,128)S(1)} %get-tuple-element.15.array.refs_2_), channel_id=1, source_target_pairs={{0,63},{1,0},{2,1},{3,2},{4,3},{5,4},{6,5},{7,6},{8,7},{9,8},{10,9... | collective-permute-start | bytes 1572872 | tf_op jit(solution)/shard_map/ppermute | solution.py:432
  19.7 15.8 %collective-permute-start.10 = (f32[2,4,16,8,128]{4,3,2,1,0:T(8,128)S(1)}, f32[2,4,16,8,128]{4,3,2,1,0:T(8,128)S(1)}, u32[]{:S(2)}, u32[]{:S(2)}) collective-permute-start(f32[2,4,16,8,128]{4,3,2,1,0:T(8,128)S(1)} %collective-permute-done.2.token.refs_4_.refs_2_), channel_id=1, source_target_pairs={{128,132},{132,136},{136,140},{140,144},{144,148},{148,152},{152,1... | collective-permute-start | bytes 1572872 | tf_op jit(solution)/shard_map/ppermute | solution.py:432
  20.4 15.8 %collective-permute-start.3 = (f32[2,4,16,8,128]{4,3,2,1,0:T(8,128)S(1)}, f32[2,4,16,8,128]{4,3,2,1,0:T(8,128)S(1)}, u32[]{:S(2)}, u32[]{:S(2)}) collective-permute-start(f32[2,4,16,8,128]{4,3,2,1,0:T(8,128)S(1)} %collective-permute-done.2.token.refs_4_.refs_2_), channel_id=1, source_target_pairs={{0,64},{1,65},{2,66},{3,67},{4,68},{5,69},{6,70},{7,71},{8,72},{9,... | collective-permute-start | bytes 1572872 | tf_op jit(solution)/shard_map/ppermute | solution.py:432
  21.9 16.3 %collective-permute-start.7 = (f32[2,4,16,8,128]{4,3,2,1,0:T(8,128)S(1)}, f32[2,4,16,8,128]{4,3,2,1,0:T(8,128)S(1)}, u32[]{:S(2)}, u32[]{:S(2)}) collective-permute-start(f32[2,4,16,8,128]{4,3,2,1,0:T(8,128)S(1)} %shard_map.39.refs_7_), channel_id=1, source_target_pairs={{64,65},{65,66},{66,67},{67,68},{68,69},{69,70},{70,71},{71,72},{7... | collective-permute-start | bytes 1572872 | tf_op jit(solution)/shard_map/ppermute | solution.py:432
  23.8 15.8 %collective-permute-start.9 = (f32[2,4,16,8,128]{4,3,2,1,0:T(8,128)S(1)}, f32[2,4,16,8,128]{4,3,2,1,0:T(8,128)S(1)}, u32[]{:S(2)}, u32[]{:S(2)}) collective-permute-start(f32[2,4,16,8,128]{4,3,2,1,0:T(8,128)S(1)} %shard_map.39.refs_7_), channel_id=1, source_target_pairs={{64,127},{65,64},{66,65},{67,66},{68,67},{69,68},{70,69},{71,70},{... | collective-permute-start | bytes 1572872 | tf_op jit(solution)/shard_map/ppermute | solution.py:432
  34.7 6.3 %collective-permute-start.8 = (f32[2,4,16,8,128]{4,3,2,1,0:T(8,128)S(1)}, f32[2,4,16,8,128]{4,3,2,1,0:T(8,128)S(1)}, u32[]{:S(2)}, u32[]{:S(2)}) collective-permute-start(f32[2,4,16,8,128]{4,3,2,1,0:T(8,128)S(1)} %shard_map.41), channel_id=1, source_target_pairs={{128,132},{131,191},{132,136},{135,131},{136,140},{139,135},{140,1... | collective-permute-start | bytes 1572872 | tf_op jit(solution)/shard_map/ppermute | solution.py:432
  35.5 6.4 %collective-permute-start.11 = (f32[2,4,16,8,128]{4,3,2,1,0:T(8,128)S(1)}, f32[2,4,16,8,128]{4,3,2,1,0:T(8,128)S(1)}, u32[]{:S(2)}, u32[]{:S(2)}) collective-permute-start(f32[2,4,16,8,128]{4,3,2,1,0:T(8,128)S(1)} %shard_map.46.refs_1_.refs_2_), channel_id=1, source_target_pairs={{128,192},{129,193},{130,194},{131,195},{132,196},{133,197},{134,1... | collective-permute-start | bytes 1572872 | tf_op jit(solution)/shard_map/ppermute | solution.py:432
  36.2 16.8 %collective-permute-start.4 = (f32[2,4,16,8,128]{4,3,2,1,0:T(8,128)S(1)}, f32[2,4,16,8,128]{4,3,2,1,0:T(8,128)S(1)}, u32[]{:S(2)}, u32[]{:S(2)}) collective-permute-start(f32[2,4,16,8,128]{4,3,2,1,0:T(8,128)S(1)} %get-tuple-element.20.refs_3_), channel_id=1, source_target_pairs={{0,65},{1,66},{2,67},{3,68},{4,69},{5,70},{6,71},{7,72},{8,73},{9,... | collective-permute-start | bytes 1572872 | tf_op jit(solution)/shard_map/ppermute | solution.py:432
  38.2 14.9 %collective-permute-start.5 = (f32[2,4,16,8,128]{4,3,2,1,0:T(8,128)S(1)}, f32[2,4,16,8,128]{4,3,2,1,0:T(8,128)S(1)}, u32[]{:S(2)}, u32[]{:S(2)}) collective-permute-start(f32[2,4,16,8,128]{4,3,2,1,0:T(8,128)S(1)} %get-tuple-element.20.refs_3_), channel_id=1, source_target_pairs={{0,127},{1,64},{2,65},{3,66},{4,67},{5,68},{6,69},{7,70},{8,71},{9... | collective-permute-start | bytes 1572872 | tf_op jit(solution)/shard_map/ppermute | solution.py:432
  39.7 13.4 %collective-permute-start.6 = (f32[2,4,16,8,128]{4,3,2,1,0:T(8,128)S(1)}, f32[2,4,16,8,128]{4,3,2,1,0:T(8,128)S(1)}, u32[]{:S(2)}, u32[]{:S(2)}) collective-permute-start(f32[2,4,16,8,128]{4,3,2,1,0:T(8,128)S(1)} %get-tuple-element.20.refs_3_), channel_id=1, source_target_pairs={{0,64},{1,65},{2,66},{3,67},{4,68},{5,69},{6,70},{7,71},{8,72},{9,... | collective-permute-start | bytes 1572872 | tf_op jit(solution)/shard_map/ppermute | solution.py:432
  41.0 18.8 %collective-permute-start.19 = (f32[2,4,16,8,128]{4,3,2,1,0:T(8,128)S(1)}, f32[2,4,16,8,128]{4,3,2,1,0:T(8,128)S(1)}, u32[]{:S(2)}, u32[]{:S(2)}) collective-permute-start(f32[2,4,16,8,128]{4,3,2,1,0:T(8,128)S(1)} %shard_map.54), channel_id=1, source_target_pairs={{192,196},{195,255},{196,200},{199,195},{200,204},{203,199},{204,2... | collective-permute-start | bytes 1572872 | tf_op jit(solution)/shard_map/ppermute | solution.py:432
  55.1 7.4 %collective-permute-start.12 = (f32[2,4,16,8,128]{4,3,2,1,0:T(8,128)S(1)}, f32[2,4,16,8,128]{4,3,2,1,0:T(8,128)S(1)}, u32[]{:S(2)}, u32[]{:S(2)}) collective-permute-start(f32[2,4,16,8,128]{4,3,2,1,0:T(8,128)S(1)} %get-tuple-element.22), channel_id=1, source_target_pairs={{64,1},{65,2},{66,3},{67,4},{68,5},{69,6},{70,7},{71,8},{72,9},{73... | collective-permute-start | bytes 1572872 | tf_op jit(solution)/shard_map/ppermute | solution.py:432
  56.4 7.5 %collective-permute-start.13 = (f32[2,4,16,8,128]{4,3,2,1,0:T(8,128)S(1)}, f32[2,4,16,8,128]{4,3,2,1,0:T(8,128)S(1)}, u32[]{:S(2)}, u32[]{:S(2)}) collective-permute-start(f32[2,4,16,8,128]{4,3,2,1,0:T(8,128)S(1)} %get-tuple-element.22), channel_id=1, source_target_pairs={{64,63},{65,0},{66,1},{67,2},{68,3},{69,4},{70,5},{71,6},{72,7},{7... | collective-permute-start | bytes 1572872 | tf_op jit(solution)/shard_map/ppermute | solution.py:432
  57.7 6.2 %collective-permute-start.14 = (f32[2,4,16,8,128]{4,3,2,1,0:T(8,128)S(1)}, f32[2,4,16,8,128]{4,3,2,1,0:T(8,128)S(1)}, u32[]{:S(2)}, u32[]{:S(2)}) collective-permute-start(f32[2,4,16,8,128]{4,3,2,1,0:T(8,128)S(1)} %get-tuple-element.22), channel_id=1, source_target_pairs={{64,0},{65,1},{66,2},{67,3},{68,4},{69,5},{70,6},{71,7},{72,8},{73... | collective-permute-start | bytes 1572872 | tf_op jit(solution)/shard_map/ppermute | solution.py:432
  59.1 4.8 %collective-permute-start.15 = (f32[2,4,16,8,128]{4,3,2,1,0:T(8,128)S(1)}, f32[2,4,16,8,128]{4,3,2,1,0:T(8,128)S(1)}, u32[]{:S(2)}, u32[]{:S(2)}) collective-permute-start(f32[2,4,16,8,128]{4,3,2,1,0:T(8,128)S(1)} %shard_map.50.refs_4_), channel_id=1, source_target_pairs={{128,0},{129,1},{130,2},{131,3},{132,4},{133,5},{134,6},{135,7},{1... | collective-permute-start | bytes 1572872 | tf_op jit(solution)/shard_map/ppermute | solution.py:432
  62.5 11.2 %collective-permute-start.20 = (f32[2,4,16,8,128]{4,3,2,1,0:T(8,128)S(1)}, f32[2,4,16,8,128]{4,3,2,1,0:T(8,128)S(1)}, u32[]{:S(2)}, u32[]{:S(2)}) collective-permute-start(f32[2,4,16,8,128]{4,3,2,1,0:T(8,128)S(1)} %shard_map.58), channel_id=1, source_target_pairs={{192,64},{193,65},{194,66},{195,67},{196,68},{197,69},{198,70},{19... | collective-permute-start | bytes 1572872 | tf_op jit(solution)/shard_map/ppermute | solution.py:432
  63.9 19.0 %collective-permute-start.16 = (f32[2,4,16,8,128]{4,3,2,1,0:T(8,128)S(1)}, f32[2,4,16,8,128]{4,3,2,1,0:T(8,128)S(1)}, u32[]{:S(2)}, u32[]{:S(2)}) collective-permute-start(f32[2,4,16,8,128]{4,3,2,1,0:T(8,128)S(1)} %get-tuple-element.23), channel_id=1, source_target_pairs={{0,65},{1,66},{2,67},{3,68},{4,69},{5,70},{6,71},{7,72},{8,73},{9,... | collective-permute-start | bytes 1572872 | tf_op jit(solution)/shard_map/ppermute | solution.py:432
  65.2 17.7 %collective-permute-start.17 = (f32[2,4,16,8,128]{4,3,2,1,0:T(8,128)S(1)}, f32[2,4,16,8,128]{4,3,2,1,0:T(8,128)S(1)}, u32[]{:S(2)}, u32[]{:S(2)}) collective-permute-start(f32[2,4,16,8,128]{4,3,2,1,0:T(8,128)S(1)} %get-tuple-element.23), channel_id=1, source_target_pairs={{0,127},{1,64},{2,65},{3,66},{4,67},{5,68},{6,69},{7,70},{8,71},{9... | collective-permute-start | bytes 1572872 | tf_op jit(solution)/shard_map/ppermute | solution.py:432
  71.0 11.9 %collective-permute-start.18 = (f32[2,4,16,8,128]{4,3,2,1,0:T(8,128)S(1)}, f32[2,4,16,8,128]{4,3,2,1,0:T(8,128)S(1)}, u32[]{:S(2)}, u32[]{:S(2)}) collective-permute-start(f32[2,4,16,8,128]{4,3,2,1,0:T(8,128)S(1)} %get-tuple-element.23), channel_id=1, source_target_pairs={{0,64},{1,65},{2,66},{3,67},{4,68},{5,69},{6,70},{7,71},{8,72},{9,... | collective-permute-start | bytes 1572872 | tf_op jit(solution)/shard_map/ppermute | solution.py:432
  83.9 5.3 %collective-permute-start.22 = (f32[1,4,16,8,128]{4,3,2,1,0:T(8,128)S(1)}, f32[1,4,16,8,128]{4,3,2,1,0:T(8,128)S(1)}, u32[]{:S(2)}, u32[]{:S(2)}) collective-permute-start(f32[1,4,16,8,128]{4,3,2,1,0:T(8,128)S(1)} %shard_map.60), channel_id=1, source_target_pairs={{0,128},{1,129},{2,130},{3,131},{4,132},{5,133},{6,134},{7,135},{8... | collective-permute-start | bytes 786440 | tf_op jit(solution)/shard_map/ppermute | solution.py:432
  85.0 7.0 %collective-permute-start.21 = (f32[1,4,16,8,128]{4,3,2,1,0:T(8,128)S(1)}, f32[1,4,16,8,128]{4,3,2,1,0:T(8,128)S(1)}, u32[]{:S(2)}, u32[]{:S(2)}) collective-permute-start(f32[1,4,16,8,128]{4,3,2,1,0:T(8,128)S(1)} %shard_map.59), channel_id=1, source_target_pairs={{0,128},{1,129},{2,130},{3,131},{4,132},{5,133},{6,134},{7,135},{8... | collective-permute-start | bytes 786440 | tf_op jit(solution)/shard_map/ppermute | solution.py:432

commit v8 on v7

--- a/solution.py
+++ b/solution.py
@@ -234,7 +234,7 @@
                     )
 
 
-def coarse_kernel(worker, position, low, high, own, correction, own_c, explicit, state):
+def coarse_kernel(worker, position, own, low, high, correction, own_c, explicit, state):
     depth = own.shape[1]
 
     @pl.when((position[0] >= worker[0]) & (position[0] <= worker[-1]))
@@ -255,12 +255,8 @@
             )
 
 
-def last_kernel(chosen, position, low, high, own, correction, third, state):
+def last_kernel(chosen, position, own, low, high, correction, state):
     depth = own.shape[1]
-
-    @pl.when(position[0] != 1)
-    def _():
-        state[0] = third[chosen]
 
     @pl.when(position[0] == 1)
     def _():
@@ -273,7 +269,7 @@
             coarse_layer(chosen, layer_of, layer + depth, put)
 
 
-def result_kernel(position, first, second, received_a, received_b, result):
+def result_kernel(position, first, second, third, received_a, received_b, result):
     def put(parts):
         for species in (0, 1):
             array, place = parts[species]
@@ -291,7 +287,11 @@
     def _():
         put([(second, 0), (second, 1)])
 
-    @pl.when(position[0] > 1)
+    @pl.when(position[0] == 2)
+    def _():
+        put([(third, 0), (third, 1)])
+
+    @pl.when(position[0] == 3)
     def _():
         put([(received_a, 0), (received_b, 0)])
 
@@ -404,9 +404,9 @@
         target[...] = source[...]
 
 
-def settled(*arrays):
+def settled(*arrays, tokens=()):
     flag = jnp.zeros(1, jnp.int32)
-    return run(settle_kernel, flag, arrays, len(arrays), settling=True)
+    return run(settle_kernel, flag, arrays, len(arrays), settling=True, tokens=tokens)
 
 
 def pick(flag, array, other, tokens=()):
@@ -470,14 +470,14 @@
         return lambda origin, slab: (target, slab + shift) if origin == source else None
 
     def spread(array, source, target, filled=False):
-        def upper(origin, slab):
+        def lower(origin, slab):
             if origin == source:
-                return target, slab - 1
+                return target, slab + 1
             return (origin ^ 1, slab) if filled else None
 
-        low = moved(array, route(source, target, 1))
-        high = moved(array, upper)
-        return low, high, moved(array, route(source, target))
+        low = moved(array, lower)
+        high = moved(array, route(source, target, -1))
+        return moved(array, route(source, target)), low, high
 
     both, own = entered(own, feed, kill)
     half = moved(both, halves)
@@ -489,7 +489,7 @@
     low_b = moved(own_b, onward(1, 1))
     high_b = moved(own_b, onward(1, -1))
     lowest, highest = place == 0, place == ring - 1
-    low, high = settled(low, high)
+    (low,) = settled(low)
     outer_2 = moved(pick(lowest, low, high), far(2))
     explicit, first_end = run(
         fine_kernel,
@@ -503,7 +503,8 @@
     second = spread(explicit, 0, 1)
     mended = pick((lowest & (index == 2)) | (highest & (index == 3)), half_far, half)
     other_x = moved(mended, lambda source, slab: swapped(source, slab) if source >= 2 else None)
-    outer_3 = moved(pick(lowest, low_b, high_b, (explicit,)), far(3))
+    low_b, high_b = settled(low_b, high_b, tokens=(second[0],))
+    outer_3 = moved(pick(lowest, low_b, high_b), far(3))
     even = index % 2 == 0
     other = pick(index == 1, other, other_x)
     low_c = pick(even, mended, other)
@@ -533,23 +534,28 @@
         coarse_kernel, position, (*second, correction, both), 2, worker=(1,)
     )
     third = spread(explicit, 1, 0)
-    crossed_3 = moved(after(correction_3, third[0]), route(3, 1))
+    crossed_3 = moved(after(correction_3, third[1]), route(3, 1))
     explicit, third_end = run(
         coarse_kernel, position, (*third, crossed_2, both), 2, worker=(0,)
     )
     fourth = spread(explicit, 0, 1, True)
+    third_home = moved(third_end, route(0, 2))
     received = []
     for chosen in (0, 1):
         (last_end,) = run(
-            last_kernel, position, (*fourth, crossed_3, third_end), 1, worker=chosen, species=1
+            last_kernel,
+            position,
+            (*fourth, crossed_3),
+            1,
+            worker=chosen,
+            species=1,
+            tokens=(third_home,),
         )
-        received.append(
-            moved(last_end, lambda source, slab: (source ^ 2, slab))
-        )
+        received.append(moved(last_end, lambda source, slab: ((1, 3, 0, 2)[source], slab)))
     (result,) = run(
         result_kernel,
         position,
-        (first_end, second_end, *received),
+        (first_end, second_end, third_home, *received),
         1,
         result=jax.ShapeDtypeStruct(starts.shape[1:], starts.dtype),
     )

time: 93.4 us -> 106 us (1.13)
  Pallas kernels: 14.1 us -> 20 us
  starting transfers between devices: 48.4 us -> 53 us
  local copies, waits for them, and re-layouts: 0 us -> 2.82 us
    pallas_call x22 -> x23, Pallas kernels: 12.6 us -> 17.7 us  [run(): pl.pallas_call(kernel, out_shape=out_shape, in_specs=[SMEM] + [VMEM] * le...]
    ppermute x23 -> x24, starting transfers between devices: 48.4 us -> 53 us  [moved(): return lax.ppermute(array, AXES, pairs)]
    unnamed x0 -> x14, local copies, waits for them, and re-layouts: none -> 2.82 us
    ppermute x23 -> x24, waiting for transfers between devices: 30.1 us -> 29.2 us  [moved(): return lax.ppermute(array, AXES, pairs)]
  transfers between devices with their start and end apart: 23 -> 24, of which waited for: 9 -> 7; matrix products, arithmetic and copies ran while one was open for 0% -> 0% of each run, Pallas kernels for 12% -> 16%
where the time goes in v8:
time: 106 us
  starting transfers between devices  53 us (50%)
  waiting for transfers between devices  29.2 us (28%)
  Pallas kernels  20 us (19%)
  local copies, waits for them, and re-layouts  2.82 us (3%)
    ppermute x24, starting transfers between devices, moved(): return lax.ppermute(array, AXES, pairs)  53 us
    ppermute x24, waiting for transfers between devices, moved(): return lax.ppermute(array, AXES, pairs)  29.2 us
    pallas_call x23, Pallas kernels, run(): pl.pallas_call(kernel, out_shape=out_shape, in_specs=[SMEM] + [VMEM] * le...  17.7 us
    unnamed x14, local copies, waits for them, and re-layouts  2.82 us
  transfers between devices with their start and end apart: 24, of which 7 were waited for; matrix products, arithmetic and copies ran while one was open for 0% of the time, Pallas kernels for 16%

profile of v8, /device:TPU:1, one launch (start us, length us, event | category | flops | bytes accessed | tf_op | source)
XLA Modules:
  0.0 105.5 jit_solution(9861240661029719891)
XLA Ops:
  0.0 1.4 %shard_map.37 = (f32[2,4,16,8,128]{4,3,2,1,0:T(8,128)S(1)}, f32[2,4,16,8,128]{4,3,2,1,0:T(8,128)S(1)}) custom-call(f32[2,4,128,128]{3,2,1,0:T(8,128)} %bitcast.8, f32[4,128,128]{2,1,0:T(8,128)} %feed.1, f32[4,128,128]{2,1,0:T(8,128)} %kill.1), custom_call_target="tpu_custom_call" | custom-call | flops 100000 | bytes 1048576 | tf_op jit(solution)/shard_map/pallas_call | solution.py:325
  1.4 0.0 copy-start.4
  1.4 11.6 %collective-permute-start.2 = (f32[2,4,16,8,128]{4,3,2,1,0:T(8,128)S(1)}, f32[2,4,16,8,128]{4,3,2,1,0:T(8,128)S(1)}, u32[]{:S(2)}, u32[]{:S(2)}) collective-permute-start(f32[2,4,16,8,128]{4,3,2,1,0:T(8,128)S(1)} %get-tuple-element.16.refs_5_), channel_id=1, source_target_pairs={{0,1},{1,2},{2,3},{3,4},{4,5},{5,6},{6,7},{7,8},{8,9},{9,10},{10,1... | collective-permute-start | bytes 1572872 | tf_op jit(solution)/shard_map/ppermute | solution.py:432
  13.0 0.7 collective-permute-start
  13.7 0.7 collective-permute-start.1
  14.4 5.3 %collective-permute-done.2.token.refs_4_.refs_2_ = f32[2,4,16,8,128]{4,3,2,1,0:T(8,128)S(1)} collective-permute-done((f32[2,4,16,8,128]{4,3,2,1,0:T(8,128)S(1)}, f32[2,4,16,8,128]{4,3,2,1,0:T(8,128)S(1)}, u32[]{:S(2)}, u32[]{:S(2)}) %collective-permute-start.2) | collective-permute-done | bytes 524320 | tf_op jit(solution)/shard_map/ppermute | solution.py:432
  19.7 0.7 collective-permute-start.10
  20.4 1.5 %collective-permute-start.3 = (f32[2,4,16,8,128]{4,3,2,1,0:T(8,128)S(1)}, f32[2,4,16,8,128]{4,3,2,1,0:T(8,128)}, u32[]{:S(2)}, u32[]{:S(2)}) collective-permute-start(f32[2,4,16,8,128]{4,3,2,1,0:T(8,128)S(1)} %collective-permute-done.2.token.refs_4_.refs_2_), channel_id=1, source_target_pairs={{0,64},{1,65},{2,66},{3,67},{4,68},{5,69},{6,70},{7,71},{8,72},{9,... | collective-permute-start | bytes 1572872 | tf_op jit(solution)/shard_map/ppermute | solution.py:432
  21.9 0.8 shard_map.39.refs_7_
  22.7 9.1 %collective-permute-start.8 = (f32[2,4,16,8,128]{4,3,2,1,0:T(8,128)}, f32[2,4,16,8,128]{4,3,2,1,0:T(8,128)}, u32[]{:S(2)}, u32[]{:S(2)}) collective-permute-start(f32[2,4,16,8,128]{4,3,2,1,0:T(8,128)} %shard_map.39.refs_7_), channel_id=1, source_target_pairs={{64,127},{65,64},{66,65},{67,66},{68,67},{69,68},{70,69},{71,70},{... | collective-permute-start | bytes 1572872 | tf_op jit(solution)/shard_map/ppermute | solution.py:432
  31.8 0.0 collective-permute-done.refs_1_
  31.8 1.9 %collective-permute-start.7 = (f32[2,4,16,8,128]{4,3,2,1,0:T(8,128)}, f32[2,4,16,8,128]{4,3,2,1,0:T(8,128)}, u32[]{:S(2)}, u32[]{:S(2)}) collective-permute-start(f32[2,4,16,8,128]{4,3,2,1,0:T(8,128)} %shard_map.39.refs_7_), channel_id=1, source_target_pairs={{64,65},{65,66},{66,67},{67,68},{68,69},{69,70},{70,71},{71,72},{7... | collective-permute-start | bytes 1572872 | tf_op jit(solution)/shard_map/ppermute | solution.py:432
  33.8 0.0 collective-permute-done.1.refs_3_.refs_2_
  33.8 0.9 shard_map.42
  34.6 0.7 collective-permute-start.9
  35.3 0.0 collective-permute-done.10.refs_1_
  35.4 0.8 copy-done
  36.2 1.0 copy-done.1
  37.2 1.6 %collective-permute-start.11 = (f32[2,4,16,8,128]{4,3,2,1,0:T(8,128)S(1)}, f32[2,4,16,8,128]{4,3,2,1,0:T(8,128)}, u32[]{:S(2)}, u32[]{:S(2)}) collective-permute-start(f32[2,4,16,8,128]{4,3,2,1,0:T(8,128)S(1)} %shard_map.47.refs_1_.refs_2_), channel_id=1, source_target_pairs={{128,192},{129,193},{130,194},{131,195},{132,196},{133,197},{134,1... | collective-permute-start | bytes 1572872 | tf_op jit(solution)/shard_map/ppermute | solution.py:432
  38.9 0.0 collective-permute-done.3.refs_6_.refs_1_
  38.9 1.8 %shard_map.40 = (f32[2,4,16,8,128]{4,3,2,1,0:T(8,128)}, f32[2,4,16,8,128]{4,3,2,1,0:T(8,128)S(1)}) custom-call(s32[1]{0:T(128)} %bitcast.refs_0_, f32[2,4,16,8,128]{4,3,2,1,0:T(8,128)S(1)} %shard_map.38.refs_1_.refs_2_, f32[2,4,16,8,128]{4,3,2,1,0:T(8,128)S(1)} %get-tuple-element.15.array.refs_2_, ...), custom_call_target="tpu_custom_call" | custom-call | flops 10000000000 | bytes 1048576 | tf_op jit(solution)/shard_map/pallas_call | solution.py:372
  40.7 0.8 copy-done.2
  41.5 1.3 %collective-permute-start.4 = (f32[2,4,16,8,128]{4,3,2,1,0:T(8,128)}, f32[2,4,16,8,128]{4,3,2,1,0:T(8,128)}, u32[]{:S(2)}, u32[]{:S(2)}) collective-permute-start(f32[2,4,16,8,128]{4,3,2,1,0:T(8,128)} %get-tuple-element.18), channel_id=1, source_target_pairs={{0,64},{1,65},{2,66},{3,67},{4,68},{5,69},{6,70},{7,71},{8,72},{9,... | collective-permute-start | bytes 1572872 | tf_op jit(solution)/shard_map/ppermute | solution.py:432
  42.8 0.0 collective-permute-done.9.refs_1_
  42.8 1.3 %collective-permute-start.6 = (f32[2,4,16,8,128]{4,3,2,1,0:T(8,128)}, f32[2,4,16,8,128]{4,3,2,1,0:T(8,128)S(1)}, u32[]{:S(2)}, u32[]{:S(2)}) collective-permute-start(f32[2,4,16,8,128]{4,3,2,1,0:T(8,128)} %get-tuple-element.18), channel_id=1, source_target_pairs={{0,127},{1,64},{2,65},{3,66},{4,67},{5,68},{6,69},{7,70},{8,71},{9... | collective-permute-start | bytes 1572872 | tf_op jit(solution)/shard_map/ppermute | solution.py:432
  44.2 0.0 collective-permute-done.11.refs_2_
  44.2 1.3 %collective-permute-start.5 = (f32[2,4,16,8,128]{4,3,2,1,0:T(8,128)}, f32[2,4,16,8,128]{4,3,2,1,0:T(8,128)S(1)}, u32[]{:S(2)}, u32[]{:S(2)}) collective-permute-start(f32[2,4,16,8,128]{4,3,2,1,0:T(8,128)} %get-tuple-element.18), channel_id=1, source_target_pairs={{0,65},{1,66},{2,67},{3,68},{4,69},{5,70},{6,71},{7,72},{8,73},{9,... | collective-permute-start | bytes 1572872 | tf_op jit(solution)/shard_map/ppermute | solution.py:432
  45.5 1.2 %shard_map.48.refs_2_.refs_1_ = f32[2,4,16,8,128]{4,3,2,1,0:T(8,128)S(1)} custom-call(s32[1]{0:T(128)} %bitcast.2.refs_0_, f32[2,4,16,8,128]{4,3,2,1,0:T(8,128)} %collective-permute-done.3.refs_6_.refs_1_, f32[2,4,16,8,128]{4,3,2,1,0:T(8,128)} %collective-permute-done.11.refs_2_), custom_call_target="tpu_custom_call" | custom-call | flops 100000 | bytes 1048576 | tf_op jit(solution)/shard_map/pallas_call | solution.py:372
  46.9 0.0 collective-permute-done.8.refs_2_
  46.9 1.5 %collective-permute-done.7.refs_1_ = f32[2,4,16,8,128]{4,3,2,1,0:T(8,128)} collective-permute-done((f32[2,4,16,8,128]{4,3,2,1,0:T(8,128)}, f32[2,4,16,8,128]{4,3,2,1,0:T(8,128)}, u32[]{:S(2)}, u32[]{:S(2)}) %collective-permute-start.7) | collective-permute-done | bytes 524320 | tf_op jit(solution)/shard_map/ppermute | solution.py:432
  48.4 0.0 collective-permute-done.4.refs_3_.refs_1_
  48.4 1.3 %shard_map.41 = (f32[2,4,16,8,128]{4,3,2,1,0:T(8,128)S(1)}, f32[2,4,16,8,128]{4,3,2,1,0:T(8,128)S(1)}) custom-call(s32[1]{0:T(128)} %constant.30.clone.1.refs_0_, f32[2,4,16,8,128]{4,3,2,1,0:T(8,128)} %collective-permute-done.7.refs_1_, f32[2,4,16,8,128]{4,3,2,1,0:T(8,128)} %collective-permute-done.8.refs_2_, ...), custom_call_target="tpu_custom_call" | custom-call | flops 1000000000 | bytes 1048576 | tf_op jit(solution)/shard_map/pallas_call | solution.py:372
  49.8 0.0 copy-start.6
  49.8 0.8 collective-permute-start.20
  50.7 0.1 copy-done.6
  50.8 5.8 %shard_map.51.refs_4_ = f32[2,4,16,8,128]{4,3,2,1,0:T(8,128)S(1)} custom-call(s32[1]{0:T(128)} %bitcast.refs_0_, f32[2,4,16,8,128]{4,3,2,1,0:T(8,128)S(1)} %shard_map.44.refs_1_, f32[2,4,16,8,128]{4,3,2,1,0:T(8,128)S(1)} %get-tuple-element.15.array.refs_2_, f32[2,4,16,8,128]{4,3,2,1,0:T(8,128)S(1)} %shard_map.46.refs_3_, ...), custom_call_target="tpu_custom_call" | custom-call | flops 10000000000 | bytes 1048576 | tf_op jit(solution)/shard_map/pallas_call | solution.py:372
  56.6 0.0 collective-permute-done.6.refs_3_
  56.6 5.5 %collective-permute-done.5.refs_2_ = f32[2,4,16,8,128]{4,3,2,1,0:T(8,128)S(1)} collective-permute-done((f32[2,4,16,8,128]{4,3,2,1,0:T(8,128)}, f32[2,4,16,8,128]{4,3,2,1,0:T(8,128)S(1)}, u32[]{:S(2)}, u32[]{:S(2)}) %collective-permute-start.5) | collective-permute-done | bytes 524320 | tf_op jit(solution)/shard_map/ppermute | solution.py:432
  62.2 3.0 %shard_map.52 = (f32[2,4,16,8,128]{4,3,2,1,0:T(8,128)S(1)}, f32[2,4,16,8,128]{4,3,2,1,0:T(8,128)S(1)}) custom-call(s32[1]{0:T(128)} %bitcast.refs_0_, f32[2,4,16,8,128]{4,3,2,1,0:T(8,128)} %collective-permute-done.4.refs_3_.refs_1_, f32[2,4,16,8,128]{4,3,2,1,0:T(8,128)S(1)} %collective-permute-done.5.refs_2_, ...), custom_call_target="tpu_custom_call" | custom-call | flops 10000000000 | bytes 1048576 | tf_op jit(solution)/shard_map/pallas_call | solution.py:372
  65.2 1.3 %collective-permute-start.14 = (f32[2,4,16,8,128]{4,3,2,1,0:T(8,128)S(1)}, f32[2,4,16,8,128]{4,3,2,1,0:T(8,128)S(1)}, u32[]{:S(2)}, u32[]{:S(2)}) collective-permute-start(f32[2,4,16,8,128]{4,3,2,1,0:T(8,128)S(1)} %get-tuple-element.22), channel_id=1, source_target_pairs={{64,63},{65,0},{66,1},{67,2},{68,3},{69,4},{70,5},{71,6},{72,7},{7... | collective-permute-start | bytes 1572872 | tf_op jit(solution)/shard_map/ppermute | solution.py:432
  66.5 1.3 %collective-permute-start.13 = (f32[2,4,16,8,128]{4,3,2,1,0:T(8,128)S(1)}, f32[2,4,16,8,128]{4,3,2,1,0:T(8,128)S(1)}, u32[]{:S(2)}, u32[]{:S(2)}) collective-permute-start(f32[2,4,16,8,128]{4,3,2,1,0:T(8,128)S(1)} %get-tuple-element.22), channel_id=1, source_target_pairs={{64,1},{65,2},{66,3},{67,4},{68,5},{69,6},{70,7},{71,8},{72,9},{73... | collective-permute-start | bytes 1572872 | tf_op jit(solution)/shard_map/ppermute | solution.py:432
  67.9 1.3 %collective-permute-start.12 = (f32[2,4,16,8,128]{4,3,2,1,0:T(8,128)S(1)}, f32[2,4,16,8,128]{4,3,2,1,0:T(8,128)S(1)}, u32[]{:S(2)}, u32[]{:S(2)}) collective-permute-start(f32[2,4,16,8,128]{4,3,2,1,0:T(8,128)S(1)} %get-tuple-element.22), channel_id=1, source_target_pairs={{64,0},{65,1},{66,2},{67,3},{68,4},{69,5},{70,6},{71,7},{72,8},{73... | collective-permute-start | bytes 1572872 | tf_op jit(solution)/shard_map/ppermute | solution.py:432
  69.2 0.7 collective-permute-start.15
  69.9 0.0 collective-permute-done.20.refs_1_
  70.0 0.2 shard_map.58.array
  70.2 3.7 %collective-permute-done.13.refs_2_.token = f32[2,4,16,8,128]{4,3,2,1,0:T(8,128)S(1)} collective-permute-done((f32[2,4,16,8,128]{4,3,2,1,0:T(8,128)S(1)}, f32[2,4,16,8,128]{4,3,2,1,0:T(8,128)S(1)}, u32[]{:S(2)}, u32[]{:S(2)}) %collective-permute-start.13) | collective-permute-done | bytes 524320 | tf_op jit(solution)/shard_map/ppermute | solution.py:432
  74.0 1.3 %collective-permute-start.21 = (f32[2,4,16,8,128]{4,3,2,1,0:T(8,128)S(1)}, f32[2,4,16,8,128]{4,3,2,1,0:T(8,128)S(1)}, u32[]{:S(2)}, u32[]{:S(2)}) collective-permute-start(f32[2,4,16,8,128]{4,3,2,1,0:T(8,128)S(1)} %shard_map.59), channel_id=1, source_target_pairs={{192,64},{193,65},{194,66},{195,67},{196,68},{197,69},{198,70},{19... | collective-permute-start | bytes 1572872 | tf_op jit(solution)/shard_map/ppermute | solution.py:432
  75.3 0.0 collective-permute-done.15.refs_1_
  75.4 0.0 collective-permute-done.12.refs_1_
  75.4 0.7 collective-permute-start.16
  76.1 1.3 %collective-permute-start.19 = (f32[2,4,16,8,128]{4,3,2,1,0:T(8,128)S(1)}, f32[2,4,16,8,128]{4,3,2,1,0:T(8,128)S(1)}, u32[]{:S(2)}, u32[]{:S(2)}) collective-permute-start(f32[2,4,16,8,128]{4,3,2,1,0:T(8,128)S(1)} %get-tuple-element.24), channel_id=1, source_target_pairs={{0,127},{1,64},{2,65},{3,66},{4,67},{5,68},{6,69},{7,70},{8,71},{9... | collective-permute-start | bytes 1572872 | tf_op jit(solution)/shard_map/ppermute | solution.py:432
  77.4 10.5 %collective-permute-start.18 = (f32[2,4,16,8,128]{4,3,2,1,0:T(8,128)S(1)}, f32[2,4,16,8,128]{4,3,2,1,0:T(8,128)S(1)}, u32[]{:S(2)}, u32[]{:S(2)}) collective-permute-start(f32[2,4,16,8,128]{4,3,2,1,0:T(8,128)S(1)} %get-tuple-element.24), channel_id=1, source_target_pairs={{0,65},{1,66},{2,67},{3,68},{4,69},{5,70},{6,71},{7,72},{8,73},{9,... | collective-permute-start | bytes 1572872 | tf_op jit(solution)/shard_map/ppermute | solution.py:432
  87.9 1.3 %collective-permute-start.17 = (f32[2,4,16,8,128]{4,3,2,1,0:T(8,128)S(1)}, f32[2,4,16,8,128]{4,3,2,1,0:T(8,128)S(1)}, u32[]{:S(2)}, u32[]{:S(2)}) collective-permute-start(f32[2,4,16,8,128]{4,3,2,1,0:T(8,128)S(1)} %get-tuple-element.24), channel_id=1, source_target_pairs={{0,64},{1,65},{2,66},{3,67},{4,68},{5,69},{6,70},{7,71},{8,72},{9,... | collective-permute-start | bytes 1572872 | tf_op jit(solution)/shard_map/ppermute | solution.py:432
  89.2 0.0 collective-permute-done.21.refs_4_
  89.2 0.0 collective-permute-done.19.refs_3_
  89.2 8.1 %collective-permute-done.18.refs_2_ = f32[2,4,16,8,128]{4,3,2,1,0:T(8,128)S(1)} collective-permute-done((f32[2,4,16,8,128]{4,3,2,1,0:T(8,128)S(1)}, f32[2,4,16,8,128]{4,3,2,1,0:T(8,128)S(1)}, u32[]{:S(2)}, u32[]{:S(2)}) %collective-permute-start.18) | collective-permute-done | bytes 524320 | tf_op jit(solution)/shard_map/ppermute | solution.py:432
  97.3 0.0 collective-permute-done.17.refs_1_
  97.3 1.0 shard_map.60
  98.3 0.1 collective-permute-start.22
  98.4 1.0 shard_map.61
  99.4 0.1 collective-permute-start.23
  99.5 2.2 %collective-permute-done.22.refs_4_ = f32[1,4,16,8,128]{4,3,2,1,0:T(8,128)S(1)} collective-permute-done((f32[1,4,16,8,128]{4,3,2,1,0:T(8,128)S(1)}, f32[1,4,16,8,128]{4,3,2,1,0:T(8,128)S(1)}, u32[]{:S(2)}, u32[]{:S(2)}) %collective-permute-start.22) | collective-permute-done | bytes 262176 | tf_op jit(solution)/shard_map/ppermute | solution.py:432
  101.7 2.8 %collective-permute-done.23.refs_5_ = f32[1,4,16,8,128]{4,3,2,1,0:T(8,128)S(1)} collective-permute-done((f32[1,4,16,8,128]{4,3,2,1,0:T(8,128)S(1)}, f32[1,4,16,8,128]{4,3,2,1,0:T(8,128)S(1)}, u32[]{:S(2)}, u32[]{:S(2)}) %collective-permute-start.23) | collective-permute-done | bytes 262176 | tf_op jit(solution)/shard_map/ppermute | solution.py:432
  104.6 1.0 shard_map.62
  (24 shorter events, 0.6 us)
Async XLA Ops:
  1.4 21.3 %copy-start.4 = (f32[2,4,16,8,128]{4,3,2,1,0:T(8,128)}, f32[2,4,16,8,128]{4,3,2,1,0:T(8,128)S(1)}, u32[]{:S(2)}) copy-start(f32[2,4,16,8,128]{4,3,2,1,0:T(8,128)S(1)} %get-tuple-element.16.refs_5_) | copy-start | bytes 1572868
  1.4 18.3 %collective-permute-start.2 = (f32[2,4,16,8,128]{4,3,2,1,0:T(8,128)S(1)}, f32[2,4,16,8,128]{4,3,2,1,0:T(8,128)S(1)}, u32[]{:S(2)}, u32[]{:S(2)}) collective-permute-start(f32[2,4,16,8,128]{4,3,2,1,0:T(8,128)S(1)} %get-tuple-element.16.refs_5_), channel_id=1, source_target_pairs={{0,1},{1,2},{2,3},{3,4},{4,5},{5,6},{6,7},{7,8},{8,9},{9,10},{10,1... | collective-permute-start | bytes 1572872 | tf_op jit(solution)/shard_map/ppermute | solution.py:432
  13.0 18.8 %collective-permute-start = (f32[2,4,16,8,128]{4,3,2,1,0:T(8,128)S(1)}, f32[2,4,16,8,128]{4,3,2,1,0:T(8,128)S(1)}, u32[]{:S(2)}, u32[]{:S(2)}) collective-permute-start(f32[2,4,16,8,128]{4,3,2,1,0:T(8,128)S(1)} %get-tuple-element.15.array.refs_2_), channel_id=1, source_target_pairs={{0,1},{1,2},{2,3},{3,4},{4,5},{5,6},{6,7},{7,8},{8,9},{9,10},{10,1... | collective-permute-start | bytes 1572872 | tf_op jit(solution)/shard_map/ppermute | solution.py:432
  13.7 20.1 %collective-permute-start.1 = (f32[2,4,16,8,128]{4,3,2,1,0:T(8,128)S(1)}, f32[2,4,16,8,128]{4,3,2,1,0:T(8,128)S(1)}, u32[]{:S(2)}, u32[]{:S(2)}) collective-permute-start(f32[2,4,16,8,128]{4,3,2,1,0:T(8,128)S(1)} %get-tuple-element.15.array.refs_2_), channel_id=1, source_target_pairs={{0,63},{1,0},{2,1},{3,2},{4,3},{5,4},{6,5},{7,6},{8,7},{9,8},{10,9... | collective-permute-start | bytes 1572872 | tf_op jit(solution)/shard_map/ppermute | solution.py:432
  19.7 15.6 %collective-permute-start.10 = (f32[2,4,16,8,128]{4,3,2,1,0:T(8,128)S(1)}, f32[2,4,16,8,128]{4,3,2,1,0:T(8,128)S(1)}, u32[]{:S(2)}, u32[]{:S(2)}) collective-permute-start(f32[2,4,16,8,128]{4,3,2,1,0:T(8,128)S(1)} %collective-permute-done.2.token.refs_4_.refs_2_), channel_id=1, source_target_pairs={{128,132},{132,136},{136,140},{140,144},{144,148},{148,152},{152,1... | collective-permute-start | bytes 1572872 | tf_op jit(solution)/shard_map/ppermute | solution.py:432
  20.4 18.5 %collective-permute-start.3 = (f32[2,4,16,8,128]{4,3,2,1,0:T(8,128)S(1)}, f32[2,4,16,8,128]{4,3,2,1,0:T(8,128)}, u32[]{:S(2)}, u32[]{:S(2)}) collective-permute-start(f32[2,4,16,8,128]{4,3,2,1,0:T(8,128)S(1)} %collective-permute-done.2.token.refs_4_.refs_2_), channel_id=1, source_target_pairs={{0,64},{1,65},{2,66},{3,67},{4,68},{5,69},{6,70},{7,71},{8,72},{9,... | collective-permute-start | bytes 1572872 | tf_op jit(solution)/shard_map/ppermute | solution.py:432
  22.7 24.2 %collective-permute-start.8 = (f32[2,4,16,8,128]{4,3,2,1,0:T(8,128)}, f32[2,4,16,8,128]{4,3,2,1,0:T(8,128)}, u32[]{:S(2)}, u32[]{:S(2)}) collective-permute-start(f32[2,4,16,8,128]{4,3,2,1,0:T(8,128)} %shard_map.39.refs_7_), channel_id=1, source_target_pairs={{64,127},{65,64},{66,65},{67,66},{68,67},{69,68},{70,69},{71,70},{... | collective-permute-start | bytes 1572872 | tf_op jit(solution)/shard_map/ppermute | solution.py:432
  31.8 16.6 %collective-permute-start.7 = (f32[2,4,16,8,128]{4,3,2,1,0:T(8,128)}, f32[2,4,16,8,128]{4,3,2,1,0:T(8,128)}, u32[]{:S(2)}, u32[]{:S(2)}) collective-permute-start(f32[2,4,16,8,128]{4,3,2,1,0:T(8,128)} %shard_map.39.refs_7_), channel_id=1, source_target_pairs={{64,65},{65,66},{66,67},{67,68},{68,69},{69,70},{70,71},{71,72},{7... | collective-permute-start | bytes 1572872 | tf_op jit(solution)/shard_map/ppermute | solution.py:432
  34.6 8.2 %collective-permute-start.9 = (f32[2,4,16,8,128]{4,3,2,1,0:T(8,128)}, f32[2,4,16,8,128]{4,3,2,1,0:T(8,128)S(1)}, u32[]{:S(2)}, u32[]{:S(2)}) collective-permute-start(f32[2,4,16,8,128]{4,3,2,1,0:T(8,128)} %shard_map.42), channel_id=1, source_target_pairs={{128,132},{131,191},{132,136},{135,131},{136,140},{139,135},{140,1... | collective-permute-start | bytes 1572872 | tf_op jit(solution)/shard_map/ppermute | solution.py:432
  35.3 0.8 copy-start
  36.2 1.0 copy-start.1
  37.2 1.7 %copy-start.5 = (f32[2,4,16,8,128]{4,3,2,1,0:T(8,128)S(1)}, f32[2,4,16,8,128]{4,3,2,1,0:T(8,128)}, u32[]{:S(2)}) copy-start(f32[2,4,16,8,128]{4,3,2,1,0:T(8,128)} %copy-done.4) | copy-start | bytes 1572868
  37.2 7.0 %collective-permute-start.11 = (f32[2,4,16,8,128]{4,3,2,1,0:T(8,128)S(1)}, f32[2,4,16,8,128]{4,3,2,1,0:T(8,128)}, u32[]{:S(2)}, u32[]{:S(2)}) collective-permute-start(f32[2,4,16,8,128]{4,3,2,1,0:T(8,128)S(1)} %shard_map.47.refs_1_.refs_2_), channel_id=1, source_target_pairs={{128,192},{129,193},{130,194},{131,195},{132,196},{133,197},{134,1... | collective-permute-start | bytes 1572872 | tf_op jit(solution)/shard_map/ppermute | solution.py:432
  40.7 0.8 copy-start.2
  41.5 6.9 %collective-permute-start.4 = (f32[2,4,16,8,128]{4,3,2,1,0:T(8,128)}, f32[2,4,16,8,128]{4,3,2,1,0:T(8,128)}, u32[]{:S(2)}, u32[]{:S(2)}) collective-permute-start(f32[2,4,16,8,128]{4,3,2,1,0:T(8,128)} %get-tuple-element.18), channel_id=1, source_target_pairs={{0,64},{1,65},{2,66},{3,67},{4,68},{5,69},{6,70},{7,71},{8,72},{9,... | collective-permute-start | bytes 1572872 | tf_op jit(solution)/shard_map/ppermute | solution.py:432
  42.8 13.8 %collective-permute-start.6 = (f32[2,4,16,8,128]{4,3,2,1,0:T(8,128)}, f32[2,4,16,8,128]{4,3,2,1,0:T(8,128)S(1)}, u32[]{:S(2)}, u32[]{:S(2)}) collective-permute-start(f32[2,4,16,8,128]{4,3,2,1,0:T(8,128)} %get-tuple-element.18), channel_id=1, source_target_pairs={{0,127},{1,64},{2,65},{3,66},{4,67},{5,68},{6,69},{7,70},{8,71},{9... | collective-permute-start | bytes 1572872 | tf_op jit(solution)/shard_map/ppermute | solution.py:432
  44.2 17.9 %collective-permute-start.5 = (f32[2,4,16,8,128]{4,3,2,1,0:T(8,128)}, f32[2,4,16,8,128]{4,3,2,1,0:T(8,128)S(1)}, u32[]{:S(2)}, u32[]{:S(2)}) collective-permute-start(f32[2,4,16,8,128]{4,3,2,1,0:T(8,128)} %get-tuple-element.18), channel_id=1, source_target_pairs={{0,65},{1,66},{2,67},{3,68},{4,69},{5,70},{6,71},{7,72},{8,73},{9,... | collective-permute-start | bytes 1572872 | tf_op jit(solution)/shard_map/ppermute | solution.py:432
  49.8 1.0 copy-start.6
  49.8 20.1 %collective-permute-start.20 = (f32[2,4,16,8,128]{4,3,2,1,0:T(8,128)S(1)}, f32[2,4,16,8,128]{4,3,2,1,0:T(8,128)S(1)}, u32[]{:S(2)}, u32[]{:S(2)}) collective-permute-start(f32[2,4,16,8,128]{4,3,2,1,0:T(8,128)S(1)} %shard_map.55), channel_id=1, source_target_pairs={{192,196},{195,255},{196,200},{199,195},{200,204},{203,199},{204,2... | collective-permute-start | bytes 1572872 | tf_op jit(solution)/shard_map/ppermute | solution.py:432
  65.2 10.1 %collective-permute-start.14 = (f32[2,4,16,8,128]{4,3,2,1,0:T(8,128)S(1)}, f32[2,4,16,8,128]{4,3,2,1,0:T(8,128)S(1)}, u32[]{:S(2)}, u32[]{:S(2)}) collective-permute-start(f32[2,4,16,8,128]{4,3,2,1,0:T(8,128)S(1)} %get-tuple-element.22), channel_id=1, source_target_pairs={{64,63},{65,0},{66,1},{67,2},{68,3},{69,4},{70,5},{71,6},{72,7},{7... | collective-permute-start | bytes 1572872 | tf_op jit(solution)/shard_map/ppermute | solution.py:432
  66.5 7.4 %collective-permute-start.13 = (f32[2,4,16,8,128]{4,3,2,1,0:T(8,128)S(1)}, f32[2,4,16,8,128]{4,3,2,1,0:T(8,128)S(1)}, u32[]{:S(2)}, u32[]{:S(2)}) collective-permute-start(f32[2,4,16,8,128]{4,3,2,1,0:T(8,128)S(1)} %get-tuple-element.22), channel_id=1, source_target_pairs={{64,1},{65,2},{66,3},{67,4},{68,5},{69,6},{70,7},{71,8},{72,9},{73... | collective-permute-start | bytes 1572872 | tf_op jit(solution)/shard_map/ppermute | solution.py:432
  67.9 7.5 %collective-permute-start.12 = (f32[2,4,16,8,128]{4,3,2,1,0:T(8,128)S(1)}, f32[2,4,16,8,128]{4,3,2,1,0:T(8,128)S(1)}, u32[]{:S(2)}, u32[]{:S(2)}) collective-permute-start(f32[2,4,16,8,128]{4,3,2,1,0:T(8,128)S(1)} %get-tuple-element.22), channel_id=1, source_target_pairs={{64,0},{65,1},{66,2},{67,3},{68,4},{69,5},{70,6},{71,7},{72,8},{73... | collective-permute-start | bytes 1572872 | tf_op jit(solution)/shard_map/ppermute | solution.py:432
  69.2 6.1 %collective-permute-start.15 = (f32[2,4,16,8,128]{4,3,2,1,0:T(8,128)S(1)}, f32[2,4,16,8,128]{4,3,2,1,0:T(8,128)S(1)}, u32[]{:S(2)}, u32[]{:S(2)}) collective-permute-start(f32[2,4,16,8,128]{4,3,2,1,0:T(8,128)S(1)} %shard_map.51.refs_4_), channel_id=1, source_target_pairs={{128,0},{129,1},{130,2},{131,3},{132,4},{133,5},{134,6},{135,7},{1... | collective-permute-start | bytes 1572872 | tf_op jit(solution)/shard_map/ppermute | solution.py:432
  74.0 15.2 %collective-permute-start.21 = (f32[2,4,16,8,128]{4,3,2,1,0:T(8,128)S(1)}, f32[2,4,16,8,128]{4,3,2,1,0:T(8,128)S(1)}, u32[]{:S(2)}, u32[]{:S(2)}) collective-permute-start(f32[2,4,16,8,128]{4,3,2,1,0:T(8,128)S(1)} %shard_map.59), channel_id=1, source_target_pairs={{192,64},{193,65},{194,66},{195,67},{196,68},{197,69},{198,70},{19... | collective-permute-start | bytes 1572872 | tf_op jit(solution)/shard_map/ppermute | solution.py:432
  75.4 13.8 %collective-permute-start.16 = (f32[2,4,16,8,128]{4,3,2,1,0:T(8,128)S(1)}, f32[2,4,16,8,128]{4,3,2,1,0:T(8,128)S(1)}, u32[]{:S(2)}, u32[]{:S(2)}) collective-permute-start(f32[2,4,16,8,128]{4,3,2,1,0:T(8,128)S(1)} %get-tuple-element.23), channel_id=1, source_target_pairs={{0,128},{1,129},{2,130},{3,131},{4,132},{5,133},{6,134},{7,135},{8... | collective-permute-start | bytes 1572872 | tf_op jit(solution)/shard_map/ppermute | solution.py:432
  76.1 13.1 %collective-permute-start.19 = (f32[2,4,16,8,128]{4,3,2,1,0:T(8,128)S(1)}, f32[2,4,16,8,128]{4,3,2,1,0:T(8,128)S(1)}, u32[]{:S(2)}, u32[]{:S(2)}) collective-permute-start(f32[2,4,16,8,128]{4,3,2,1,0:T(8,128)S(1)} %get-tuple-element.24), channel_id=1, source_target_pairs={{0,127},{1,64},{2,65},{3,66},{4,67},{5,68},{6,69},{7,70},{8,71},{9... | collective-permute-start | bytes 1572872 | tf_op jit(solution)/shard_map/ppermute | solution.py:432
  77.4 19.9 %collective-permute-start.18 = (f32[2,4,16,8,128]{4,3,2,1,0:T(8,128)S(1)}, f32[2,4,16,8,128]{4,3,2,1,0:T(8,128)S(1)}, u32[]{:S(2)}, u32[]{:S(2)}) collective-permute-start(f32[2,4,16,8,128]{4,3,2,1,0:T(8,128)S(1)} %get-tuple-element.24), channel_id=1, source_target_pairs={{0,65},{1,66},{2,67},{3,68},{4,69},{5,70},{6,71},{7,72},{8,73},{9,... | collective-permute-start | bytes 1572872 | tf_op jit(solution)/shard_map/ppermute | solution.py:432
  87.9 9.4 %collective-permute-start.17 = (f32[2,4,16,8,128]{4,3,2,1,0:T(8,128)S(1)}, f32[2,4,16,8,128]{4,3,2,1,0:T(8,128)S(1)}, u32[]{:S(2)}, u32[]{:S(2)}) collective-permute-start(f32[2,4,16,8,128]{4,3,2,1,0:T(8,128)S(1)} %get-tuple-element.24), channel_id=1, source_target_pairs={{0,64},{1,65},{2,66},{3,67},{4,68},{5,69},{6,70},{7,71},{8,72},{9,... | collective-permute-start | bytes 1572872 | tf_op jit(solution)/shard_map/ppermute | solution.py:432
  98.3 6.2 %copy-start.3 = (f32[2,4,16,8,128]{4,3,2,1,0:T(8,128)S(1)}, f32[2,4,16,8,128]{4,3,2,1,0:T(8,128)}, u32[]{:S(2)}) copy-start(f32[2,4,16,8,128]{4,3,2,1,0:T(8,128)} %copy-done.2) | copy-start | bytes 1572868
  98.3 3.4 %collective-permute-start.22 = (f32[1,4,16,8,128]{4,3,2,1,0:T(8,128)S(1)}, f32[1,4,16,8,128]{4,3,2,1,0:T(8,128)S(1)}, u32[]{:S(2)}, u32[]{:S(2)}) collective-permute-start(f32[1,4,16,8,128]{4,3,2,1,0:T(8,128)S(1)} %shard_map.60), channel_id=1, source_target_pairs={{0,64},{1,65},{2,66},{3,67},{4,68},{5,69},{6,70},{7,71},{8,72},{9,... | collective-permute-start | bytes 786440 | tf_op jit(solution)/shard_map/ppermute | solution.py:432
  99.4 5.1 %collective-permute-start.23 = (f32[1,4,16,8,128]{4,3,2,1,0:T(8,128)S(1)}, f32[1,4,16,8,128]{4,3,2,1,0:T(8,128)S(1)}, u32[]{:S(2)}, u32[]{:S(2)}) collective-permute-start(f32[1,4,16,8,128]{4,3,2,1,0:T(8,128)S(1)} %shard_map.61), channel_id=1, source_target_pairs={{0,64},{1,65},{2,66},{3,67},{4,68},{5,69},{6,70},{7,71},{8,72},{9,... | collective-permute-start | bytes 786440 | tf_op jit(solution)/shard_map/ppermute | solution.py:432

commit v9 on v8

--- a/solution.py
+++ b/solution.py
@@ -234,7 +234,7 @@
                     )
 
 
-def coarse_kernel(worker, position, own, low, high, correction, own_c, explicit, state):
+def coarse_kernel(worker, position, low, high, own, correction, own_c, explicit, state):
     depth = own.shape[1]
 
     @pl.when((position[0] >= worker[0]) & (position[0] <= worker[-1]))
@@ -255,7 +255,7 @@
             )
 
 
-def last_kernel(chosen, position, own, low, high, correction, state):
+def last_kernel(chosen, position, low, high, own, correction, state):
     depth = own.shape[1]
 
     @pl.when(position[0] == 1)
@@ -404,9 +404,9 @@
         target[...] = source[...]
 
 
-def settled(*arrays, tokens=()):
+def settled(*arrays):
     flag = jnp.zeros(1, jnp.int32)
-    return run(settle_kernel, flag, arrays, len(arrays), settling=True, tokens=tokens)
+    return run(settle_kernel, flag, arrays, len(arrays), settling=True)
 
 
 def pick(flag, array, other, tokens=()):
@@ -470,14 +470,14 @@
         return lambda origin, slab: (target, slab + shift) if origin == source else None
 
     def spread(array, source, target, filled=False):
-        def lower(origin, slab):
+        def upper(origin, slab):
             if origin == source:
-                return target, slab + 1
+                return target, slab - 1
             return (origin ^ 1, slab) if filled else None
 
-        low = moved(array, lower)
-        high = moved(array, route(source, target, -1))
-        return moved(array, route(source, target)), low, high
+        low = moved(array, route(source, target, 1))
+        high = moved(array, upper)
+        return low, high, moved(array, route(source, target))
 
     both, own = entered(own, feed, kill)
     half = moved(both, halves)
@@ -489,7 +489,7 @@
     low_b = moved(own_b, onward(1, 1))
     high_b = moved(own_b, onward(1, -1))
     lowest, highest = place == 0, place == ring - 1
-    (low,) = settled(low)
+    low, high = settled(low, high)
     outer_2 = moved(pick(lowest, low, high), far(2))
     explicit, first_end = run(
         fine_kernel,
@@ -503,8 +503,7 @@
     second = spread(explicit, 0, 1)
     mended = pick((lowest & (index == 2)) | (highest & (index == 3)), half_far, half)
     other_x = moved(mended, lambda source, slab: swapped(source, slab) if source >= 2 else None)
-    low_b, high_b = settled(low_b, high_b, tokens=(second[0],))
-    outer_3 = moved(pick(lowest, low_b, high_b), far(3))
+    outer_3 = moved(pick(lowest, low_b, high_b, (explicit,)), far(3))
     even = index % 2 == 0
     other = pick(index == 1, other, other_x)
     low_c = pick(even, mended, other)
@@ -534,7 +533,7 @@
         coarse_kernel, position, (*second, correction, both), 2, worker=(1,)
     )
     third = spread(explicit, 1, 0)
-    crossed_3 = moved(after(correction_3, third[1]), route(3, 1))
+    crossed_3 = moved(after(correction_3, third[0]), route(3, 1))
     explicit, third_end = run(
         coarse_kernel, position, (*third, crossed_2, both), 2, worker=(0,)
     )

time: 106 us -> 97.1 us (0.916)
  Pallas kernels: 20 us -> 14.1 us
  starting transfers between devices: 53 us -> 49.2 us
  waiting for transfers between devices: 29.2 us -> 32.9 us
  local copies, waits for them, and re-layouts: 2.82 us -> 0 us
    pallas_call x23 -> x22, Pallas kernels: 17.7 us -> 12.6 us  [run(): pl.pallas_call(kernel, out_shape=out_shape, in_specs=[SMEM] + [VMEM] * le...]
    ppermute x24, starting transfers between devices: 53 us -> 49.2 us  [moved(): return lax.ppermute(array, AXES, pairs)]
    ppermute x24, waiting for transfers between devices: 29.2 us -> 32.9 us  [moved(): return lax.ppermute(array, AXES, pairs)]
    unnamed x14 -> x0, local copies, waits for them, and re-layouts: 2.82 us -> none
  transfers between devices with their start and end apart: 24 -> 24, of which waited for: 7 -> 9; matrix products, arithmetic and copies ran while one was open for 0% -> 0% of each run, Pallas kernels for 16% -> 11%
where the time goes in v9:
time: 97.1 us; the launch traced here: 96.7 us
  starting transfers between devices  49.2 us (51%)
  waiting for transfers between devices  32.9 us (34%)
  Pallas kernels  14.1 us (15%)
    ppermute x24, starting transfers between devices, moved(): return lax.ppermute(array, AXES, pairs)  49.2 us
    ppermute x24, waiting for transfers between devices, moved(): return lax.ppermute(array, AXES, pairs)  32.9 us
    pallas_call x22, Pallas kernels, run(): pl.pallas_call(kernel, out_shape=out_shape, in_specs=[SMEM] + [VMEM] * le...  12.6 us
  transfers between devices with their start and end apart: 24, of which 9 were waited for; matrix products, arithmetic and copies ran while one was open for 0% of the time, Pallas kernels for 11%

profile of v9, /device:TPU:1, one launch (start us, length us, event | category | flops | bytes accessed | tf_op | source)
XLA Modules:
  0.0 96.7 jit_solution(18258105841437607310)
XLA Ops:
  0.0 1.4 %shard_map.37 = (f32[2,4,16,8,128]{4,3,2,1,0:T(8,128)S(1)}, f32[2,4,16,8,128]{4,3,2,1,0:T(8,128)S(1)}) custom-call(f32[2,4,128,128]{3,2,1,0:T(8,128)} %bitcast.8, f32[4,128,128]{2,1,0:T(8,128)} %feed.1, f32[4,128,128]{2,1,0:T(8,128)} %kill.1), custom_call_target="tpu_custom_call" | custom-call | flops 100000 | bytes 1048576 | tf_op jit(solution)/shard_map/pallas_call | solution.py:325
  1.4 11.6 %collective-permute-start.2 = (f32[2,4,16,8,128]{4,3,2,1,0:T(8,128)S(1)}, f32[2,4,16,8,128]{4,3,2,1,0:T(8,128)S(1)}, u32[]{:S(2)}, u32[]{:S(2)}) collective-permute-start(f32[2,4,16,8,128]{4,3,2,1,0:T(8,128)S(1)} %get-tuple-element.18.refs_5_), channel_id=1, source_target_pairs={{0,1},{1,2},{2,3},{3,4},{4,5},{5,6},{6,7},{7,8},{8,9},{9,10},{10,1... | collective-permute-start | bytes 1572872 | tf_op jit(solution)/shard_map/ppermute | solution.py:432
  13.0 0.7 collective-permute-start
  13.7 1.5 %collective-permute-start.1 = (f32[2,4,16,8,128]{4,3,2,1,0:T(8,128)S(1)}, f32[2,4,16,8,128]{4,3,2,1,0:T(8,128)}, u32[]{:S(2)}, u32[]{:S(2)}) collective-permute-start(f32[2,4,16,8,128]{4,3,2,1,0:T(8,128)S(1)} %get-tuple-element.15.array.refs_2_), channel_id=1, source_target_pairs={{0,63},{1,0},{2,1},{3,2},{4,3},{5,4},{6,5},{7,6},{8,7},{9,8},{10,9... | collective-permute-start | bytes 1572872 | tf_op jit(solution)/shard_map/ppermute | solution.py:432
  15.1 4.5 %collective-permute-done.2.token.refs_4_.refs_2_ = f32[2,4,16,8,128]{4,3,2,1,0:T(8,128)S(1)} collective-permute-done((f32[2,4,16,8,128]{4,3,2,1,0:T(8,128)S(1)}, f32[2,4,16,8,128]{4,3,2,1,0:T(8,128)S(1)}, u32[]{:S(2)}, u32[]{:S(2)}) %collective-permute-start.2) | collective-permute-done | bytes 524320 | tf_op jit(solution)/shard_map/ppermute | solution.py:432
  19.7 0.7 collective-permute-start.10
  20.4 1.5 %collective-permute-start.3 = (f32[2,4,16,8,128]{4,3,2,1,0:T(8,128)S(1)}, f32[2,4,16,8,128]{4,3,2,1,0:T(8,128)S(1)}, u32[]{:S(2)}, u32[]{:S(2)}) collective-permute-start(f32[2,4,16,8,128]{4,3,2,1,0:T(8,128)S(1)} %collective-permute-done.2.token.refs_4_.refs_2_), channel_id=1, source_target_pairs={{0,64},{1,65},{2,66},{3,67},{4,68},{5,69},{6,70},{7,71},{8,72},{9,... | collective-permute-start | bytes 1572872 | tf_op jit(solution)/shard_map/ppermute | solution.py:432
  21.9 1.9 %collective-permute-start.7 = (f32[2,4,16,8,128]{4,3,2,1,0:T(8,128)S(1)}, f32[2,4,16,8,128]{4,3,2,1,0:T(8,128)S(1)}, u32[]{:S(2)}, u32[]{:S(2)}) collective-permute-start(f32[2,4,16,8,128]{4,3,2,1,0:T(8,128)S(1)} %shard_map.39.refs_7_), channel_id=1, source_target_pairs={{64,65},{65,66},{66,67},{67,68},{68,69},{69,70},{70,71},{71,72},{7... | collective-permute-start | bytes 1572872 | tf_op jit(solution)/shard_map/ppermute | solution.py:432
  23.8 0.0 collective-permute-done.refs_1_
  23.8 9.7 %collective-permute-start.9 = (f32[2,4,16,8,128]{4,3,2,1,0:T(8,128)S(1)}, f32[2,4,16,8,128]{4,3,2,1,0:T(8,128)S(1)}, u32[]{:S(2)}, u32[]{:S(2)}) collective-permute-start(f32[2,4,16,8,128]{4,3,2,1,0:T(8,128)S(1)} %shard_map.39.refs_7_), channel_id=1, source_target_pairs={{64,127},{65,64},{66,65},{67,66},{68,67},{69,68},{70,69},{71,70},{... | collective-permute-start | bytes 1572872 | tf_op jit(solution)/shard_map/ppermute | solution.py:432
  33.5 0.0 collective-permute-done.1.refs_2_
  33.6 1.1 %shard_map.38 = (f32[2,4,16,8,128]{4,3,2,1,0:T(8,128)S(1)}, f32[2,4,16,8,128]{4,3,2,1,0:T(8,128)S(1)}) custom-call(s32[1]{0:T(128)} %constant.30.clone.1.refs_0_, f32[2,4,16,8,128]{4,3,2,1,0:T(8,128)S(1)} %collective-permute-done.refs_1_, f32[2,4,16,8,128]{4,3,2,1,0:T(8,128)} %collective-permute-done.1.refs_2_), custom_call_target="tpu_custom_call" | custom-call | flops 1000000000 | bytes 1048576 | tf_op jit(solution)/shard_map/pallas_call | solution.py:372
  34.7 0.7 collective-permute-start.8
  35.4 0.0 collective-permute-done.10.refs_1_
  35.5 0.7 collective-permute-start.11
  36.2 0.0 collective-permute-done.3.refs_6_.refs_1_
  36.2 1.3 %collective-permute-start.4 = (f32[2,4,16,8,128]{4,3,2,1,0:T(8,128)S(1)}, f32[2,4,16,8,128]{4,3,2,1,0:T(8,128)S(1)}, u32[]{:S(2)}, u32[]{:S(2)}) collective-permute-start(f32[2,4,16,8,128]{4,3,2,1,0:T(8,128)S(1)} %get-tuple-element.20.refs_3_), channel_id=1, source_target_pairs={{0,65},{1,66},{2,67},{3,68},{4,69},{5,70},{6,71},{7,72},{8,73},{9,... | collective-permute-start | bytes 1572872 | tf_op jit(solution)/shard_map/ppermute | solution.py:432
  37.5 0.6 collective-permute-done.7.refs_1_.refs_2_
  38.2 1.3 %collective-permute-start.5 = (f32[2,4,16,8,128]{4,3,2,1,0:T(8,128)S(1)}, f32[2,4,16,8,128]{4,3,2,1,0:T(8,128)S(1)}, u32[]{:S(2)}, u32[]{:S(2)}) collective-permute-start(f32[2,4,16,8,128]{4,3,2,1,0:T(8,128)S(1)} %get-tuple-element.20.refs_3_), channel_id=1, source_target_pairs={{0,127},{1,64},{2,65},{3,66},{4,67},{5,68},{6,69},{7,70},{8,71},{9... | collective-permute-start | bytes 1572872 | tf_op jit(solution)/shard_map/ppermute | solution.py:432
  39.5 0.2 collective-permute-done.9.refs_1_.refs_2_
  39.7 1.3 %collective-permute-start.6 = (f32[2,4,16,8,128]{4,3,2,1,0:T(8,128)S(1)}, f32[2,4,16,8,128]{4,3,2,1,0:T(8,128)S(1)}, u32[]{:S(2)}, u32[]{:S(2)}) collective-permute-start(f32[2,4,16,8,128]{4,3,2,1,0:T(8,128)S(1)} %get-tuple-element.20.refs_3_), channel_id=1, source_target_pairs={{0,64},{1,65},{2,66},{3,67},{4,68},{5,69},{6,70},{7,71},{8,72},{9,... | collective-permute-start | bytes 1572872 | tf_op jit(solution)/shard_map/ppermute | solution.py:432
  41.0 0.0 collective-permute-done.8.refs_1_
  41.0 0.7 collective-permute-start.20
  41.9 0.0 collective-permute-done.11.refs_2_
  42.1 5.8 %shard_map.50.refs_4_ = f32[2,4,16,8,128]{4,3,2,1,0:T(8,128)S(1)} custom-call(s32[1]{0:T(128)} %bitcast.refs_0_, f32[2,4,16,8,128]{4,3,2,1,0:T(8,128)S(1)} %shard_map.43.refs_1_, f32[2,4,16,8,128]{4,3,2,1,0:T(8,128)S(1)} %get-tuple-element.15.array.refs_2_, f32[2,4,16,8,128]{4,3,2,1,0:T(8,128)S(1)} %shard_map.45.refs_3_, ...), custom_call_target="tpu_custom_call" | custom-call | flops 10000000000 | bytes 1048576 | tf_op jit(solution)/shard_map/pallas_call | solution.py:372
  47.9 5.2 %collective-permute-done.4.refs_1_ = f32[2,4,16,8,128]{4,3,2,1,0:T(8,128)S(1)} collective-permute-done((f32[2,4,16,8,128]{4,3,2,1,0:T(8,128)S(1)}, f32[2,4,16,8,128]{4,3,2,1,0:T(8,128)S(1)}, u32[]{:S(2)}, u32[]{:S(2)}) %collective-permute-start.4) | collective-permute-done | bytes 524320 | tf_op jit(solution)/shard_map/ppermute | solution.py:432
  53.1 0.0 collective-permute-done.5.refs_2_
  53.1 0.0 collective-permute-done.6.refs_3_
  53.1 2.0 %shard_map.51 = (f32[2,4,16,8,128]{4,3,2,1,0:T(8,128)S(1)}, f32[2,4,16,8,128]{4,3,2,1,0:T(8,128)S(1)}) custom-call(s32[1]{0:T(128)} %bitcast.refs_0_, f32[2,4,16,8,128]{4,3,2,1,0:T(8,128)S(1)} %collective-permute-done.4.refs_1_, f32[2,4,16,8,128]{4,3,2,1,0:T(8,128)S(1)} %collective-permute-done.5.refs_2_, ...), custom_call_target="tpu_custom_call" | custom-call | flops 10000000000 | bytes 1048576 | tf_op jit(solution)/shard_map/pallas_call | solution.py:372
  55.1 1.3 %collective-permute-start.12 = (f32[2,4,16,8,128]{4,3,2,1,0:T(8,128)S(1)}, f32[2,4,16,8,128]{4,3,2,1,0:T(8,128)S(1)}, u32[]{:S(2)}, u32[]{:S(2)}) collective-permute-start(f32[2,4,16,8,128]{4,3,2,1,0:T(8,128)S(1)} %get-tuple-element.22), channel_id=1, source_target_pairs={{64,1},{65,2},{66,3},{67,4},{68,5},{69,6},{70,7},{71,8},{72,9},{73... | collective-permute-start | bytes 1572872 | tf_op jit(solution)/shard_map/ppermute | solution.py:432
  56.4 1.3 %collective-permute-start.13 = (f32[2,4,16,8,128]{4,3,2,1,0:T(8,128)S(1)}, f32[2,4,16,8,128]{4,3,2,1,0:T(8,128)S(1)}, u32[]{:S(2)}, u32[]{:S(2)}) collective-permute-start(f32[2,4,16,8,128]{4,3,2,1,0:T(8,128)S(1)} %get-tuple-element.22), channel_id=1, source_target_pairs={{64,63},{65,0},{66,1},{67,2},{68,3},{69,4},{70,5},{71,6},{72,7},{7... | collective-permute-start | bytes 1572872 | tf_op jit(solution)/shard_map/ppermute | solution.py:432
  57.7 1.3 %collective-permute-start.14 = (f32[2,4,16,8,128]{4,3,2,1,0:T(8,128)S(1)}, f32[2,4,16,8,128]{4,3,2,1,0:T(8,128)S(1)}, u32[]{:S(2)}, u32[]{:S(2)}) collective-permute-start(f32[2,4,16,8,128]{4,3,2,1,0:T(8,128)S(1)} %get-tuple-element.22), channel_id=1, source_target_pairs={{64,0},{65,1},{66,2},{67,3},{68,4},{69,5},{70,6},{71,7},{72,8},{73... | collective-permute-start | bytes 1572872 | tf_op jit(solution)/shard_map/ppermute | solution.py:432
  59.1 0.7 collective-permute-start.15
  59.8 0.0 collective-permute-done.20.refs_1_
  59.9 0.2 shard_map.57.array
  60.1 2.4 %collective-permute-done.12.refs_1_.token = f32[2,4,16,8,128]{4,3,2,1,0:T(8,128)S(1)} collective-permute-done((f32[2,4,16,8,128]{4,3,2,1,0:T(8,128)S(1)}, f32[2,4,16,8,128]{4,3,2,1,0:T(8,128)S(1)}, u32[]{:S(2)}, u32[]{:S(2)}) %collective-permute-start.12) | collective-permute-done | bytes 524320 | tf_op jit(solution)/shard_map/ppermute | solution.py:432
  62.5 1.3 %collective-permute-start.21 = (f32[2,4,16,8,128]{4,3,2,1,0:T(8,128)S(1)}, f32[2,4,16,8,128]{4,3,2,1,0:T(8,128)S(1)}, u32[]{:S(2)}, u32[]{:S(2)}) collective-permute-start(f32[2,4,16,8,128]{4,3,2,1,0:T(8,128)S(1)} %shard_map.58), channel_id=1, source_target_pairs={{192,64},{193,65},{194,66},{195,67},{196,68},{197,69},{198,70},{19... | collective-permute-start | bytes 1572872 | tf_op jit(solution)/shard_map/ppermute | solution.py:432
  63.8 0.0 collective-permute-done.15.refs_1_
  63.9 0.0 collective-permute-done.13.refs_2_
  63.9 0.0 collective-permute-done.14.refs_3_
  63.9 0.7 collective-permute-start.16
  64.6 1.3 %collective-permute-start.17 = (f32[2,4,16,8,128]{4,3,2,1,0:T(8,128)S(1)}, f32[2,4,16,8,128]{4,3,2,1,0:T(8,128)S(1)}, u32[]{:S(2)}, u32[]{:S(2)}) collective-permute-start(f32[2,4,16,8,128]{4,3,2,1,0:T(8,128)S(1)} %get-tuple-element.24), channel_id=1, source_target_pairs={{0,65},{1,66},{2,67},{3,68},{4,69},{5,70},{6,71},{7,72},{8,73},{9,... | collective-permute-start | bytes 1572872 | tf_op jit(solution)/shard_map/ppermute | solution.py:432
  65.9 6.4 %collective-permute-start.18 = (f32[2,4,16,8,128]{4,3,2,1,0:T(8,128)S(1)}, f32[2,4,16,8,128]{4,3,2,1,0:T(8,128)S(1)}, u32[]{:S(2)}, u32[]{:S(2)}) collective-permute-start(f32[2,4,16,8,128]{4,3,2,1,0:T(8,128)S(1)} %get-tuple-element.24), channel_id=1, source_target_pairs={{0,127},{1,64},{2,65},{3,66},{4,67},{5,68},{6,69},{7,70},{8,71},{9... | collective-permute-start | bytes 1572872 | tf_op jit(solution)/shard_map/ppermute | solution.py:432
  72.3 1.3 %collective-permute-start.19 = (f32[2,4,16,8,128]{4,3,2,1,0:T(8,128)S(1)}, f32[2,4,16,8,128]{4,3,2,1,0:T(8,128)S(1)}, u32[]{:S(2)}, u32[]{:S(2)}) collective-permute-start(f32[2,4,16,8,128]{4,3,2,1,0:T(8,128)S(1)} %get-tuple-element.24), channel_id=1, source_target_pairs={{0,64},{1,65},{2,66},{3,67},{4,68},{5,69},{6,70},{7,71},{8,72},{9,... | collective-permute-start | bytes 1572872 | tf_op jit(solution)/shard_map/ppermute | solution.py:432
  73.6 1.5 %collective-permute-done.21.refs_4_ = f32[2,4,16,8,128]{4,3,2,1,0:T(8,128)S(1)} collective-permute-done((f32[2,4,16,8,128]{4,3,2,1,0:T(8,128)S(1)}, f32[2,4,16,8,128]{4,3,2,1,0:T(8,128)S(1)}, u32[]{:S(2)}, u32[]{:S(2)}) %collective-permute-start.21) | collective-permute-done | bytes 524320 | tf_op jit(solution)/shard_map/ppermute | solution.py:432
  75.1 0.0 collective-permute-done.16.refs_5_.refs_3_
  75.1 13.4 %collective-permute-done.17.refs_1_ = f32[2,4,16,8,128]{4,3,2,1,0:T(8,128)S(1)} collective-permute-done((f32[2,4,16,8,128]{4,3,2,1,0:T(8,128)S(1)}, f32[2,4,16,8,128]{4,3,2,1,0:T(8,128)S(1)}, u32[]{:S(2)}, u32[]{:S(2)}) %collective-permute-start.17) | collective-permute-done | bytes 524320 | tf_op jit(solution)/shard_map/ppermute | solution.py:432
  88.5 0.0 collective-permute-done.18.refs_2_
  88.5 0.0 collective-permute-done.19.refs_3_
  88.5 1.0 %shard_map.60 = f32[1,4,16,8,128]{4,3,2,1,0:T(8,128)S(1)} custom-call(s32[1]{0:T(128)} %bitcast.refs_0_, f32[2,4,16,8,128]{4,3,2,1,0:T(8,128)S(1)} %collective-permute-done.17.refs_1_, f32[2,4,16,8,128]{4,3,2,1,0:T(8,128)S(1)} %collective-permute-done.18.refs_2_, f32[2,4,16,8,128]{4,3,2,1,0:T(8,128)S(1)} %collective-permute-done.19.refs_3_, ...), custom_call_target="tpu_custom_call" | custom-call | flops 10000000000 | bytes 1048576 | tf_op jit(solution)/shard_map/pallas_call | solution.py:372
  89.5 0.1 collective-permute-start.23
  89.6 1.0 %shard_map.59 = f32[1,4,16,8,128]{4,3,2,1,0:T(8,128)S(1)} custom-call(s32[1]{0:T(128)} %bitcast.refs_0_, f32[2,4,16,8,128]{4,3,2,1,0:T(8,128)S(1)} %collective-permute-done.17.refs_1_, f32[2,4,16,8,128]{4,3,2,1,0:T(8,128)S(1)} %collective-permute-done.18.refs_2_, f32[2,4,16,8,128]{4,3,2,1,0:T(8,128)S(1)} %collective-permute-done.19.refs_3_, ...), custom_call_target="tpu_custom_call" | custom-call | flops 10000000000 | bytes 1048576 | tf_op jit(solution)/shard_map/pallas_call | solution.py:372
  90.6 0.1 collective-permute-start.22
  90.7 2.2 %collective-permute-done.23.refs_5_ = f32[1,4,16,8,128]{4,3,2,1,0:T(8,128)S(1)} collective-permute-done((f32[1,4,16,8,128]{4,3,2,1,0:T(8,128)S(1)}, f32[1,4,16,8,128]{4,3,2,1,0:T(8,128)S(1)}, u32[]{:S(2)}, u32[]{:S(2)}) %collective-permute-start.23) | collective-permute-done | bytes 262176 | tf_op jit(solution)/shard_map/ppermute | solution.py:432
  92.9 2.8 %collective-permute-done.22.refs_4_ = f32[1,4,16,8,128]{4,3,2,1,0:T(8,128)S(1)} collective-permute-done((f32[1,4,16,8,128]{4,3,2,1,0:T(8,128)S(1)}, f32[1,4,16,8,128]{4,3,2,1,0:T(8,128)S(1)}, u32[]{:S(2)}, u32[]{:S(2)}) %collective-permute-start.22) | collective-permute-done | bytes 262176 | tf_op jit(solution)/shard_map/ppermute | solution.py:432
  95.7 1.0 shard_map.61
  (17 shorter events, 0.7 us)
Async XLA Ops:
  1.4 18.3 %collective-permute-start.2 = (f32[2,4,16,8,128]{4,3,2,1,0:T(8,128)S(1)}, f32[2,4,16,8,128]{4,3,2,1,0:T(8,128)S(1)}, u32[]{:S(2)}, u32[]{:S(2)}) collective-permute-start(f32[2,4,16,8,128]{4,3,2,1,0:T(8,128)S(1)} %get-tuple-element.18.refs_5_), channel_id=1, source_target_pairs={{0,1},{1,2},{2,3},{3,4},{4,5},{5,6},{6,7},{7,8},{8,9},{9,10},{10,1... | collective-permute-start | bytes 1572872 | tf_op jit(solution)/shard_map/ppermute | solution.py:432
  13.0 10.9 %collective-permute-start = (f32[2,4,16,8,128]{4,3,2,1,0:T(8,128)S(1)}, f32[2,4,16,8,128]{4,3,2,1,0:T(8,128)S(1)}, u32[]{:S(2)}, u32[]{:S(2)}) collective-permute-start(f32[2,4,16,8,128]{4,3,2,1,0:T(8,128)S(1)} %get-tuple-element.15.array.refs_2_), channel_id=1, source_target_pairs={{0,1},{1,2},{2,3},{3,4},{4,5},{5,6},{6,7},{7,8},{8,9},{9,10},{10,1... | collective-permute-start | bytes 1572872 | tf_op jit(solution)/shard_map/ppermute | solution.py:432
  13.7 19.9 %collective-permute-start.1 = (f32[2,4,16,8,128]{4,3,2,1,0:T(8,128)S(1)}, f32[2,4,16,8,128]{4,3,2,1,0:T(8,128)}, u32[]{:S(2)}, u32[]{:S(2)}) collective-permute-start(f32[2,4,16,8,128]{4,3,2,1,0:T(8,128)S(1)} %get-tuple-element.15.array.refs_2_), channel_id=1, source_target_pairs={{0,63},{1,0},{2,1},{3,2},{4,3},{5,4},{6,5},{7,6},{8,7},{9,8},{10,9... | collective-permute-start | bytes 1572872 | tf_op jit(solution)/shard_map/ppermute | solution.py:432
  19.7 15.8 %collective-permute-start.10 = (f32[2,4,16,8,128]{4,3,2,1,0:T(8,128)S(1)}, f32[2,4,16,8,128]{4,3,2,1,0:T(8,128)S(1)}, u32[]{:S(2)}, u32[]{:S(2)}) collective-permute-start(f32[2,4,16,8,128]{4,3,2,1,0:T(8,128)S(1)} %collective-permute-done.2.token.refs_4_.refs_2_), channel_id=1, source_target_pairs={{128,132},{132,136},{136,140},{140,144},{144,148},{148,152},{152,1... | collective-permute-start | bytes 1572872 | tf_op jit(solution)/shard_map/ppermute | solution.py:432
  20.4 15.8 %collective-permute-start.3 = (f32[2,4,16,8,128]{4,3,2,1,0:T(8,128)S(1)}, f32[2,4,16,8,128]{4,3,2,1,0:T(8,128)S(1)}, u32[]{:S(2)}, u32[]{:S(2)}) collective-permute-start(f32[2,4,16,8,128]{4,3,2,1,0:T(8,128)S(1)} %collective-permute-done.2.token.refs_4_.refs_2_), channel_id=1, source_target_pairs={{0,64},{1,65},{2,66},{3,67},{4,68},{5,69},{6,70},{7,71},{8,72},{9,... | collective-permute-start | bytes 1572872 | tf_op jit(solution)/shard_map/ppermute | solution.py:432
  21.9 16.3 %collective-permute-start.7 = (f32[2,4,16,8,128]{4,3,2,1,0:T(8,128)S(1)}, f32[2,4,16,8,128]{4,3,2,1,0:T(8,128)S(1)}, u32[]{:S(2)}, u32[]{:S(2)}) collective-permute-start(f32[2,4,16,8,128]{4,3,2,1,0:T(8,128)S(1)} %shard_map.39.refs_7_), channel_id=1, source_target_pairs={{64,65},{65,66},{66,67},{67,68},{68,69},{69,70},{70,71},{71,72},{7... | collective-permute-start | bytes 1572872 | tf_op jit(solution)/shard_map/ppermute | solution.py:432
  23.8 15.8 %collective-permute-start.9 = (f32[2,4,16,8,128]{4,3,2,1,0:T(8,128)S(1)}, f32[2,4,16,8,128]{4,3,2,1,0:T(8,128)S(1)}, u32[]{:S(2)}, u32[]{:S(2)}) collective-permute-start(f32[2,4,16,8,128]{4,3,2,1,0:T(8,128)S(1)} %shard_map.39.refs_7_), channel_id=1, source_target_pairs={{64,127},{65,64},{66,65},{67,66},{68,67},{69,68},{70,69},{71,70},{... | collective-permute-start | bytes 1572872 | tf_op jit(solution)/shard_map/ppermute | solution.py:432
  34.7 6.3 %collective-permute-start.8 = (f32[2,4,16,8,128]{4,3,2,1,0:T(8,128)S(1)}, f32[2,4,16,8,128]{4,3,2,1,0:T(8,128)S(1)}, u32[]{:S(2)}, u32[]{:S(2)}) collective-permute-start(f32[2,4,16,8,128]{4,3,2,1,0:T(8,128)S(1)} %shard_map.41), channel_id=1, source_target_pairs={{128,132},{131,191},{132,136},{135,131},{136,140},{139,135},{140,1... | collective-permute-start | bytes 1572872 | tf_op jit(solution)/shard_map/ppermute | solution.py:432
  35.5 6.4 %collective-permute-start.11 = (f32[2,4,16,8,128]{4,3,2,1,0:T(8,128)S(1)}, f32[2,4,16,8,128]{4,3,2,1,0:T(8,128)S(1)}, u32[]{:S(2)}, u32[]{:S(2)}) collective-permute-start(f32[2,4,16,8,128]{4,3,2,1,0:T(8,128)S(1)} %shard_map.46.refs_1_.refs_2_), channel_id=1, source_target_pairs={{128,192},{129,193},{130,194},{131,195},{132,196},{133,197},{134,1... | collective-permute-start | bytes 1572872 | tf_op jit(solution)/shard_map/ppermute | solution.py:432
  36.2 16.8 %collective-permute-start.4 = (f32[2,4,16,8,128]{4,3,2,1,0:T(8,128)S(1)}, f32[2,4,16,8,128]{4,3,2,1,0:T(8,128)S(1)}, u32[]{:S(2)}, u32[]{:S(2)}) collective-permute-start(f32[2,4,16,8,128]{4,3,2,1,0:T(8,128)S(1)} %get-tuple-element.20.refs_3_), channel_id=1, source_target_pairs={{0,65},{1,66},{2,67},{3,68},{4,69},{5,70},{6,71},{7,72},{8,73},{9,... | collective-permute-start | bytes 1572872 | tf_op jit(solution)/shard_map/ppermute | solution.py:432
  38.2 14.9 %collective-permute-start.5 = (f32[2,4,16,8,128]{4,3,2,1,0:T(8,128)S(1)}, f32[2,4,16,8,128]{4,3,2,1,0:T(8,128)S(1)}, u32[]{:S(2)}, u32[]{:S(2)}) collective-permute-start(f32[2,4,16,8,128]{4,3,2,1,0:T(8,128)S(1)} %get-tuple-element.20.refs_3_), channel_id=1, source_target_pairs={{0,127},{1,64},{2,65},{3,66},{4,67},{5,68},{6,69},{7,70},{8,71},{9... | collective-permute-start | bytes 1572872 | tf_op jit(solution)/shard_map/ppermute | solution.py:432
  39.7 13.4 %collective-permute-start.6 = (f32[2,4,16,8,128]{4,3,2,1,0:T(8,128)S(1)}, f32[2,4,16,8,128]{4,3,2,1,0:T(8,128)S(1)}, u32[]{:S(2)}, u32[]{:S(2)}) collective-permute-start(f32[2,4,16,8,128]{4,3,2,1,0:T(8,128)S(1)} %get-tuple-element.20.refs_3_), channel_id=1, source_target_pairs={{0,64},{1,65},{2,66},{3,67},{4,68},{5,69},{6,70},{7,71},{8,72},{9,... | collective-permute-start | bytes 1572872 | tf_op jit(solution)/shard_map/ppermute | solution.py:432
  41.0 18.8 %collective-permute-start.20 = (f32[2,4,16,8,128]{4,3,2,1,0:T(8,128)S(1)}, f32[2,4,16,8,128]{4,3,2,1,0:T(8,128)S(1)}, u32[]{:S(2)}, u32[]{:S(2)}) collective-permute-start(f32[2,4,16,8,128]{4,3,2,1,0:T(8,128)S(1)} %shard_map.54), channel_id=1, source_target_pairs={{192,196},{195,255},{196,200},{199,195},{200,204},{203,199},{204,2... | collective-permute-start | bytes 1572872 | tf_op jit(solution)/shard_map/ppermute | solution.py:432
  55.1 7.4 %collective-permute-start.12 = (f32[2,4,16,8,128]{4,3,2,1,0:T(8,128)S(1)}, f32[2,4,16,8,128]{4,3,2,1,0:T(8,128)S(1)}, u32[]{:S(2)}, u32[]{:S(2)}) collective-permute-start(f32[2,4,16,8,128]{4,3,2,1,0:T(8,128)S(1)} %get-tuple-element.22), channel_id=1, source_target_pairs={{64,1},{65,2},{66,3},{67,4},{68,5},{69,6},{70,7},{71,8},{72,9},{73... | collective-permute-start | bytes 1572872 | tf_op jit(solution)/shard_map/ppermute | solution.py:432
  56.4 7.5 %collective-permute-start.13 = (f32[2,4,16,8,128]{4,3,2,1,0:T(8,128)S(1)}, f32[2,4,16,8,128]{4,3,2,1,0:T(8,128)S(1)}, u32[]{:S(2)}, u32[]{:S(2)}) collective-permute-start(f32[2,4,16,8,128]{4,3,2,1,0:T(8,128)S(1)} %get-tuple-element.22), channel_id=1, source_target_pairs={{64,63},{65,0},{66,1},{67,2},{68,3},{69,4},{70,5},{71,6},{72,7},{7... | collective-permute-start | bytes 1572872 | tf_op jit(solution)/shard_map/ppermute | solution.py:432
  57.7 6.2 %collective-permute-start.14 = (f32[2,4,16,8,128]{4,3,2,1,0:T(8,128)S(1)}, f32[2,4,16,8,128]{4,3,2,1,0:T(8,128)S(1)}, u32[]{:S(2)}, u32[]{:S(2)}) collective-permute-start(f32[2,4,16,8,128]{4,3,2,1,0:T(8,128)S(1)} %get-tuple-element.22), channel_id=1, source_target_pairs={{64,0},{65,1},{66,2},{67,3},{68,4},{69,5},{70,6},{71,7},{72,8},{73... | collective-permute-start | bytes 1572872 | tf_op jit(solution)/shard_map/ppermute | solution.py:432
  59.1 4.8 %collective-permute-start.15 = (f32[2,4,16,8,128]{4,3,2,1,0:T(8,128)S(1)}, f32[2,4,16,8,128]{4,3,2,1,0:T(8,128)S(1)}, u32[]{:S(2)}, u32[]{:S(2)}) collective-permute-start(f32[2,4,16,8,128]{4,3,2,1,0:T(8,128)S(1)} %shard_map.50.refs_4_), channel_id=1, source_target_pairs={{128,0},{129,1},{130,2},{131,3},{132,4},{133,5},{134,6},{135,7},{1... | collective-permute-start | bytes 1572872 | tf_op jit(solution)/shard_map/ppermute | solution.py:432
  62.5 12.6 %collective-permute-start.21 = (f32[2,4,16,8,128]{4,3,2,1,0:T(8,128)S(1)}, f32[2,4,16,8,128]{4,3,2,1,0:T(8,128)S(1)}, u32[]{:S(2)}, u32[]{:S(2)}) collective-permute-start(f32[2,4,16,8,128]{4,3,2,1,0:T(8,128)S(1)} %shard_map.58), channel_id=1, source_target_pairs={{192,64},{193,65},{194,66},{195,67},{196,68},{197,69},{198,70},{19... | collective-permute-start | bytes 1572872 | tf_op jit(solution)/shard_map/ppermute | solution.py:432
  63.9 11.2 %collective-permute-start.16 = (f32[2,4,16,8,128]{4,3,2,1,0:T(8,128)S(1)}, f32[2,4,16,8,128]{4,3,2,1,0:T(8,128)S(1)}, u32[]{:S(2)}, u32[]{:S(2)}) collective-permute-start(f32[2,4,16,8,128]{4,3,2,1,0:T(8,128)S(1)} %get-tuple-element.23), channel_id=1, source_target_pairs={{0,128},{1,129},{2,130},{3,131},{4,132},{5,133},{6,134},{7,135},{8... | collective-permute-start | bytes 1572872 | tf_op jit(solution)/shard_map/ppermute | solution.py:432
  64.6 23.9 %collective-permute-start.17 = (f32[2,4,16,8,128]{4,3,2,1,0:T(8,128)S(1)}, f32[2,4,16,8,128]{4,3,2,1,0:T(8,128)S(1)}, u32[]{:S(2)}, u32[]{:S(2)}) collective-permute-start(f32[2,4,16,8,128]{4,3,2,1,0:T(8,128)S(1)} %get-tuple-element.24), channel_id=1, source_target_pairs={{0,65},{1,66},{2,67},{3,68},{4,69},{5,70},{6,71},{7,72},{8,73},{9,... | collective-permute-start | bytes 1572872 | tf_op jit(solution)/shard_map/ppermute | solution.py:432
  65.9 22.6 %collective-permute-start.18 = (f32[2,4,16,8,128]{4,3,2,1,0:T(8,128)S(1)}, f32[2,4,16,8,128]{4,3,2,1,0:T(8,128)S(1)}, u32[]{:S(2)}, u32[]{:S(2)}) collective-permute-start(f32[2,4,16,8,128]{4,3,2,1,0:T(8,128)S(1)} %get-tuple-element.24), channel_id=1, source_target_pairs={{0,127},{1,64},{2,65},{3,66},{4,67},{5,68},{6,69},{7,70},{8,71},{9... | collective-permute-start | bytes 1572872 | tf_op jit(solution)/shard_map/ppermute | solution.py:432
  72.3 16.2 %collective-permute-start.19 = (f32[2,4,16,8,128]{4,3,2,1,0:T(8,128)S(1)}, f32[2,4,16,8,128]{4,3,2,1,0:T(8,128)S(1)}, u32[]{:S(2)}, u32[]{:S(2)}) collective-permute-start(f32[2,4,16,8,128]{4,3,2,1,0:T(8,128)S(1)} %get-tuple-element.24), channel_id=1, source_target_pairs={{0,64},{1,65},{2,66},{3,67},{4,68},{5,69},{6,70},{7,71},{8,72},{9,... | collective-permute-start | bytes 1572872 | tf_op jit(solution)/shard_map/ppermute | solution.py:432
  89.5 3.4 %collective-permute-start.23 = (f32[1,4,16,8,128]{4,3,2,1,0:T(8,128)S(1)}, f32[1,4,16,8,128]{4,3,2,1,0:T(8,128)S(1)}, u32[]{:S(2)}, u32[]{:S(2)}) collective-permute-start(f32[1,4,16,8,128]{4,3,2,1,0:T(8,128)S(1)} %shard_map.60), channel_id=1, source_target_pairs={{0,64},{1,65},{2,66},{3,67},{4,68},{5,69},{6,70},{7,71},{8,72},{9,... | collective-permute-start | bytes 786440 | tf_op jit(solution)/shard_map/ppermute | solution.py:432
  90.6 5.1 %collective-permute-start.22 = (f32[1,4,16,8,128]{4,3,2,1,0:T(8,128)S(1)}, f32[1,4,16,8,128]{4,3,2,1,0:T(8,128)S(1)}, u32[]{:S(2)}, u32[]{:S(2)}) collective-permute-start(f32[1,4,16,8,128]{4,3,2,1,0:T(8,128)S(1)} %shard_map.59), channel_id=1, source_target_pairs={{0,64},{1,65},{2,66},{3,67},{4,68},{5,69},{6,70},{7,71},{8,72},{9,... | collective-permute-start | bytes 786440 | tf_op jit(solution)/shard_map/ppermute | solution.py:432
